TPU v7x, 256 devices: a whole 4x4x8 slice. The times are simulated.
256 devices in a mesh: rows: 8 (over x, core), cols: 32 (over z, y).
Axes of the slice: x: 4, y: 4, z: 8, core: 2. Of those that a mesh axis runs over, the one named last changes fastest.
Arguments:
- hidden_states: bfloat16 [2, 2048, 1024], P(None, 'rows', 'cols'), may hold values from -24 to 24
- ln_in_gain: bfloat16 [1024], P('cols'), may hold values from 0.25 to 1.75
- w_in: bfloat16 [1024, 4096], P(None, 'cols'), may hold values from -0.1875 to 0.1875
- w_out: bfloat16 [4096, 1024], P('cols'), may hold values from -0.09375 to 0.09375
- ln_out_gain: bfloat16 [1024], P('cols'), may hold values from 0.25 to 1.75
- prototypes: bfloat16 [65536, 1024], P('cols'), may hold values from -0.375 to 0.375
Outputs:
- embed_grad: float32 [2, 2048, 1024], P(None, 'rows', 'cols')
- proto_grad: float32 [1024, 65536], P('rows', 'cols')
All inputs are finite; a program needn't handle non-finite values.
Results may differ from a plain program's by a relative error of at most 0.0031.
Values may be sent and summed in bfloat16 or wider, within the bound.
No kernel may reach another device: no remote copies, remote signals or barrier semaphores. Data moves between devices by JAX's collectives and lax.ppermute only.
A program may use at most 128 MiB of HBM per device.

v0:
```python
import math

import jax
import jax.numpy as jnp
from jax import lax
from jax.sharding import PartitionSpec as P

D = 1024
PROTOS = 65536
SINK_ITERS = 3


sink_temp = 0.05
soft_temp = 0.1
norm_eps = 1e-05
unit_eps = 1e-06


def normalize(values, total, square, gain):
    center = total / D
    spread = square / D - center * center
    return (
        (values - center[:, None])
        * lax.rsqrt(spread + norm_eps)[:, None]
        * gain.astype(jnp.float32)
    )


def body(hidden_states, ln_in_gain, w_in, w_out, ln_out_gain, prototypes):
    view_count, image_rows, local_width = hidden_states.shape
    row_count = view_count * image_rows
    inputs = hidden_states.reshape(row_count, local_width)
    inputs_f = inputs.astype(jnp.float32)
    total, square = lax.psum(
        (jnp.sum(inputs_f, axis=1), jnp.sum(inputs_f * inputs_f, axis=1)), "cols"
    )
    normed = normalize(inputs_f, total, square, ln_in_gain).astype(jnp.bfloat16)
    whole = lax.all_gather(normed, "cols", axis=1, tiled=True)
    hidden = jax.nn.gelu(
        jnp.dot(whole, w_in, preferred_element_type=jnp.float32), approximate=False
    ).astype(jnp.bfloat16)
    block_part = jnp.dot(hidden, w_out, preferred_element_type=jnp.float32)
    resid = inputs_f + lax.psum_scatter(block_part, "cols", scatter_dimension=1, tiled=True)
    total, square = lax.psum((jnp.sum(resid, axis=1), jnp.sum(resid * resid, axis=1)), "cols")
    final = normalize(resid, total, square, ln_out_gain)
    squared = lax.psum(jnp.sum(final * final, axis=1), "cols")
    embed_part = (final * lax.rsqrt(squared + unit_eps)[:, None]).astype(jnp.bfloat16)
    embed = lax.all_gather(embed_part, "cols", axis=1, tiled=True)
    proto_count = prototypes.shape[0]
    proto_f = prototypes.astype(jnp.float32)
    proto_len = jnp.sqrt(jnp.sum(proto_f * proto_f, axis=1) + unit_eps)
    unit = (proto_f / proto_len[:, None]).astype(jnp.bfloat16)
    flat_scores = lax.dot_general(
        embed, unit, (((1,), (1,)), ((), ())), preferred_element_type=jnp.float32
    )
    scores = flat_scores.reshape(view_count, image_rows, proto_count)
    base = jnp.exp(scores / sink_temp)
    soft = jnp.exp(scores / soft_temp)
    soft_total = lax.psum(jnp.sum(soft, axis=2), "cols")
    scale_image = jnp.ones((view_count, image_rows), jnp.float32)
    scale_proto = jnp.ones((view_count, proto_count), jnp.float32)
    for repeat in range(SINK_ITERS):
        proto_mass = lax.psum(jnp.sum(base * scale_image[:, :, None], axis=1), "rows")
        scale_proto = 1.0 / proto_mass
        image_mass = lax.psum(jnp.sum(base * scale_proto[:, None, :], axis=2), "cols")
        scale_image = 1.0 / image_mass
    codes = base * scale_proto[:, None, :] * scale_image[:, :, None]
    prob = soft / soft_total[:, :, None]
    factor = 0.5 * math.sqrt(PROTOS * D)
    grad_scores = (factor * (prob - codes[::-1])).astype(jnp.bfloat16)
    grad_flat = grad_scores.reshape(row_count, proto_count)
    embed_terms = jnp.dot(grad_flat, unit, preferred_element_type=jnp.float32)
    embed_grad = lax.psum_scatter(embed_terms, "cols", scatter_dimension=1, tiled=True)
    radial = lax.psum(jnp.sum(grad_scores.astype(jnp.float32) * scores, axis=(0, 1)), "rows")
    slice_width = D // lax.axis_size("rows")
    offset = lax.axis_index("rows") * slice_width
    direct = lax.psum_scatter(
        lax.dot_general(
            embed, grad_flat, (((0,), (0,)), ((), ())), preferred_element_type=jnp.float32
        ),
        "rows",
        scatter_dimension=0,
        tiled=True,
    )
    proto_slice = lax.dynamic_slice_in_dim(proto_f, offset, slice_width, 1).T
    proto_grad = (direct - proto_slice * (radial / proto_len)[None, :]) / proto_len[None, :]
    return (embed_grad.reshape(view_count, image_rows, local_width), proto_grad)


def solution(mesh):
    placed = (
        P(None, "rows", "cols"),
        P("cols"),
        P(None, "cols"),
        P("cols", None),
        P("cols"),
        P("cols", None),
    )
    return jax.shard_map(
        body,
        mesh=mesh,
        in_specs=placed,
        out_specs=(P(None, "rows", "cols"), P("rows", "cols")),
        check_vma=False,
    )
```

profile of v0, /device:TPU:1, one launch (start us, length us, event | category | flops | bytes accessed | tf_op | source)
XLA Modules:
  0.0 1189.3 jit_solution(1928385476125420550)
XLA Ops:
  9.5 64.6 %all-reduce.2 = (f32[512]{0:T(512)S(1)}, f32[512]{0:T(512)S(1)}) all-reduce(f32[512]{0:T(512)S(1)} %bitcast.50, f32[512]{0:T(512)S(1)} %bitcast.51), channel_id=1, replica_groups=mesh['rows'=8,'cols'=32] {'cols'}, use_global_device_ids=true, to_apply=%region_3.0 | all-reduce | flops 1024 | bytes 8192 | tf_op jit(solution)/shard_map/psum | solution.py:34
  74.8 80.7 %all-gather.3.cloned.1.call-done = bf16[512,1024]{0,1:T(8,128)(2,1)} async-done(((bf16[512,32]{0,1:T(8,128)(2,1)}), bf16[512,1024]{0,1:T(8,128)(2,1)}) %all-gather.3.cloned.1.call-update) | async-done | bytes 1048592 | tf_op jit(solution)/shard_map/all_gather | solution.py:38
  155.5 4.4 fusion.15
  160.0 212.9 %reduce-scatter.4.cloned.1.call-done = f32[512,32]{0,1:T(8,128)} async-done(((f32[512,1024]{0,1:T(8,128)}), f32[512,32]{0,1:T(8,128)}) %reduce-scatter.4.cloned.1.call-update) | async-done | bytes 65552 | tf_op jit(solution)/shard_map/reduce_scatter | solution.py:43
  372.9 0.9 fusion.80
  373.8 58.3 %all-reduce.1 = (f32[512]{0:T(512)S(1)}, f32[512]{0:T(512)S(1)}) all-reduce(f32[512]{0:T(512)S(1)} %get-tuple-element.7, f32[512]{0:T(512)S(1)} %get-tuple-element.6), channel_id=1, replica_groups=mesh['rows'=8,'cols'=32] {'cols'}, use_global_device_ids=true, to_apply=%region_8.0 | all-reduce | flops 1024 | bytes 8192 | tf_op jit(solution)/shard_map/psum | solution.py:44
  432.2 55.9 %psum.95 = f32[512]{0:T(512)S(1)} all-reduce(f32[512]{0:T(512)S(1)} %multiply_reduce_fusion.4), channel_id=1, replica_groups=mesh['rows'=8,'cols'=32] {'cols'}, use_global_device_ids=true, to_apply=%region_10.0 | all-reduce | flops 512 | bytes 4096 | tf_op jit(solution)/shard_map/psum | solution.py:46
  488.8 6.5 copy.9
  495.3 3.1 multiply_reduce_fusion
  498.4 94.2 %all-gather.5.cloned.1.call-done = bf16[512,1024]{0,1:T(8,128)(2,1)} async-done(((bf16[512,32]{0,1:T(8,128)(2,1)}), bf16[512,1024]{0,1:T(8,128)(2,1)}) %all-gather.5.cloned.1.call-update) | async-done | bytes 1048592 | tf_op jit(solution)/shard_map/all_gather | solution.py:48
  592.6 7.1 fusion.3
  599.7 25.1 %psum.97 = f32[2,2048]{1,0:T(2,128)S(1)} all-reduce(f32[2,2048]{1,0:T(2,128)S(1)} %get-tuple-element.23), channel_id=1, replica_groups=mesh['rows'=8,'cols'=32] {'rows'}, use_global_device_ids=true, to_apply=%region_15.0 | all-reduce | flops 4096 | bytes 32768 | tf_op jit(solution)/shard_map/psum | solution.py:63
  624.9 3.0 fusion.2
  627.8 58.4 %psum.98 = f32[2,256]{1,0:T(2,128)S(1)} all-reduce(f32[2,256]{1,0:T(2,128)S(1)} %reduce_sum.150), channel_id=1, replica_groups=mesh['rows'=8,'cols'=32] {'cols'}, use_global_device_ids=true, to_apply=%region_17.0 | all-reduce | flops 512 | bytes 4096 | tf_op jit(solution)/shard_map/psum | solution.py:65
  686.2 2.9 multiply_reduce_fusion.3
  689.2 37.4 %psum.99 = f32[2,2048]{1,0:T(2,128)S(1)} all-reduce(f32[2,2048]{1,0:T(2,128)S(1)} %multiply_reduce_fusion.3), channel_id=1, replica_groups=mesh['rows'=8,'cols'=32] {'rows'}, use_global_device_ids=true, to_apply=%region_19.0 | all-reduce | flops 4096 | bytes 32768 | tf_op jit(solution)/shard_map/psum | solution.py:63
  726.6 3.6 exponential_reduce_fusion
  730.3 55.8 %psum.100 = f32[2,256]{1,0:T(2,128)S(1)} all-reduce(f32[2,256]{1,0:T(2,128)S(1)} %reduce_sum.153), channel_id=1, replica_groups=mesh['rows'=8,'cols'=32] {'cols'}, use_global_device_ids=true, to_apply=%region_21.0 | all-reduce | flops 512 | bytes 4096 | tf_op jit(solution)/shard_map/psum | solution.py:65
  786.0 2.9 multiply_reduce_fusion.2
  789.0 37.6 %psum.101 = f32[2,2048]{1,0:T(2,128)S(1)} all-reduce(f32[2,2048]{1,0:T(2,128)S(1)} %multiply_reduce_fusion.2), channel_id=1, replica_groups=mesh['rows'=8,'cols'=32] {'rows'}, use_global_device_ids=true, to_apply=%region_23.0 | all-reduce | flops 4096 | bytes 32768 | tf_op jit(solution)/shard_map/psum | solution.py:63
  826.6 2.9 fusion
  829.6 57.8 %all-reduce = (f32[2,256]{1,0:T(2,128)S(1)}, f32[2,256]{1,0:T(2,128)S(1)}) all-reduce(f32[2,256]{1,0:T(2,128)S(1)} %reduce_sum.156, f32[2,256]{1,0:T(2,128)S(1)} %reduce_sum.147), channel_id=1, replica_groups=mesh['rows'=8,'cols'=32] {'cols'}, use_global_device_ids=true, to_apply=%region_25.0 | all-reduce | flops 1024 | bytes 8192 | tf_op jit(solution)/shard_map/psum | solution.py:65
  887.3 3.0 multiply_multiply_fusion
  890.8 1.4 multiply_reduce_fusion.1
  893.0 3.7 fusion.78
  896.8 5.6 fusion.83
  902.4 6.5 convert_element_type.45
  908.9 29.4 %psum.103 = f32[2048]{0:T(1024)S(1)} all-reduce(f32[2048]{0:T(1024)S(1)} %get-tuple-element.16), channel_id=1, replica_groups=mesh['rows'=8,'cols'=32] {'rows'}, use_global_device_ids=true, to_apply=%region_29.0 | all-reduce | flops 2048 | bytes 16384 | tf_op jit(solution)/shard_map/psum | solution.py:74
  938.3 181.5 %reduce-scatter.6.cloned.1.call-done = f32[512,32]{0,1:T(8,128)} async-done(((f32[512,1024]{0,1:T(8,128)}), f32[512,32]{0,1:T(8,128)}) %reduce-scatter.6.cloned.1.call-update) | async-done | bytes 65552 | tf_op jit(solution)/shard_map/reduce_scatter | solution.py:73
  1119.8 1.5 copy.16
  1121.2 58.8 %reduce-scatter.8.cloned.1.call-done = f32[128,2048]{1,0:T(8,128)} async-done(((f32[1024,2048]{1,0:T(8,128)}), f32[128,2048]{1,0:T(8,128)}) %reduce-scatter.8.cloned.1.call-update) | async-done | bytes 1048592 | tf_op jit(solution)/shard_map/reduce_scatter | solution.py:77
  1180.1 2.7 fusion.4
  (45 shorter events, 5.4 us)
Async XLA Ops:
  7.2 148.4 %copy-start = (bf16[128,1024]{1,0:T(8,128)(2,1)S(1)}, bf16[128,1024]{1,0:T(8,128)(2,1)}, u32[]{:S(2)}) copy-start(bf16[128,1024]{1,0:T(8,128)(2,1)} %param.9) | copy-start | bytes 786436
  7.2 148.3 %all-gather.3.cloned.1.call-start = ((), (), s32[]{:S(2)}) async-start(), calls=%async_computation.3 | async-start | bytes 1081344 | tf_op jit(solution)/shard_map/all_gather | solution.py:38
  74.8 85.2 %copy-start.4 = (bf16[32]{0:T(256)(128)(2,1)S(1)}, bf16[32]{0:T(256)(128)(2,1)}, u32[]{:S(2)}) copy-start(bf16[32]{0:T(256)(128)(2,1)} %param.10) | copy-start | bytes 196
  74.8 298.2 %reduce-scatter.4.cloned.1.call-start = ((), (), s32[]{:S(2)}) async-start(), calls=%async_computation.4 | async-start | bytes 2162688 | tf_op jit(solution)/shard_map/reduce_scatter | solution.py:43
  159.9 432.7 %all-gather.5.cloned.1.call-start = ((), (), s32[]{:S(2)}) async-start(), calls=%async_computation.5 | async-start | bytes 1081344 | tf_op jit(solution)/shard_map/all_gather | solution.py:48
  488.8 631.0 %reduce-scatter.6.cloned.1.call-start = ((), (), s32[]{:S(2)}) async-start(), calls=%async_computation.6 | async-start | bytes 2162688 | tf_op jit(solution)/shard_map/reduce_scatter | solution.py:73
  887.3 3.5 copy-start.1
  890.8 2.2 copy-start.2
  893.0 3.8 copy-start.3
  896.8 283.3 %reduce-scatter.8.cloned.1.call-start = ((), (), s32[]{:S(2)}) async-start(), calls=%async_computation.7 | async-start | bytes 9437184 | tf_op jit(solution)/shard_map/reduce_scatter | solution.py:77
Sparse Core Ops, SparseCore 0:
  74.9 80.5 all-gather.2
  160.1 212.8 reduce-scatter.3
  488.9 103.6 all-gather.4
  896.9 222.8 reduce-scatter.5
  1122.2 57.8 reduce-scatter.7
where the time goes:
time: 1190 us
  waiting for transfers between devices  628 us (53%)
  blocking collectives  480 us (40%)
  other arithmetic  36.8 us (3%)
  matrix products  20.8 us (2%)
  between operations  13.9 us (1%)
    reduce_scatter x1, waiting for transfers between devices, body(): lax.psum_scatter(block_part, 'cols', scatter_dimension=1, tiled=True)  213 us
    reduce_scatter x1, waiting for transfers between devices, body(): lax.psum_scatter(embed_terms, 'cols', scatter_dimension=1, tiled=True)  181 us
    psum x3, blocking collectives, body(): lax.psum(jnp.sum(base * scale_proto[:, None, :], axis=2), 'cols')  172 us
    psum x3, blocking collectives, body(): lax.psum(jnp.sum(base * scale_image[:, :, None], axis=1), 'rows')  100 us
    all_gather x1, waiting for transfers between devices, body(): embed = lax.all_gather(embed_part, 'cols', axis=1, tiled=True)  94.2 us
    all_gather x1, waiting for transfers between devices, body(): whole = lax.all_gather(normed, 'cols', axis=1, tiled=True)  80.7 us
    psum x1, blocking collectives, body(): lax.psum((jnp.sum(inputs_f, axis=1), jnp.sum(inputs_f * inputs_f, axis=1)...  64.6 us
    reduce_scatter x1, waiting for transfers between devices, body(): lax.psum_scatter(lax.dot_general(embed, grad_flat, (((0,), (0,)), ((), ()...  58.8 us
  transfers between devices with their start and end apart: 5, of which 5 were waited for; matrix products, arithmetic and copies ran while one was open for 2% of the time, Pallas kernels for 0%

commit v1 on v0

v1 whole, which is shorter than its diff:
```python
import math

import jax
import jax.numpy as jnp
from jax import lax
from jax.sharding import Mesh, PartitionSpec as P

D = 1024
PROTOS = 65536
SINK_ITERS = 3


sink_temp = 0.05
soft_temp = 0.1
norm_eps = 1e-05
unit_eps = 1e-06

ROWS = ("x", "core")
COLS = ("z", "y")
f32 = jnp.float32
bf16 = jnp.bfloat16


def gather_all(values, axes):
    count = lax.axis_size(axes)
    copies = jnp.broadcast_to(values[None], (count,) + values.shape)
    return lax.all_to_all(copies, axes, 0, 0)


def sum_small(values, axes):
    return jnp.sum(gather_all(values, axes), axis=0)


def scatter_sum(blocks, axes):
    return jnp.sum(lax.all_to_all(blocks, axes, 0, 0).astype(f32), axis=0)


def body(hidden_states, ln_in_gain, w_in, w_out, ln_out_gain, prototypes):
    view_count, image_rows, local_width = hidden_states.shape
    row_count = view_count * image_rows
    col_count = lax.axis_size(COLS)
    row_block = row_count // col_count
    col_index = lax.axis_index(COLS)

    gains = gather_all(jnp.stack([ln_in_gain, ln_out_gain]), COLS)
    gain_in = gains[:, 0].reshape(D).astype(f32)
    gain_out = gains[:, 1].reshape(D).astype(f32)

    inputs_t = gather_all(hidden_states.reshape(row_count, local_width).T, COLS).reshape(D, row_count)
    inputs_f = inputs_t.astype(f32)
    center = jnp.mean(inputs_f, axis=0)
    spread = jnp.mean(inputs_f * inputs_f, axis=0) - center * center
    normed_t = (
        (inputs_f - center[None, :]) * lax.rsqrt(spread + norm_eps)[None, :] * gain_in[:, None]
    ).astype(bf16)
    hidden_t = jax.nn.gelu(
        lax.dot_general(w_in, normed_t, (((0,), (0,)), ((), ())), preferred_element_type=f32),
        approximate=False,
    ).astype(bf16)
    block_part = lax.dot_general(
        hidden_t, w_out, (((0,), (0,)), ((), ())), preferred_element_type=f32
    ).astype(bf16)
    block = scatter_sum(block_part.reshape(col_count, row_block, D), COLS)
    picked = (
        jnp.arange(row_count)[None, :] == col_index * row_block + jnp.arange(row_block)[:, None]
    ).astype(bf16)
    own = lax.dot_general(picked, inputs_t, (((1,), (1,)), ((), ())), preferred_element_type=f32)
    resid = own + block
    center = jnp.mean(resid, axis=1, keepdims=True)
    spread = jnp.mean(resid * resid, axis=1, keepdims=True) - center * center
    final = (resid - center) * lax.rsqrt(spread + norm_eps) * gain_out[None, :]
    squared = jnp.sum(final * final, axis=1, keepdims=True)
    embed_part = (final * lax.rsqrt(squared + unit_eps)).astype(bf16)
    embed = gather_all(embed_part, COLS).reshape(row_count, D)

    proto_count = prototypes.shape[0]
    proto_f = prototypes.astype(f32)
    proto_len = jnp.sqrt(jnp.sum(proto_f * proto_f, axis=1) + unit_eps)
    unit = (proto_f / proto_len[:, None]).astype(bf16)
    proto_t = prototypes.T

    flat_scores = lax.dot_general(
        embed, unit, (((1,), (1,)), ((), ())), preferred_element_type=f32
    )
    scores = flat_scores.reshape(view_count, image_rows, proto_count)
    base = jnp.exp(scores / sink_temp)
    soft = jnp.exp(scores / soft_temp)
    soft_part = jnp.sum(soft, axis=2)
    scale_image = jnp.ones((view_count, image_rows), f32)
    scale_proto = jnp.ones((view_count, proto_count), f32)
    soft_total = scale_image
    for repeat in range(SINK_ITERS):
        proto_mass = sum_small(jnp.sum(base * scale_image[:, :, None], axis=1), ROWS)
        scale_proto = 1.0 / proto_mass
        image_part = jnp.sum(base * scale_proto[:, None, :], axis=2)
        if repeat == 0:
            image_mass, soft_total = sum_small(jnp.stack([image_part, soft_part]), COLS)
        else:
            image_mass = sum_small(image_part, COLS)
        scale_image = 1.0 / image_mass
    codes = base * scale_proto[:, None, :] * scale_image[:, :, None]
    prob = soft / soft_total[:, :, None]
    factor = 0.5 * math.sqrt(PROTOS * D)
    grad_scores = (factor * (prob - codes[::-1])).astype(bf16)
    grad_flat = grad_scores.reshape(row_count, proto_count)

    radial = jnp.sum(grad_scores.astype(f32) * scores, axis=(0, 1))
    direct = lax.dot_general(embed, grad_flat, (((0,), (0,)), ((), ())), preferred_element_type=f32)
    proto_part = (direct - proto_t.astype(f32) * (radial / proto_len)[None, :]) / proto_len[None, :]
    core = lax.axis_index("core")
    halves = proto_part.reshape(lax.axis_size("x"), 2, -1, proto_count)
    away = lax.dynamic_index_in_dim(halves, 1 - core, 1, False).astype(bf16)
    stay = lax.dynamic_index_in_dim(halves, core, 1, False)
    arrived = lax.ppermute(away, "core", [(0, 1), (1, 0)])
    paired = (stay + arrived.astype(f32)).astype(bf16)
    proto_grad = scatter_sum(paired, "x")

    embed_terms = lax.dot_general(
        unit, grad_flat, (((0,), (1,)), ((), ())), preferred_element_type=f32
    ).astype(bf16)
    embed_grad_t = scatter_sum(embed_terms.reshape(col_count, local_width, row_count), COLS)
    embed_grad = embed_grad_t.T.reshape(view_count, image_rows, local_width)
    return (embed_grad, proto_grad)


def solution(mesh):
    sizes = {"x": mesh.shape["rows"] // 2, "core": 2, "z": mesh.shape["cols"] // 4, "y": 4}
    fine = Mesh(mesh.devices.reshape(tuple(sizes.values())), tuple(sizes))
    placed = (
        P(None, ROWS, COLS),
        P(COLS),
        P(None, COLS),
        P(COLS, None),
        P(COLS),
        P(COLS, None),
    )
    return jax.shard_map(
        body,
        mesh=fine,
        in_specs=placed,
        out_specs=(P(None, ROWS, COLS), P(ROWS, COLS)),
        check_vma=False,
    )
```

time: 1190 us -> 296 us (0.25)
  waiting for transfers between devices: 628 us -> 127 us
  blocking collectives: 480 us -> 59.7 us
  starting transfers between devices: 0.21 us -> 43.5 us
  between operations: 13.9 us -> 0.9 us
    psum x10 -> x0, blocking collectives: 480 us -> none  [the longest x3 172 us: body(): lax.psum(jnp.sum(base * scale_proto[:, None, :], axis=2), 'cols')]
    reduce_scatter x3 -> x0, waiting for transfers between devices: 453 us -> none  [the longest x1 213 us: body(): lax.psum_scatter(block_part, 'cols', scatter_dimension=1, tiled=True)]
    all_gather x2 -> x0, waiting for transfers between devices: 175 us -> none  [the longest x1 94.2 us: body(): embed = lax.all_gather(embed_part, 'cols', axis=1, tiled=True)]
    all_to_all x0 -> x7, waiting for transfers between devices: none -> 127 us  [the longest x3 70.2 us: scatter_sum(): return jnp.sum(lax.all_to_all(blocks, axes, 0, 0).astype(f32), axis=0)]
    all_to_all x0 -> x5, blocking collectives: none -> 59.7 us  [gather_all(): return lax.all_to_all(copies, axes, 0, 0)]
    all_to_all x0 -> x7, starting transfers between devices: none -> 41.5 us  [the longest x4 27.2 us: gather_all(): return lax.all_to_all(copies, axes, 0, 0)]
  transfers between devices with their start and end apart: 5 -> 8, of which waited for: 5 -> 7; matrix products, arithmetic and copies ran while one was open for 2% -> 7% of each run, Pallas kernels for 0% -> 0%
where the time goes in v1:
time: 296 us; the launch traced here: 292 us
  waiting for transfers between devices  127 us (43%)
  blocking collectives  59.7 us (20%)
  starting transfers between devices  43.5 us (15%)
  other arithmetic  31.1 us (11%)
  matrix products  16 us (5%)
  local copies, waits for them, and re-layouts  13.2 us (4%)
    all_to_all x3, waiting for transfers between devices, scatter_sum(): return jnp.sum(lax.all_to_all(blocks, axes, 0, 0).astype(f32), axis=0)  70.2 us
    all_to_all x5, blocking collectives, gather_all(): return lax.all_to_all(copies, axes, 0, 0)  59.7 us
    all_to_all x4, waiting for transfers between devices, gather_all(): return lax.all_to_all(copies, axes, 0, 0)  57 us
    all_to_all x4, starting transfers between devices, gather_all(): return lax.all_to_all(copies, axes, 0, 0)  27.2 us
    all_to_all x3, starting transfers between devices, scatter_sum(): return jnp.sum(lax.all_to_all(blocks, axes, 0, 0).astype(f32), axis=0)  14.3 us
    reduce_sum x3, other arithmetic, body(): image_part = jnp.sum(base * scale_proto[:, None, :], axis=2)  9.38 us
    unnamed x11, local copies, waits for them, and re-layouts  7.72 us
    dot_general x1, matrix products, body(): lax.dot_general(embed, unit, (((1,), (1,)), ((), ())), preferred_element_...  6.62 us
  transfers between devices with their start and end apart: 8, of which 7 were waited for; matrix products, arithmetic and copies ran while one was open for 7% of the time, Pallas kernels for 0%

profile of v1, /device:TPU:1, one launch (start us, length us, event | category | flops | bytes accessed | tf_op | source)
XLA Modules:
  0.0 291.6 jit_solution(17967825407294176162)
XLA Ops:
  2.0 12.0 %all-to-all-start.1 = ((bf16[32,2,32]{2,1,0:T(2,128)(2,1)}), bf16[32,2,32]{2,1,0:T(2,128)(2,1)S(1)}, u32[]{:S(2)}, u32[]{:S(2)}) async-start(bf16[32,2,32]{2,1,0:T(2,128)(2,1)} %broadcast_in_dim.19), calls=%async_computation.1 | async-start | bytes 32768 | tf_op jit(solution)/shard_map/all_to_all | solution.py:27
  14.8 7.7 %all-to-all-done.1 = bf16[32,2,32]{2,1,0:T(2,128)(2,1)S(1)} async-done(((bf16[32,2,32]{2,1,0:T(2,128)(2,1)}), bf16[32,2,32]{2,1,0:T(2,128)(2,1)S(1)}, u32[]{:S(2)}, u32[]{:S(2)}) %all-to-all-start.1) | async-done | bytes 4128 | tf_op jit(solution)/shard_map/all_to_all | solution.py:27
  23.6 3.9 %all-to-all-start = ((bf16[32,32,512]{2,1,0:T(8,128)(2,1)}), bf16[32,32,512]{2,1,0:T(8,128)(2,1)S(1)}, u32[]{:S(2)}, u32[]{:S(2)}) async-start(bf16[32,32,512]{2,1,0:T(8,128)(2,1)} %broadcast_in_dim.18), calls=%async_computation | async-start | bytes 2097152 | tf_op jit(solution)/shard_map/all_to_all | solution.py:27
  27.8 25.0 %all-to-all-done = bf16[32,32,512]{2,1,0:T(8,128)(2,1)S(1)} async-done(((bf16[32,32,512]{2,1,0:T(8,128)(2,1)}), bf16[32,32,512]{2,1,0:T(8,128)(2,1)S(1)}, u32[]{:S(2)}, u32[]{:S(2)}) %all-to-all-start) | async-done | bytes 1048608 | tf_op jit(solution)/shard_map/all_to_all | solution.py:27
  53.2 2.8 convolution_convert_fusion
  56.0 6.8 %all-to-all-start.2 = ((bf16[32,16,1024]{2,1,0:T(8,128)(2,1)}), bf16[32,16,1024]{2,1,0:T(8,128)(2,1)S(1)}, u32[]{:S(2)}, u32[]{:S(2)}) async-start(bf16[32,16,1024]{2,1,0:T(8,128)(2,1)} %bitcast.6), calls=%async_computation.2 | async-start | bytes 2097152 | tf_op jit(solution)/shard_map/all_to_all | solution.py:35
  62.9 24.3 %all-to-all-done.2 = bf16[32,16,1024]{2,1,0:T(8,128)(2,1)S(1)} async-done(((bf16[32,16,1024]{2,1,0:T(8,128)(2,1)}), bf16[32,16,1024]{2,1,0:T(8,128)(2,1)S(1)}, u32[]{:S(2)}, u32[]{:S(2)}) %all-to-all-start.2) | async-done | bytes 1048608 | tf_op jit(solution)/shard_map/all_to_all | solution.py:35
  89.2 7.4 %all-to-all-start.3 = ((bf16[32,16,1024]{2,1,0:T(8,128)(2,1)}), bf16[32,16,1024]{2,1,0:T(8,128)(2,1)S(1)}, u32[]{:S(2)}, u32[]{:S(2)}) async-start(bf16[32,16,1024]{2,1,0:T(8,128)(2,1)} %broadcast_in_dim.20), calls=%async_computation.3 | async-start | bytes 2097152 | tf_op jit(solution)/shard_map/all_to_all | solution.py:27
  96.6 6.5 %copy.19 = bf16[2048,1024]{0,1:T(8,128)(2,1)} copy(bf16[2048,1024]{1,0:T(8,128)(2,1)} %param.11) | data formatting | bytes 8388608 | tf_op args[5]
  103.1 3.1 %fusion = f32[2048]{0:T(1024)S(1)} fusion(bf16[2048,1024]{0,1:T(8,128)(2,1)} %copy.19), kind=kLoop, calls=%fused_computation.3 | loop fusion | flops 6289408 | bytes 4202496 | tf_op jit(solution)/shard_map/reduce_sum | solution.py:78
  106.2 15.2 %all-to-all-done.3 = bf16[32,16,1024]{2,1,0:T(8,128)(2,1)S(1)} async-done(((bf16[32,16,1024]{2,1,0:T(8,128)(2,1)}), bf16[32,16,1024]{2,1,0:T(8,128)(2,1)S(1)}, u32[]{:S(2)}, u32[]{:S(2)}) %all-to-all-start.3) | async-done | bytes 1048608 | tf_op jit(solution)/shard_map/all_to_all | solution.py:27
  121.4 6.6 %fusion.11 = (f32[2,2048]{1,0:T(2,128)S(1)}, f32[2,256,2048]{2,1,0:T(8,128)}) fusion(bf16[2,256,1024]{2,1,0:T(8,128)(2,1)S(1)} %bitcast.121, f32[2048]{0:T(1024)S(1)} %add_sqrt_fusion, bf16[2048,1024]{0,1:T(8,128)(2,1)} %copy.19), kind=kOutput, calls=%fused_computation.34 | convolution fusion | flops 2155868160 | bytes 9461760 | tf_op jit(solution)/shard_map/dot_general | solution.py:82
  128.1 13.6 %all_to_all.60 = f32[8,2,2048]{2,1,0:T(2,128)S(1)} all-to-all(f32[8,2,2048]{2,1,0:T(2,128)S(1)} %broadcast_in_dim.21), channel_id=1, replica_groups=mesh['x'=4,'core'=2,'z'=8,'y'=4] {'x','core'}, dimensions={0} | all-to-all | bytes 262144 | tf_op jit(solution)/shard_map/all_to_all | solution.py:27
  141.8 3.5 %multiply_reduce_fusion.4 = (f32[2,256]{1,0:T(2,128)S(1)}, f32[2,256]{1,0:T(2,128)S(1)}) fusion(f32[2,2048]{1,0:T(2,128)S(1)} %broadcast_divide_fusion.2, f32[2,256,2048]{2,1,0:T(8,128)} %get-tuple-element.26), kind=kLoop, calls=%fused_computation.19 | loop fusion | flops 5241856 | bytes 4214784 | tf_op jit(solution)/shard_map/reduce_sum | solution.py:95
  145.3 14.4 %all_to_all.61 = f32[32,2,2,256]{3,2,1,0:T(2,128)S(1)} all-to-all(f32[32,2,2,256]{3,2,1,0:T(2,128)S(1)} %broadcast_in_dim.22), channel_id=1, replica_groups=mesh['x'=4,'core'=2,'z'=8,'y'=4] {'z','y'}, dimensions={0} | all-to-all | bytes 262144 | tf_op jit(solution)/shard_map/all_to_all | solution.py:27
  159.8 2.9 %multiply_reduce_fusion.3 = f32[2,2048]{1,0:T(2,128)S(1)} fusion(f32[2,256]{1,0:T(2,128)S(1)} %get-tuple-element.19, f32[2,256,2048]{2,1,0:T(8,128)} %get-tuple-element.26), kind=kLoop, calls=%fused_computation.18 | loop fusion | flops 3141632 | bytes 4212736 | tf_op jit(solution)/shard_map/reduce_sum | solution.py:93
  162.8 10.0 %all_to_all.62 = f32[8,2,2048]{2,1,0:T(2,128)S(1)} all-to-all(f32[8,2,2048]{2,1,0:T(2,128)S(1)} %broadcast_in_dim.23), channel_id=1, replica_groups=mesh['x'=4,'core'=2,'z'=8,'y'=4] {'x','core'}, dimensions={0} | all-to-all | bytes 262144 | tf_op jit(solution)/shard_map/all_to_all | solution.py:27
  172.8 2.9 %multiply_reduce_fusion.2 = f32[2,256]{1,0:T(2,128)S(1)} fusion(f32[2,2048]{1,0:T(2,128)S(1)} %broadcast_divide_fusion.1, f32[2,256,2048]{2,1,0:T(8,128)} %get-tuple-element.26), kind=kLoop, calls=%fused_computation.17 | loop fusion | flops 3145216 | bytes 4212736 | tf_op jit(solution)/shard_map/reduce_sum | solution.py:95
  175.8 11.8 %all_to_all.63 = f32[32,2,256]{2,1,0:T(2,128)S(1)} all-to-all(f32[32,2,256]{2,1,0:T(2,128)S(1)} %broadcast_in_dim.24), channel_id=1, replica_groups=mesh['x'=4,'core'=2,'z'=8,'y'=4] {'z','y'}, dimensions={0} | all-to-all | bytes 131072 | tf_op jit(solution)/shard_map/all_to_all | solution.py:27
  187.6 2.9 %multiply_reduce_fusion.1 = f32[2,2048]{1,0:T(2,128)S(1)} fusion(f32[2,256]{1,0:T(2,128)S(1)} %broadcast_divide_fusion.4, f32[2,256,2048]{2,1,0:T(8,128)} %get-tuple-element.26), kind=kLoop, calls=%fused_computation.16 | loop fusion | flops 3141632 | bytes 4212736 | tf_op jit(solution)/shard_map/reduce_sum | solution.py:93
  190.6 9.9 %all_to_all.64 = f32[8,2,2048]{2,1,0:T(2,128)S(1)} all-to-all(f32[8,2,2048]{2,1,0:T(2,128)S(1)} %broadcast_in_dim.25), channel_id=1, replica_groups=mesh['x'=4,'core'=2,'z'=8,'y'=4] {'x','core'}, dimensions={0} | all-to-all | bytes 262144 | tf_op jit(solution)/shard_map/all_to_all | solution.py:27
  200.6 2.9 %multiply_reduce_fusion.5 = f32[2,256]{1,0:T(2,128)S(1)} fusion(f32[2,2048]{1,0:T(2,128)S(1)} %broadcast_divide_fusion, f32[2,256,2048]{2,1,0:T(8,128)} %get-tuple-element.26), kind=kLoop, calls=%fused_computation.23 | loop fusion | flops 3145216 | bytes 4212736 | tf_op jit(solution)/shard_map/reduce_sum | solution.py:95
  204.2 3.9 %all-to-all-start.9 = ((f32[32,2,256]{2,1,0:T(2,128)}), f32[32,2,256]{2,1,0:T(2,128)S(1)}, u32[]{:S(2)}, u32[]{:S(2)}) async-start(f32[32,2,256]{2,1,0:T(2,128)} %broadcast_in_dim.26), calls=%async_computation.9 | async-start | bytes 131072 | tf_op jit(solution)/shard_map/all_to_all | solution.py:27
  208.1 8.9 %all-to-all-done.9 = f32[32,2,256]{2,1,0:T(2,128)S(1)} async-done(((f32[32,2,256]{2,1,0:T(2,128)}), f32[32,2,256]{2,1,0:T(2,128)S(1)}, u32[]{:S(2)}, u32[]{:S(2)}) %all-to-all-start.9) | async-done | bytes 65568 | tf_op jit(solution)/shard_map/all_to_all | solution.py:27
  217.1 3.0 %multiply_multiply_fusion = f32[2,256,2048]{2,1,0:T(8,128)S(1)} fusion(f32[2,256]{1,0:T(2,128)S(1)} %broadcast_divide_fusion.3, f32[2,2048]{1,0:T(2,128)S(1)} %broadcast_divide_fusion, f32[2,256,2048]{2,1,0:T(8,128)} %get-tuple-element.26), kind=kLoop, calls=%fused_computation.22 | loop fusion | flops 3145728 | bytes 8407040 | tf_op jit(solution)/shard_map/mul | solution.py:101
  222.7 2.7 fusion.4
  227.8 3.3 %convolution_convert_fusion.1 = bf16[1024,512]{1,0:T(8,128)(2,1)} fusion(bf16[512,2048]{1,0:T(8,128)(2,1)S(1)} %bitcast.120, bf16[2048,1024]{0,1:T(8,128)(2,1)S(1)} %copy-done.2, f32[2048]{0:T(1024)S(1)} %add_sqrt_fusion), kind=kOutput, calls=%fused_computation.33 | convolution fusion | flops 2154299392 | bytes 7348224 | tf_op jit(solution)/shard_map/dot_general | solution.py:118
  231.2 3.9 %all-to-all-start.10 = ((bf16[32,32,512]{2,1,0:T(8,128)(2,1)}), bf16[32,32,512]{2,1,0:T(8,128)(2,1)S(1)}, u32[]{:S(2)}, u32[]{:S(2)}) async-start(bf16[32,32,512]{2,1,0:T(8,128)(2,1)} %bitcast.123), calls=%async_computation.10 | async-start | bytes 2097152 | tf_op jit(solution)/shard_map/all_to_all | solution.py:35
  235.1 4.8 %fusion.5 = bf16[4,128,2048]{2,1,0:T(8,128)(2,1)} fusion(bf16[4,128,2048]{2,1,0:T(8,128)(2,1)} %collective-permute-done, f32[4,2,128,2048]{3,2,1,0:T(8,128)} %bitcast.118, s32[]{:T(128)S(6)} %select_n.7), kind=kLoop, calls=%fused_computation.9 | loop fusion | flops 3145728 | bytes 8388612 | tf_op jit(solution)/shard_map/convert_element_type | solution.py:115
  240.0 22.4 %all-to-all-done.10 = bf16[32,32,512]{2,1,0:T(8,128)(2,1)S(1)} async-done(((bf16[32,32,512]{2,1,0:T(8,128)(2,1)}), bf16[32,32,512]{2,1,0:T(8,128)(2,1)S(1)}, u32[]{:S(2)}, u32[]{:S(2)}) %all-to-all-start.10) | async-done | bytes 1048608 | tf_op jit(solution)/shard_map/all_to_all | solution.py:35
  262.4 3.6 %all-to-all-start.11 = ((bf16[4,128,2048]{2,1,0:T(8,128)(2,1)}), bf16[4,128,2048]{2,1,0:T(8,128)(2,1)S(1)}, u32[]{:S(2)}, u32[]{:S(2)}) async-start(bf16[4,128,2048]{2,1,0:T(8,128)(2,1)} %fusion.5), calls=%async_computation.11 | async-start | bytes 4194304 | tf_op jit(solution)/shard_map/all_to_all | solution.py:35
  266.8 23.5 %all-to-all-done.11 = bf16[4,128,2048]{2,1,0:T(8,128)(2,1)S(1)} async-done(((bf16[4,128,2048]{2,1,0:T(8,128)(2,1)}), bf16[4,128,2048]{2,1,0:T(8,128)(2,1)S(1)}, u32[]{:S(2)}, u32[]{:S(2)}) %all-to-all-start.11) | async-done | bytes 2097184 | tf_op jit(solution)/shard_map/all_to_all | solution.py:35
  (55 shorter events, 14.1 us)
Async XLA Ops:
  0.6 52.5 %copy-start = (bf16[128,1024]{1,0:T(8,128)(2,1)S(1)}, bf16[128,1024]{1,0:T(8,128)(2,1)}, u32[]{:S(2)}) copy-start(bf16[128,1024]{1,0:T(8,128)(2,1)} %param.9) | copy-start | bytes 786436
  0.6 52.5 %copy-start.4 = (bf16[1024,128]{1,0:T(8,128)(2,1)S(1)}, bf16[1024,128]{1,0:T(8,128)(2,1)}, u32[]{:S(2)}) copy-start(bf16[1024,128]{1,0:T(8,128)(2,1)} %param.8) | copy-start | bytes 786436
  2.0 20.5 %all-to-all-start.1 = ((bf16[32,2,32]{2,1,0:T(2,128)(2,1)}), bf16[32,2,32]{2,1,0:T(2,128)(2,1)S(1)}, u32[]{:S(2)}, u32[]{:S(2)}) async-start(bf16[32,2,32]{2,1,0:T(2,128)(2,1)} %broadcast_in_dim.19), calls=%async_computation.1 | async-start | bytes 32768 | tf_op jit(solution)/shard_map/all_to_all | solution.py:27
  23.6 29.2 %all-to-all-start = ((bf16[32,32,512]{2,1,0:T(8,128)(2,1)}), bf16[32,32,512]{2,1,0:T(8,128)(2,1)S(1)}, u32[]{:S(2)}, u32[]{:S(2)}) async-start(bf16[32,32,512]{2,1,0:T(8,128)(2,1)} %broadcast_in_dim.18), calls=%async_computation | async-start | bytes 2097152 | tf_op jit(solution)/shard_map/all_to_all | solution.py:27
  56.0 31.2 %all-to-all-start.2 = ((bf16[32,16,1024]{2,1,0:T(8,128)(2,1)}), bf16[32,16,1024]{2,1,0:T(8,128)(2,1)S(1)}, u32[]{:S(2)}, u32[]{:S(2)}) async-start(bf16[32,16,1024]{2,1,0:T(8,128)(2,1)} %bitcast.6), calls=%async_computation.2 | async-start | bytes 2097152 | tf_op jit(solution)/shard_map/all_to_all | solution.py:35
  89.2 32.2 %all-to-all-start.3 = ((bf16[32,16,1024]{2,1,0:T(8,128)(2,1)}), bf16[32,16,1024]{2,1,0:T(8,128)(2,1)S(1)}, u32[]{:S(2)}, u32[]{:S(2)}) async-start(bf16[32,16,1024]{2,1,0:T(8,128)(2,1)} %broadcast_in_dim.20), calls=%async_computation.3 | async-start | bytes 2097152 | tf_op jit(solution)/shard_map/all_to_all | solution.py:27
  204.2 12.8 %all-to-all-start.9 = ((f32[32,2,256]{2,1,0:T(2,128)}), f32[32,2,256]{2,1,0:T(2,128)S(1)}, u32[]{:S(2)}, u32[]{:S(2)}) async-start(f32[32,2,256]{2,1,0:T(2,128)} %broadcast_in_dim.26), calls=%async_computation.9 | async-start | bytes 131072 | tf_op jit(solution)/shard_map/all_to_all | solution.py:27
  217.1 3.5 %copy-start.1 = (f32[2,256,2048]{2,1,0:T(8,128)S(1)}, f32[2,256,2048]{2,1,0:T(8,128)}, u32[]{:S(2)}) copy-start(f32[2,256,2048]{2,1,0:T(8,128)} %get-tuple-element.26) | copy-start | bytes 12582916
  220.6 2.2 copy-start.2
  225.5 5.7 %copy-start.3 = (f32[1024,2048]{1,0:T(8,128)}, f32[1024,2048]{1,0:T(8,128)S(1)}, u32[]{:S(2)}) copy-start(f32[1024,2048]{1,0:T(8,128)S(1)} %fusion.4) | copy-start | bytes 25165828
  225.8 9.3 %collective-permute-start = (bf16[4,128,2048]{2,1,0:T(8,128)(2,1)S(1)}, bf16[4,128,2048]{2,1,0:T(8,128)(2,1)}, u32[]{:S(2)}, u32[]{:S(2)}) collective-permute-start(bf16[4,128,2048]{2,1,0:T(8,128)(2,1)S(1)} %fusion.10), channel_id=1, source_target_pairs={{0,32},{32,0},{1,33},{33,1},{2,34},{34,2},{3,35},{35,3},{4,36},{36... | collective-permute-start | bytes 6291464 | tf_op jit(solution)/shard_map/ppermute | solution.py:114
  231.2 31.2 %all-to-all-start.10 = ((bf16[32,32,512]{2,1,0:T(8,128)(2,1)}), bf16[32,32,512]{2,1,0:T(8,128)(2,1)S(1)}, u32[]{:S(2)}, u32[]{:S(2)}) async-start(bf16[32,32,512]{2,1,0:T(8,128)(2,1)} %bitcast.123), calls=%async_computation.10 | async-start | bytes 2097152 | tf_op jit(solution)/shard_map/all_to_all | solution.py:35
  262.4 27.9 %all-to-all-start.11 = ((bf16[4,128,2048]{2,1,0:T(8,128)(2,1)}), bf16[4,128,2048]{2,1,0:T(8,128)(2,1)S(1)}, u32[]{:S(2)}, u32[]{:S(2)}) async-start(bf16[4,128,2048]{2,1,0:T(8,128)(2,1)} %fusion.5), calls=%async_computation.11 | async-start | bytes 4194304 | tf_op jit(solution)/shard_map/all_to_all | solution.py:35

commit v2 on v1

--- a/solution.py
+++ b/solution.py
@@ -40,29 +40,52 @@
     row_count = view_count * image_rows
     col_count = lax.axis_size(COLS)
     row_block = row_count // col_count
-    col_index = lax.axis_index(COLS)
 
-    gains = gather_all(jnp.stack([ln_in_gain, ln_out_gain]), COLS)
-    gain_in = gains[:, 0].reshape(D).astype(f32)
-    gain_out = gains[:, 1].reshape(D).astype(f32)
+    y_count = lax.axis_size("y")
+    z_count = lax.axis_size("z")
+    tall = row_count // y_count
 
-    inputs_t = gather_all(hidden_states.reshape(row_count, local_width).T, COLS).reshape(D, row_count)
+    states_t = hidden_states.reshape(row_count, local_width).T
+    gain_row = jnp.pad(jnp.concatenate([ln_in_gain, ln_out_gain]), (0, tall - 2 * local_width))
+    pieces = jnp.concatenate(
+        [
+            states_t.reshape(local_width, y_count, tall).transpose(1, 0, 2),
+            jnp.broadcast_to(gain_row[None, None], (y_count, 8, tall)),
+        ],
+        axis=1,
+    )
+    sent = jnp.broadcast_to(pieces[None], (z_count,) + pieces.shape)
+    received = lax.all_to_all(
+        sent.reshape(col_count, local_width + 8, tall), COLS, 0, 0
+    )
+    gains = received[:, local_width]
+    gain_in = gains[:, :local_width].reshape(D).astype(f32)
+    gain_out = gains[:, local_width : 2 * local_width].reshape(D).astype(f32)
+    inputs_t = received[:, :local_width].reshape(D, tall)
+
+    turns = [[(i, (i + step) % y_count) for i in range(y_count)] for step in range(y_count)]
+    first = [w_in] + [lax.ppermute(w_in, "y", turns[step]) for step in range(1, y_count)]
+    second = [w_out] + [lax.ppermute(w_out, "y", turns[step]) for step in range(1, y_count)]
+
     inputs_f = inputs_t.astype(f32)
     center = jnp.mean(inputs_f, axis=0)
     spread = jnp.mean(inputs_f * inputs_f, axis=0) - center * center
     normed_t = (
         (inputs_f - center[None, :]) * lax.rsqrt(spread + norm_eps)[None, :] * gain_in[:, None]
     ).astype(bf16)
-    hidden_t = jax.nn.gelu(
-        lax.dot_general(w_in, normed_t, (((0,), (0,)), ((), ())), preferred_element_type=f32),
-        approximate=False,
-    ).astype(bf16)
-    block_part = lax.dot_general(
-        hidden_t, w_out, (((0,), (0,)), ((), ())), preferred_element_type=f32
-    ).astype(bf16)
-    block = scatter_sum(block_part.reshape(col_count, row_block, D), COLS)
+    block_part = jnp.zeros((tall, D), f32)
+    for enter, leave in zip(first, second):
+        hidden_t = jax.nn.gelu(
+            lax.dot_general(enter, normed_t, (((0,), (0,)), ((), ())), preferred_element_type=f32),
+            approximate=False,
+        ).astype(bf16)
+        block_part = block_part + lax.dot_general(
+            hidden_t, leave, (((0,), (0,)), ((), ())), preferred_element_type=f32
+        )
+    block = scatter_sum(block_part.astype(bf16).reshape(z_count, row_block, D), "z")
     picked = (
-        jnp.arange(row_count)[None, :] == col_index * row_block + jnp.arange(row_block)[:, None]
+        jnp.arange(tall)[None, :]
+        == lax.axis_index("z") * row_block + jnp.arange(row_block)[:, None]
     ).astype(bf16)
     own = lax.dot_general(picked, inputs_t, (((1,), (1,)), ((), ())), preferred_element_type=f32)
     resid = own + block
@@ -71,7 +94,7 @@
     final = (resid - center) * lax.rsqrt(spread + norm_eps) * gain_out[None, :]
     squared = jnp.sum(final * final, axis=1, keepdims=True)
     embed_part = (final * lax.rsqrt(squared + unit_eps)).astype(bf16)
-    embed = gather_all(embed_part, COLS).reshape(row_count, D)
+    embed = gather_all(embed_part, ("y", "z")).reshape(row_count, D)
 
     proto_count = prototypes.shape[0]
     proto_f = prototypes.astype(f32)
@@ -105,15 +128,35 @@
     grad_flat = grad_scores.reshape(row_count, proto_count)
 
     radial = jnp.sum(grad_scores.astype(f32) * scores, axis=(0, 1))
-    direct = lax.dot_general(embed, grad_flat, (((0,), (0,)), ((), ())), preferred_element_type=f32)
-    proto_part = (direct - proto_t.astype(f32) * (radial / proto_len)[None, :]) / proto_len[None, :]
     core = lax.axis_index("core")
-    halves = proto_part.reshape(lax.axis_size("x"), 2, -1, proto_count)
-    away = lax.dynamic_index_in_dim(halves, 1 - core, 1, False).astype(bf16)
-    stay = lax.dynamic_index_in_dim(halves, core, 1, False)
-    arrived = lax.ppermute(away, "core", [(0, 1), (1, 0)])
-    paired = (stay + arrived.astype(f32)).astype(bf16)
-    proto_grad = scatter_sum(paired, "x")
+    x_index = lax.axis_index("x")
+    x_count = lax.axis_size("x")
+    scaled = radial / proto_len
+
+    def proto_part(side):
+        left = lax.dynamic_index_in_dim(embed.reshape(row_count, x_count, 2, -1), side, 2, False)
+        mine = lax.dynamic_index_in_dim(proto_t.reshape(x_count, 2, -1, proto_count), side, 1, False)
+        direct = lax.dot_general(
+            left.reshape(row_count, -1), grad_flat, (((0,), (0,)), ((), ())), preferred_element_type=f32
+        )
+        return (
+            direct - mine.reshape(-1, proto_count).astype(f32) * scaled[None, :]
+        ) / proto_len[None, :]
+
+    away = proto_part(1 - core).astype(bf16)
+    arrived = lax.ppermute(away, "core", [(0, 1), (1, 0)]).reshape(x_count, -1, proto_count)
+    stay = proto_part(core).reshape(x_count, -1, proto_count)
+
+    def paired(block):
+        return lax.dynamic_index_in_dim(stay, block, 0, False) + lax.dynamic_index_in_dim(
+            arrived, block, 0, False
+        ).astype(f32)
+
+    proto_grad = paired(x_index)
+    for step in (2, 1, 3):
+        moved = paired((x_index + step) % x_count).astype(bf16)
+        turn = [(i, (i + step) % x_count) for i in range(x_count)]
+        proto_grad = proto_grad + lax.ppermute(moved, "x", turn).astype(f32)
 
     embed_terms = lax.dot_general(
         unit, grad_flat, (((0,), (1,)), ((), ())), preferred_element_type=f32

time: 296 us -> 281 us (0.949)
  waiting for transfers between devices: 127 us -> 74.6 us
  local copies, waits for them, and re-layouts: 13.2 us -> 53.9 us
  blocking collectives: 59.7 us -> 40 us
  starting transfers between devices: 43.5 us -> 57.9 us
  matrix products: 16 us -> 21 us
    all_to_all x3 -> x2, waiting for transfers between devices: 70.2 us -> 11 us  [scatter_sum(): return jnp.sum(lax.all_to_all(blocks, axes, 0, 0).astype(f32), axis=0)]
    ppermute x1 -> x10, waiting for transfers between devices: 0.01 us -> 31.8 us  [the longest x3 20.3 us: body(): proto_grad = proto_grad + lax.ppermute(moved, 'x', turn).astype(f32)]
    all_to_all x4, waiting for transfers between devices: 57 us -> 26.2 us  [gather_all(): return lax.all_to_all(copies, axes, 0, 0)]
    all_to_all x5 -> x3, blocking collectives: 59.7 us -> 40 us  [gather_all(): return lax.all_to_all(copies, axes, 0, 0)]
    dynamic_slice x0 -> x4, local copies, waits for them, and re-layouts: none -> 16.1 us  [the longest x1 11.3 us: proto_part(): lax.dynamic_index_in_dim(proto_t.reshape(x_count, 2, -1, proto_count), si...]
    unnamed x11 -> x15, local copies, waits for them, and re-layouts: 7.72 us -> 23.7 us
    ppermute x1 -> x10, starting transfers between devices: 2 us -> 15.1 us  [the longest x3 4.71 us: body(): lax.ppermute(w_out, 'y', turns[step])]
    all_to_all x0 -> x1, starting transfers between devices: none -> 12 us  [body(): lax.all_to_all(sent.reshape(col_count, local_width + 8, tall), COLS, 0, 0)]
  transfers between devices with their start and end apart: 8 -> 17, of which waited for: 7 -> 11; matrix products, arithmetic and copies ran while one was open for 7% -> 23% of each run, Pallas kernels for 0% -> 0%
where the time goes in v2:
time: 281 us; the launch traced here: 279 us
  waiting for transfers between devices  74.6 us (27%)
  starting transfers between devices  57.9 us (21%)
  local copies, waits for them, and re-layouts  53.9 us (19%)
  blocking collectives  40 us (14%)
  other arithmetic  30.4 us (11%)
  matrix products  21 us (7%)
    all_to_all x3, blocking collectives, gather_all(): return lax.all_to_all(copies, axes, 0, 0)  40 us
    all_to_all x4, waiting for transfers between devices, gather_all(): return lax.all_to_all(copies, axes, 0, 0)  26.2 us
    unnamed x15, local copies, waits for them, and re-layouts  23.7 us
    all_to_all x4, starting transfers between devices, gather_all(): return lax.all_to_all(copies, axes, 0, 0)  20.4 us
    ppermute x3, waiting for transfers between devices, body(): proto_grad = proto_grad + lax.ppermute(moved, 'x', turn).astype(f32)  20.3 us
    all_to_all x1, starting transfers between devices, body(): lax.all_to_all(sent.reshape(col_count, local_width + 8, tall), COLS, 0, 0)  12 us
    ppermute x3, waiting for transfers between devices, body(): lax.ppermute(w_out, 'y', turns[step])  11.5 us
    dynamic_slice x1, local copies, waits for them, and re-layouts, proto_part(): lax.dynamic_index_in_dim(proto_t.reshape(x_count, 2, -1, proto_count), si...  11.3 us
  transfers between devices with their start and end apart: 17, of which 11 were waited for; matrix products, arithmetic and copies ran while one was open for 23% of the time, Pallas kernels for 0%

profile of v2, /device:TPU:1, one launch (start us, length us, event | category | flops | bytes accessed | tf_op | source)
XLA Modules:
  0.0 278.8 jit_solution(14659978289368373377)
XLA Ops:
  3.0 12.0 %all-to-all-start = ((bf16[32,40,128]{2,1,0:T(8,128)(2,1)}), bf16[32,40,128]{2,1,0:T(8,128)(2,1)S(1)}, u32[]{:S(2)}, u32[]{:S(2)}) async-start(bf16[32,40,128]{2,1,0:T(8,128)(2,1)} %bitcast.2), calls=%async_computation | async-start | bytes 655360 | tf_op jit(solution)/shard_map/all_to_all | solution.py:58
  22.0 5.6 %all-to-all-done = bf16[32,40,128]{2,1,0:T(8,128)(2,1)S(1)} async-done(((bf16[32,40,128]{2,1,0:T(8,128)(2,1)}), bf16[32,40,128]{2,1,0:T(8,128)(2,1)S(1)}, u32[]{:S(2)}, u32[]{:S(2)}) %all-to-all-start) | async-done | bytes 327712 | tf_op jit(solution)/shard_map/all_to_all | solution.py:58
  31.9 6.5 %collective-permute-done.1 = bf16[128,1024]{1,0:T(8,128)(2,1)S(1)} collective-permute-done((bf16[128,1024]{1,0:T(8,128)(2,1)}, bf16[128,1024]{1,0:T(8,128)(2,1)S(1)}, u32[]{:S(2)}, u32[]{:S(2)}) %collective-permute-start.1) | collective-permute-done | bytes 262176 | tf_op jit(solution)/shard_map/ppermute | solution.py:68
  39.6 5.0 %collective-permute-done.3 = bf16[128,1024]{1,0:T(8,128)(2,1)S(1)} collective-permute-done((bf16[128,1024]{1,0:T(8,128)(2,1)S(1)}, bf16[128,1024]{1,0:T(8,128)(2,1)S(1)}, u32[]{:S(2)}, u32[]{:S(2)}) %collective-permute-start.3) | collective-permute-done | bytes 262176 | tf_op jit(solution)/shard_map/ppermute | solution.py:68
  45.9 6.3 %all-to-all-start.1 = ((bf16[8,16,1024]{2,1,0:T(8,128)(2,1)}), bf16[8,16,1024]{2,1,0:T(8,128)(2,1)S(1)}, u32[]{:S(2)}, u32[]{:S(2)}) async-start(bf16[8,16,1024]{2,1,0:T(8,128)(2,1)} %bitcast.12), calls=%async_computation.1 | async-start | bytes 524288 | tf_op jit(solution)/shard_map/all_to_all | solution.py:35
  52.3 9.7 %all-to-all-done.1 = bf16[8,16,1024]{2,1,0:T(8,128)(2,1)S(1)} async-done(((bf16[8,16,1024]{2,1,0:T(8,128)(2,1)}), bf16[8,16,1024]{2,1,0:T(8,128)(2,1)S(1)}, u32[]{:S(2)}, u32[]{:S(2)}) %all-to-all-start.1) | async-done | bytes 262176 | tf_op jit(solution)/shard_map/all_to_all | solution.py:35
  63.8 3.9 %all-to-all-start.2 = ((bf16[32,16,1024]{2,1,0:T(8,128)(2,1)}), bf16[32,16,1024]{2,1,0:T(8,128)(2,1)S(1)}, u32[]{:S(2)}, u32[]{:S(2)}) async-start(bf16[32,16,1024]{2,1,0:T(8,128)(2,1)} %broadcast_in_dim.20), calls=%async_computation.2 | async-start | bytes 2097152 | tf_op jit(solution)/shard_map/all_to_all | solution.py:27
  67.8 3.1 %fusion = f32[2048]{0:T(1024)S(1)} fusion(bf16[2048,1024]{1,0:T(8,128)(2,1)} %param.11), kind=kLoop, calls=%fused_computation.2 | loop fusion | flops 6289408 | bytes 4202496 | tf_op jit(solution)/shard_map/reduce_sum | solution.py:101
  70.9 19.8 %all-to-all-done.2 = bf16[32,16,1024]{2,1,0:T(8,128)(2,1)S(1)} async-done(((bf16[32,16,1024]{2,1,0:T(8,128)(2,1)}), bf16[32,16,1024]{2,1,0:T(8,128)(2,1)S(1)}, u32[]{:S(2)}, u32[]{:S(2)}) %all-to-all-start.2) | async-done | bytes 1048608 | tf_op jit(solution)/shard_map/all_to_all | solution.py:27
  90.7 6.6 %fusion.11 = (f32[2,2048]{1,0:T(2,128)S(1)}, f32[2,256,2048]{2,1,0:T(8,128)}) fusion(bf16[2,256,1024]{2,1,0:T(8,128)(2,1)S(1)} %bitcast.336, f32[2048]{0:T(1024)S(1)} %add_sqrt_fusion, bf16[2048,1024]{1,0:T(8,128)(2,1)} %param.11), kind=kOutput, calls=%fused_computation.29 | convolution fusion | flops 2155868160 | bytes 9461760 | tf_op jit(solution)/shard_map/dot_general | solution.py:105
  97.4 16.0 %all_to_all.50 = f32[8,2,2048]{2,1,0:T(2,128)S(1)} all-to-all(f32[8,2,2048]{2,1,0:T(2,128)S(1)} %broadcast_in_dim.21), channel_id=1, replica_groups=mesh['x'=4,'core'=2,'z'=8,'y'=4] {'x','core'}, dimensions={0} | all-to-all | bytes 262144 | tf_op jit(solution)/shard_map/all_to_all | solution.py:27
  113.5 3.5 %multiply_reduce_fusion.4 = (f32[2,256]{1,0:T(2,128)S(1)}, f32[2,256]{1,0:T(2,128)S(1)}) fusion(f32[2,2048]{1,0:T(2,128)S(1)} %broadcast_divide_fusion.2, f32[2,256,2048]{2,1,0:T(8,128)} %get-tuple-element.35), kind=kLoop, calls=%fused_computation.18 | loop fusion | flops 5241856 | bytes 4214784 | tf_op jit(solution)/shard_map/reduce_sum | solution.py:118
  117.0 13.9 %all_to_all.51 = f32[32,2,2,256]{3,2,1,0:T(2,128)S(1)} all-to-all(f32[32,2,2,256]{3,2,1,0:T(2,128)S(1)} %broadcast_in_dim.22), channel_id=1, replica_groups=mesh['x'=4,'core'=2,'z'=8,'y'=4] {'z','y'}, dimensions={0} | all-to-all | bytes 262144 | tf_op jit(solution)/shard_map/all_to_all | solution.py:27
  131.1 2.9 %multiply_reduce_fusion.3 = f32[2,2048]{1,0:T(2,128)S(1)} fusion(f32[2,256]{1,0:T(2,128)S(1)} %get-tuple-element.28, f32[2,256,2048]{2,1,0:T(8,128)} %get-tuple-element.35), kind=kLoop, calls=%fused_computation.17 | loop fusion | flops 3141632 | bytes 4212736 | tf_op jit(solution)/shard_map/reduce_sum | solution.py:116
  134.0 10.0 %all_to_all.52 = f32[8,2,2048]{2,1,0:T(2,128)S(1)} all-to-all(f32[8,2,2048]{2,1,0:T(2,128)S(1)} %broadcast_in_dim.23), channel_id=1, replica_groups=mesh['x'=4,'core'=2,'z'=8,'y'=4] {'x','core'}, dimensions={0} | all-to-all | bytes 262144 | tf_op jit(solution)/shard_map/all_to_all | solution.py:27
  144.1 2.9 %multiply_reduce_fusion.2 = f32[2,256]{1,0:T(2,128)S(1)} fusion(f32[2,2048]{1,0:T(2,128)S(1)} %broadcast_divide_fusion.1, f32[2,256,2048]{2,1,0:T(8,128)} %get-tuple-element.35), kind=kLoop, calls=%fused_computation.16 | loop fusion | flops 3145216 | bytes 4212736 | tf_op jit(solution)/shard_map/reduce_sum | solution.py:118
  147.7 3.9 %all-to-all-start.6 = ((f32[32,2,256]{2,1,0:T(2,128)}), f32[32,2,256]{2,1,0:T(2,128)S(1)}, u32[]{:S(2)}, u32[]{:S(2)}) async-start(f32[32,2,256]{2,1,0:T(2,128)} %broadcast_in_dim.24), calls=%async_computation.6 | async-start | bytes 131072 | tf_op jit(solution)/shard_map/all_to_all | solution.py:27
  151.6 7.7 %reshape.181 = bf16[4,2,128,2048]{2,1,0,3:T(2,128)(2,1)} reshape(bf16[1024,2048]{0,1:T(8,128)(2,1)} %bitcast.333) | data formatting | bytes 8388608 | tf_op jit(solution)/shard_map/reshape | solution.py:138
  164.2 5.2 %all-to-all-start.7 = ((f32[8,2,2048]{2,1,0:T(2,128)}), f32[8,2,2048]{2,1,0:T(2,128)S(1)}, u32[]{:S(2)}, u32[]{:S(2)}) async-start(f32[8,2,2048]{2,1,0:T(2,128)} %broadcast_in_dim.25), calls=%async_computation.7 | async-start | bytes 262144 | tf_op jit(solution)/shard_map/all_to_all | solution.py:27
  169.4 11.3 %constant_dynamic-slice_fusion = (bf16[4,1,128,2048]{2,1,0,3:T(2,128)(2,1)}, bf16[4,1,128,2048]{2,1,0,3:T(2,128)(2,1)}) fusion(bf16[4,2,128,2048]{2,1,0,3:T(2,128)(2,1)} %reshape.181, s32[]{:T(128)S(6)} %select_n.45, s32[]{:T(128)S(6)} %select_n.43), kind=kLoop, calls=%fused_computation.281 | loop fusion | bytes 8388616 | tf_op jit(solution)/shard_map/jit(dynamic_index_in_dim)/dynamic_slice | solution.py:138
  180.7 10.6 %copy.52 = bf16[4,1,128,2048]{3,2,0,1:T(8,128)(2,1)} copy(bf16[4,1,128,2048]{2,1,0,3:T(2,128)(2,1)} %get-tuple-element.21) | data formatting | bytes 4194304
  192.1 2.9 %multiply_reduce_fusion.5 = f32[2,256]{1,0:T(2,128)S(1)} fusion(f32[2,2048]{1,0:T(2,128)S(1)} %broadcast_divide_fusion, f32[2,256,2048]{2,1,0:T(8,128)} %get-tuple-element.35), kind=kLoop, calls=%fused_computation.22 | loop fusion | flops 3145216 | bytes 4212736 | tf_op jit(solution)/shard_map/reduce_sum | solution.py:118
  195.7 7.4 %all-to-all-start.8 = ((f32[32,2,256]{2,1,0:T(2,128)}), f32[32,2,256]{2,1,0:T(2,128)S(1)}, u32[]{:S(2)}, u32[]{:S(2)}) async-start(f32[32,2,256]{2,1,0:T(2,128)} %broadcast_in_dim.26), calls=%async_computation.8 | async-start | bytes 131072 | tf_op jit(solution)/shard_map/all_to_all | solution.py:27
  206.7 5.1 %all-to-all-done.8 = f32[32,2,256]{2,1,0:T(2,128)S(1)} async-done(((f32[32,2,256]{2,1,0:T(2,128)}), f32[32,2,256]{2,1,0:T(2,128)S(1)}, u32[]{:S(2)}, u32[]{:S(2)}) %all-to-all-start.8) | async-done | bytes 65568 | tf_op jit(solution)/shard_map/all_to_all | solution.py:27
  211.8 3.0 %multiply_multiply_fusion = f32[2,256,2048]{2,1,0:T(8,128)S(1)} fusion(f32[2,256]{1,0:T(2,128)S(1)} %broadcast_divide_fusion.3, f32[2,2048]{1,0:T(2,128)S(1)} %broadcast_divide_fusion, f32[2,256,2048]{2,1,0:T(8,128)} %get-tuple-element.35), kind=kLoop, calls=%fused_computation.21 | loop fusion | flops 3145728 | bytes 8407040 | tf_op jit(solution)/shard_map/mul | solution.py:124
  221.1 3.8 %convolution_convert_fusion = bf16[1024,512]{1,0:T(8,128)(2,1)} fusion(bf16[512,2048]{1,0:T(8,128)(2,1)S(1)} %bitcast.339, bf16[2048,1024]{1,0:T(8,128)(2,1)S(1)} %copy-done.1, f32[2048]{0:T(1024)S(1)} %add_sqrt_fusion), kind=kOutput, calls=%fused_computation.25 | convolution fusion | flops 2154299392 | bytes 7348224 | tf_op jit(solution)/shard_map/dot_general | solution.py:161
  224.9 3.9 %all-to-all-start.9 = ((bf16[32,32,512]{2,1,0:T(8,128)(2,1)}), bf16[32,32,512]{2,1,0:T(8,128)(2,1)S(1)}, u32[]{:S(2)}, u32[]{:S(2)}) async-start(bf16[32,32,512]{2,1,0:T(8,128)(2,1)} %bitcast.20), calls=%async_computation.9 | async-start | bytes 2097152 | tf_op jit(solution)/shard_map/all_to_all | solution.py:35
  228.9 10.6 %copy.51 = bf16[4,1,128,2048]{3,2,0,1:T(8,128)(2,1)} copy(bf16[4,1,128,2048]{2,1,0,3:T(2,128)(2,1)} %get-tuple-element.22) | data formatting | bytes 4194304
  240.8 3.5 %fusion.6 = f32[512,2048]{1,0:T(8,128)S(1)} fusion(bf16[512,2048]{1,0:T(8,128)(2,1)} %bitcast.342, bf16[512,512]{0,1:T(8,128)(2,1)S(1)} %bitcast.344, bf16[512,2048]{1,0:T(8,128)(2,1)} %bitcast.340, f32[2048]{0:T(1024)S(1)} %add_sqrt_fusion, f32[2048]{0:T(1024)S(1)} %rsqrt_multiply_fusion), kind=kOutput, calls=%fused_computation.10 | convolution fusion | flops 1077936128 | bytes 8929280 | tf_op jit(solution)/shard_map/dot_general | solution.py:139
  249.1 3.1 %collective-permute-start.7 = (bf16[128,2048]{1,0:T(8,128)(2,1)}, bf16[128,2048]{1,0:T(8,128)(2,1)S(1)}, u32[]{:S(2)}, u32[]{:S(2)}) collective-permute-start(bf16[128,2048]{1,0:T(8,128)(2,1)} %get-tuple-element.18), channel_id=1, source_target_pairs={{0,128},{64,192},{128,0},{192,64},{1,129},{65,193},{129,1},{193,65... | collective-permute-start | bytes 1572872 | tf_op jit(solution)/shard_map/ppermute | solution.py:159
  255.8 8.1 %collective-permute-done.7 = bf16[128,2048]{1,0:T(8,128)(2,1)S(1)} collective-permute-done((bf16[128,2048]{1,0:T(8,128)(2,1)}, bf16[128,2048]{1,0:T(8,128)(2,1)S(1)}, u32[]{:S(2)}, u32[]{:S(2)}) %collective-permute-start.7) | collective-permute-done | bytes 524320 | tf_op jit(solution)/shard_map/ppermute | solution.py:159
  263.8 11.6 %collective-permute-done.9 = bf16[128,2048]{1,0:T(8,128)(2,1)S(1)} collective-permute-done((bf16[128,2048]{1,0:T(8,128)(2,1)}, bf16[128,2048]{1,0:T(8,128)(2,1)S(1)}, u32[]{:S(2)}, u32[]{:S(2)}) %collective-permute-start.9) | collective-permute-done | bytes 524320 | tf_op jit(solution)/shard_map/ppermute | solution.py:159
  (90 shorter events, 47.8 us)
Async XLA Ops:
  0.6 29.2 %copy-start.5 = (bf16[128,1024]{1,0:T(8,128)(2,1)S(1)}, bf16[128,1024]{1,0:T(8,128)(2,1)}, u32[]{:S(2)}) copy-start(bf16[128,1024]{1,0:T(8,128)(2,1)} %param.9) | copy-start | bytes 786436
  3.0 24.6 %all-to-all-start = ((bf16[32,40,128]{2,1,0:T(8,128)(2,1)}), bf16[32,40,128]{2,1,0:T(8,128)(2,1)S(1)}, u32[]{:S(2)}, u32[]{:S(2)}) async-start(bf16[32,40,128]{2,1,0:T(8,128)(2,1)} %bitcast.2), calls=%async_computation | async-start | bytes 655360 | tf_op jit(solution)/shard_map/all_to_all | solution.py:58
  15.1 14.7 %collective-permute-start = (bf16[1024,128]{1,0:T(8,128)(2,1)}, bf16[1024,128]{1,0:T(8,128)(2,1)S(1)}, u32[]{:S(2)}, u32[]{:S(2)}) collective-permute-start(bf16[1024,128]{1,0:T(8,128)(2,1)} %param.8), channel_id=1, source_target_pairs={{0,1},{1,2},{2,3},{3,0},{4,5},{5,6},{6,7},{7,4},{8,9},{9,10},{10,1... | collective-permute-start | bytes 786440 | tf_op jit(solution)/shard_map/ppermute | solution.py:67
  16.4 22.6 %collective-permute-start.4 = (bf16[1024,128]{1,0:T(8,128)(2,1)}, bf16[1024,128]{1,0:T(8,128)(2,1)S(1)}, u32[]{:S(2)}, u32[]{:S(2)}) collective-permute-start(bf16[1024,128]{1,0:T(8,128)(2,1)} %param.8), channel_id=1, source_target_pairs={{0,3},{1,0},{2,1},{3,2},{4,7},{5,4},{6,5},{7,6},{8,11},{9,8},{10,9... | collective-permute-start | bytes 786440 | tf_op jit(solution)/shard_map/ppermute | solution.py:67
  17.8 21.7 %collective-permute-start.2 = (bf16[1024,128]{1,0:T(8,128)(2,1)}, bf16[1024,128]{1,0:T(8,128)(2,1)S(1)}, u32[]{:S(2)}, u32[]{:S(2)}) collective-permute-start(bf16[1024,128]{1,0:T(8,128)(2,1)} %param.8), channel_id=1, source_target_pairs={{0,2},{1,3},{2,0},{3,1},{4,6},{5,7},{6,4},{7,5},{8,10},{9,11},{10,... | collective-permute-start | bytes 786440 | tf_op jit(solution)/shard_map/ppermute | solution.py:67
  19.4 19.0 %collective-permute-start.1 = (bf16[128,1024]{1,0:T(8,128)(2,1)}, bf16[128,1024]{1,0:T(8,128)(2,1)S(1)}, u32[]{:S(2)}, u32[]{:S(2)}) collective-permute-start(bf16[128,1024]{1,0:T(8,128)(2,1)} %param.9), channel_id=1, source_target_pairs={{0,1},{1,2},{2,3},{3,0},{4,5},{5,6},{6,7},{7,4},{8,9},{9,10},{10,1... | collective-permute-start | bytes 786440 | tf_op jit(solution)/shard_map/ppermute | solution.py:68
  19.6 19.3 %collective-permute-start.5 = (bf16[128,1024]{1,0:T(8,128)(2,1)}, bf16[128,1024]{1,0:T(8,128)(2,1)S(1)}, u32[]{:S(2)}, u32[]{:S(2)}) collective-permute-start(bf16[128,1024]{1,0:T(8,128)(2,1)} %param.9), channel_id=1, source_target_pairs={{0,3},{1,0},{2,1},{3,2},{4,7},{5,4},{6,5},{7,6},{8,11},{9,8},{10,9... | collective-permute-start | bytes 786440 | tf_op jit(solution)/shard_map/ppermute | solution.py:68
  29.8 14.8 %collective-permute-start.3 = (bf16[128,1024]{1,0:T(8,128)(2,1)S(1)}, bf16[128,1024]{1,0:T(8,128)(2,1)S(1)}, u32[]{:S(2)}, u32[]{:S(2)}) collective-permute-start(bf16[128,1024]{1,0:T(8,128)(2,1)S(1)} %copy-done.5), channel_id=1, source_target_pairs={{0,2},{1,3},{2,0},{3,1},{4,6},{5,7},{6,4},{7,5},{8,10},{9,11},{10,... | collective-permute-start | bytes 786440 | tf_op jit(solution)/shard_map/ppermute | solution.py:68
  45.9 16.2 %all-to-all-start.1 = ((bf16[8,16,1024]{2,1,0:T(8,128)(2,1)}), bf16[8,16,1024]{2,1,0:T(8,128)(2,1)S(1)}, u32[]{:S(2)}, u32[]{:S(2)}) async-start(bf16[8,16,1024]{2,1,0:T(8,128)(2,1)} %bitcast.12), calls=%async_computation.1 | async-start | bytes 524288 | tf_op jit(solution)/shard_map/all_to_all | solution.py:35
  63.8 26.9 %all-to-all-start.2 = ((bf16[32,16,1024]{2,1,0:T(8,128)(2,1)}), bf16[32,16,1024]{2,1,0:T(8,128)(2,1)S(1)}, u32[]{:S(2)}, u32[]{:S(2)}) async-start(bf16[32,16,1024]{2,1,0:T(8,128)(2,1)} %broadcast_in_dim.20), calls=%async_computation.2 | async-start | bytes 2097152 | tf_op jit(solution)/shard_map/all_to_all | solution.py:27
  147.7 12.8 %all-to-all-start.6 = ((f32[32,2,256]{2,1,0:T(2,128)}), f32[32,2,256]{2,1,0:T(2,128)S(1)}, u32[]{:S(2)}, u32[]{:S(2)}) async-start(f32[32,2,256]{2,1,0:T(2,128)} %broadcast_in_dim.24), calls=%async_computation.6 | async-start | bytes 131072 | tf_op jit(solution)/shard_map/all_to_all | solution.py:27
  164.2 27.8 %all-to-all-start.7 = ((f32[8,2,2048]{2,1,0:T(2,128)}), f32[8,2,2048]{2,1,0:T(2,128)S(1)}, u32[]{:S(2)}, u32[]{:S(2)}) async-start(f32[8,2,2048]{2,1,0:T(2,128)} %broadcast_in_dim.25), calls=%async_computation.7 | async-start | bytes 262144 | tf_op jit(solution)/shard_map/all_to_all | solution.py:27
  195.7 16.1 %all-to-all-start.8 = ((f32[32,2,256]{2,1,0:T(2,128)}), f32[32,2,256]{2,1,0:T(2,128)S(1)}, u32[]{:S(2)}, u32[]{:S(2)}) async-start(f32[32,2,256]{2,1,0:T(2,128)} %broadcast_in_dim.26), calls=%async_computation.8 | async-start | bytes 131072 | tf_op jit(solution)/shard_map/all_to_all | solution.py:27
  211.8 3.5 %copy-start = (f32[2,256,2048]{2,1,0:T(8,128)S(1)}, f32[2,256,2048]{2,1,0:T(8,128)}, u32[]{:S(2)}) copy-start(f32[2,256,2048]{2,1,0:T(8,128)} %get-tuple-element.35) | copy-start | bytes 12582916
  215.3 1.6 copy-start.4
  216.7 4.4 %copy-start.3 = (bf16[2,256,2048]{2,1,0:T(8,128)(2,1)}, bf16[2,256,2048]{2,1,0:T(8,128)(2,1)S(1)}, u32[]{:S(2)}) copy-start(bf16[2,256,2048]{2,1,0:T(8,128)(2,1)S(1)} %get-tuple-element.17) | copy-start | bytes 6291460
  216.9 4.2 %copy-start.1 = (bf16[2048,1024]{1,0:T(8,128)(2,1)S(1)}, bf16[2048,1024]{1,0:T(8,128)(2,1)}, u32[]{:S(2)}) copy-start(bf16[2048,1024]{1,0:T(8,128)(2,1)} %param.11) | copy-start | bytes 12582916
  219.6 24.8 %collective-permute-start.6 = (bf16[512,2048]{1,0:T(8,128)(2,1)}, bf16[512,2048]{1,0:T(8,128)(2,1)}, u32[]{:S(2)}, u32[]{:S(2)}) collective-permute-start(bf16[512,2048]{1,0:T(8,128)(2,1)} %fusion.4), channel_id=1, source_target_pairs={{0,32},{32,0},{1,33},{33,1},{2,34},{34,2},{3,35},{35,3},{4,36},{36... | collective-permute-start | bytes 6291464 | tf_op jit(solution)/shard_map/ppermute | solution.py:147
  224.9 30.1 %all-to-all-start.9 = ((bf16[32,32,512]{2,1,0:T(8,128)(2,1)}), bf16[32,32,512]{2,1,0:T(8,128)(2,1)S(1)}, u32[]{:S(2)}, u32[]{:S(2)}) async-start(bf16[32,32,512]{2,1,0:T(8,128)(2,1)} %bitcast.20), calls=%async_computation.9 | async-start | bytes 2097152 | tf_op jit(solution)/shard_map/all_to_all | solution.py:35
  244.3 1.9 copy-start.2
  249.1 14.7 %collective-permute-start.7 = (bf16[128,2048]{1,0:T(8,128)(2,1)}, bf16[128,2048]{1,0:T(8,128)(2,1)S(1)}, u32[]{:S(2)}, u32[]{:S(2)}) collective-permute-start(bf16[128,2048]{1,0:T(8,128)(2,1)} %get-tuple-element.18), channel_id=1, source_target_pairs={{0,128},{64,192},{128,0},{192,64},{1,129},{65,193},{129,1},{193,65... | collective-permute-start | bytes 1572872 | tf_op jit(solution)/shard_map/ppermute | solution.py:159
  252.3 23.2 %collective-permute-start.9 = (bf16[128,2048]{1,0:T(8,128)(2,1)}, bf16[128,2048]{1,0:T(8,128)(2,1)S(1)}, u32[]{:S(2)}, u32[]{:S(2)}) collective-permute-start(bf16[128,2048]{1,0:T(8,128)(2,1)} %get-tuple-element.19), channel_id=1, source_target_pairs={{0,192},{64,0},{128,64},{192,128},{1,193},{65,1},{129,65},{193,129... | collective-permute-start | bytes 1572872 | tf_op jit(solution)/shard_map/ppermute | solution.py:159
  253.1 22.9 %collective-permute-start.8 = (bf16[128,2048]{1,0:T(8,128)(2,1)S(1)}, bf16[128,2048]{1,0:T(8,128)(2,1)S(1)}, u32[]{:S(2)}, u32[]{:S(2)}) collective-permute-start(bf16[128,2048]{1,0:T(8,128)(2,1)S(1)} %get-tuple-element.20), channel_id=1, source_target_pairs={{0,64},{64,128},{128,192},{192,0},{1,65},{65,129},{129,193},{193,1... | collective-permute-start | bytes 1572872 | tf_op jit(solution)/shard_map/ppermute | solution.py:159

commit v3 on v2

--- a/solution.py
+++ b/solution.py
@@ -63,9 +63,19 @@
     gain_out = gains[:, local_width : 2 * local_width].reshape(D).astype(f32)
     inputs_t = received[:, :local_width].reshape(D, tall)
 
-    turns = [[(i, (i + step) % y_count) for i in range(y_count)] for step in range(y_count)]
-    first = [w_in] + [lax.ppermute(w_in, "y", turns[step]) for step in range(1, y_count)]
-    second = [w_out] + [lax.ppermute(w_out, "y", turns[step]) for step in range(1, y_count)]
+    core = lax.axis_index("core")
+    swap = [(0, 1), (1, 0)]
+    w_in_t = w_in.T
+    share = jnp.where(core == 0, w_in_t, w_out)
+    shares = jnp.stack(
+        [
+            lax.ppermute(share, "y", [(i, (i + step) % y_count) for i in range(y_count)])
+            for step in range(1, y_count)
+        ]
+    )
+    others = lax.ppermute(shares, "core", swap)
+    first = [w_in_t] + list(jnp.where(core == 0, shares, others))
+    second = [w_out] + list(jnp.where(core == 0, others, shares))
 
     inputs_f = inputs_t.astype(f32)
     center = jnp.mean(inputs_f, axis=0)
@@ -76,7 +86,7 @@
     block_part = jnp.zeros((tall, D), f32)
     for enter, leave in zip(first, second):
         hidden_t = jax.nn.gelu(
-            lax.dot_general(enter, normed_t, (((0,), (0,)), ((), ())), preferred_element_type=f32),
+            jnp.dot(enter, normed_t, preferred_element_type=f32),
             approximate=False,
         ).astype(bf16)
         block_part = block_part + lax.dot_general(
@@ -100,7 +110,10 @@
     proto_f = prototypes.astype(f32)
     proto_len = jnp.sqrt(jnp.sum(proto_f * proto_f, axis=1) + unit_eps)
     unit = (proto_f / proto_len[:, None]).astype(bf16)
-    proto_t = prototypes.T
+    slice_width = D // lax.axis_size(ROWS)
+    proto_slice = (
+        lax.dynamic_slice_in_dim(prototypes, lax.axis_index(ROWS) * slice_width, slice_width, 1).T
+    ).astype(f32)
 
     flat_scores = lax.dot_general(
         embed, unit, (((1,), (1,)), ((), ())), preferred_element_type=f32
@@ -127,39 +140,40 @@
     grad_scores = (factor * (prob - codes[::-1])).astype(bf16)
     grad_flat = grad_scores.reshape(row_count, proto_count)
 
-    radial = jnp.sum(grad_scores.astype(f32) * scores, axis=(0, 1))
-    core = lax.axis_index("core")
     x_index = lax.axis_index("x")
     x_count = lax.axis_size("x")
-    scaled = radial / proto_len
-
-    def proto_part(side):
+    x_turns = {
+        step: [(i, (i + step) % x_count) for i in range(x_count)] for step in range(1, x_count)
+    }
+
+    def half(side):
         left = lax.dynamic_index_in_dim(embed.reshape(row_count, x_count, 2, -1), side, 2, False)
-        mine = lax.dynamic_index_in_dim(proto_t.reshape(x_count, 2, -1, proto_count), side, 1, False)
-        direct = lax.dot_general(
+        return lax.dot_general(
             left.reshape(row_count, -1), grad_flat, (((0,), (0,)), ((), ())), preferred_element_type=f32
-        )
-        return (
-            direct - mine.reshape(-1, proto_count).astype(f32) * scaled[None, :]
-        ) / proto_len[None, :]
-
-    away = proto_part(1 - core).astype(bf16)
-    arrived = lax.ppermute(away, "core", [(0, 1), (1, 0)]).reshape(x_count, -1, proto_count)
-    stay = proto_part(core).reshape(x_count, -1, proto_count)
+        ).reshape(x_count, slice_width, proto_count)
+
+    away = half(1 - core).astype(bf16)
+    arrived = lax.ppermute(away, "core", swap)
+    stay = half(core)
 
     def paired(block):
         return lax.dynamic_index_in_dim(stay, block, 0, False) + lax.dynamic_index_in_dim(
             arrived, block, 0, False
         ).astype(f32)
 
-    proto_grad = paired(x_index)
+    moved = {step: paired((x_index + step) % x_count).astype(bf16) for step in (2, 1, 3)}
+    moved, grad_later = lax.optimization_barrier((moved, grad_flat))
+    direct = paired(x_index)
     for step in (2, 1, 3):
-        moved = paired((x_index + step) % x_count).astype(bf16)
-        turn = [(i, (i + step) % x_count) for i in range(x_count)]
-        proto_grad = proto_grad + lax.ppermute(moved, "x", turn).astype(f32)
+        direct = direct + lax.ppermute(moved[step], "x", x_turns[step]).astype(f32)
+
+    radial = jnp.sum(grad_scores.astype(f32) * scores, axis=(0, 1))
+    radial = radial + lax.ppermute(radial, "core", swap)
+    radial = radial + sum(lax.ppermute(radial, "x", x_turns[step]) for step in (2, 1, 3))
+    proto_grad = (direct - proto_slice * (radial / proto_len)[None, :]) / proto_len[None, :]
 
     embed_terms = lax.dot_general(
-        unit, grad_flat, (((0,), (1,)), ((), ())), preferred_element_type=f32
+        unit, grad_later, (((0,), (1,)), ((), ())), preferred_element_type=f32
     ).astype(bf16)
     embed_grad_t = scatter_sum(embed_terms.reshape(col_count, local_width, row_count), COLS)
     embed_grad = embed_grad_t.T.reshape(view_count, image_rows, local_width)

time: 281 us -> 260 us (0.925)
  local copies, waits for them, and re-layouts: 53.9 us -> 18.7 us
  blocking collectives: 40 us -> 49.4 us
  starting transfers between devices: 57.9 us -> 50.2 us
  other arithmetic: 30.4 us -> 36.1 us
  waiting for transfers between devices: 74.6 us -> 79 us
    unnamed x15 -> x21, local copies, waits for them, and re-layouts: 23.7 us -> 3.84 us
    all_to_all x3 -> x4, blocking collectives: 40 us -> 49.4 us  [gather_all(): return lax.all_to_all(copies, axes, 0, 0)]
    dynamic_slice x4, local copies, waits for them, and re-layouts: 16.1 us -> 7.8 us  [the longest x3 6.73 us: half(): lax.dynamic_index_in_dim(embed.reshape(row_count, x_count, 2, -1), side,...]
    reshape x1 -> x0, local copies, waits for them, and re-layouts: 7.74 us -> none  [proto_part(): proto_t.reshape(x_count, 2, -1, proto_count)]
    all_to_all x4 -> x3, starting transfers between devices: 20.4 us -> 13.3 us  [gather_all(): return lax.all_to_all(copies, axes, 0, 0)]
    all_to_all x1, waiting for transfers between devices: 5.6 us -> 0.01 us  [body(): lax.all_to_all(sent.reshape(col_count, local_width + 8, tall), COLS, 0, 0)]
    all_to_all x4 -> x3, waiting for transfers between devices: 26.2 us -> 31.2 us  [gather_all(): return lax.all_to_all(copies, axes, 0, 0)]
    ppermute x10 -> x12, waiting for transfers between devices: 31.8 us -> 35.6 us  [the longest x3 21.2 us: body(): lax.ppermute(radial, 'x', x_turns[step])]
  transfers between devices with their start and end apart: 17 -> 18, of which waited for: 11 -> 9; matrix products, arithmetic and copies ran while one was open for 23% -> 10% of each run, Pallas kernels for 0% -> 0%
where the time goes in v3:
time: 260 us; the launch traced here: 258 us
  waiting for transfers between devices  79 us (30%)
  starting transfers between devices  50.2 us (19%)
  blocking collectives  49.4 us (19%)
  other arithmetic  36.1 us (14%)
  matrix products  23.6 us (9%)
  local copies, waits for them, and re-layouts  18.7 us (7%)
    all_to_all x4, blocking collectives, gather_all(): return lax.all_to_all(copies, axes, 0, 0)  49.4 us
    all_to_all x3, waiting for transfers between devices, gather_all(): return lax.all_to_all(copies, axes, 0, 0)  31.2 us
    ppermute x3, waiting for transfers between devices, body(): lax.ppermute(radial, 'x', x_turns[step])  21.2 us
    ppermute x3, waiting for transfers between devices, body(): lax.ppermute(share, 'y', [(i, (i + step) % y_count) for i in range(y_coun...  13.6 us
    all_to_all x3, starting transfers between devices, gather_all(): return lax.all_to_all(copies, axes, 0, 0)  13.3 us
    all_to_all x2, waiting for transfers between devices, scatter_sum(): return jnp.sum(lax.all_to_all(blocks, axes, 0, 0).astype(f32), axis=0)  12.3 us
    all_to_all x1, starting transfers between devices, body(): lax.all_to_all(sent.reshape(col_count, local_width + 8, tall), COLS, 0, 0)  12 us
    all_to_all x2, starting transfers between devices, scatter_sum(): return jnp.sum(lax.all_to_all(blocks, axes, 0, 0).astype(f32), axis=0)  9.45 us
  transfers between devices with their start and end apart: 18, of which 9 were waited for; matrix products, arithmetic and copies ran while one was open for 10% of the time, Pallas kernels for 0%

profile of v3, /device:TPU:1, one launch (start us, length us, event | category | flops | bytes accessed | tf_op | source)
XLA Modules:
  0.0 258.2 jit_solution(16047117205320090893)
XLA Ops:
  3.0 12.0 %all-to-all-start = ((bf16[32,40,128]{2,1,0:T(8,128)(2,1)}), bf16[32,40,128]{2,1,0:T(8,128)(2,1)S(1)}, u32[]{:S(2)}, u32[]{:S(2)}) async-start(bf16[32,40,128]{2,1,0:T(8,128)(2,1)} %bitcast.2), calls=%async_computation | async-start | bytes 655360 | tf_op jit(solution)/shard_map/all_to_all | solution.py:58
  18.5 2.4 collective-permute-start.1
  22.1 7.3 %collective-permute-done = bf16[128,1024]{1,0:T(8,128)(2,1)S(1)} collective-permute-done((bf16[128,1024]{1,0:T(8,128)(2,1)S(1)}, bf16[128,1024]{1,0:T(8,128)(2,1)S(1)}, u32[]{:S(2)}, u32[]{:S(2)}) %collective-permute-start) | collective-permute-done | bytes 262176 | tf_op jit(solution)/shard_map/ppermute | solution.py:72
  29.4 6.2 %collective-permute-done.1 = bf16[128,1024]{1,0:T(8,128)(2,1)S(1)} collective-permute-done((bf16[128,1024]{1,0:T(8,128)(2,1)S(1)}, bf16[128,1024]{1,0:T(8,128)(2,1)S(1)}, u32[]{:S(2)}, u32[]{:S(2)}) %collective-permute-start.1) | collective-permute-done | bytes 262176 | tf_op jit(solution)/shard_map/ppermute | solution.py:72
  50.2 5.5 %all-to-all-start.1 = ((bf16[8,16,1024]{2,1,0:T(8,128)(2,1)}), bf16[8,16,1024]{2,1,0:T(8,128)(2,1)S(1)}, u32[]{:S(2)}, u32[]{:S(2)}) async-start(bf16[8,16,1024]{2,1,0:T(8,128)(2,1)} %bitcast.17), calls=%async_computation.1 | async-start | bytes 524288 | tf_op jit(solution)/shard_map/all_to_all | solution.py:35
  55.8 12.3 %all-to-all-done.1 = bf16[8,16,1024]{2,1,0:T(8,128)(2,1)S(1)} async-done(((bf16[8,16,1024]{2,1,0:T(8,128)(2,1)}), bf16[8,16,1024]{2,1,0:T(8,128)(2,1)S(1)}, u32[]{:S(2)}, u32[]{:S(2)}) %all-to-all-start.1) | async-done | bytes 262176 | tf_op jit(solution)/shard_map/all_to_all | solution.py:35
  69.9 3.9 %all-to-all-start.2 = ((bf16[32,16,1024]{2,1,0:T(8,128)(2,1)}), bf16[32,16,1024]{2,1,0:T(8,128)(2,1)S(1)}, u32[]{:S(2)}, u32[]{:S(2)}) async-start(bf16[32,16,1024]{2,1,0:T(8,128)(2,1)} %broadcast_in_dim.20), calls=%async_computation.2 | async-start | bytes 2097152 | tf_op jit(solution)/shard_map/all_to_all | solution.py:27
  73.8 3.1 %fusion = f32[2048]{0:T(1024)S(1)} fusion(bf16[2048,1024]{1,0:T(8,128)(2,1)} %param.11), kind=kLoop, calls=%fused_computation.2 | loop fusion | flops 6289408 | bytes 4202496 | tf_op jit(solution)/shard_map/reduce_sum | solution.py:111
  76.9 22.2 %all-to-all-done.2 = bf16[32,16,1024]{2,1,0:T(8,128)(2,1)S(1)} async-done(((bf16[32,16,1024]{2,1,0:T(8,128)(2,1)}), bf16[32,16,1024]{2,1,0:T(8,128)(2,1)S(1)}, u32[]{:S(2)}, u32[]{:S(2)}) %all-to-all-start.2) | async-done | bytes 1048608 | tf_op jit(solution)/shard_map/all_to_all | solution.py:27
  99.1 6.6 %fusion.6 = (f32[2,2048]{1,0:T(2,128)S(1)}, f32[2,256,2048]{2,1,0:T(8,128)}) fusion(bf16[2,256,1024]{2,1,0:T(8,128)(2,1)S(1)} %bitcast.123, f32[2048]{0:T(1024)S(1)} %add_sqrt_fusion, bf16[2048,1024]{1,0:T(8,128)(2,1)} %param.11), kind=kOutput, calls=%fused_computation.23 | convolution fusion | flops 2155868160 | bytes 9461760 | tf_op jit(solution)/shard_map/dot_general | solution.py:118
  105.7 13.7 %all_to_all.50 = f32[8,2,2048]{2,1,0:T(2,128)S(1)} all-to-all(f32[8,2,2048]{2,1,0:T(2,128)S(1)} %broadcast_in_dim.21), channel_id=1, replica_groups=mesh['x'=4,'core'=2,'z'=8,'y'=4] {'x','core'}, dimensions={0} | all-to-all | bytes 262144 | tf_op jit(solution)/shard_map/all_to_all | solution.py:27
  119.5 3.5 %multiply_reduce_fusion.4 = (f32[2,256]{1,0:T(2,128)S(1)}, f32[2,256]{1,0:T(2,128)S(1)}) fusion(f32[2,2048]{1,0:T(2,128)S(1)} %broadcast_divide_fusion.2, f32[2,256,2048]{2,1,0:T(8,128)} %get-tuple-element.46), kind=kLoop, calls=%fused_computation.11 | loop fusion | flops 5241856 | bytes 4214784 | tf_op jit(solution)/shard_map/reduce_sum | solution.py:131
  123.0 14.0 %all_to_all.51 = f32[32,2,2,256]{3,2,1,0:T(2,128)S(1)} all-to-all(f32[32,2,2,256]{3,2,1,0:T(2,128)S(1)} %broadcast_in_dim.22), channel_id=1, replica_groups=mesh['x'=4,'core'=2,'z'=8,'y'=4] {'z','y'}, dimensions={0} | all-to-all | bytes 262144 | tf_op jit(solution)/shard_map/all_to_all | solution.py:27
  137.1 2.9 %multiply_reduce_fusion.3 = f32[2,2048]{1,0:T(2,128)S(1)} fusion(f32[2,256]{1,0:T(2,128)S(1)} %get-tuple-element.39, f32[2,256,2048]{2,1,0:T(8,128)} %get-tuple-element.46), kind=kLoop, calls=%fused_computation.10 | loop fusion | flops 3141632 | bytes 4212736 | tf_op jit(solution)/shard_map/reduce_sum | solution.py:129
  140.0 10.0 %all_to_all.52 = f32[8,2,2048]{2,1,0:T(2,128)S(1)} all-to-all(f32[8,2,2048]{2,1,0:T(2,128)S(1)} %broadcast_in_dim.23), channel_id=1, replica_groups=mesh['x'=4,'core'=2,'z'=8,'y'=4] {'x','core'}, dimensions={0} | all-to-all | bytes 262144 | tf_op jit(solution)/shard_map/all_to_all | solution.py:27
  150.1 2.9 %multiply_reduce_fusion.2 = f32[2,256]{1,0:T(2,128)S(1)} fusion(f32[2,2048]{1,0:T(2,128)S(1)} %broadcast_divide_fusion.1, f32[2,256,2048]{2,1,0:T(8,128)} %get-tuple-element.46), kind=kLoop, calls=%fused_computation.9 | loop fusion | flops 3145216 | bytes 4212736 | tf_op jit(solution)/shard_map/reduce_sum | solution.py:131
  153.1 11.8 %all_to_all.53 = f32[32,2,256]{2,1,0:T(2,128)S(1)} all-to-all(f32[32,2,256]{2,1,0:T(2,128)S(1)} %broadcast_in_dim.24), channel_id=1, replica_groups=mesh['x'=4,'core'=2,'z'=8,'y'=4] {'z','y'}, dimensions={0} | all-to-all | bytes 131072 | tf_op jit(solution)/shard_map/all_to_all | solution.py:27
  164.9 2.9 %multiply_reduce_fusion.1 = f32[2,2048]{1,0:T(2,128)S(1)} fusion(f32[2,256]{1,0:T(2,128)S(1)} %broadcast_divide_fusion.4, f32[2,256,2048]{2,1,0:T(8,128)} %get-tuple-element.46), kind=kLoop, calls=%fused_computation.8 | loop fusion | flops 3141632 | bytes 4212736 | tf_op jit(solution)/shard_map/reduce_sum | solution.py:129
  168.5 5.6 %all-to-all-start.7 = ((f32[8,2,2048]{2,1,0:T(2,128)}), f32[8,2,2048]{2,1,0:T(2,128)S(1)}, u32[]{:S(2)}, u32[]{:S(2)}) async-start(f32[8,2,2048]{2,1,0:T(2,128)} %broadcast_in_dim.25), calls=%async_computation.7 | async-start | bytes 262144 | tf_op jit(solution)/shard_map/all_to_all | solution.py:27
  174.9 4.5 %all-to-all-done.7 = f32[8,2,2048]{2,1,0:T(2,128)S(1)} async-done(((f32[8,2,2048]{2,1,0:T(2,128)}), f32[8,2,2048]{2,1,0:T(2,128)S(1)}, u32[]{:S(2)}, u32[]{:S(2)}) %all-to-all-start.7) | async-done | bytes 131104 | tf_op jit(solution)/shard_map/all_to_all | solution.py:27
  179.5 2.9 %multiply_reduce_fusion.5 = f32[2,256]{1,0:T(2,128)S(1)} fusion(f32[2,2048]{1,0:T(2,128)S(1)} %broadcast_divide_fusion, f32[2,256,2048]{2,1,0:T(8,128)} %get-tuple-element.46), kind=kLoop, calls=%fused_computation.15 | loop fusion | flops 3145216 | bytes 4212736 | tf_op jit(solution)/shard_map/reduce_sum | solution.py:131
  183.1 3.9 %all-to-all-start.8 = ((f32[32,2,256]{2,1,0:T(2,128)}), f32[32,2,256]{2,1,0:T(2,128)S(1)}, u32[]{:S(2)}, u32[]{:S(2)}) async-start(f32[32,2,256]{2,1,0:T(2,128)} %broadcast_in_dim.26), calls=%async_computation.8 | async-start | bytes 131072 | tf_op jit(solution)/shard_map/all_to_all | solution.py:27
  191.4 4.5 %all-to-all-done.8 = f32[32,2,256]{2,1,0:T(2,128)S(1)} async-done(((f32[32,2,256]{2,1,0:T(2,128)}), f32[32,2,256]{2,1,0:T(2,128)S(1)}, u32[]{:S(2)}, u32[]{:S(2)}) %all-to-all-start.8) | async-done | bytes 65568 | tf_op jit(solution)/shard_map/all_to_all | solution.py:27
  195.9 3.0 %multiply_multiply_fusion = f32[2,256,2048]{2,1,0:T(8,128)S(1)} fusion(f32[2,256]{1,0:T(2,128)S(1)} %broadcast_divide_fusion.3, f32[2,2048]{1,0:T(2,128)S(1)} %broadcast_divide_fusion, f32[2,256,2048]{2,1,0:T(8,128)} %get-tuple-element.46), kind=kLoop, calls=%fused_computation.14 | loop fusion | flops 3145728 | bytes 8407040 | tf_op jit(solution)/shard_map/mul | solution.py:137
  200.8 2.6 %convolution_convert_fusion = bf16[4,128,2048]{2,1,0:T(8,128)(2,1)} fusion(bf16[512,2048,1]{1,0,2:T(8,128)(2,1)S(1)} %bitcast.120, bf16[512,4,1,128]{0,3,1,2:T(8,128)(2,1)S(1)} %copy-done.4), kind=kOutput, calls=%fused_computation.17 | convolution fusion | flops 1074790400 | bytes 4718592 | tf_op jit(solution)/shard_map/dot_general | solution.py:151
  207.6 2.3 fusion.19
  212.1 3.5 %fusion.17 = (bf16[128,2048]{1,0:T(8,128)(2,1)}, bf16[128,2048]{1,0:T(8,128)(2,1)}, bf16[128,2048]{1,0:T(8,128)(2,1)}) fusion(f32[4,128,2048]{2,1,0:T(8,128)S(1)} %fusion.19, s32[]{:T(128)S(6)} %select_n.75, bf16[4,128,2048]{2,1,0:T(8,128)(2,1)} %collective-permute-done.4, s32[]{:T(128)S(6)} %select_n.73, s32[]{:T(128)S(6)} %select_n.70), kind=kLoop, calls=%fused_computation.46 | loop fusion | flops 2359296 | bytes 6291468 | tf_op jit(solution)/shard_map/convert_element_type | solution.py:164
  215.5 3.8 %convolution_convert_fusion.1 = bf16[1024,512]{1,0:T(8,128)(2,1)} fusion(bf16[512,2048]{1,0:T(8,128)(2,1)S(1)} %bitcast.122, bf16[2048,1024]{1,0:T(8,128)(2,1)S(1)} %copy-done.2, f32[2048]{0:T(1024)S(1)} %add_sqrt_fusion), kind=kOutput, calls=%fused_computation.19 | convolution fusion | flops 2154299392 | bytes 7348224 | tf_op jit(solution)/shard_map/dot_general | solution.py:175
  219.4 3.9 %all-to-all-start.9 = ((bf16[32,32,512]{2,1,0:T(8,128)(2,1)}), bf16[32,32,512]{2,1,0:T(8,128)(2,1)S(1)}, u32[]{:S(2)}, u32[]{:S(2)}) async-start(bf16[32,32,512]{2,1,0:T(8,128)(2,1)} %bitcast.36), calls=%async_computation.9 | async-start | bytes 2097152 | tf_op jit(solution)/shard_map/all_to_all | solution.py:35
  228.6 2.7 %collective-permute-start.11 = (f32[2048]{0:T(1024)S(1)}, f32[2048]{0:T(1024)S(1)}, u32[]{:S(2)}, u32[]{:S(2)}) collective-permute-start(f32[2048]{0:T(1024)S(1)} %add.189), channel_id=1, source_target_pairs={{0,192},{64,0},{128,64},{192,128},{1,193},{65,1},{129,65},{193,129... | collective-permute-start | bytes 24584 | tf_op jit(solution)/shard_map/ppermute | solution.py:172
  231.3 19.1 %collective-permute-done.10 = f32[2048]{0:T(1024)S(1)} collective-permute-done((f32[2048]{0:T(1024)S(1)}, f32[2048]{0:T(1024)S(1)}, u32[]{:S(2)}, u32[]{:S(2)}) %collective-permute-start.10) | collective-permute-done | bytes 8224 | tf_op jit(solution)/shard_map/ppermute | solution.py:172
  254.4 3.0 %fusion.8 = f32[128,2048]{1,0:T(8,128)} fusion(bf16[2048,128]{0,1:T(8,128)(2,1)S(1)} %copy.101, bf16[128,2048]{1,0:T(8,128)(2,1)} %collective-permute-done.7, bf16[128,2048]{1,0:T(8,128)(2,1)S(1)} %collective-permute-done.6, bf16[128,2048]{1,0:T(8,128)(2,1)S(1)} %collective-permute-done.5, f32[4,128,2048]{2,1,0:T(8,128)} %copy-done.1, s32[]{:T(128)S(6)} %select_n.76, ...), kind=kLoop, calls=%fused_computation.27 | loop fusion | flops 3145728 | bytes 4734980 | tf_op jit(solution)/shard_map/div | solution.py:173
  (111 shorter events, 48.5 us)
Async XLA Ops:
  0.6 42.1 %copy-start.3 = (bf16[128,1024]{1,0:T(8,128)(2,1)S(1)}, bf16[128,1024]{1,0:T(8,128)(2,1)}, u32[]{:S(2)}) copy-start(bf16[128,1024]{1,0:T(8,128)(2,1)} %param.9) | copy-start | bytes 786436
  3.0 33.5 %all-to-all-start = ((bf16[32,40,128]{2,1,0:T(8,128)(2,1)}), bf16[32,40,128]{2,1,0:T(8,128)(2,1)S(1)}, u32[]{:S(2)}, u32[]{:S(2)}) async-start(bf16[32,40,128]{2,1,0:T(8,128)(2,1)} %bitcast.2), calls=%async_computation | async-start | bytes 655360 | tf_op jit(solution)/shard_map/all_to_all | solution.py:58
  17.2 12.2 %collective-permute-start = (bf16[128,1024]{1,0:T(8,128)(2,1)S(1)}, bf16[128,1024]{1,0:T(8,128)(2,1)S(1)}, u32[]{:S(2)}, u32[]{:S(2)}) collective-permute-start(bf16[128,1024]{1,0:T(8,128)(2,1)S(1)} %bitcast_select_fusion), channel_id=1, source_target_pairs={{0,1},{1,2},{2,3},{3,0},{4,5},{5,6},{6,7},{7,4},{8,9},{9,10},{10,1... | collective-permute-start | bytes 786440 | tf_op jit(solution)/shard_map/ppermute | solution.py:72
  18.5 17.2 %collective-permute-start.1 = (bf16[128,1024]{1,0:T(8,128)(2,1)S(1)}, bf16[128,1024]{1,0:T(8,128)(2,1)S(1)}, u32[]{:S(2)}, u32[]{:S(2)}) collective-permute-start(bf16[128,1024]{1,0:T(8,128)(2,1)S(1)} %bitcast_select_fusion), channel_id=1, source_target_pairs={{0,2},{1,3},{2,0},{3,1},{4,6},{5,7},{6,4},{7,5},{8,10},{9,11},{10,... | collective-permute-start | bytes 786440 | tf_op jit(solution)/shard_map/ppermute | solution.py:72
  20.9 14.8 %collective-permute-start.2 = (bf16[128,1024]{1,0:T(8,128)(2,1)S(1)}, bf16[128,1024]{1,0:T(8,128)(2,1)S(1)}, u32[]{:S(2)}, u32[]{:S(2)}) collective-permute-start(bf16[128,1024]{1,0:T(8,128)(2,1)S(1)} %bitcast_select_fusion), channel_id=1, source_target_pairs={{0,3},{1,0},{2,1},{3,2},{4,7},{5,4},{6,5},{7,6},{8,11},{9,8},{10,9... | collective-permute-start | bytes 786440 | tf_op jit(solution)/shard_map/ppermute | solution.py:72
  35.7 8.0 %collective-permute-start.3 = (bf16[3,128,1024]{2,1,0:T(8,128)(2,1)S(1)}, bf16[3,128,1024]{2,1,0:T(8,128)(2,1)S(1)}, u32[]{:S(2)}, u32[]{:S(2)}) collective-permute-start(bf16[3,128,1024]{2,1,0:T(8,128)(2,1)S(1)} %pad_maximum_fusion), channel_id=1, source_target_pairs={{0,32},{32,0},{1,33},{33,1},{2,34},{34,2},{3,35},{35,3},{4,36},{36... | collective-permute-start | bytes 2359304 | tf_op jit(solution)/shard_map/ppermute | solution.py:76
  37.5 1.5 copy-start.7
  37.5 1.5 copy-start.8
  42.7 2.0 copy-start.5
  44.7 11.0 %copy-start.6 = (f32[32,32]{1,0:T(8,128)S(1)}, f32[32,32]{1,0:T(8,128)}, u32[]{:S(2)}) copy-start(f32[32,32]{1,0:T(8,128)} %get-tuple-element.36) | copy-start | bytes 12292
  50.2 17.9 %all-to-all-start.1 = ((bf16[8,16,1024]{2,1,0:T(8,128)(2,1)}), bf16[8,16,1024]{2,1,0:T(8,128)(2,1)S(1)}, u32[]{:S(2)}, u32[]{:S(2)}) async-start(bf16[8,16,1024]{2,1,0:T(8,128)(2,1)} %bitcast.17), calls=%async_computation.1 | async-start | bytes 524288 | tf_op jit(solution)/shard_map/all_to_all | solution.py:35
  69.9 29.2 %all-to-all-start.2 = ((bf16[32,16,1024]{2,1,0:T(8,128)(2,1)}), bf16[32,16,1024]{2,1,0:T(8,128)(2,1)S(1)}, u32[]{:S(2)}, u32[]{:S(2)}) async-start(bf16[32,16,1024]{2,1,0:T(8,128)(2,1)} %broadcast_in_dim.20), calls=%async_computation.2 | async-start | bytes 2097152 | tf_op jit(solution)/shard_map/all_to_all | solution.py:27
  168.5 10.8 %all-to-all-start.7 = ((f32[8,2,2048]{2,1,0:T(2,128)}), f32[8,2,2048]{2,1,0:T(2,128)S(1)}, u32[]{:S(2)}, u32[]{:S(2)}) async-start(f32[8,2,2048]{2,1,0:T(2,128)} %broadcast_in_dim.25), calls=%async_computation.7 | async-start | bytes 262144 | tf_op jit(solution)/shard_map/all_to_all | solution.py:27
  183.1 12.8 %all-to-all-start.8 = ((f32[32,2,256]{2,1,0:T(2,128)}), f32[32,2,256]{2,1,0:T(2,128)S(1)}, u32[]{:S(2)}, u32[]{:S(2)}) async-start(f32[32,2,256]{2,1,0:T(2,128)} %broadcast_in_dim.26), calls=%async_computation.8 | async-start | bytes 131072 | tf_op jit(solution)/shard_map/all_to_all | solution.py:27
  195.9 3.5 %copy-start = (f32[2,256,2048]{2,1,0:T(8,128)S(1)}, f32[2,256,2048]{2,1,0:T(8,128)}, u32[]{:S(2)}) copy-start(f32[2,256,2048]{2,1,0:T(8,128)} %get-tuple-element.46) | copy-start | bytes 12582916
  199.4 1.4 copy-start.4
  203.4 6.5 %collective-permute-start.4 = (bf16[4,128,2048]{2,1,0:T(8,128)(2,1)}, bf16[4,128,2048]{2,1,0:T(8,128)(2,1)}, u32[]{:S(2)}, u32[]{:S(2)}) collective-permute-start(bf16[4,128,2048]{2,1,0:T(8,128)(2,1)} %convolution_convert_fusion), channel_id=1, source_target_pairs={{0,32},{32,0},{1,33},{33,1},{2,34},{34,2},{3,35},{35,3},{4,36},{36... | collective-permute-start | bytes 6291464 | tf_op jit(solution)/shard_map/ppermute | solution.py:156
  209.9 2.1 copy-start.1
  209.9 5.6 %copy-start.2 = (bf16[2048,1024]{1,0:T(8,128)(2,1)S(1)}, bf16[2048,1024]{1,0:T(8,128)(2,1)}, u32[]{:S(2)}) copy-start(bf16[2048,1024]{1,0:T(8,128)(2,1)} %param.11) | copy-start | bytes 12582916
  219.4 38.0 %all-to-all-start.9 = ((bf16[32,32,512]{2,1,0:T(8,128)(2,1)}), bf16[32,32,512]{2,1,0:T(8,128)(2,1)S(1)}, u32[]{:S(2)}, u32[]{:S(2)}) async-start(bf16[32,32,512]{2,1,0:T(8,128)(2,1)} %bitcast.36), calls=%async_computation.9 | async-start | bytes 2097152 | tf_op jit(solution)/shard_map/all_to_all | solution.py:35
  223.3 31.1 %collective-permute-start.5 = (bf16[128,2048]{1,0:T(8,128)(2,1)}, bf16[128,2048]{1,0:T(8,128)(2,1)S(1)}, u32[]{:S(2)}, u32[]{:S(2)}) collective-permute-start(bf16[128,2048]{1,0:T(8,128)(2,1)} %get-tuple-element.7), channel_id=1, source_target_pairs={{0,128},{64,192},{128,0},{192,64},{1,129},{65,193},{129,1},{193,65... | collective-permute-start | bytes 1572872 | tf_op jit(solution)/shard_map/ppermute | solution.py:168
  223.9 30.4 %collective-permute-start.6 = (bf16[128,2048]{1,0:T(8,128)(2,1)}, bf16[128,2048]{1,0:T(8,128)(2,1)S(1)}, u32[]{:S(2)}, u32[]{:S(2)}) collective-permute-start(bf16[128,2048]{1,0:T(8,128)(2,1)} %get-tuple-element.8), channel_id=1, source_target_pairs={{0,64},{64,128},{128,192},{192,0},{1,65},{65,129},{129,193},{193,1... | collective-permute-start | bytes 1572872 | tf_op jit(solution)/shard_map/ppermute | solution.py:168
  224.8 29.6 %collective-permute-start.7 = (bf16[128,2048]{1,0:T(8,128)(2,1)}, bf16[128,2048]{1,0:T(8,128)(2,1)}, u32[]{:S(2)}, u32[]{:S(2)}) collective-permute-start(bf16[128,2048]{1,0:T(8,128)(2,1)} %get-tuple-element.9), channel_id=1, source_target_pairs={{0,192},{64,0},{128,64},{192,128},{1,193},{65,1},{129,65},{193,129... | collective-permute-start | bytes 1572872 | tf_op jit(solution)/shard_map/ppermute | solution.py:168
  226.6 2.0 collective-permute-start.8
  228.6 21.8 %collective-permute-start.10 = (f32[2048]{0:T(1024)S(1)}, f32[2048]{0:T(1024)S(1)}, u32[]{:S(2)}, u32[]{:S(2)}) collective-permute-start(f32[2048]{0:T(1024)S(1)} %add.189), channel_id=1, source_target_pairs={{0,64},{64,128},{128,192},{192,0},{1,65},{65,129},{129,193},{193,1... | collective-permute-start | bytes 24584 | tf_op jit(solution)/shard_map/ppermute | solution.py:172
  228.6 23.7 %collective-permute-start.11 = (f32[2048]{0:T(1024)S(1)}, f32[2048]{0:T(1024)S(1)}, u32[]{:S(2)}, u32[]{:S(2)}) collective-permute-start(f32[2048]{0:T(1024)S(1)} %add.189), channel_id=1, source_target_pairs={{0,192},{64,0},{128,64},{192,128},{1,193},{65,1},{129,65},{193,129... | collective-permute-start | bytes 24584 | tf_op jit(solution)/shard_map/ppermute | solution.py:172
  250.4 4.0 %collective-permute-start.9 = (f32[2048]{0:T(1024)S(1)}, f32[2048]{0:T(1024)S(1)}, u32[]{:S(2)}, u32[]{:S(2)}) collective-permute-start(f32[2048]{0:T(1024)S(1)} %add.189), channel_id=1, source_target_pairs={{0,128},{64,192},{128,0},{192,64},{1,129},{65,193},{129,1},{193,65... | collective-permute-start | bytes 24584 | tf_op jit(solution)/shard_map/ppermute | solution.py:172

commit v4 on v3

--- a/solution.py
+++ b/solution.py
@@ -1,8 +1,11 @@
+import functools
 import math
 
 import jax
 import jax.numpy as jnp
 from jax import lax
+from jax.experimental import pallas as pl
+from jax.experimental.pallas import tpu as pltpu
 from jax.sharding import Mesh, PartitionSpec as P
 
 D = 1024
@@ -33,6 +36,248 @@
 
 def scatter_sum(blocks, axes):
     return jnp.sum(lax.all_to_all(blocks, axes, 0, 0).astype(f32), axis=0)
+
+
+TILE = 512
+LANES = 128
+factor = 0.5 * math.sqrt(PROTOS * D)
+NT = (((1,), (1,)), ((), ()))
+
+
+def params():
+    return pltpu.CompilerParams(
+        dimension_semantics=("arbitrary",), vmem_limit_bytes=32 * 1024 * 1024
+    )
+
+
+def whole(shape):
+    return pl.BlockSpec(shape, lambda i: (0,) * len(shape))
+
+
+def cost(flops, bytes_accessed, transcendentals=0):
+    return pl.CostEstimate(
+        flops=flops, bytes_accessed=bytes_accessed, transcendentals=transcendentals
+    )
+
+
+def fold_lanes(values):
+    width = values.shape[1]
+    return sum(values[:, j : j + LANES] for j in range(0, width, LANES))
+
+
+def as_column(row):
+    return jnp.broadcast_to(row, (LANES, row.shape[1])).T
+
+
+def spread_lanes(column, width):
+    return jnp.concatenate([column] * (width // LANES), axis=1)
+
+
+def view_rows(pair, count):
+    half = count // 2
+    width = pair.shape[1]
+    return jnp.concatenate(
+        [jnp.broadcast_to(pair[v : v + 1], (half, width)) for v in range(2)], axis=0
+    )
+
+
+def view_sums(values):
+    half = values.shape[0] // 2
+    return jnp.concatenate(
+        [jnp.sum(values[v * half : (v + 1) * half], axis=0, keepdims=True) for v in range(2)],
+        axis=0,
+    )
+
+
+def accumulate(total, part):
+    @pl.when(pl.program_id(0) == 0)
+    def _():
+        total[...] = part
+
+    @pl.when(pl.program_id(0) > 0)
+    def _():
+        total[...] += part
+
+
+def ffn_kernel(core_ref, normed_ref, w_in_ref, w_out_ref, shares_ref, others_ref, out_ref):
+    normed = normed_ref[...]
+    even = core_ref[0] == 0
+    total = jnp.zeros(out_ref.shape, f32)
+    for step in range(shares_ref.shape[0] + 1):
+        if step == 0:
+            enter, leave = w_in_ref[...], w_out_ref[...]
+        else:
+            one, other = shares_ref[step - 1], others_ref[step - 1]
+            enter, leave = jnp.where(even, one, other), jnp.where(even, other, one)
+        wide = lax.dot_general(normed, enter, NT, preferred_element_type=f32)
+        hidden = (0.5 * wide * (1.0 + lax.erf(wide * math.sqrt(0.5)))).astype(bf16)
+        total = total + jnp.dot(hidden, leave, preferred_element_type=f32)
+    out_ref[...] = total.astype(bf16)
+
+
+def feed_forward(core, normed, w_in_t, w_out, shares, others):
+    rows = normed.shape[0]
+    arrays = (normed, w_in_t, w_out, shares, others)
+    return pl.pallas_call(
+        ffn_kernel,
+        grid=(1,),
+        in_specs=[pl.BlockSpec(memory_space=pltpu.SMEM)] + [whole(a.shape) for a in arrays],
+        out_specs=whole((rows, D)),
+        out_shape=jax.ShapeDtypeStruct((rows, D), bf16),
+        compiler_params=params(),
+        cost_estimate=cost(4 * rows * D * 4 * w_out.shape[0], 8 * w_out.size),
+    )(core.reshape(1), *arrays)
+
+
+def scores_kernel(copies, embed_ref, unit_ref, scores_ref, base_ref, mass_ref, soft_ref, total):
+    scores = lax.dot_general(embed_ref[...], unit_ref[...], NT, preferred_element_type=f32)
+    scores_ref[...] = scores
+    soft = jnp.exp(scores * (1.0 / soft_temp))
+    base = soft * soft
+    base_ref[...] = base.astype(bf16)
+    mass = view_sums(base)
+    mass_ref[...] = jnp.broadcast_to(mass[None], (copies,) + mass.shape)
+    accumulate(total, fold_lanes(soft))
+
+    @pl.when(pl.program_id(0) == pl.num_programs(0) - 1)
+    def _():
+        soft_ref[...] = jnp.sum(total[...].T, axis=0, keepdims=True)
+
+
+def score_pass(embed, unit, copies):
+    rows, protos = embed.shape[0], unit.shape[0]
+    return pl.pallas_call(
+        functools.partial(scores_kernel, copies),
+        grid=(protos // TILE,),
+        in_specs=[whole(embed.shape), pl.BlockSpec((TILE, D), lambda i: (i, 0))],
+        out_specs=[
+            pl.BlockSpec((rows, TILE), lambda i: (0, i)),
+            pl.BlockSpec((rows, TILE), lambda i: (0, i)),
+            pl.BlockSpec((copies, 2, TILE), lambda i: (0, 0, i)),
+            whole((1, rows)),
+        ],
+        out_shape=[
+            jax.ShapeDtypeStruct((rows, protos), f32),
+            jax.ShapeDtypeStruct((rows, protos), bf16),
+            jax.ShapeDtypeStruct((copies, 2, protos), f32),
+            jax.ShapeDtypeStruct((1, rows), f32),
+        ],
+        scratch_shapes=[pltpu.VMEM((rows, LANES), f32)],
+        compiler_params=params(),
+        cost_estimate=cost(2 * rows * protos * D, 14 * rows * protos, rows * protos),
+    )(embed, unit)
+
+
+def image_kernel(copies, mass_ref, base_ref, *rest):
+    *extra, out_ref, total = rest
+    scale = 1.0 / jnp.sum(mass_ref[...], axis=0)
+    values = base_ref[...].astype(f32) * view_rows(scale, base_ref.shape[0])
+    accumulate(total, fold_lanes(values))
+
+    @pl.when(pl.program_id(0) == pl.num_programs(0) - 1)
+    def _():
+        row = jnp.sum(total[...].T, axis=0, keepdims=True)
+        row = jnp.concatenate([row] + [ref[...] for ref in extra], axis=0)
+        out_ref[...] = jnp.broadcast_to(row[None], (copies,) + row.shape)
+
+
+def image_pass(masses, base, copies, *extra):
+    rows, protos = base.shape
+    out = (copies, 1 + len(extra), rows)
+    return pl.pallas_call(
+        functools.partial(image_kernel, copies),
+        grid=(protos // TILE,),
+        in_specs=[
+            pl.BlockSpec((masses.shape[0], 2, TILE), lambda i: (0, 0, i)),
+            pl.BlockSpec((rows, TILE), lambda i: (0, i)),
+        ]
+        + [whole(e.shape) for e in extra],
+        out_specs=whole(out),
+        out_shape=jax.ShapeDtypeStruct(out, f32),
+        scratch_shapes=[pltpu.VMEM((rows, LANES), f32)],
+        compiler_params=params(),
+        cost_estimate=cost(3 * rows * protos, 2 * rows * protos),
+    )(masses, base, *extra)
+
+
+def proto_kernel(copies, image_ref, base_ref, mass_ref, column):
+    @pl.when(pl.program_id(0) == 0)
+    def _():
+        column[...] = as_column(1.0 / jnp.sum(image_ref[...], axis=0)[:1])
+
+    values = base_ref[...].astype(f32) * spread_lanes(column[...], base_ref.shape[1])
+    mass = view_sums(values)
+    mass_ref[...] = jnp.broadcast_to(mass[None], (copies,) + mass.shape)
+
+
+def proto_pass(images, base, copies):
+    rows, protos = base.shape
+    return pl.pallas_call(
+        functools.partial(proto_kernel, copies),
+        grid=(protos // TILE,),
+        in_specs=[whole(images.shape), pl.BlockSpec((rows, TILE), lambda i: (0, i))],
+        out_specs=pl.BlockSpec((copies, 2, TILE), lambda i: (0, 0, i)),
+        out_shape=jax.ShapeDtypeStruct((copies, 2, protos), f32),
+        scratch_shapes=[pltpu.VMEM((rows, LANES), f32)],
+        compiler_params=params(),
+        cost_estimate=cost(3 * rows * protos, 2 * rows * protos),
+    )(images, base)
+
+
+def grad_kernel(
+    image_ref, soft_ref, mass_ref, scores_ref, away_t_ref, stay_t_ref,
+    grad_ref, radial_ref, away_ref, stay_ref, code_column, prob_column,
+):
+    @pl.when(pl.program_id(0) == 0)
+    def _():
+        code_column[...] = as_column(factor / jnp.sum(image_ref[...], axis=0)[:1])
+        prob_column[...] = as_column(factor / jnp.sum(soft_ref[...], axis=0)[1:2])
+
+    scores = scores_ref[...]
+    rows, width = scores.shape
+    half = rows // 2
+    soft = jnp.exp(scores * (1.0 / soft_temp))
+    scale = 1.0 / jnp.sum(mass_ref[...], axis=0)
+    codes = (
+        soft * soft * view_rows(scale, rows) * spread_lanes(code_column[...], width)
+    )
+    swapped = jnp.concatenate([codes[half:], codes[:half]], axis=0)
+    grad = (soft * spread_lanes(prob_column[...], width) - swapped).astype(bf16)
+    grad_ref[...] = grad
+    radial_ref[...] = jnp.sum(grad.astype(f32) * scores, axis=0, keepdims=True)
+    away_ref[...] = jnp.dot(away_t_ref[...], grad, preferred_element_type=f32).astype(bf16)
+    stay_ref[...] = jnp.dot(stay_t_ref[...], grad, preferred_element_type=f32)
+
+
+def grad_pass(images, softs, masses, scores, away_t, stay_t):
+    rows, protos = scores.shape
+    depth = away_t.shape[0]
+
+    def tile(height):
+        return pl.BlockSpec((height, TILE), lambda i: (0, i))
+
+    return pl.pallas_call(
+        grad_kernel,
+        grid=(protos // TILE,),
+        in_specs=[
+            whole(images.shape),
+            whole(softs.shape),
+            pl.BlockSpec((masses.shape[0], 2, TILE), lambda i: (0, 0, i)),
+            tile(rows),
+            whole(away_t.shape),
+            whole(stay_t.shape),
+        ],
+        out_specs=[tile(rows), tile(1), tile(depth), tile(depth)],
+        out_shape=[
+            jax.ShapeDtypeStruct((rows, protos), bf16),
+            jax.ShapeDtypeStruct((1, protos), f32),
+            jax.ShapeDtypeStruct((depth, protos), bf16),
+            jax.ShapeDtypeStruct((depth, protos), f32),
+        ],
+        scratch_shapes=[pltpu.VMEM((rows, LANES), f32)] * 2,
+        compiler_params=params(),
+        cost_estimate=cost(4 * depth * rows * protos, 12 * rows * protos, rows * protos),
+    )(images, softs, masses, scores, away_t, stay_t)
 
 
 def body(hidden_states, ln_in_gain, w_in, w_out, ln_out_gain, prototypes):
@@ -74,8 +319,6 @@
         ]
     )
     others = lax.ppermute(shares, "core", swap)
-    first = [w_in_t] + list(jnp.where(core == 0, shares, others))
-    second = [w_out] + list(jnp.where(core == 0, others, shares))
 
     inputs_f = inputs_t.astype(f32)
     center = jnp.mean(inputs_f, axis=0)
@@ -83,16 +326,8 @@
     normed_t = (
         (inputs_f - center[None, :]) * lax.rsqrt(spread + norm_eps)[None, :] * gain_in[:, None]
     ).astype(bf16)
-    block_part = jnp.zeros((tall, D), f32)
-    for enter, leave in zip(first, second):
-        hidden_t = jax.nn.gelu(
-            jnp.dot(enter, normed_t, preferred_element_type=f32),
-            approximate=False,
-        ).astype(bf16)
-        block_part = block_part + lax.dot_general(
-            hidden_t, leave, (((0,), (0,)), ((), ())), preferred_element_type=f32
-        )
-    block = scatter_sum(block_part.astype(bf16).reshape(z_count, row_block, D), "z")
+    block_part = feed_forward(core, normed_t.T, w_in_t, w_out, shares, others)
+    block = scatter_sum(block_part.reshape(z_count, row_block, D), "z")
     picked = (
         jnp.arange(tall)[None, :]
         == lax.axis_index("z") * row_block + jnp.arange(row_block)[:, None]
@@ -115,46 +350,27 @@
         lax.dynamic_slice_in_dim(prototypes, lax.axis_index(ROWS) * slice_width, slice_width, 1).T
     ).astype(f32)
 
-    flat_scores = lax.dot_general(
-        embed, unit, (((1,), (1,)), ((), ())), preferred_element_type=f32
-    )
-    scores = flat_scores.reshape(view_count, image_rows, proto_count)
-    base = jnp.exp(scores / sink_temp)
-    soft = jnp.exp(scores / soft_temp)
-    soft_part = jnp.sum(soft, axis=2)
-    scale_image = jnp.ones((view_count, image_rows), f32)
-    scale_proto = jnp.ones((view_count, proto_count), f32)
-    soft_total = scale_image
-    for repeat in range(SINK_ITERS):
-        proto_mass = sum_small(jnp.sum(base * scale_image[:, :, None], axis=1), ROWS)
-        scale_proto = 1.0 / proto_mass
-        image_part = jnp.sum(base * scale_proto[:, None, :], axis=2)
-        if repeat == 0:
-            image_mass, soft_total = sum_small(jnp.stack([image_part, soft_part]), COLS)
-        else:
-            image_mass = sum_small(image_part, COLS)
-        scale_image = 1.0 / image_mass
-    codes = base * scale_proto[:, None, :] * scale_image[:, :, None]
-    prob = soft / soft_total[:, :, None]
-    factor = 0.5 * math.sqrt(PROTOS * D)
-    grad_scores = (factor * (prob - codes[::-1])).astype(bf16)
-    grad_flat = grad_scores.reshape(row_count, proto_count)
+    row_parts = lax.axis_size(ROWS)
+    scores, base, masses, soft_part = score_pass(embed, unit, row_parts)
+    masses = lax.all_to_all(masses, ROWS, 0, 0)
+    softs = images = lax.all_to_all(image_pass(masses, base, col_count, soft_part), COLS, 0, 0)
+    for repeat in range(1, SINK_ITERS):
+        masses = lax.all_to_all(proto_pass(images, base, row_parts), ROWS, 0, 0)
+        images = lax.all_to_all(image_pass(masses, base, col_count), COLS, 0, 0)
 
     x_index = lax.axis_index("x")
     x_count = lax.axis_size("x")
     x_turns = {
         step: [(i, (i + step) % x_count) for i in range(x_count)] for step in range(1, x_count)
     }
-
-    def half(side):
-        left = lax.dynamic_index_in_dim(embed.reshape(row_count, x_count, 2, -1), side, 2, False)
-        return lax.dot_general(
-            left.reshape(row_count, -1), grad_flat, (((0,), (0,)), ((), ())), preferred_element_type=f32
-        ).reshape(x_count, slice_width, proto_count)
-
-    away = half(1 - core).astype(bf16)
-    arrived = lax.ppermute(away, "core", swap)
-    stay = half(core)
+    embed_t = embed.T.reshape(x_count, 2, slice_width, row_count)
+    away_t, stay_t = (
+        lax.dynamic_index_in_dim(embed_t, side, 1, False).reshape(-1, row_count)
+        for side in (1 - core, core)
+    )
+    grad_flat, radial, away, stay = grad_pass(images, softs, masses, scores, away_t, stay_t)
+    arrived = lax.ppermute(away, "core", swap).reshape(x_count, slice_width, proto_count)
+    stay = stay.reshape(x_count, slice_width, proto_count)
 
     def paired(block):
         return lax.dynamic_index_in_dim(stay, block, 0, False) + lax.dynamic_index_in_dim(
@@ -167,7 +383,7 @@
     for step in (2, 1, 3):
         direct = direct + lax.ppermute(moved[step], "x", x_turns[step]).astype(f32)
 
-    radial = jnp.sum(grad_scores.astype(f32) * scores, axis=(0, 1))
+    radial = radial[0]
     radial = radial + lax.ppermute(radial, "core", swap)
     radial = radial + sum(lax.ppermute(radial, "x", x_turns[step]) for step in (2, 1, 3))
     proto_grad = (direct - proto_slice * (radial / proto_len)[None, :]) / proto_len[None, :]

time: 260 us -> 245 us (0.942)
  other arithmetic: 36.1 us -> 15.7 us
  matrix products: 23.6 us -> 3.72 us
  Pallas kernels: 0 us -> 19 us
  local copies, waits for them, and re-layouts: 18.7 us -> 25.9 us
  waiting for transfers between devices: 79 us -> 73.8 us
  starting transfers between devices: 50.2 us -> 54.6 us
    dot_general x8 -> x0, matrix products: 19.4 us -> none  [the longest x1 6.6 us: body(): lax.dot_general(embed, unit, (((1,), (1,)), ((), ())), preferred_element_...]
    pallas_call x0 -> x8, Pallas kernels: none -> 19 us  [the longest x1 5.71 us: grad_pass(): pl.pallas_call(grad_kernel, grid=(protos // TILE,), in_specs=[whole(image...]
    reduce_sum x12 -> x0, other arithmetic: 16.9 us -> none  [the longest x3 9.38 us: body(): image_part = jnp.sum(base * scale_proto[:, None, :], axis=2)]
    all_to_all x3 -> x1, waiting for transfers between devices: 31.2 us -> 18.1 us  [gather_all(): return lax.all_to_all(copies, axes, 0, 0)]
    unnamed x21 -> x23, local copies, waits for them, and re-layouts: 3.84 us -> 14.9 us
    all_to_all x3 -> x1, starting transfers between devices: 13.3 us -> 3.93 us  [gather_all(): return lax.all_to_all(copies, axes, 0, 0)]
    all_to_all x0 -> x2, starting transfers between devices: none -> 9.41 us  [the longest x1 5.55 us: body(): masses = lax.all_to_all(proto_pass(images, base, row_parts), ROWS, 0, 0)]
    all_to_all x0 -> x2, waiting for transfers between devices: none -> 4.26 us  [the longest x1 3.76 us: body(): masses = lax.all_to_all(proto_pass(images, base, row_parts), ROWS, 0, 0)]
  transfers between devices with their start and end apart: 18 -> 18, of which waited for: 9 -> 11; matrix products, arithmetic and copies ran while one was open for 10% -> 10% of each run, Pallas kernels for 0% -> 0%
where the time goes in v4:
time: 245 us; the launch traced here: 244 us
  waiting for transfers between devices  73.8 us (30%)
  starting transfers between devices  54.6 us (22%)
  blocking collectives  50.1 us (20%)
  local copies, waits for them, and re-layouts  25.9 us (11%)
  Pallas kernels  19 us (8%)
  other arithmetic  15.7 us (6%)
  matrix products  3.72 us (2%)
    ppermute x3, waiting for transfers between devices, body(): lax.ppermute(radial, 'x', x_turns[step])  20.8 us
    all_to_all x1, waiting for transfers between devices, gather_all(): return lax.all_to_all(copies, axes, 0, 0)  18.1 us
    unnamed x23, local copies, waits for them, and re-layouts  14.9 us
    all_to_all x1, blocking collectives, body(): masses = lax.all_to_all(masses, ROWS, 0, 0)  14.7 us
    all_to_all x1, blocking collectives, body(): lax.all_to_all(image_pass(masses, base, col_count, soft_part), COLS, 0, 0)  13.7 us
    ppermute x3, waiting for transfers between devices, body(): lax.ppermute(share, 'y', [(i, (i + step) % y_count) for i in range(y_coun...  13.6 us
    all_to_all x2, starting transfers between devices, scatter_sum(): return jnp.sum(lax.all_to_all(blocks, axes, 0, 0).astype(f32), axis=0)  13.5 us
    all_to_all x1, starting transfers between devices, body(): lax.all_to_all(sent.reshape(col_count, local_width + 8, tall), COLS, 0, 0)  12 us
  transfers between devices with their start and end apart: 18, of which 11 were waited for; matrix products, arithmetic and copies ran while one was open for 10% of the time, Pallas kernels for 0%

profile of v4, /device:TPU:1, one launch (start us, length us, event | category | flops | bytes accessed | tf_op | source)
XLA Modules:
  0.0 243.7 jit_solution(8141876110934432961)
XLA Ops:
  3.0 12.0 %all-to-all-start = ((bf16[32,40,128]{2,1,0:T(8,128)(2,1)}), bf16[32,40,128]{2,1,0:T(8,128)(2,1)S(1)}, u32[]{:S(2)}, u32[]{:S(2)}) async-start(bf16[32,40,128]{2,1,0:T(8,128)(2,1)} %bitcast.2), calls=%async_computation | async-start | bytes 655360 | tf_op jit(solution)/shard_map/all_to_all | solution.py:303
  18.5 2.4 collective-permute-start.1
  22.1 7.3 %collective-permute-done = bf16[128,1024]{1,0:T(8,128)(2,1)S(1)} collective-permute-done((bf16[128,1024]{1,0:T(8,128)(2,1)S(1)}, bf16[128,1024]{1,0:T(8,128)(2,1)S(1)}, u32[]{:S(2)}, u32[]{:S(2)}) %collective-permute-start) | collective-permute-done | bytes 262176 | tf_op jit(solution)/shard_map/ppermute | solution.py:317
  29.4 6.3 %collective-permute-done.1 = bf16[128,1024]{1,0:T(8,128)(2,1)S(1)} collective-permute-done((bf16[128,1024]{1,0:T(8,128)(2,1)S(1)}, bf16[128,1024]{1,0:T(8,128)(2,1)S(1)}, u32[]{:S(2)}, u32[]{:S(2)}) %collective-permute-start.1) | collective-permute-done | bytes 262176 | tf_op jit(solution)/shard_map/ppermute | solution.py:317
  40.3 5.5 %all-to-all-start.1 = ((bf16[8,16,1024]{2,1,0:T(8,128)(2,1)}), bf16[8,16,1024]{2,1,0:T(8,128)(2,1)S(1)}, u32[]{:S(2)}, u32[]{:S(2)}) async-start(bf16[8,16,1024]{2,1,0:T(8,128)(2,1)} %bitcast.10), calls=%async_computation.1 | async-start | bytes 524288 | tf_op jit(solution)/shard_map/all_to_all | solution.py:38
  45.9 11.0 %all-to-all-done.1 = bf16[8,16,1024]{2,1,0:T(8,128)(2,1)S(1)} async-done(((bf16[8,16,1024]{2,1,0:T(8,128)(2,1)}), bf16[8,16,1024]{2,1,0:T(8,128)(2,1)S(1)}, u32[]{:S(2)}, u32[]{:S(2)}) %all-to-all-start.1) | async-done | bytes 262176 | tf_op jit(solution)/shard_map/all_to_all | solution.py:38
  58.7 3.9 %all-to-all-start.2 = ((bf16[32,16,1024]{2,1,0:T(8,128)(2,1)}), bf16[32,16,1024]{2,1,0:T(8,128)(2,1)S(1)}, u32[]{:S(2)}, u32[]{:S(2)}) async-start(bf16[32,16,1024]{2,1,0:T(8,128)(2,1)} %broadcast_in_dim.8), calls=%async_computation.2 | async-start | bytes 2097152 | tf_op jit(solution)/shard_map/all_to_all | solution.py:30
  62.7 3.2 %fusion = f32[2048]{0:T(1024)S(1)} fusion(bf16[2048,1024]{1,0:T(8,128)(2,1)} %param.11), kind=kLoop, calls=%fused_computation.2 | loop fusion | flops 6289408 | bytes 4202496 | tf_op jit(solution)/shard_map/reduce_sum | solution.py:346
  66.1 3.0 %fusion.1.unit_ref = bf16[2048,1024]{1,0:T(8,128)(2,1)} fusion(bf16[2048,1024]{1,0:T(8,128)(2,1)S(1)} %copy-done.8, f32[2048]{0:T(1024)S(1)} %add_sqrt_fusion), kind=kLoop, calls=%fused_computation.3 | loop fusion | flops 6291456 | bytes 8396800 | tf_op jit(solution)/shard_map/convert_element_type | solution.py:347
  69.1 18.1 %all-to-all-done.2 = bf16[32,16,1024]{2,1,0:T(8,128)(2,1)S(1)} async-done(((bf16[32,16,1024]{2,1,0:T(8,128)(2,1)}), bf16[32,16,1024]{2,1,0:T(8,128)(2,1)S(1)}, u32[]{:S(2)}, u32[]{:S(2)}) %all-to-all-start.2) | async-done | bytes 1048608 | tf_op jit(solution)/shard_map/all_to_all | solution.py:30
  87.2 2.2 copy-done
  89.4 4.1 %shard_map.78 = (f32[512,2048]{1,0:T(8,128)S(1)}, bf16[512,2048]{1,0:T(8,128)(2,1)S(1)}, f32[8,2,2048]{2,1,0:T(2,128)S(1)}, f32[1,512]{1,0:T(1,128)S(1)}) custom-call(bf16[512,1024]{1,0:T(8,128)(2,1)S(1)} %bitcast.58, bf16[2048,1024]{1,0:T(8,128)(2,1)S(1)} %copy-done), custom_call_target="tpu_custom_call" | custom-call | flops 2147483648 | bytes 14680064 | tf_op jit(solution)/shard_map/pallas_call | solution.py:149
  95.5 14.7 %all_to_all.50.mass_ref = f32[8,2,2048]{2,1,0:T(2,128)S(1)} all-to-all(f32[8,2,2048]{2,1,0:T(2,128)S(1)} %get-tuple-element.14), channel_id=1, replica_groups=mesh['x'=4,'core'=2,'z'=8,'y'=4] {'x','core'}, dimensions={0} | all-to-all | bytes 262144 | tf_op jit(solution)/shard_map/all_to_all | solution.py:355
  111.3 13.7 %all_to_all.51.image_ref.soft_ref = f32[32,2,512]{2,1,0:T(2,128)S(1)} all-to-all(f32[32,2,512]{2,1,0:T(2,128)S(1)} %shard_map.79), channel_id=1, replica_groups=mesh['x'=4,'core'=2,'z'=8,'y'=4] {'z','y'}, dimensions={0} | all-to-all | bytes 262144 | tf_op jit(solution)/shard_map/all_to_all | solution.py:356
  126.1 10.0 %all_to_all.52.mass_ref = f32[8,2,2048]{2,1,0:T(2,128)S(1)} all-to-all(f32[8,2,2048]{2,1,0:T(2,128)S(1)} %shard_map.80), channel_id=1, replica_groups=mesh['x'=4,'core'=2,'z'=8,'y'=4] {'x','core'}, dimensions={0} | all-to-all | bytes 262144 | tf_op jit(solution)/shard_map/all_to_all | solution.py:358
  137.3 11.8 %all_to_all.53.image_ref = f32[32,1,512]{2,1,0:T(1,128)S(1)} all-to-all(f32[32,1,512]{2,1,0:T(1,128)S(1)} %shard_map.81), channel_id=1, replica_groups=mesh['x'=4,'core'=2,'z'=8,'y'=4] {'z','y'}, dimensions={0} | all-to-all | bytes 131072 | tf_op jit(solution)/shard_map/all_to_all | solution.py:359
  149.1 2.0 shard_map.82
  151.1 5.6 %all-to-all-start.7 = ((f32[8,2,2048]{2,1,0:T(2,128)}), f32[8,2,2048]{2,1,0:T(2,128)S(1)}, u32[]{:S(2)}, u32[]{:S(2)}) async-start(f32[8,2,2048]{2,1,0:T(2,128)} %shard_map.82), calls=%async_computation.7 | async-start | bytes 262144 | tf_op jit(solution)/shard_map/all_to_all | solution.py:358
  158.2 3.8 %all-to-all-done.7.mass_ref = f32[8,2,2048]{2,1,0:T(2,128)S(1)} async-done(((f32[8,2,2048]{2,1,0:T(2,128)}), f32[8,2,2048]{2,1,0:T(2,128)S(1)}, u32[]{:S(2)}, u32[]{:S(2)}) %all-to-all-start.7) | async-done | bytes 131104 | tf_op jit(solution)/shard_map/all_to_all | solution.py:358
  163.8 3.9 %all-to-all-start.8 = ((f32[32,1,512]{2,1,0:T(1,128)}), f32[32,1,512]{2,1,0:T(1,128)S(1)}, u32[]{:S(2)}, u32[]{:S(2)}) async-start(f32[32,1,512]{2,1,0:T(1,128)} %shard_map.83), calls=%async_computation.8 | async-start | bytes 131072 | tf_op jit(solution)/shard_map/all_to_all | solution.py:359
  167.6 4.8 %constant_dynamic-slice_fusion.1 = (bf16[4,1,128,512]{2,1,0,3:T(2,128)(2,1)S(1)}, bf16[4,1,128,512]{2,1,0,3:T(2,128)(2,1)}) fusion(bf16[4,2,128,512]{2,1,0,3:T(2,128)(2,1)} %reshape.135, s32[]{:T(128)S(6)} %select_n.54, s32[]{:T(128)S(6)} %select_n.53), kind=kLoop, calls=%fused_computation.40 | loop fusion | bytes 2097160 | tf_op jit(solution)/shard_map/jit(dynamic_index_in_dim)/dynamic_slice | solution.py:368
  172.4 2.3 copy.21
  176.6 2.2 copy-done.5
  178.8 5.7 %shard_map.84 = (bf16[512,2048]{1,0:T(8,128)(2,1)S(1)}, f32[1,2048]{1,0:T(1,128)S(1)}, bf16[512,2048]{1,0:T(8,128)(2,1)}, f32[512,2048]{1,0:T(8,128)S(1)}) custom-call(f32[32,1,512]{2,1,0:T(1,128)S(1)} %all-to-all-done.8.image_ref, f32[32,2,512]{2,1,0:T(2,128)S(1)} %all_to_all.51.image_ref.soft_ref, f32[8,2,2048]{2,1,0:T(2,128)S(1)} %all-to-all-done.7.mass_ref, ...), custom_call_target="tpu_custom_call" | custom-call | flops 2147483648 | bytes 12582912 | tf_op jit(solution)/shard_map/pallas_call | solution.py:259
  189.7 4.1 %collective-permute-done.4 = bf16[512,2048]{1,0:T(8,128)(2,1)} collective-permute-done((bf16[512,2048]{1,0:T(8,128)(2,1)}, bf16[512,2048]{1,0:T(8,128)(2,1)}, u32[]{:S(2)}, u32[]{:S(2)}) %collective-permute-start.4) | collective-permute-done | bytes 2097184 | tf_op jit(solution)/shard_map/ppermute | solution.py:372
  193.9 3.7 %fusion.8 = (bf16[128,2048]{1,0:T(8,128)(2,1)}, bf16[128,2048]{1,0:T(8,128)(2,1)}, bf16[128,2048]{1,0:T(8,128)(2,1)}) fusion(f32[4,128,2048]{2,1,0:T(8,128)} %bitcast.56, s32[]{:T(128)S(6)} %select_n.60, bf16[4,128,2048]{2,1,0:T(8,128)(2,1)} %bitcast.16, s32[]{:T(128)S(6)} %select_n.58, s32[]{:T(128)S(6)} %select_n.56), kind=kLoop, calls=%fused_computation.21 | loop fusion | flops 2359296 | bytes 6291468 | tf_op jit(solution)/shard_map/convert_element_type | solution.py:380
  197.5 3.4 %convolution_convert_fusion = bf16[1024,512]{1,0:T(8,128)(2,1)} fusion(bf16[2048,1024]{1,0:T(8,128)(2,1)S(1)} %copy-done.1, bf16[512,2048]{1,0:T(8,128)(2,1)S(1)} %copy-done.7), kind=kOutput, calls=%fused_computation.5 | convolution fusion | flops 2148007936 | bytes 7340032 | tf_op jit(solution)/shard_map/dot_general | solution.py:391
  200.9 7.9 %all-to-all-start.9 = ((bf16[32,32,512]{2,1,0:T(8,128)(2,1)}), bf16[32,32,512]{2,1,0:T(8,128)(2,1)S(1)}, u32[]{:S(2)}, u32[]{:S(2)}) async-start(bf16[32,32,512]{2,1,0:T(8,128)(2,1)} %bitcast.20), calls=%async_computation.9 | async-start | bytes 2097152 | tf_op jit(solution)/shard_map/all_to_all | solution.py:38
  214.5 2.7 %collective-permute-start.11 = (f32[2048]{0:T(1024)S(1)}, f32[2048]{0:T(1024)S(1)}, u32[]{:S(2)}, u32[]{:S(2)}) collective-permute-start(f32[2048]{0:T(1024)S(1)} %add.177), channel_id=1, source_target_pairs={{0,192},{64,0},{128,64},{192,128},{1,193},{65,1},{129,65},{193,129... | collective-permute-start | bytes 24584 | tf_op jit(solution)/shard_map/ppermute | solution.py:388
  217.2 18.7 %collective-permute-done.10 = f32[2048]{0:T(1024)S(1)} collective-permute-done((f32[2048]{0:T(1024)S(1)}, f32[2048]{0:T(1024)S(1)}, u32[]{:S(2)}, u32[]{:S(2)}) %collective-permute-start.10) | collective-permute-done | bytes 8224 | tf_op jit(solution)/shard_map/ppermute | solution.py:388
  237.9 2.0 collective-permute-done.9
  240.0 3.0 %fusion.2 = f32[128,2048]{1,0:T(8,128)} fusion(bf16[2048,128]{0,1:T(8,128)(2,1)S(1)} %copy.23, bf16[128,2048]{1,0:T(8,128)(2,1)} %collective-permute-done.7, bf16[128,2048]{1,0:T(8,128)(2,1)S(1)} %collective-permute-done.6, bf16[128,2048]{1,0:T(8,128)(2,1)S(1)} %collective-permute-done.5, f32[4,128,2048]{2,1,0:T(8,128)} %bitcast.57, s32[]{:T(128)S(6)} %select_n.61, ...), kind=kLoop, calls=%fused_computation.8 | loop fusion | flops 3145728 | bytes 4734980 | tf_op jit(solution)/shard_map/div | solution.py:389
  (78 shorter events, 37.9 us)
Async XLA Ops:
  0.6 37.8 %copy-start.3 = (bf16[128,1024]{1,0:T(8,128)(2,1)S(1)}, bf16[128,1024]{1,0:T(8,128)(2,1)}, u32[]{:S(2)}) copy-start(bf16[128,1024]{1,0:T(8,128)(2,1)} %w_out_ref.1) | copy-start | bytes 786436
  3.0 33.5 %all-to-all-start = ((bf16[32,40,128]{2,1,0:T(8,128)(2,1)}), bf16[32,40,128]{2,1,0:T(8,128)(2,1)S(1)}, u32[]{:S(2)}, u32[]{:S(2)}) async-start(bf16[32,40,128]{2,1,0:T(8,128)(2,1)} %bitcast.2), calls=%async_computation | async-start | bytes 655360 | tf_op jit(solution)/shard_map/all_to_all | solution.py:303
  17.2 12.2 %collective-permute-start = (bf16[128,1024]{1,0:T(8,128)(2,1)S(1)}, bf16[128,1024]{1,0:T(8,128)(2,1)S(1)}, u32[]{:S(2)}, u32[]{:S(2)}) collective-permute-start(bf16[128,1024]{1,0:T(8,128)(2,1)S(1)} %broadcast_select_fusion), channel_id=1, source_target_pairs={{0,1},{1,2},{2,3},{3,0},{4,5},{5,6},{6,7},{7,4},{8,9},{9,10},{10,1... | collective-permute-start | bytes 786440 | tf_op jit(solution)/shard_map/ppermute | solution.py:317
  18.5 17.2 %collective-permute-start.1 = (bf16[128,1024]{1,0:T(8,128)(2,1)S(1)}, bf16[128,1024]{1,0:T(8,128)(2,1)S(1)}, u32[]{:S(2)}, u32[]{:S(2)}) collective-permute-start(bf16[128,1024]{1,0:T(8,128)(2,1)S(1)} %broadcast_select_fusion), channel_id=1, source_target_pairs={{0,2},{1,3},{2,0},{3,1},{4,6},{5,7},{6,4},{7,5},{8,10},{9,11},{10,... | collective-permute-start | bytes 786440 | tf_op jit(solution)/shard_map/ppermute | solution.py:317
  20.9 14.8 %collective-permute-start.2 = (bf16[128,1024]{1,0:T(8,128)(2,1)S(1)}, bf16[128,1024]{1,0:T(8,128)(2,1)S(1)}, u32[]{:S(2)}, u32[]{:S(2)}) collective-permute-start(bf16[128,1024]{1,0:T(8,128)(2,1)S(1)} %broadcast_select_fusion), channel_id=1, source_target_pairs={{0,3},{1,0},{2,1},{3,2},{4,7},{5,4},{6,5},{7,6},{8,11},{9,8},{10,9... | collective-permute-start | bytes 786440 | tf_op jit(solution)/shard_map/ppermute | solution.py:317
  35.7 2.7 %collective-permute-start.3 = (bf16[3,128,1024]{2,1,0:T(8,128)(2,1)S(1)}, bf16[3,128,1024]{2,1,0:T(8,128)(2,1)S(1)}, u32[]{:S(2)}, u32[]{:S(2)}) collective-permute-start(bf16[3,128,1024]{2,1,0:T(8,128)(2,1)S(1)} %pad_maximum_fusion.shares_ref), channel_id=1, source_target_pairs={{0,32},{32,0},{1,33},{33,1},{2,34},{34,2},{3,35},{35,3},{4,36},{36... | collective-permute-start | bytes 2359304 | tf_op jit(solution)/shard_map/ppermute | solution.py:321
  40.3 16.6 %all-to-all-start.1 = ((bf16[8,16,1024]{2,1,0:T(8,128)(2,1)}), bf16[8,16,1024]{2,1,0:T(8,128)(2,1)S(1)}, u32[]{:S(2)}, u32[]{:S(2)}) async-start(bf16[8,16,1024]{2,1,0:T(8,128)(2,1)} %bitcast.10), calls=%async_computation.1 | async-start | bytes 524288 | tf_op jit(solution)/shard_map/all_to_all | solution.py:38
  58.7 28.4 %all-to-all-start.2 = ((bf16[32,16,1024]{2,1,0:T(8,128)(2,1)}), bf16[32,16,1024]{2,1,0:T(8,128)(2,1)S(1)}, u32[]{:S(2)}, u32[]{:S(2)}) async-start(bf16[32,16,1024]{2,1,0:T(8,128)(2,1)} %broadcast_in_dim.8), calls=%async_computation.2 | async-start | bytes 2097152 | tf_op jit(solution)/shard_map/all_to_all | solution.py:30
  62.7 3.5 %copy-start.8 = (bf16[2048,1024]{1,0:T(8,128)(2,1)S(1)}, bf16[2048,1024]{1,0:T(8,128)(2,1)}, u32[]{:S(2)}) copy-start(bf16[2048,1024]{1,0:T(8,128)(2,1)} %param.11) | copy-start | bytes 12582916
  87.2 2.2 copy-start
  93.5 2.0 copy-start.4
  151.1 10.8 %all-to-all-start.7 = ((f32[8,2,2048]{2,1,0:T(2,128)}), f32[8,2,2048]{2,1,0:T(2,128)S(1)}, u32[]{:S(2)}, u32[]{:S(2)}) async-start(f32[8,2,2048]{2,1,0:T(2,128)} %shard_map.82), calls=%async_computation.7 | async-start | bytes 262144 | tf_op jit(solution)/shard_map/all_to_all | solution.py:358
  163.8 12.8 %all-to-all-start.8 = ((f32[32,1,512]{2,1,0:T(1,128)}), f32[32,1,512]{2,1,0:T(1,128)S(1)}, u32[]{:S(2)}, u32[]{:S(2)}) async-start(f32[32,1,512]{2,1,0:T(1,128)} %shard_map.83), calls=%async_computation.8 | async-start | bytes 131072 | tf_op jit(solution)/shard_map/all_to_all | solution.py:359
  176.6 2.2 copy-start.5
  184.5 2.0 copy-start.2
  186.5 1.3 copy-start.6
  187.8 9.7 %copy-start.7 = (bf16[512,2048]{1,0:T(8,128)(2,1)S(1)}, bf16[512,2048]{1,0:T(8,128)(2,1)}, u32[]{:S(2)}) copy-start(bf16[512,2048]{1,0:T(8,128)(2,1)} %copy-done.6) | copy-start | bytes 6291460
  187.8 6.1 %collective-permute-start.4 = (bf16[512,2048]{1,0:T(8,128)(2,1)}, bf16[512,2048]{1,0:T(8,128)(2,1)}, u32[]{:S(2)}, u32[]{:S(2)}) collective-permute-start(bf16[512,2048]{1,0:T(8,128)(2,1)} %get-tuple-element.19), channel_id=1, source_target_pairs={{0,32},{32,0},{1,33},{33,1},{2,34},{34,2},{3,35},{35,3},{4,36},{36... | collective-permute-start | bytes 6291464 | tf_op jit(solution)/shard_map/ppermute | solution.py:372
  189.7 7.8 %copy-start.1 = (bf16[2048,1024]{1,0:T(8,128)(2,1)S(1)}, bf16[2048,1024]{1,0:T(8,128)(2,1)}, u32[]{:S(2)}) copy-start(bf16[2048,1024]{1,0:T(8,128)(2,1)} %fusion.1.unit_ref) | copy-start | bytes 12582916
  200.9 42.0 %all-to-all-start.9 = ((bf16[32,32,512]{2,1,0:T(8,128)(2,1)}), bf16[32,32,512]{2,1,0:T(8,128)(2,1)S(1)}, u32[]{:S(2)}, u32[]{:S(2)}) async-start(bf16[32,32,512]{2,1,0:T(8,128)(2,1)} %bitcast.20), calls=%async_computation.9 | async-start | bytes 2097152 | tf_op jit(solution)/shard_map/all_to_all | solution.py:38
  208.9 31.1 %collective-permute-start.5 = (bf16[128,2048]{1,0:T(8,128)(2,1)}, bf16[128,2048]{1,0:T(8,128)(2,1)S(1)}, u32[]{:S(2)}, u32[]{:S(2)}) collective-permute-start(bf16[128,2048]{1,0:T(8,128)(2,1)} %get-tuple-element.22), channel_id=1, source_target_pairs={{0,128},{64,192},{128,0},{192,64},{1,129},{65,193},{129,1},{193,65... | collective-permute-start | bytes 1572872 | tf_op jit(solution)/shard_map/ppermute | solution.py:384
  209.5 30.4 %collective-permute-start.6 = (bf16[128,2048]{1,0:T(8,128)(2,1)}, bf16[128,2048]{1,0:T(8,128)(2,1)S(1)}, u32[]{:S(2)}, u32[]{:S(2)}) collective-permute-start(bf16[128,2048]{1,0:T(8,128)(2,1)} %get-tuple-element.23), channel_id=1, source_target_pairs={{0,64},{64,128},{128,192},{192,0},{1,65},{65,129},{129,193},{193,1... | collective-permute-start | bytes 1572872 | tf_op jit(solution)/shard_map/ppermute | solution.py:384
  210.4 29.6 %collective-permute-start.7 = (bf16[128,2048]{1,0:T(8,128)(2,1)}, bf16[128,2048]{1,0:T(8,128)(2,1)}, u32[]{:S(2)}, u32[]{:S(2)}) collective-permute-start(bf16[128,2048]{1,0:T(8,128)(2,1)} %get-tuple-element.24), channel_id=1, source_target_pairs={{0,192},{64,0},{128,64},{192,128},{1,193},{65,1},{129,65},{193,129... | collective-permute-start | bytes 1572872 | tf_op jit(solution)/shard_map/ppermute | solution.py:384
  212.2 2.3 collective-permute-start.8
  214.5 21.4 %collective-permute-start.10 = (f32[2048]{0:T(1024)S(1)}, f32[2048]{0:T(1024)S(1)}, u32[]{:S(2)}, u32[]{:S(2)}) collective-permute-start(f32[2048]{0:T(1024)S(1)} %add.177), channel_id=1, source_target_pairs={{0,64},{64,128},{128,192},{192,0},{1,65},{65,129},{129,193},{193,1... | collective-permute-start | bytes 24584 | tf_op jit(solution)/shard_map/ppermute | solution.py:388
  214.5 23.4 %collective-permute-start.11 = (f32[2048]{0:T(1024)S(1)}, f32[2048]{0:T(1024)S(1)}, u32[]{:S(2)}, u32[]{:S(2)}) collective-permute-start(f32[2048]{0:T(1024)S(1)} %add.177), channel_id=1, source_target_pairs={{0,192},{64,0},{128,64},{192,128},{1,193},{65,1},{129,65},{193,129... | collective-permute-start | bytes 24584 | tf_op jit(solution)/shard_map/ppermute | solution.py:388
  235.9 4.0 %collective-permute-start.9 = (f32[2048]{0:T(1024)S(1)}, f32[2048]{0:T(1024)S(1)}, u32[]{:S(2)}, u32[]{:S(2)}) collective-permute-start(f32[2048]{0:T(1024)S(1)} %add.177), channel_id=1, source_target_pairs={{0,128},{64,192},{128,0},{192,64},{1,129},{65,193},{129,1},{193,65... | collective-permute-start | bytes 24584 | tf_op jit(solution)/shard_map/ppermute | solution.py:388

commit v5 on v4

--- a/solution.py
+++ b/solution.py
@@ -44,9 +44,9 @@
 NT = (((1,), (1,)), ((), ()))
 
 
-def params():
+def params(mib):
     return pltpu.CompilerParams(
-        dimension_semantics=("arbitrary",), vmem_limit_bytes=32 * 1024 * 1024
+        dimension_semantics=("arbitrary",), vmem_limit_bytes=mib * 1024 * 1024
     )
 
 
@@ -97,6 +97,24 @@
     @pl.when(pl.program_id(0) > 0)
     def _():
         total[...] += part
+
+
+def stack_kernel(first_ref, second_ref, third_ref, out_ref):
+    for place, ref in enumerate((first_ref, second_ref, third_ref)):
+        out_ref[place] = ref[...]
+
+
+def stack_shares(parts):
+    shape = parts[0].shape
+    return pl.pallas_call(
+        stack_kernel,
+        grid=(1,),
+        in_specs=[whole(shape)] * 3,
+        out_specs=whole((3,) + shape),
+        out_shape=jax.ShapeDtypeStruct((3,) + shape, bf16),
+        compiler_params=params(6),
+        cost_estimate=cost(40 * 10**9, 4 * parts[0].size),
+    )(*parts)
 
 
 def ffn_kernel(core_ref, normed_ref, w_in_ref, w_out_ref, shares_ref, others_ref, out_ref):
@@ -124,9 +142,50 @@
         in_specs=[pl.BlockSpec(memory_space=pltpu.SMEM)] + [whole(a.shape) for a in arrays],
         out_specs=whole((rows, D)),
         out_shape=jax.ShapeDtypeStruct((rows, D), bf16),
-        compiler_params=params(),
+        compiler_params=params(8),
         cost_estimate=cost(4 * rows * D * 4 * w_out.shape[0], 8 * w_out.size),
     )(core.reshape(1), *arrays)
+
+
+def prepare_kernel(core_ref, proto_ref, unit_ref, length_ref, turned_ref):
+    values = proto_ref[...].astype(f32)
+    squares = values * values
+    inverse = lax.rsqrt(jnp.sum(squares, axis=1, keepdims=True) + unit_eps)
+    unit_ref[...] = (values * inverse).astype(bf16)
+    length_ref[...] = jnp.sqrt(
+        jnp.sum(fold_lanes(squares).T, axis=0, keepdims=True) + unit_eps
+    )
+    even = core_ref[0] == 0
+    for block in range(turned_ref.shape[0]):
+        start = 2 * block * LANES
+        picked = jnp.where(
+            even, values[:, start : start + LANES], values[:, start + LANES : start + 2 * LANES]
+        )
+        turned_ref[block] = picked.T.astype(bf16)
+
+
+def prepare(core, prototypes, x_count):
+    protos = prototypes.shape[0]
+    return pl.pallas_call(
+        prepare_kernel,
+        grid=(protos // TILE,),
+        in_specs=[
+            pl.BlockSpec(memory_space=pltpu.SMEM),
+            pl.BlockSpec((TILE, D), lambda i: (i, 0)),
+        ],
+        out_specs=[
+            pl.BlockSpec((TILE, D), lambda i: (i, 0)),
+            pl.BlockSpec((1, TILE), lambda i: (0, i)),
+            pl.BlockSpec((x_count, LANES, TILE), lambda i: (0, 0, i)),
+        ],
+        out_shape=[
+            jax.ShapeDtypeStruct((protos, D), bf16),
+            jax.ShapeDtypeStruct((1, protos), f32),
+            jax.ShapeDtypeStruct((x_count, LANES, protos), bf16),
+        ],
+        compiler_params=params(18),
+        cost_estimate=cost(6 * protos * D, 5 * protos * D),
+    )(core.reshape(1), prototypes)
 
 
 def scores_kernel(copies, embed_ref, unit_ref, scores_ref, base_ref, mass_ref, soft_ref, total):
@@ -163,7 +222,7 @@
             jax.ShapeDtypeStruct((1, rows), f32),
         ],
         scratch_shapes=[pltpu.VMEM((rows, LANES), f32)],
-        compiler_params=params(),
+        compiler_params=params(18),
         cost_estimate=cost(2 * rows * protos * D, 14 * rows * protos, rows * protos),
     )(embed, unit)
 
@@ -195,7 +254,7 @@
         out_specs=whole(out),
         out_shape=jax.ShapeDtypeStruct(out, f32),
         scratch_shapes=[pltpu.VMEM((rows, LANES), f32)],
-        compiler_params=params(),
+        compiler_params=params(10),
         cost_estimate=cost(3 * rows * protos, 2 * rows * protos),
     )(masses, base, *extra)
 
@@ -219,7 +278,7 @@
         out_specs=pl.BlockSpec((copies, 2, TILE), lambda i: (0, 0, i)),
         out_shape=jax.ShapeDtypeStruct((copies, 2, protos), f32),
         scratch_shapes=[pltpu.VMEM((rows, LANES), f32)],
-        compiler_params=params(),
+        compiler_params=params(10),
         cost_estimate=cost(3 * rows * protos, 2 * rows * protos),
     )(images, base)
 
@@ -275,9 +334,53 @@
             jax.ShapeDtypeStruct((depth, protos), f32),
         ],
         scratch_shapes=[pltpu.VMEM((rows, LANES), f32)] * 2,
-        compiler_params=params(),
+        compiler_params=params(20),
         cost_estimate=cost(4 * depth * rows * protos, 12 * rows * protos, rows * protos),
     )(images, softs, masses, scores, away_t, stay_t)
+
+
+def pair(stay, arrived, turned, radials, length):
+    radial = radials[0] + radials[1]
+    inverse = 1.0 / length
+    return (stay + arrived.astype(f32) - turned.astype(f32) * (radial * inverse)) * inverse
+
+
+def pair_kernel(place_ref, stay_ref, arrived_ref, turned_ref, one_ref, two_ref, length_ref, out_ref):
+    out_ref[...] = pair(
+        stay_ref[0], arrived_ref[0], turned_ref[0], (one_ref[...], two_ref[...]), length_ref[...]
+    ).astype(bf16)
+
+
+def final_kernel(
+    place_ref, stay_ref, arrived_ref, turned_ref, one_ref, two_ref, length_ref, *rest
+):
+    *others, out_ref = rest
+    total = pair(
+        stay_ref[0], arrived_ref[0], turned_ref[0], (one_ref[...], two_ref[...]), length_ref[...]
+    )
+    for ref in others:
+        total = total + ref[...].astype(f32)
+    out_ref[...] = total
+
+
+def pair_call(place, stay, arrived, turned, radials, length, others=()):
+    blocks, height, protos = stay.shape
+    wide = 2 * TILE
+    picked = pl.BlockSpec((1, height, wide), lambda i, p: (p[0], 0, i))
+    line = pl.BlockSpec((1, wide), lambda i, p: (0, i))
+    flat = pl.BlockSpec((height, wide), lambda i, p: (0, i))
+    return pl.pallas_call(
+        final_kernel if others else pair_kernel,
+        grid_spec=pltpu.PrefetchScalarGridSpec(
+            num_scalar_prefetch=1,
+            grid=(protos // wide,),
+            in_specs=[picked] * 3 + [line] * 3 + [flat] * len(others),
+            out_specs=flat,
+        ),
+        out_shape=jax.ShapeDtypeStruct((height, protos), f32 if others else bf16),
+        compiler_params=params(12),
+        cost_estimate=cost(6 * height * protos, 10 * height * protos),
+    )(place.reshape(1), stay, arrived, turned, *radials, length, *others)
 
 
 def body(hidden_states, ln_in_gain, w_in, w_out, ln_out_gain, prototypes):
@@ -312,7 +415,7 @@
     swap = [(0, 1), (1, 0)]
     w_in_t = w_in.T
     share = jnp.where(core == 0, w_in_t, w_out)
-    shares = jnp.stack(
+    shares = stack_shares(
         [
             lax.ppermute(share, "y", [(i, (i + step) % y_count) for i in range(y_count)])
             for step in range(1, y_count)
@@ -341,14 +444,11 @@
     embed_part = (final * lax.rsqrt(squared + unit_eps)).astype(bf16)
     embed = gather_all(embed_part, ("y", "z")).reshape(row_count, D)
 
+    x_index = lax.axis_index("x")
+    x_count = lax.axis_size("x")
+    unit, proto_len, turned = prepare(core, prototypes, x_count)
     proto_count = prototypes.shape[0]
-    proto_f = prototypes.astype(f32)
-    proto_len = jnp.sqrt(jnp.sum(proto_f * proto_f, axis=1) + unit_eps)
-    unit = (proto_f / proto_len[:, None]).astype(bf16)
-    slice_width = D // lax.axis_size(ROWS)
-    proto_slice = (
-        lax.dynamic_slice_in_dim(prototypes, lax.axis_index(ROWS) * slice_width, slice_width, 1).T
-    ).astype(f32)
+    slice_width = turned.shape[1]
 
     row_parts = lax.axis_size(ROWS)
     scores, base, masses, soft_part = score_pass(embed, unit, row_parts)
@@ -358,39 +458,30 @@
         masses = lax.all_to_all(proto_pass(images, base, row_parts), ROWS, 0, 0)
         images = lax.all_to_all(image_pass(masses, base, col_count), COLS, 0, 0)
 
-    x_index = lax.axis_index("x")
-    x_count = lax.axis_size("x")
-    x_turns = {
-        step: [(i, (i + step) % x_count) for i in range(x_count)] for step in range(1, x_count)
-    }
     embed_t = embed.T.reshape(x_count, 2, slice_width, row_count)
     away_t, stay_t = (
         lax.dynamic_index_in_dim(embed_t, side, 1, False).reshape(-1, row_count)
         for side in (1 - core, core)
     )
     grad_flat, radial, away, stay = grad_pass(images, softs, masses, scores, away_t, stay_t)
-    arrived = lax.ppermute(away, "core", swap).reshape(x_count, slice_width, proto_count)
-    stay = stay.reshape(x_count, slice_width, proto_count)
-
-    def paired(block):
-        return lax.dynamic_index_in_dim(stay, block, 0, False) + lax.dynamic_index_in_dim(
-            arrived, block, 0, False
-        ).astype(f32)
-
-    moved = {step: paired((x_index + step) % x_count).astype(bf16) for step in (2, 1, 3)}
-    moved, grad_later = lax.optimization_barrier((moved, grad_flat))
-    direct = paired(x_index)
-    for step in (2, 1, 3):
-        direct = direct + lax.ppermute(moved[step], "x", x_turns[step]).astype(f32)
-
-    radial = radial[0]
-    radial = radial + lax.ppermute(radial, "core", swap)
-    radial = radial + sum(lax.ppermute(radial, "x", x_turns[step]) for step in (2, 1, 3))
-    proto_grad = (direct - proto_slice * (radial / proto_len)[None, :]) / proto_len[None, :]
-
     embed_terms = lax.dot_general(
-        unit, grad_later, (((0,), (1,)), ((), ())), preferred_element_type=f32
+        unit, grad_flat, (((0,), (1,)), ((), ())), preferred_element_type=f32
     ).astype(bf16)
+    stay, arrived = (
+        part.reshape(x_count, slice_width, proto_count)
+        for part in (stay, lax.ppermute(away, "core", swap))
+    )
+    radials = (radial, lax.ppermute(radial, "core", swap))
+
+    def paired(step, others=()):
+        place = (x_index + step) % x_count
+        return pair_call(place, stay, arrived, turned, radials, proto_len, others)
+
+    landed = tuple(
+        lax.ppermute(paired(step), "x", [(i, (i + step) % x_count) for i in range(x_count)])
+        for step in (2, 1, 3)
+    )
+    proto_grad = paired(0, landed)
     embed_grad_t = scatter_sum(embed_terms.reshape(col_count, local_width, row_count), COLS)
     embed_grad = embed_grad_t.T.reshape(view_count, image_rows, local_width)
     return (embed_grad, proto_grad)

time: 245 us -> 226 us (0.922)
  other arithmetic: 15.7 us -> 3.96 us
  Pallas kernels: 19 us -> 29.6 us
  waiting for transfers between devices: 73.8 us -> 63.2 us
  starting transfers between devices: 54.6 us -> 44.4 us
    ppermute x8 -> x5, waiting for transfers between devices: 25.7 us -> 5.52 us  [the longest x3 4.64 us: body(): lax.ppermute(paired(step), 'x', [(i, (i + step) % x_count) for i in range...]
    all_to_all x2, waiting for transfers between devices: 11 us -> 25 us  [scatter_sum(): return jnp.sum(lax.all_to_all(blocks, axes, 0, 0).astype(f32), axis=0)]
    ppermute x3, waiting for transfers between devices: 13.6 us -> 0.15 us  [body(): lax.ppermute(share, 'y', [(i, (i + step) % y_count) for i in range(y_coun...]
    all_to_all x1, waiting for transfers between devices: 0.01 us -> 11.6 us  [body(): lax.all_to_all(sent.reshape(col_count, local_width + 8, tall), COLS, 0, 0)]
    pallas_call x0 -> x6, Pallas kernels: none -> 10.6 us  [the longest x4 8.28 us: pair_call(): pl.pallas_call(final_kernel if others else pair_kernel, grid_spec=pltpu.P...]
    convert_element_type x2 -> x0, other arithmetic: 6.63 us -> none  [the longest x1 3.67 us: body(): paired((x_index + step) % x_count).astype(bf16)]
    ppermute x8 -> x5, starting transfers between devices: 10.1 us -> 4.39 us  [the longest x3 2.09 us: body(): lax.ppermute(paired(step), 'x', [(i, (i + step) % x_count) for i in range...]
    unnamed x23 -> x32, local copies, waits for them, and re-layouts: 14.9 us -> 19.1 us
  transfers between devices with their start and end apart: 18 -> 15, of which waited for: 11 -> 9; matrix products, arithmetic and copies ran while one was open for 10% -> 8% of each run, Pallas kernels for 0% -> 4%
where the time goes in v5:
time: 226 us; the launch traced here: 225 us
  waiting for transfers between devices  63.2 us (28%)
  blocking collectives  51.1 us (23%)
  starting transfers between devices  44.4 us (20%)
  Pallas kernels  29.6 us (13%)
  local copies, waits for them, and re-layouts  27.8 us (12%)
  other arithmetic  3.96 us (2%)
  matrix products  3.71 us (2%)
    all_to_all x2, waiting for transfers between devices, scatter_sum(): return jnp.sum(lax.all_to_all(blocks, axes, 0, 0).astype(f32), axis=0)  25 us
    unnamed x32, local copies, waits for them, and re-layouts  19.1 us
    all_to_all x1, waiting for transfers between devices, gather_all(): return lax.all_to_all(copies, axes, 0, 0)  15.8 us
    all_to_all x1, blocking collectives, body(): masses = lax.all_to_all(masses, ROWS, 0, 0)  15.4 us
    all_to_all x1, blocking collectives, body(): lax.all_to_all(image_pass(masses, base, col_count, soft_part), COLS, 0, 0)  14 us
    all_to_all x1, blocking collectives, body(): images = lax.all_to_all(image_pass(masses, base, col_count), COLS, 0, 0)  11.8 us
    all_to_all x1, waiting for transfers between devices, body(): lax.all_to_all(sent.reshape(col_count, local_width + 8, tall), COLS, 0, 0)  11.6 us
    all_to_all x2, starting transfers between devices, scatter_sum(): return jnp.sum(lax.all_to_all(blocks, axes, 0, 0).astype(f32), axis=0)  10.5 us
  transfers between devices with their start and end apart: 15, of which 9 were waited for; matrix products, arithmetic and copies ran while one was open for 8% of the time, Pallas kernels for 4%

profile of v5, /device:TPU:1, one launch (start us, length us, event | category | flops | bytes accessed | tf_op | source)
XLA Modules:
  0.0 224.8 jit_solution(10380077175046099161)
XLA Ops:
  2.7 2.2 collective-permute-start
  4.9 2.6 %collective-permute-start.1 = (bf16[128,1024]{1,0:T(8,128)(2,1)S(1)}, bf16[128,1024]{1,0:T(8,128)(2,1)S(1)}, u32[]{:S(2)}, u32[]{:S(2)}) collective-permute-start(bf16[128,1024]{1,0:T(8,128)(2,1)S(1)} %broadcast_select_fusion), channel_id=1, source_target_pairs={{0,2},{1,3},{2,0},{3,1},{4,6},{5,7},{6,4},{7,5},{8,10},{9,11},{10,... | collective-permute-start | bytes 786440 | tf_op jit(solution)/shard_map/ppermute | solution.py:420
  11.0 8.7 %all-to-all-start = ((bf16[32,40,128]{2,1,0:T(8,128)(2,1)}), bf16[32,40,128]{2,1,0:T(8,128)(2,1)S(1)}, u32[]{:S(2)}, u32[]{:S(2)}) async-start(bf16[32,40,128]{2,1,0:T(8,128)(2,1)} %bitcast.3), calls=%async_computation | async-start | bytes 655360 | tf_op jit(solution)/shard_map/all_to_all | solution.py:406
  20.7 11.6 %all-to-all-done = bf16[32,40,128]{2,1,0:T(8,128)(2,1)S(1)} async-done(((bf16[32,40,128]{2,1,0:T(8,128)(2,1)}), bf16[32,40,128]{2,1,0:T(8,128)(2,1)S(1)}, u32[]{:S(2)}, u32[]{:S(2)}) %all-to-all-start) | async-done | bytes 327712 | tf_op jit(solution)/shard_map/all_to_all | solution.py:406
  35.0 3.4 %all-to-all-start.1 = ((bf16[8,16,1024]{2,1,0:T(8,128)(2,1)}), bf16[8,16,1024]{2,1,0:T(8,128)(2,1)S(1)}, u32[]{:S(2)}, u32[]{:S(2)}) async-start(bf16[8,16,1024]{2,1,0:T(8,128)(2,1)} %bitcast.7), calls=%async_computation.1 | async-start | bytes 524288 | tf_op jit(solution)/shard_map/all_to_all | solution.py:38
  38.5 9.3 %all-to-all-done.1 = bf16[8,16,1024]{2,1,0:T(8,128)(2,1)S(1)} async-done(((bf16[8,16,1024]{2,1,0:T(8,128)(2,1)}), bf16[8,16,1024]{2,1,0:T(8,128)(2,1)S(1)}, u32[]{:S(2)}, u32[]{:S(2)}) %all-to-all-start.1) | async-done | bytes 262176 | tf_op jit(solution)/shard_map/all_to_all | solution.py:38
  49.5 4.5 %all-to-all-start.2 = ((bf16[32,16,1024]{2,1,0:T(8,128)(2,1)}), bf16[32,16,1024]{2,1,0:T(8,128)(2,1)S(1)}, u32[]{:S(2)}, u32[]{:S(2)}) async-start(bf16[32,16,1024]{2,1,0:T(8,128)(2,1)} %broadcast_in_dim.8), calls=%async_computation.2 | async-start | bytes 2097152 | tf_op jit(solution)/shard_map/all_to_all | solution.py:30
  54.1 2.2 copy-done.5
  56.2 2.3 %shard_map.77 = (bf16[2048,1024]{1,0:T(8,128)(2,1)S(1)}, f32[1,2048]{1,0:T(1,128)S(1)}, bf16[4,128,2048]{2,1,0:T(8,128)(2,1)S(1)}) custom-call(s32[1]{0:T(128)} %bitcast.core_ref, bf16[2048,1024]{1,0:T(8,128)(2,1)S(1)} %copy-done.5), custom_call_target="tpu_custom_call" | custom-call | flops 12582912 | bytes 10485760 | tf_op jit(solution)/shard_map/pallas_call | solution.py:169
  59.9 2.0 copy-done.7
  61.9 15.8 %all-to-all-done.2 = bf16[32,16,1024]{2,1,0:T(8,128)(2,1)S(1)} async-done(((bf16[32,16,1024]{2,1,0:T(8,128)(2,1)}), bf16[32,16,1024]{2,1,0:T(8,128)(2,1)S(1)}, u32[]{:S(2)}, u32[]{:S(2)}) %all-to-all-start.2) | async-done | bytes 1048608 | tf_op jit(solution)/shard_map/all_to_all | solution.py:30
  77.6 2.2 copy-done.8
  79.8 4.1 %shard_map.80 = (f32[512,2048]{1,0:T(8,128)S(1)}, bf16[512,2048]{1,0:T(8,128)(2,1)S(1)}, f32[8,2,2048]{2,1,0:T(2,128)S(1)}, f32[1,512]{1,0:T(1,128)S(1)}) custom-call(bf16[512,1024]{1,0:T(8,128)(2,1)S(1)} %bitcast.42, bf16[2048,1024]{1,0:T(8,128)(2,1)S(1)} %copy-done.8), custom_call_target="tpu_custom_call" | custom-call | flops 2147483648 | bytes 14680064 | tf_op jit(solution)/shard_map/pallas_call | solution.py:208
  83.9 15.4 %all_to_all.50.mass_ref = f32[8,2,2048]{2,1,0:T(2,128)S(1)} all-to-all(f32[8,2,2048]{2,1,0:T(2,128)S(1)} %get-tuple-element.14), channel_id=1, replica_groups=mesh['x'=4,'core'=2,'z'=8,'y'=4] {'x','core'}, dimensions={0} | all-to-all | bytes 262144 | tf_op jit(solution)/shard_map/all_to_all | solution.py:455
  100.5 14.0 %all_to_all.51.image_ref.soft_ref = f32[32,2,512]{2,1,0:T(2,128)S(1)} all-to-all(f32[32,2,512]{2,1,0:T(2,128)S(1)} %shard_map.81), channel_id=1, replica_groups=mesh['x'=4,'core'=2,'z'=8,'y'=4] {'z','y'}, dimensions={0} | all-to-all | bytes 262144 | tf_op jit(solution)/shard_map/all_to_all | solution.py:456
  115.5 10.0 %all_to_all.52.mass_ref = f32[8,2,2048]{2,1,0:T(2,128)S(1)} all-to-all(f32[8,2,2048]{2,1,0:T(2,128)S(1)} %shard_map.82), channel_id=1, replica_groups=mesh['x'=4,'core'=2,'z'=8,'y'=4] {'x','core'}, dimensions={0} | all-to-all | bytes 262144 | tf_op jit(solution)/shard_map/all_to_all | solution.py:458
  126.7 11.8 %all_to_all.53.image_ref = f32[32,1,512]{2,1,0:T(1,128)S(1)} all-to-all(f32[32,1,512]{2,1,0:T(1,128)S(1)} %shard_map.83), channel_id=1, replica_groups=mesh['x'=4,'core'=2,'z'=8,'y'=4] {'z','y'}, dimensions={0} | all-to-all | bytes 131072 | tf_op jit(solution)/shard_map/all_to_all | solution.py:459
  138.5 2.0 shard_map.84
  140.5 5.6 %all-to-all-start.7 = ((f32[8,2,2048]{2,1,0:T(2,128)}), f32[8,2,2048]{2,1,0:T(2,128)S(1)}, u32[]{:S(2)}, u32[]{:S(2)}) async-start(f32[8,2,2048]{2,1,0:T(2,128)} %shard_map.84), calls=%async_computation.7 | async-start | bytes 262144 | tf_op jit(solution)/shard_map/all_to_all | solution.py:458
  147.6 3.8 %all-to-all-done.7.mass_ref = f32[8,2,2048]{2,1,0:T(2,128)S(1)} async-done(((f32[8,2,2048]{2,1,0:T(2,128)}), f32[8,2,2048]{2,1,0:T(2,128)S(1)}, u32[]{:S(2)}, u32[]{:S(2)}) %all-to-all-start.7) | async-done | bytes 131104 | tf_op jit(solution)/shard_map/all_to_all | solution.py:458
  153.2 4.0 %all-to-all-start.8 = ((f32[32,1,512]{2,1,0:T(1,128)}), f32[32,1,512]{2,1,0:T(1,128)S(1)}, u32[]{:S(2)}, u32[]{:S(2)}) async-start(f32[32,1,512]{2,1,0:T(1,128)} %shard_map.85), calls=%async_computation.8 | async-start | bytes 131072 | tf_op jit(solution)/shard_map/all_to_all | solution.py:459
  157.3 3.6 %constant_dynamic-slice_fusion = (bf16[4,1,128,512]{2,1,0,3:T(2,128)(2,1)}, bf16[4,1,128,512]{2,1,0,3:T(2,128)(2,1)}) fusion(bf16[4,2,128,512]{2,1,0,3:T(2,128)(2,1)S(1)} %copy-done.12, s32[]{:T(128)S(6)} %select_n.37, s32[]{:T(128)S(6)} %select_n.36), kind=kLoop, calls=%fused_computation.26 | loop fusion | bytes 2097160 | tf_op jit(solution)/shard_map/jit(dynamic_index_in_dim)/dynamic_slice | solution.py:463
  160.8 2.4 %copy.19 = bf16[4,1,128,512]{3,2,0,1:T(8,128)(2,1)S(1)} copy(bf16[4,1,128,512]{2,1,0,3:T(2,128)(2,1)} %get-tuple-element.31) | data formatting | bytes 1048576
  166.0 2.2 copy-done.11
  168.2 5.7 %shard_map.86 = (bf16[512,2048]{1,0:T(8,128)(2,1)S(1)}, f32[1,2048]{1,0:T(1,128)S(1)}, bf16[512,2048]{1,0:T(8,128)(2,1)}, f32[512,2048]{1,0:T(8,128)S(1)}) custom-call(f32[32,1,512]{2,1,0:T(1,128)S(1)} %all-to-all-done.8.image_ref, f32[32,2,512]{2,1,0:T(2,128)S(1)} %all_to_all.51.image_ref.soft_ref, f32[8,2,2048]{2,1,0:T(2,128)S(1)} %all-to-all-done.7.mass_ref, ...), custom_call_target="tpu_custom_call" | custom-call | flops 2147483648 | bytes 12582912 | tf_op jit(solution)/shard_map/pallas_call | solution.py:318
  175.9 3.4 %convolution_convert_fusion = bf16[1024,512]{1,0:T(8,128)(2,1)} fusion(bf16[2048,1024]{1,0:T(8,128)(2,1)S(1)} %copy-done.9, bf16[512,2048]{1,0:T(8,128)(2,1)S(1)} %get-tuple-element.18), kind=kOutput, calls=%fused_computation.1 | convolution fusion | flops 2148007936 | bytes 7340032 | tf_op jit(solution)/shard_map/dot_general | solution.py:467
  179.3 7.1 %all-to-all-start.9 = ((bf16[32,32,512]{2,1,0:T(8,128)(2,1)}), bf16[32,32,512]{2,1,0:T(8,128)(2,1)}, u32[]{:S(2)}, u32[]{:S(2)}) async-start(bf16[32,32,512]{2,1,0:T(8,128)(2,1)} %bitcast.12), calls=%async_computation.9 | async-start | bytes 2097152 | tf_op jit(solution)/shard_map/all_to_all | solution.py:38
  187.6 2.2 copy-done.1
  197.9 15.7 %all-to-all-done.9 = bf16[32,32,512]{2,1,0:T(8,128)(2,1)} async-done(((bf16[32,32,512]{2,1,0:T(8,128)(2,1)}), bf16[32,32,512]{2,1,0:T(8,128)(2,1)}, u32[]{:S(2)}, u32[]{:S(2)}) %all-to-all-start.9) | async-done | bytes 1048608 | tf_op jit(solution)/shard_map/all_to_all | solution.py:38
  215.6 4.6 %collective-permute-done.7.rest_1_ = bf16[128,2048]{1,0:T(8,128)(2,1)S(1)} collective-permute-done((bf16[128,2048]{1,0:T(8,128)(2,1)}, bf16[128,2048]{1,0:T(8,128)(2,1)S(1)}, u32[]{:S(2)}, u32[]{:S(2)}) %collective-permute-start.7) | collective-permute-done | bytes 524320 | tf_op jit(solution)/shard_map/ppermute | solution.py:481
  220.3 2.2 copy-done.2
  222.4 2.3 %shard_map.90 = f32[128,2048]{1,0:T(8,128)} custom-call(s32[1]{0:T(128)} %bitcast.14.place_ref, f32[4,128,2048]{2,1,0:T(8,128)S(1)} %bitcast.41, bf16[4,128,2048]{2,1,0:T(8,128)(2,1)} %bitcast.16.arrived_ref, bf16[4,128,2048]{2,1,0:T(8,128)(2,1)S(1)} %copy-done.4, f32[1,2048]{1,0:T(1,128)S(1)} %get-tuple-element.22.one_ref, ...), custom_call_target="tpu_custom_call" | custom-call | flops 1572864 | bytes 2621440 | tf_op jit(solution)/shard_map/pallas_call | solution.py:372
  (78 shorter events, 35.2 us)
Async XLA Ops:
  2.7 16.9 %collective-permute-start = (bf16[128,1024]{1,0:T(8,128)(2,1)S(1)}, bf16[128,1024]{1,0:T(8,128)(2,1)S(1)}, u32[]{:S(2)}, u32[]{:S(2)}) collective-permute-start(bf16[128,1024]{1,0:T(8,128)(2,1)S(1)} %broadcast_select_fusion), channel_id=1, source_target_pairs={{0,1},{1,2},{2,3},{3,0},{4,5},{5,6},{6,7},{7,4},{8,9},{9,10},{10,1... | collective-permute-start | bytes 786440 | tf_op jit(solution)/shard_map/ppermute | solution.py:420
  4.9 14.9 %collective-permute-start.1 = (bf16[128,1024]{1,0:T(8,128)(2,1)S(1)}, bf16[128,1024]{1,0:T(8,128)(2,1)S(1)}, u32[]{:S(2)}, u32[]{:S(2)}) collective-permute-start(bf16[128,1024]{1,0:T(8,128)(2,1)S(1)} %broadcast_select_fusion), channel_id=1, source_target_pairs={{0,2},{1,3},{2,0},{3,1},{4,6},{5,7},{6,4},{7,5},{8,10},{9,11},{10,... | collective-permute-start | bytes 786440 | tf_op jit(solution)/shard_map/ppermute | solution.py:420
  7.5 12.3 %collective-permute-start.2 = (bf16[128,1024]{1,0:T(8,128)(2,1)S(1)}, bf16[128,1024]{1,0:T(8,128)(2,1)S(1)}, u32[]{:S(2)}, u32[]{:S(2)}) collective-permute-start(bf16[128,1024]{1,0:T(8,128)(2,1)S(1)} %broadcast_select_fusion), channel_id=1, source_target_pairs={{0,3},{1,0},{2,1},{3,2},{4,7},{5,4},{6,5},{7,6},{8,11},{9,8},{10,9... | collective-permute-start | bytes 786440 | tf_op jit(solution)/shard_map/ppermute | solution.py:420
  11.0 21.3 %all-to-all-start = ((bf16[32,40,128]{2,1,0:T(8,128)(2,1)}), bf16[32,40,128]{2,1,0:T(8,128)(2,1)S(1)}, u32[]{:S(2)}, u32[]{:S(2)}) async-start(bf16[32,40,128]{2,1,0:T(8,128)(2,1)} %bitcast.3), calls=%async_computation | async-start | bytes 655360 | tf_op jit(solution)/shard_map/all_to_all | solution.py:406
  19.9 13.2 %copy-start.6 = (bf16[128,1024]{1,0:T(8,128)(2,1)S(1)}, bf16[128,1024]{1,0:T(8,128)(2,1)}, u32[]{:S(2)}) copy-start(bf16[128,1024]{1,0:T(8,128)(2,1)} %w_out_ref.1) | copy-start | bytes 786436
  19.9 13.2 %collective-permute-start.3 = (bf16[3,128,1024]{2,1,0:T(8,128)(2,1)S(1)}, bf16[3,128,1024]{2,1,0:T(8,128)(2,1)S(1)}, u32[]{:S(2)}, u32[]{:S(2)}) collective-permute-start(bf16[3,128,1024]{2,1,0:T(8,128)(2,1)S(1)} %shard_map.78.shares_ref), channel_id=1, source_target_pairs={{0,32},{32,0},{1,33},{33,1},{2,34},{34,2},{3,35},{35,3},{4,36},{36... | collective-permute-start | bytes 2359304 | tf_op jit(solution)/shard_map/ppermute | solution.py:424
  35.0 12.8 %all-to-all-start.1 = ((bf16[8,16,1024]{2,1,0:T(8,128)(2,1)}), bf16[8,16,1024]{2,1,0:T(8,128)(2,1)S(1)}, u32[]{:S(2)}, u32[]{:S(2)}) async-start(bf16[8,16,1024]{2,1,0:T(8,128)(2,1)} %bitcast.7), calls=%async_computation.1 | async-start | bytes 524288 | tf_op jit(solution)/shard_map/all_to_all | solution.py:38
  49.5 28.1 %all-to-all-start.2 = ((bf16[32,16,1024]{2,1,0:T(8,128)(2,1)}), bf16[32,16,1024]{2,1,0:T(8,128)(2,1)S(1)}, u32[]{:S(2)}, u32[]{:S(2)}) async-start(bf16[32,16,1024]{2,1,0:T(8,128)(2,1)} %broadcast_in_dim.8), calls=%async_computation.2 | async-start | bytes 2097152 | tf_op jit(solution)/shard_map/all_to_all | solution.py:30
  54.1 2.2 copy-start.5
  58.5 1.3 copy-start.3
  59.9 2.0 copy-start.7
  77.6 2.2 copy-start.8
  83.9 31.6 %copy-start.10 = (f32[512,2048]{1,0:T(8,128)}, f32[512,2048]{1,0:T(8,128)S(1)}, u32[]{:S(2)}) copy-start(f32[512,2048]{1,0:T(8,128)S(1)} %get-tuple-element.17.scores_ref) | copy-start | bytes 12582916
  140.5 10.8 %all-to-all-start.7 = ((f32[8,2,2048]{2,1,0:T(2,128)}), f32[8,2,2048]{2,1,0:T(2,128)S(1)}, u32[]{:S(2)}, u32[]{:S(2)}) async-start(f32[8,2,2048]{2,1,0:T(2,128)} %shard_map.84), calls=%async_computation.7 | async-start | bytes 262144 | tf_op jit(solution)/shard_map/all_to_all | solution.py:458
  147.6 9.6 %copy-start.12 = (bf16[4,2,128,512]{2,1,0,3:T(2,128)(2,1)S(1)}, bf16[4,2,128,512]{2,1,0,3:T(2,128)(2,1)}, u32[]{:S(2)}) copy-start(bf16[4,2,128,512]{2,1,0,3:T(2,128)(2,1)} %reshape.128) | copy-start | bytes 3145732
  153.2 12.8 %all-to-all-start.8 = ((f32[32,1,512]{2,1,0:T(1,128)}), f32[32,1,512]{2,1,0:T(1,128)S(1)}, u32[]{:S(2)}, u32[]{:S(2)}) async-start(f32[32,1,512]{2,1,0:T(1,128)} %shard_map.85), calls=%async_computation.8 | async-start | bytes 131072 | tf_op jit(solution)/shard_map/all_to_all | solution.py:459
  160.8 2.4 %copy-start.13 = (bf16[4,1,128,512]{2,1,0,3:T(2,128)(2,1)S(1)}, bf16[4,1,128,512]{2,1,0,3:T(2,128)(2,1)}, u32[]{:S(2)}) copy-start(bf16[4,1,128,512]{2,1,0,3:T(2,128)(2,1)} %get-tuple-element.30) | copy-start | bytes 1572868
  166.0 2.2 copy-start.11
  168.2 7.6 %copy-start.9 = (bf16[2048,1024]{1,0:T(8,128)(2,1)S(1)}, bf16[2048,1024]{1,0:T(8,128)(2,1)}, u32[]{:S(2)}) copy-start(bf16[2048,1024]{1,0:T(8,128)(2,1)} %copy-done.7) | copy-start | bytes 12582916
  173.9 5.3 %copy-start = (f32[512,2048]{1,0:T(8,128)}, f32[512,2048]{1,0:T(8,128)S(1)}, u32[]{:S(2)}) copy-start(f32[512,2048]{1,0:T(8,128)S(1)} %get-tuple-element.19) | copy-start | bytes 12582916
  173.9 13.7 %collective-permute-start.4 = (bf16[512,2048]{1,0:T(8,128)(2,1)}, bf16[512,2048]{1,0:T(8,128)(2,1)}, u32[]{:S(2)}, u32[]{:S(2)}) collective-permute-start(bf16[512,2048]{1,0:T(8,128)(2,1)} %get-tuple-element.20), channel_id=1, source_target_pairs={{0,32},{32,0},{1,33},{33,1},{2,34},{34,2},{3,35},{35,3},{4,36},{36... | collective-permute-start | bytes 6291464 | tf_op jit(solution)/shard_map/ppermute | solution.py:472
  179.2 8.4 %copy-start.4 = (bf16[4,128,2048]{2,1,0:T(8,128)(2,1)S(1)}, bf16[4,128,2048]{2,1,0:T(8,128)(2,1)}, u32[]{:S(2)}) copy-start(bf16[4,128,2048]{2,1,0:T(8,128)(2,1)} %copy-done.3) | copy-start | bytes 6291460
  179.3 34.3 %all-to-all-start.9 = ((bf16[32,32,512]{2,1,0:T(8,128)(2,1)}), bf16[32,32,512]{2,1,0:T(8,128)(2,1)}, u32[]{:S(2)}, u32[]{:S(2)}) async-start(bf16[32,32,512]{2,1,0:T(8,128)(2,1)} %bitcast.12), calls=%async_computation.9 | async-start | bytes 2097152 | tf_op jit(solution)/shard_map/all_to_all | solution.py:38
  186.4 1.3 collective-permute-start.5
  187.6 2.2 copy-start.1
  191.8 23.8 %collective-permute-start.8 = (bf16[128,2048]{1,0:T(8,128)(2,1)}, bf16[128,2048]{1,0:T(8,128)(2,1)S(1)}, u32[]{:S(2)}, u32[]{:S(2)}) collective-permute-start(bf16[128,2048]{1,0:T(8,128)(2,1)} %shard_map.89), channel_id=1, source_target_pairs={{0,192},{64,0},{128,64},{192,128},{1,193},{65,1},{129,65},{193,129... | collective-permute-start | bytes 1572872 | tf_op jit(solution)/shard_map/ppermute | solution.py:481
  194.7 25.6 %collective-permute-start.7 = (bf16[128,2048]{1,0:T(8,128)(2,1)}, bf16[128,2048]{1,0:T(8,128)(2,1)S(1)}, u32[]{:S(2)}, u32[]{:S(2)}) collective-permute-start(bf16[128,2048]{1,0:T(8,128)(2,1)} %shard_map.88), channel_id=1, source_target_pairs={{0,64},{64,128},{128,192},{192,0},{1,65},{65,129},{129,193},{193,1... | collective-permute-start | bytes 1572872 | tf_op jit(solution)/shard_map/ppermute | solution.py:481
  197.2 23.0 %collective-permute-start.6 = (bf16[128,2048]{1,0:T(8,128)(2,1)}, bf16[128,2048]{1,0:T(8,128)(2,1)}, u32[]{:S(2)}, u32[]{:S(2)}) collective-permute-start(bf16[128,2048]{1,0:T(8,128)(2,1)} %shard_map.87), channel_id=1, source_target_pairs={{0,128},{64,192},{128,0},{192,64},{1,129},{65,193},{129,1},{193,65... | collective-permute-start | bytes 1572872 | tf_op jit(solution)/shard_map/ppermute | solution.py:481
  220.3 2.2 copy-start.2

commit v6 on v5

--- a/solution.py
+++ b/solution.py
@@ -97,6 +97,14 @@
     @pl.when(pl.program_id(0) > 0)
     def _():
         total[...] += part
+
+
+def in_hbm(shape, dtype):
+    return pltpu.HBM(shape, dtype)
+
+
+def keep_hbm(values):
+    return pltpu.with_memory_space_constraint(values, pltpu.HBM)
 
 
 def stack_kernel(first_ref, second_ref, third_ref, out_ref):
@@ -179,23 +187,43 @@
             pl.BlockSpec((x_count, LANES, TILE), lambda i: (0, 0, i)),
         ],
         out_shape=[
-            jax.ShapeDtypeStruct((protos, D), bf16),
+            in_hbm((protos, D), bf16),
             jax.ShapeDtypeStruct((1, protos), f32),
-            jax.ShapeDtypeStruct((x_count, LANES, protos), bf16),
+            in_hbm((x_count, LANES, protos), bf16),
         ],
         compiler_params=params(18),
         cost_estimate=cost(6 * protos * D, 5 * protos * D),
-    )(core.reshape(1), prototypes)
-
-
-def scores_kernel(copies, embed_ref, unit_ref, scores_ref, base_ref, mass_ref, soft_ref, total):
+    )(core.reshape(1), keep_hbm(prototypes))
+
+
+def scores_kernel(first, last, blocks, place_ref, embed_ref, unit_ref, *rest):
+    before_ref = None if first else rest[0]
+    scores_ref, base_ref, mass_ref, soft_ref, turned_ref, total = rest[-6:]
+
+    @pl.when(pl.program_id(0) == 0)
+    def _():
+        even = place_ref[1] == 0
+        values = embed_ref[...].astype(f32)
+        for block in range(D // (2 * LANES)):
+            start = 2 * block * LANES
+            low = values[:, start : start + LANES]
+            high = values[:, start + LANES : start + 2 * LANES]
+            rows = slice(block * LANES, (block + 1) * LANES)
+            turned_ref[0, rows, :] = jnp.where(even, high, low).T.astype(bf16)
+            turned_ref[1, rows, :] = jnp.where(even, low, high).T.astype(bf16)
+
     scores = lax.dot_general(embed_ref[...], unit_ref[...], NT, preferred_element_type=f32)
     scores_ref[...] = scores
     soft = jnp.exp(scores * (1.0 / soft_temp))
     base = soft * soft
     base_ref[...] = base.astype(bf16)
-    mass = view_sums(base)
-    mass_ref[...] = jnp.broadcast_to(mass[None], (copies,) + mass.shape)
+    line = jnp.sum(base, axis=0, keepdims=True)
+    later = place_ref[0] >= blocks // 2
+    none = jnp.zeros_like(line)
+    mass = jnp.concatenate([jnp.where(later, none, line), jnp.where(later, line, none)], axis=0)
+    if not first:
+        mass = mass + before_ref[...]
+    mass_ref[...] = jnp.broadcast_to(mass, mass_ref.shape) if last else mass
     accumulate(total, fold_lanes(soft))
 
     @pl.when(pl.program_id(0) == pl.num_programs(0) - 1)
@@ -203,28 +231,55 @@
         soft_ref[...] = jnp.sum(total[...].T, axis=0, keepdims=True)
 
 
-def score_pass(embed, unit, copies):
-    rows, protos = embed.shape[0], unit.shape[0]
-    return pl.pallas_call(
-        functools.partial(scores_kernel, copies),
-        grid=(protos // TILE,),
-        in_specs=[whole(embed.shape), pl.BlockSpec((TILE, D), lambda i: (i, 0))],
-        out_specs=[
-            pl.BlockSpec((rows, TILE), lambda i: (0, i)),
-            pl.BlockSpec((rows, TILE), lambda i: (0, i)),
-            pl.BlockSpec((copies, 2, TILE), lambda i: (0, 0, i)),
-            whole((1, rows)),
-        ],
-        out_shape=[
-            jax.ShapeDtypeStruct((rows, protos), f32),
-            jax.ShapeDtypeStruct((rows, protos), bf16),
-            jax.ShapeDtypeStruct((copies, 2, protos), f32),
-            jax.ShapeDtypeStruct((1, rows), f32),
-        ],
-        scratch_shapes=[pltpu.VMEM((rows, LANES), f32)],
-        compiler_params=params(18),
-        cost_estimate=cost(2 * rows * protos * D, 14 * rows * protos, rows * protos),
-    )(embed, unit)
+def score_pass(place, embed, unit, blocks, copies, last, before=None):
+    height, protos = embed.shape[0], unit.shape[0]
+    rows = height * blocks
+    first = before is None
+    mass = (copies, 2, protos) if last else (2, protos)
+    mass_spec = (
+        pl.BlockSpec((copies, 2, TILE), lambda i, p: (0, 0, i))
+        if last
+        else pl.BlockSpec((2, TILE), lambda i, p: (0, i))
+    )
+    shapes = [
+        in_hbm((rows, protos), f32),
+        jax.ShapeDtypeStruct((rows, protos), bf16),
+        jax.ShapeDtypeStruct(mass, f32),
+        jax.ShapeDtypeStruct((1, rows), f32),
+        jax.ShapeDtypeStruct((2, D // 2, rows), bf16),
+    ]
+    in_specs = [
+        pl.BlockSpec((height, D), lambda i, p: (0, 0)),
+        pl.BlockSpec((TILE, D), lambda i, p: (i, 0)),
+    ]
+    arrays = [embed, keep_hbm(unit)]
+    aliases = {}
+    if not first:
+        scores, base, mass_before, soft, turned = before
+        in_specs.append(pl.BlockSpec((2, TILE), lambda i, p: (0, i)))
+        in_specs += [pl.BlockSpec(memory_space=pl.ANY)] * 4
+        arrays += [mass_before, scores, base, soft, turned]
+        aliases = {4: 0, 5: 1, 6: 3, 7: 4}
+    return pl.pallas_call(
+        functools.partial(scores_kernel, first, last, blocks),
+        grid_spec=pltpu.PrefetchScalarGridSpec(
+            num_scalar_prefetch=1,
+            grid=(protos // TILE,),
+            in_specs=in_specs,
+            out_specs=[
+                pl.BlockSpec((height, TILE), lambda i, p: (p[0], i)),
+                pl.BlockSpec((height, TILE), lambda i, p: (p[0], i)),
+                mass_spec,
+                pl.BlockSpec((1, height), lambda i, p: (0, p[0])),
+                pl.BlockSpec((2, D // 2, height), lambda i, p: (0, 0, p[0])),
+            ],
+            scratch_shapes=[pltpu.VMEM((height, LANES), f32)],
+        ),
+        out_shape=shapes,
+        input_output_aliases=aliases,
+        compiler_params=params(12),
+        cost_estimate=cost(2 * height * protos * D, 8 * height * protos, height * protos),
+    )(place, *arrays)
 
 
 def image_kernel(copies, mass_ref, base_ref, *rest):
@@ -284,7 +339,7 @@
 
 
 def grad_kernel(
-    image_ref, soft_ref, mass_ref, scores_ref, away_t_ref, stay_t_ref,
+    image_ref, soft_ref, mass_ref, scores_ref, embed_t_ref,
     grad_ref, radial_ref, away_ref, stay_ref, code_column, prob_column,
 ):
     @pl.when(pl.program_id(0) == 0)
@@ -304,17 +359,21 @@
     grad = (soft * spread_lanes(prob_column[...], width) - swapped).astype(bf16)
     grad_ref[...] = grad
     radial_ref[...] = jnp.sum(grad.astype(f32) * scores, axis=0, keepdims=True)
-    away_ref[...] = jnp.dot(away_t_ref[...], grad, preferred_element_type=f32).astype(bf16)
-    stay_ref[...] = jnp.dot(stay_t_ref[...], grad, preferred_element_type=f32)
-
-
-def grad_pass(images, softs, masses, scores, away_t, stay_t):
+    away = jnp.dot(embed_t_ref[0], grad, preferred_element_type=f32).astype(bf16)
+    away_ref[...] = away.reshape(away_ref.shape)
+    stay = jnp.dot(embed_t_ref[1], grad, preferred_element_type=f32)
+    stay_ref[...] = stay.reshape(stay_ref.shape)
+
+
+def grad_pass(images, softs, masses, scores, embed_t):
     rows, protos = scores.shape
-    depth = away_t.shape[0]
+    depth = embed_t.shape[1]
+    blocks = depth // LANES
 
     def tile(height):
         return pl.BlockSpec((height, TILE), lambda i: (0, i))
 
+    halves = pl.BlockSpec((blocks, LANES, TILE), lambda i: (0, 0, i))
     return pl.pallas_call(
         grad_kernel,
         grid=(protos // TILE,),
@@ -323,20 +382,19 @@
             whole(softs.shape),
             pl.BlockSpec((masses.shape[0], 2, TILE), lambda i: (0, 0, i)),
             tile(rows),
-            whole(away_t.shape),
-            whole(stay_t.shape),
+            whole(embed_t.shape),
         ],
-        out_specs=[tile(rows), tile(1), tile(depth), tile(depth)],
+        out_specs=[tile(rows), tile(1), halves, halves],
         out_shape=[
             jax.ShapeDtypeStruct((rows, protos), bf16),
             jax.ShapeDtypeStruct((1, protos), f32),
-            jax.ShapeDtypeStruct((depth, protos), bf16),
-            jax.ShapeDtypeStruct((depth, protos), f32),
+            in_hbm((blocks, LANES, protos), bf16),
+            in_hbm((blocks, LANES, protos), f32),
         ],
         scratch_shapes=[pltpu.VMEM((rows, LANES), f32)] * 2,
         compiler_params=params(20),
         cost_estimate=cost(4 * depth * rows * protos, 12 * rows * protos, rows * protos),
-    )(images, softs, masses, scores, away_t, stay_t)
+    )(images, softs, masses, keep_hbm(scores), embed_t)
 
 
 def pair(stay, arrived, turned, radials, length):
@@ -365,7 +423,7 @@
 
 def pair_call(place, stay, arrived, turned, radials, length, others=()):
     blocks, height, protos = stay.shape
-    wide = 2 * TILE
+    wide = TILE
     picked = pl.BlockSpec((1, height, wide), lambda i, p: (p[0], 0, i))
     line = pl.BlockSpec((1, wide), lambda i, p: (0, i))
     flat = pl.BlockSpec((height, wide), lambda i, p: (0, i))
@@ -379,8 +437,8 @@
         ),
         out_shape=jax.ShapeDtypeStruct((height, protos), f32 if others else bf16),
         compiler_params=params(12),
-        cost_estimate=cost(6 * height * protos, 10 * height * protos),
-    )(place.reshape(1), stay, arrived, turned, *radials, length, *others)
+        cost_estimate=cost(40 * 10**9 if others else 10**9, 10 * height * protos),
+    )(place.reshape(1), keep_hbm(stay), keep_hbm(arrived), keep_hbm(turned), *radials, length, *others)
 
 
 def body(hidden_states, ln_in_gain, w_in, w_out, ln_out_gain, prototypes):
@@ -442,7 +500,7 @@
     final = (resid - center) * lax.rsqrt(spread + norm_eps) * gain_out[None, :]
     squared = jnp.sum(final * final, axis=1, keepdims=True)
     embed_part = (final * lax.rsqrt(squared + unit_eps)).astype(bf16)
-    embed = gather_all(embed_part, ("y", "z")).reshape(row_count, D)
+    own_rows = gather_all(embed_part, "z").reshape(tall, D)
 
     x_index = lax.axis_index("x")
     x_count = lax.axis_size("x")
@@ -451,26 +509,29 @@
     slice_width = turned.shape[1]
 
     row_parts = lax.axis_size(ROWS)
-    scores, base, masses, soft_part = score_pass(embed, unit, row_parts)
+    y_index = lax.axis_index("y")
+    steps = (1, 3, 2)
+    rows_in = {
+        step: lax.ppermute(own_rows, "y", [(i, (i + step) % y_count) for i in range(y_count)])
+        for step in steps
+    }
+    state = None
+    for step in (0,) + steps:
+        place = jnp.stack([(y_index + y_count - step) % y_count, core])
+        block_rows = rows_in[step] if step else own_rows
+        state = score_pass(place, block_rows, unit, y_count, row_parts, step == steps[-1], state)
+    scores, base, masses, soft_part, embed_t = state
     masses = lax.all_to_all(masses, ROWS, 0, 0)
     softs = images = lax.all_to_all(image_pass(masses, base, col_count, soft_part), COLS, 0, 0)
     for repeat in range(1, SINK_ITERS):
         masses = lax.all_to_all(proto_pass(images, base, row_parts), ROWS, 0, 0)
         images = lax.all_to_all(image_pass(masses, base, col_count), COLS, 0, 0)
 
-    embed_t = embed.T.reshape(x_count, 2, slice_width, row_count)
-    away_t, stay_t = (
-        lax.dynamic_index_in_dim(embed_t, side, 1, False).reshape(-1, row_count)
-        for side in (1 - core, core)
-    )
-    grad_flat, radial, away, stay = grad_pass(images, softs, masses, scores, away_t, stay_t)
+    grad_flat, radial, away, stay = grad_pass(images, softs, masses, scores, embed_t)
     embed_terms = lax.dot_general(
         unit, grad_flat, (((0,), (1,)), ((), ())), preferred_element_type=f32
     ).astype(bf16)
-    stay, arrived = (
-        part.reshape(x_count, slice_width, proto_count)
-        for part in (stay, lax.ppermute(away, "core", swap))
-    )
+    arrived = lax.ppermute(away, "core", swap)
     radials = (radial, lax.ppermute(radial, "core", swap))
 
     def paired(step, others=()):

time: 226 us -> 228 us (level)
  Pallas kernels: 29.6 us -> 55.9 us
  local copies, waits for them, and re-layouts: 27.8 us -> 4.34 us
  blocking collectives: 51.1 us -> 71.5 us
  waiting for transfers between devices: 63.2 us -> 51 us
  starting transfers between devices: 44.4 us -> 34.6 us
    pallas_call x1 -> x4, Pallas kernels: 4.07 us -> 23.3 us  [score_pass(): pl.pallas_call(functools.partial(scores_kernel, first, last, blocks), gri...]
    unnamed x32 -> x6, local copies, waits for them, and re-layouts: 19.1 us -> 1.1 us
    all_to_all x1 -> x2, blocking collectives: 11.8 us -> 23.6 us  [body(): images = lax.all_to_all(image_pass(masses, base, col_count), COLS, 0, 0)]
    all_to_all x1 -> x2, blocking collectives: 9.98 us -> 19.9 us  [body(): masses = lax.all_to_all(proto_pass(images, base, row_parts), ROWS, 0, 0)]
    all_to_all x2 -> x0, starting transfers between devices: 9.59 us -> none  [the longest x1 5.55 us: body(): masses = lax.all_to_all(proto_pass(images, base, row_parts), ROWS, 0, 0)]
    all_to_all x1, waiting for transfers between devices: 15.8 us -> 9.17 us  [gather_all(): return lax.all_to_all(copies, axes, 0, 0)]
    all_to_all x2 -> x0, waiting for transfers between devices: 5.18 us -> none  [the longest x1 3.76 us: body(): masses = lax.all_to_all(proto_pass(images, base, row_parts), ROWS, 0, 0)]
    pallas_call x1, Pallas kernels: 2.28 us -> 5.86 us  [prepare(): pl.pallas_call(prepare_kernel, grid=(protos // TILE,), in_specs=[pl.Block...]
  transfers between devices with their start and end apart: 15 -> 16, of which waited for: 9 -> 7; matrix products, arithmetic and copies ran while one was open for 8% -> 4% of each run, Pallas kernels for 4% -> 14%
where the time goes in v6:
time: 228 us; the launch traced here: 226 us
  blocking collectives  71.5 us (31%)
  Pallas kernels  55.9 us (25%)
  waiting for transfers between devices  51 us (22%)
  starting transfers between devices  34.6 us (15%)
  local copies, waits for them, and re-layouts  4.34 us (2%)
  other arithmetic  4.26 us (2%)
  matrix products  3.69 us (2%)
    all_to_all x2, waiting for transfers between devices, scatter_sum(): return jnp.sum(lax.all_to_all(blocks, axes, 0, 0).astype(f32), axis=0)  26.2 us
    all_to_all x2, blocking collectives, body(): images = lax.all_to_all(image_pass(masses, base, col_count), COLS, 0, 0)  23.6 us
    pallas_call x4, Pallas kernels, score_pass(): pl.pallas_call(functools.partial(scores_kernel, first, last, blocks), gri...  23.3 us
    all_to_all x2, blocking collectives, body(): masses = lax.all_to_all(proto_pass(images, base, row_parts), ROWS, 0, 0)  19.9 us
    all_to_all x1, blocking collectives, body(): masses = lax.all_to_all(masses, ROWS, 0, 0)  14.8 us
    all_to_all x1, blocking collectives, body(): lax.all_to_all(image_pass(masses, base, col_count, soft_part), COLS, 0, 0)  13.2 us
    all_to_all x1, waiting for transfers between devices, body(): lax.all_to_all(sent.reshape(col_count, local_width + 8, tall), COLS, 0, 0)  11.6 us
    pallas_call x4, Pallas kernels, pair_call(): pl.pallas_call(final_kernel if others else pair_kernel, grid_spec=pltpu.P...  11.2 us
  transfers between devices with their start and end apart: 16, of which 7 were waited for; matrix products, arithmetic and copies ran while one was open for 4% of the time, Pallas kernels for 14%

profile of v6, /device:TPU:1, one launch (start us, length us, event | category | flops | bytes accessed | tf_op | source)
XLA Modules:
  0.0 226.3 jit_solution(3675113835773922614)
XLA Ops:
  2.7 2.2 collective-permute-start
  4.9 2.6 %collective-permute-start.1 = (bf16[128,1024]{1,0:T(8,128)(2,1)S(1)}, bf16[128,1024]{1,0:T(8,128)(2,1)S(1)}, u32[]{:S(2)}, u32[]{:S(2)}) collective-permute-start(bf16[128,1024]{1,0:T(8,128)(2,1)S(1)} %broadcast_select_fusion), channel_id=1, source_target_pairs={{0,2},{1,3},{2,0},{3,1},{4,6},{5,7},{6,4},{7,5},{8,10},{9,11},{10,... | collective-permute-start | bytes 786440 | tf_op jit(solution)/shard_map/ppermute | solution.py:478
  11.0 8.7 %all-to-all-start = ((bf16[32,40,128]{2,1,0:T(8,128)(2,1)}), bf16[32,40,128]{2,1,0:T(8,128)(2,1)S(1)}, u32[]{:S(2)}, u32[]{:S(2)}) async-start(bf16[32,40,128]{2,1,0:T(8,128)(2,1)} %bitcast.4), calls=%async_computation | async-start | bytes 655360 | tf_op jit(solution)/shard_map/all_to_all | solution.py:464
  20.7 11.6 %all-to-all-done = bf16[32,40,128]{2,1,0:T(8,128)(2,1)S(1)} async-done(((bf16[32,40,128]{2,1,0:T(8,128)(2,1)}), bf16[32,40,128]{2,1,0:T(8,128)(2,1)S(1)}, u32[]{:S(2)}, u32[]{:S(2)}) %all-to-all-start) | async-done | bytes 327712 | tf_op jit(solution)/shard_map/all_to_all | solution.py:464
  33.1 1.9 shard_map.79
  35.0 3.4 %all-to-all-start.1 = ((bf16[8,16,1024]{2,1,0:T(8,128)(2,1)}), bf16[8,16,1024]{2,1,0:T(8,128)(2,1)S(1)}, u32[]{:S(2)}, u32[]{:S(2)}) async-start(bf16[8,16,1024]{2,1,0:T(8,128)(2,1)} %bitcast.8), calls=%async_computation.1 | async-start | bytes 524288 | tf_op jit(solution)/shard_map/all_to_all | solution.py:38
  38.5 9.3 %all-to-all-done.1 = bf16[8,16,1024]{2,1,0:T(8,128)(2,1)S(1)} async-done(((bf16[8,16,1024]{2,1,0:T(8,128)(2,1)}), bf16[8,16,1024]{2,1,0:T(8,128)(2,1)S(1)}, u32[]{:S(2)}, u32[]{:S(2)}) %all-to-all-start.1) | async-done | bytes 262176 | tf_op jit(solution)/shard_map/all_to_all | solution.py:38
  49.2 3.4 %all-to-all-start.2 = ((bf16[8,16,1024]{2,1,0:T(8,128)(2,1)}), bf16[8,16,1024]{2,1,0:T(8,128)(2,1)S(1)}, u32[]{:S(2)}, u32[]{:S(2)}) async-start(bf16[8,16,1024]{2,1,0:T(8,128)(2,1)} %broadcast_in_dim.8), calls=%async_computation.2 | async-start | bytes 524288 | tf_op jit(solution)/shard_map/all_to_all | solution.py:30
  52.8 9.2 %all-to-all-done.2 = bf16[8,16,1024]{2,1,0:T(8,128)(2,1)S(1)} async-done(((bf16[8,16,1024]{2,1,0:T(8,128)(2,1)}), bf16[8,16,1024]{2,1,0:T(8,128)(2,1)S(1)}, u32[]{:S(2)}, u32[]{:S(2)}) %all-to-all-start.2) | async-done | bytes 262176 | tf_op jit(solution)/shard_map/all_to_all | solution.py:30
  62.2 2.4 %collective-permute-start.5 = (bf16[128,1024]{1,0:T(8,128)(2,1)S(1)}, bf16[128,1024]{1,0:T(8,128)(2,1)S(1)}, u32[]{:S(2)}, u32[]{:S(2)}) collective-permute-start(bf16[128,1024]{1,0:T(8,128)(2,1)S(1)} %bitcast.36), channel_id=1, source_target_pairs={{0,3},{1,0},{2,1},{3,2},{4,7},{5,4},{6,5},{7,6},{8,11},{9,8},{10,9... | collective-permute-start | bytes 786440 | tf_op jit(solution)/shard_map/ppermute | solution.py:515
  64.7 5.9 %shard_map.77 = (bf16[2048,1024]{1,0:T(8,128)(2,1)}, f32[1,2048]{1,0:T(1,128)S(1)}, bf16[4,128,2048]{2,1,0:T(8,128)(2,1)}) custom-call(s32[1]{0:T(128)} %bitcast.core_ref, bf16[2048,1024]{1,0:T(8,128)(2,1)} %proto_ref.1), custom_call_target="tpu_custom_call" | custom-call | flops 12582912 | bytes 10485760 | tf_op jit(solution)/shard_map/pallas_call | solution.py:177
  71.2 5.8 %shard_map.80 = (f32[512,2048]{1,0:T(8,128)}, bf16[512,2048]{1,0:T(8,128)(2,1)S(1)}, f32[2,2048]{1,0:T(2,128)S(1)}, f32[1,512]{1,0:T(1,128)S(1)}, bf16[2,512,512]{2,1,0:T(8,128)(2,1)S(1)}) custom-call(s32[2]{0:T(128)S(1)} %pad_add_fusion.3.place_ref, bf16[128,1024]{1,0:T(8,128)(2,1)S(1)} %bitcast.38, bf16[2048,1024]{1,0:T(8,128)(2,1)} %get-tuple-element.29.unit_ref), custom_call_target="tpu_custom_call" | custom-call | flops 536870912 | bytes 2097152 | tf_op jit(solution)/shard_map/pallas_call | solution.py:263
  77.0 5.8 %shard_map.81 = (f32[512,2048]{1,0:T(8,128)}, bf16[512,2048]{1,0:T(8,128)(2,1)S(1)}, f32[2,2048]{1,0:T(2,128)S(1)}, f32[1,512]{1,0:T(1,128)S(1)}, bf16[2,512,512]{2,1,0:T(8,128)(2,1)S(1)}) custom-call(s32[2]{0:T(128)S(1)} %pad_add_fusion.2.place_ref, ...), custom_call_target="tpu_custom_call", output_to_operand_aliasing={{0}: (4, {}), {1}: (5, {}), {3}: (6, {}), {4}: (7, {})} | custom-call | flops 536870912 | bytes 2097152 | tf_op jit(solution)/shard_map/pallas_call | solution.py:263
  82.8 5.8 %shard_map.82 = (f32[512,2048]{1,0:T(8,128)}, bf16[512,2048]{1,0:T(8,128)(2,1)S(1)}, f32[2,2048]{1,0:T(2,128)S(1)}, f32[1,512]{1,0:T(1,128)S(1)}, bf16[2,512,512]{2,1,0:T(8,128)(2,1)S(1)}) custom-call(s32[2]{0:T(128)S(1)} %pad_add_fusion.1.place_ref, ...), custom_call_target="tpu_custom_call", output_to_operand_aliasing={{0}: (4, {}), {1}: (5, {}), {3}: (6, {}), {4}: (7, {})} | custom-call | flops 536870912 | bytes 2097152 | tf_op jit(solution)/shard_map/pallas_call | solution.py:263
  88.7 5.9 %shard_map.83 = (f32[512,2048]{1,0:T(8,128)}, bf16[512,2048]{1,0:T(8,128)(2,1)S(1)}, f32[8,2,2048]{2,1,0:T(2,128)S(1)}, f32[1,512]{1,0:T(1,128)S(1)}, bf16[2,512,512]{2,1,0:T(8,128)(2,1)S(1)}) custom-call(s32[2]{0:T(128)S(1)} %pad_add_fusion.place_ref, ...), custom_call_target="tpu_custom_call", output_to_operand_aliasing={{0}: (4, {}), {1}: (5, {}), {3}: (6, {}), {4}: (7, {})} | custom-call | flops 536870912 | bytes 2097152 | tf_op jit(solution)/shard_map/pallas_call | solution.py:263
  94.5 14.8 %all_to_all.50.mass_ref = f32[8,2,2048]{2,1,0:T(2,128)S(1)} all-to-all(f32[8,2,2048]{2,1,0:T(2,128)S(1)} %get-tuple-element.45), channel_id=1, replica_groups=mesh['x'=4,'core'=2,'z'=8,'y'=4] {'x','core'}, dimensions={0} | all-to-all | bytes 262144 | tf_op jit(solution)/shard_map/all_to_all | solution.py:524
  110.5 13.2 %all_to_all.51.image_ref.soft_ref = f32[32,2,512]{2,1,0:T(2,128)S(1)} all-to-all(f32[32,2,512]{2,1,0:T(2,128)S(1)} %shard_map.84), channel_id=1, replica_groups=mesh['x'=4,'core'=2,'z'=8,'y'=4] {'z','y'}, dimensions={0} | all-to-all | bytes 262144 | tf_op jit(solution)/shard_map/all_to_all | solution.py:525
  124.8 10.0 %all_to_all.52.mass_ref = f32[8,2,2048]{2,1,0:T(2,128)S(1)} all-to-all(f32[8,2,2048]{2,1,0:T(2,128)S(1)} %shard_map.85), channel_id=1, replica_groups=mesh['x'=4,'core'=2,'z'=8,'y'=4] {'x','core'}, dimensions={0} | all-to-all | bytes 262144 | tf_op jit(solution)/shard_map/all_to_all | solution.py:527
  136.0 11.8 %all_to_all.53.image_ref = f32[32,1,512]{2,1,0:T(1,128)S(1)} all-to-all(f32[32,1,512]{2,1,0:T(1,128)S(1)} %shard_map.86), channel_id=1, replica_groups=mesh['x'=4,'core'=2,'z'=8,'y'=4] {'z','y'}, dimensions={0} | all-to-all | bytes 131072 | tf_op jit(solution)/shard_map/all_to_all | solution.py:528
  148.8 9.9 %all_to_all.54.mass_ref = f32[8,2,2048]{2,1,0:T(2,128)S(1)} all-to-all(f32[8,2,2048]{2,1,0:T(2,128)S(1)} %shard_map.87), channel_id=1, replica_groups=mesh['x'=4,'core'=2,'z'=8,'y'=4] {'x','core'}, dimensions={0} | all-to-all | bytes 262144 | tf_op jit(solution)/shard_map/all_to_all | solution.py:527
  159.9 11.8 %all_to_all.55.image_ref = f32[32,1,512]{2,1,0:T(1,128)S(1)} all-to-all(f32[32,1,512]{2,1,0:T(1,128)S(1)} %shard_map.88), channel_id=1, replica_groups=mesh['x'=4,'core'=2,'z'=8,'y'=4] {'z','y'}, dimensions={0} | all-to-all | bytes 131072 | tf_op jit(solution)/shard_map/all_to_all | solution.py:528
  171.8 7.8 %shard_map.89 = (bf16[512,2048]{1,0:T(8,128)(2,1)S(1)}, f32[1,2048]{1,0:T(1,128)S(1)}, bf16[4,128,2048]{2,1,0:T(8,128)(2,1)}, f32[4,128,2048]{2,1,0:T(8,128)}) custom-call(f32[32,1,512]{2,1,0:T(1,128)S(1)} %all_to_all.55.image_ref, f32[32,2,512]{2,1,0:T(2,128)S(1)} %all_to_all.51.image_ref.soft_ref, f32[8,2,2048]{2,1,0:T(2,128)S(1)} %all_to_all.54.mass_ref, ...), custom_call_target="tpu_custom_call" | custom-call | flops 2147483648 | bytes 12582912 | tf_op jit(solution)/shard_map/pallas_call | solution.py:377
  179.6 2.1 collective-permute-start.7
  181.7 3.4 %convolution_convert_fusion = bf16[1024,512]{1,0:T(8,128)(2,1)} fusion(bf16[2048,1024]{1,0:T(8,128)(2,1)S(1)} %copy-done.1, bf16[512,2048]{1,0:T(8,128)(2,1)S(1)} %get-tuple-element.50), kind=kOutput, calls=%fused_computation.1 | convolution fusion | flops 2148007936 | bytes 7340032 | tf_op jit(solution)/shard_map/dot_general | solution.py:531
  185.1 4.7 %all-to-all-start.9 = ((bf16[32,32,512]{2,1,0:T(8,128)(2,1)}), bf16[32,32,512]{2,1,0:T(8,128)(2,1)}, u32[]{:S(2)}, u32[]{:S(2)}) async-start(bf16[32,32,512]{2,1,0:T(8,128)(2,1)} %bitcast.13), calls=%async_computation.9 | async-start | bytes 2097152 | tf_op jit(solution)/shard_map/all_to_all | solution.py:38
  191.0 2.5 %shard_map.92 = bf16[128,2048]{1,0:T(8,128)(2,1)S(1)} custom-call(s32[1]{0:T(128)} %bitcast.18.place_ref, f32[4,128,2048]{2,1,0:T(8,128)} %get-tuple-element.51.stay_ref, bf16[4,128,2048]{2,1,0:T(8,128)(2,1)} %collective-permute-done.7.arrived_ref, bf16[4,128,2048]{2,1,0:T(8,128)(2,1)} %get-tuple-element.53.turned_ref, ...), custom_call_target="tpu_custom_call" | custom-call | flops 1000000000 | bytes 2621440 | tf_op jit(solution)/shard_map/pallas_call | solution.py:430
  194.5 2.5 %shard_map.91 = bf16[128,2048]{1,0:T(8,128)(2,1)S(1)} custom-call(s32[1]{0:T(128)} %bitcast.17.place_ref, f32[4,128,2048]{2,1,0:T(8,128)} %get-tuple-element.51.stay_ref, bf16[4,128,2048]{2,1,0:T(8,128)(2,1)} %collective-permute-done.7.arrived_ref, bf16[4,128,2048]{2,1,0:T(8,128)(2,1)} %get-tuple-element.53.turned_ref, ...), custom_call_target="tpu_custom_call" | custom-call | flops 1000000000 | bytes 2621440 | tf_op jit(solution)/shard_map/pallas_call | solution.py:430
  197.6 2.5 %shard_map.90 = bf16[128,2048]{1,0:T(8,128)(2,1)S(1)} custom-call(s32[1]{0:T(128)} %bitcast.16.place_ref, f32[4,128,2048]{2,1,0:T(8,128)} %get-tuple-element.51.stay_ref, bf16[4,128,2048]{2,1,0:T(8,128)(2,1)} %collective-permute-done.7.arrived_ref, bf16[4,128,2048]{2,1,0:T(8,128)(2,1)} %get-tuple-element.53.turned_ref, ...), custom_call_target="tpu_custom_call" | custom-call | flops 1000000000 | bytes 2621440 | tf_op jit(solution)/shard_map/pallas_call | solution.py:430
  200.9 16.9 %all-to-all-done.9 = bf16[32,32,512]{2,1,0:T(8,128)(2,1)} async-done(((bf16[32,32,512]{2,1,0:T(8,128)(2,1)}), bf16[32,32,512]{2,1,0:T(8,128)(2,1)}, u32[]{:S(2)}, u32[]{:S(2)}) %all-to-all-start.9) | async-done | bytes 1048608 | tf_op jit(solution)/shard_map/all_to_all | solution.py:38
  217.8 1.4 convert_reduce_fusion
  219.8 2.8 %collective-permute-done.10.rest_1_ = bf16[128,2048]{1,0:T(8,128)(2,1)S(1)} collective-permute-done((bf16[128,2048]{1,0:T(8,128)(2,1)S(1)}, bf16[128,2048]{1,0:T(8,128)(2,1)S(1)}, u32[]{:S(2)}, u32[]{:S(2)}) %collective-permute-start.10) | collective-permute-done | bytes 524320 | tf_op jit(solution)/shard_map/ppermute | solution.py:542
  222.6 3.8 %shard_map.93 = f32[128,2048]{1,0:T(8,128)} custom-call(s32[1]{0:T(128)} %bitcast.15.place_ref, f32[4,128,2048]{2,1,0:T(8,128)} %get-tuple-element.51.stay_ref, bf16[4,128,2048]{2,1,0:T(8,128)(2,1)} %collective-permute-done.7.arrived_ref, bf16[4,128,2048]{2,1,0:T(8,128)(2,1)} %get-tuple-element.53.turned_ref, f32[1,2048]{1,0:T(1,128)S(1)} %get-tuple-element.54.one_ref, ...), custom_call_target="tpu_custom_call" | custom-call | flops 40000000000 | bytes 2621440 | tf_op jit(solution)/shard_map/pallas_call | solution.py:430
  (61 shorter events, 19.7 us)
Async XLA Ops:
  2.7 16.9 %collective-permute-start = (bf16[128,1024]{1,0:T(8,128)(2,1)S(1)}, bf16[128,1024]{1,0:T(8,128)(2,1)S(1)}, u32[]{:S(2)}, u32[]{:S(2)}) collective-permute-start(bf16[128,1024]{1,0:T(8,128)(2,1)S(1)} %broadcast_select_fusion), channel_id=1, source_target_pairs={{0,1},{1,2},{2,3},{3,0},{4,5},{5,6},{6,7},{7,4},{8,9},{9,10},{10,1... | collective-permute-start | bytes 786440 | tf_op jit(solution)/shard_map/ppermute | solution.py:478
  4.9 14.9 %collective-permute-start.1 = (bf16[128,1024]{1,0:T(8,128)(2,1)S(1)}, bf16[128,1024]{1,0:T(8,128)(2,1)S(1)}, u32[]{:S(2)}, u32[]{:S(2)}) collective-permute-start(bf16[128,1024]{1,0:T(8,128)(2,1)S(1)} %broadcast_select_fusion), channel_id=1, source_target_pairs={{0,2},{1,3},{2,0},{3,1},{4,6},{5,7},{6,4},{7,5},{8,10},{9,11},{10,... | collective-permute-start | bytes 786440 | tf_op jit(solution)/shard_map/ppermute | solution.py:478
  7.5 12.3 %collective-permute-start.2 = (bf16[128,1024]{1,0:T(8,128)(2,1)S(1)}, bf16[128,1024]{1,0:T(8,128)(2,1)S(1)}, u32[]{:S(2)}, u32[]{:S(2)}) collective-permute-start(bf16[128,1024]{1,0:T(8,128)(2,1)S(1)} %broadcast_select_fusion), channel_id=1, source_target_pairs={{0,3},{1,0},{2,1},{3,2},{4,7},{5,4},{6,5},{7,6},{8,11},{9,8},{10,9... | collective-permute-start | bytes 786440 | tf_op jit(solution)/shard_map/ppermute | solution.py:478
  11.0 21.3 %all-to-all-start = ((bf16[32,40,128]{2,1,0:T(8,128)(2,1)}), bf16[32,40,128]{2,1,0:T(8,128)(2,1)S(1)}, u32[]{:S(2)}, u32[]{:S(2)}) async-start(bf16[32,40,128]{2,1,0:T(8,128)(2,1)} %bitcast.4), calls=%async_computation | async-start | bytes 655360 | tf_op jit(solution)/shard_map/all_to_all | solution.py:464
  19.9 13.2 %copy-start = (bf16[128,1024]{1,0:T(8,128)(2,1)S(1)}, bf16[128,1024]{1,0:T(8,128)(2,1)}, u32[]{:S(2)}) copy-start(bf16[128,1024]{1,0:T(8,128)(2,1)} %w_out_ref.1) | copy-start | bytes 786436
  19.9 13.2 %collective-permute-start.3 = (bf16[3,128,1024]{2,1,0:T(8,128)(2,1)S(1)}, bf16[3,128,1024]{2,1,0:T(8,128)(2,1)S(1)}, u32[]{:S(2)}, u32[]{:S(2)}) collective-permute-start(bf16[3,128,1024]{2,1,0:T(8,128)(2,1)S(1)} %shard_map.78.shares_ref), channel_id=1, source_target_pairs={{0,32},{32,0},{1,33},{33,1},{2,34},{34,2},{3,35},{35,3},{4,36},{36... | collective-permute-start | bytes 2359304 | tf_op jit(solution)/shard_map/ppermute | solution.py:482
  35.0 12.8 %all-to-all-start.1 = ((bf16[8,16,1024]{2,1,0:T(8,128)(2,1)}), bf16[8,16,1024]{2,1,0:T(8,128)(2,1)S(1)}, u32[]{:S(2)}, u32[]{:S(2)}) async-start(bf16[8,16,1024]{2,1,0:T(8,128)(2,1)} %bitcast.8), calls=%async_computation.1 | async-start | bytes 524288 | tf_op jit(solution)/shard_map/all_to_all | solution.py:38
  49.2 12.8 %all-to-all-start.2 = ((bf16[8,16,1024]{2,1,0:T(8,128)(2,1)}), bf16[8,16,1024]{2,1,0:T(8,128)(2,1)S(1)}, u32[]{:S(2)}, u32[]{:S(2)}) async-start(bf16[8,16,1024]{2,1,0:T(8,128)(2,1)} %broadcast_in_dim.8), calls=%async_computation.2 | async-start | bytes 524288 | tf_op jit(solution)/shard_map/all_to_all | solution.py:30
  62.0 15.0 %collective-permute-start.6 = (bf16[128,1024]{1,0:T(8,128)(2,1)S(1)}, bf16[128,1024]{1,0:T(8,128)(2,1)S(1)}, u32[]{:S(2)}, u32[]{:S(2)}) collective-permute-start(bf16[128,1024]{1,0:T(8,128)(2,1)S(1)} %bitcast.35), channel_id=1, source_target_pairs={{0,1},{1,2},{2,3},{3,0},{4,5},{5,6},{6,7},{7,4},{8,9},{9,10},{10,1... | collective-permute-start | bytes 786440 | tf_op jit(solution)/shard_map/ppermute | solution.py:515
  62.2 20.6 %collective-permute-start.5 = (bf16[128,1024]{1,0:T(8,128)(2,1)S(1)}, bf16[128,1024]{1,0:T(8,128)(2,1)S(1)}, u32[]{:S(2)}, u32[]{:S(2)}) collective-permute-start(bf16[128,1024]{1,0:T(8,128)(2,1)S(1)} %bitcast.36), channel_id=1, source_target_pairs={{0,3},{1,0},{2,1},{3,2},{4,7},{5,4},{6,5},{7,6},{8,11},{9,8},{10,9... | collective-permute-start | bytes 786440 | tf_op jit(solution)/shard_map/ppermute | solution.py:515
  70.6 18.1 %collective-permute-start.4 = (bf16[128,1024]{1,0:T(8,128)(2,1)S(1)}, bf16[128,1024]{1,0:T(8,128)(2,1)S(1)}, u32[]{:S(2)}, u32[]{:S(2)}) collective-permute-start(bf16[128,1024]{1,0:T(8,128)(2,1)S(1)} %bitcast.37), channel_id=1, source_target_pairs={{0,2},{1,3},{2,0},{3,1},{4,6},{5,7},{6,4},{7,5},{8,10},{9,11},{10,... | collective-permute-start | bytes 786440 | tf_op jit(solution)/shard_map/ppermute | solution.py:515
  171.8 9.9 %copy-start.1 = (bf16[2048,1024]{1,0:T(8,128)(2,1)S(1)}, bf16[2048,1024]{1,0:T(8,128)(2,1)}, u32[]{:S(2)}) copy-start(bf16[2048,1024]{1,0:T(8,128)(2,1)} %get-tuple-element.29.unit_ref) | copy-start | bytes 12582916
  179.6 11.4 %collective-permute-start.7 = (bf16[4,128,2048]{2,1,0:T(8,128)(2,1)}, bf16[4,128,2048]{2,1,0:T(8,128)(2,1)}, u32[]{:S(2)}, u32[]{:S(2)}) collective-permute-start(bf16[4,128,2048]{2,1,0:T(8,128)(2,1)} %get-tuple-element.52), channel_id=1, source_target_pairs={{0,32},{32,0},{1,33},{33,1},{2,34},{34,2},{3,35},{35,3},{4,36},{36... | collective-permute-start | bytes 6291464 | tf_op jit(solution)/shard_map/ppermute | solution.py:534
  185.1 32.7 %all-to-all-start.9 = ((bf16[32,32,512]{2,1,0:T(8,128)(2,1)}), bf16[32,32,512]{2,1,0:T(8,128)(2,1)}, u32[]{:S(2)}, u32[]{:S(2)}) async-start(bf16[32,32,512]{2,1,0:T(8,128)(2,1)} %bitcast.13), calls=%async_computation.9 | async-start | bytes 2097152 | tf_op jit(solution)/shard_map/all_to_all | solution.py:38
  189.7 1.3 collective-permute-start.8
  193.5 26.3 %collective-permute-start.11 = (bf16[128,2048]{1,0:T(8,128)(2,1)S(1)}, bf16[128,2048]{1,0:T(8,128)(2,1)S(1)}, u32[]{:S(2)}, u32[]{:S(2)}) collective-permute-start(bf16[128,2048]{1,0:T(8,128)(2,1)S(1)} %shard_map.92), channel_id=1, source_target_pairs={{0,192},{64,0},{128,64},{192,128},{1,193},{65,1},{129,65},{193,129... | collective-permute-start | bytes 1572872 | tf_op jit(solution)/shard_map/ppermute | solution.py:542
  197.0 25.6 %collective-permute-start.10 = (bf16[128,2048]{1,0:T(8,128)(2,1)S(1)}, bf16[128,2048]{1,0:T(8,128)(2,1)S(1)}, u32[]{:S(2)}, u32[]{:S(2)}) collective-permute-start(bf16[128,2048]{1,0:T(8,128)(2,1)S(1)} %shard_map.91), channel_id=1, source_target_pairs={{0,64},{64,128},{128,192},{192,0},{1,65},{65,129},{129,193},{193,1... | collective-permute-start | bytes 1572872 | tf_op jit(solution)/shard_map/ppermute | solution.py:542
  200.1 22.4 %collective-permute-start.9 = (bf16[128,2048]{1,0:T(8,128)(2,1)S(1)}, bf16[128,2048]{1,0:T(8,128)(2,1)S(1)}, u32[]{:S(2)}, u32[]{:S(2)}) collective-permute-start(bf16[128,2048]{1,0:T(8,128)(2,1)S(1)} %shard_map.90), channel_id=1, source_target_pairs={{0,128},{64,192},{128,0},{192,64},{1,129},{65,193},{129,1},{193,65... | collective-permute-start | bytes 1572872 | tf_op jit(solution)/shard_map/ppermute | solution.py:542

commit v7 on v3

v7 whole, which is shorter than its diff:
```python
import math

import jax
import jax.numpy as jnp
from jax import lax
from jax.experimental import pallas as pl
from jax.experimental.pallas import tpu as pltpu
from jax.sharding import Mesh, PartitionSpec as P

D = 1024
PROTOS = 65536
SINK_ITERS = 3


sink_temp = 0.05
soft_temp = 0.1
norm_eps = 1e-05
unit_eps = 1e-06

ROWS = ("x", "core")
COLS = ("z", "y")
f32 = jnp.float32
bf16 = jnp.bfloat16


def gather_all(values, axes):
    count = lax.axis_size(axes)
    copies = jnp.broadcast_to(values[None], (count,) + values.shape)
    return lax.all_to_all(copies, axes, 0, 0)


def sum_small(values, axes):
    return jnp.sum(gather_all(values, axes), axis=0)


def scatter_sum(blocks, axes):
    return jnp.sum(lax.all_to_all(blocks, axes, 0, 0).astype(f32), axis=0)


TILE = 512
LANES = 128
factor = 0.5 * math.sqrt(PROTOS * D)
NT = (((1,), (1,)), ((), ()))
VMEM = pl.BlockSpec(memory_space=pltpu.VMEM)
SMEM = pl.BlockSpec(memory_space=pltpu.SMEM)


def keep_hbm(values):
    return pltpu.with_memory_space_constraint(values, pltpu.HBM)


def call(kernel, scalars, arrays, outs, mib, flops, moved, in_hbm=()):
    shapes = [
        pltpu.HBM(shape, dtype) if place in in_hbm else jax.ShapeDtypeStruct(shape, dtype)
        for place, (shape, dtype) in enumerate(outs)
    ]
    many = len(shapes) > 1
    return pl.pallas_call(
        kernel,
        in_specs=[SMEM] * len(scalars) + [VMEM] * len(arrays),
        out_specs=[VMEM] * len(shapes) if many else VMEM,
        out_shape=shapes if many else shapes[0],
        compiler_params=pltpu.CompilerParams(vmem_limit_bytes=mib * 1024 * 1024),
        cost_estimate=pl.CostEstimate(flops=flops, bytes_accessed=moved, transcendentals=0),
    )(*scalars, *arrays)


def fold_lanes(values):
    width = values.shape[1]
    return sum(values[:, j : j + LANES] for j in range(0, width, LANES))


def as_column(row):
    return jnp.broadcast_to(row, (LANES, row.shape[1])).T


def as_row(column):
    return jnp.sum(column.T, axis=0, keepdims=True)


def spread_lanes(column, width):
    return jnp.concatenate([column] * (width // LANES), axis=1)


def view_rows(pair, count):
    half = count // 2
    width = pair.shape[1]
    return jnp.concatenate(
        [jnp.broadcast_to(pair[v : v + 1], (half, width)) for v in range(2)], axis=0
    )


def view_sums(values):
    half = values.shape[0] // 2
    return jnp.concatenate(
        [jnp.sum(values[v * half : (v + 1) * half], axis=0, keepdims=True) for v in range(2)],
        axis=0,
    )


def tiles(count):
    return [slice(j, j + TILE) for j in range(0, count, TILE)]


def stack_kernel(first_ref, second_ref, third_ref, out_ref):
    for place, ref in enumerate((first_ref, second_ref, third_ref)):
        out_ref[place] = ref[...]


def stack_shares(parts):
    return call(
        stack_kernel, (), parts, [((3,) + parts[0].shape, bf16)], 2, 40 * 10**9, 4 * parts[0].size
    )


def ffn_kernel(core_ref, normed_ref, w_in_ref, w_out_ref, shares_ref, others_ref, out_ref):
    normed = normed_ref[...]
    even = core_ref[0] == 0
    total = jnp.zeros(out_ref.shape, f32)
    for step in range(shares_ref.shape[0] + 1):
        if step == 0:
            enter, leave = w_in_ref[...], w_out_ref[...]
        else:
            one, other = shares_ref[step - 1], others_ref[step - 1]
            enter, leave = jnp.where(even, one, other), jnp.where(even, other, one)
        wide = lax.dot_general(normed, enter, NT, preferred_element_type=f32)
        hidden = (0.5 * wide * (1.0 + lax.erf(wide * math.sqrt(0.5)))).astype(bf16)
        total = total + jnp.dot(hidden, leave, preferred_element_type=f32)
    out_ref[...] = total.astype(bf16)


def feed_forward(core, normed, w_in_t, w_out, shares, others):
    rows = normed.shape[0]
    return call(
        ffn_kernel,
        (core.reshape(1),),
        (normed, w_in_t, w_out, shares, others),
        [((rows, D), bf16)],
        8,
        4 * rows * D * 4 * w_out.shape[0],
        8 * w_out.size,
    )


def prepare_kernel(core_ref, proto_ref, unit_ref, length_ref, turned_ref):
    even = core_ref[0] == 0
    for part in tiles(proto_ref.shape[0]):
        values = proto_ref[part, :].astype(f32)
        squares = values * values
        inverse = lax.rsqrt(jnp.sum(squares, axis=1, keepdims=True) + unit_eps)
        unit_ref[part, :] = (values * inverse).astype(bf16)
        length_ref[:, part] = jnp.sqrt(as_row(fold_lanes(squares)) + unit_eps)
        for block in range(turned_ref.shape[0]):
            start = 2 * block * LANES
            low = values[:, start : start + LANES]
            high = values[:, start + LANES : start + 2 * LANES]
            turned_ref[block, :, part] = jnp.where(even, low, high).T.astype(bf16)


def prepare(core, prototypes, x_count):
    protos = prototypes.shape[0]
    return call(
        prepare_kernel,
        (core.reshape(1),),
        (prototypes,),
        [((protos, D), bf16), ((1, protos), f32), ((x_count, LANES, protos), bf16)],
        12,
        6 * protos * D,
        5 * protos * D,
        (2,),
    )


def scores_kernel(place_ref, *rest):
    *block_refs, unit_ref, base_ref, mass_ref, soft_ref, embed_ref = rest
    height = block_refs[0].shape[0]
    for n, ref in enumerate(block_refs):
        embed_ref[pl.ds(pl.multiple_of(place_ref[n] * height, height), height), :] = ref[...]
    total = jnp.zeros((base_ref.shape[0], LANES), f32)
    for part in tiles(unit_ref.shape[0]):
        scores = lax.dot_general(
            embed_ref[...], unit_ref[part, :], NT, preferred_element_type=f32
        )
        soft = jnp.exp(scores * (1.0 / soft_temp))
        base = soft * soft
        base_ref[:, part] = base.astype(bf16)
        mass = view_sums(base)
        mass_ref[:, :, part] = jnp.broadcast_to(mass[None], (mass_ref.shape[0],) + mass.shape)
        total = total + fold_lanes(soft)
    soft_ref[...] = as_row(total)


def score_pass(places, parts, unit, copies):
    height, protos = parts[0].shape[0], unit.shape[0]
    rows = height * len(parts)
    return call(
        scores_kernel,
        (places,),
        (*parts, unit),
        [
            ((rows, protos), bf16),
            ((copies, 2, protos), f32),
            ((1, rows), f32),
            ((rows, D), bf16),
        ],
        10,
        2 * rows * protos * D,
        8 * rows * protos,
    )


def turn_kernel(core_ref, embed_ref, turned_ref):
    even = core_ref[0] == 0
    for block in range(D // (2 * LANES)):
        start = 2 * block * LANES
        low = embed_ref[:, start : start + LANES].astype(f32)
        high = embed_ref[:, start + LANES : start + 2 * LANES].astype(f32)
        rows = slice(block * LANES, (block + 1) * LANES)
        turned_ref[0, rows, :] = jnp.where(even, high, low).T.astype(bf16)
        turned_ref[1, rows, :] = jnp.where(even, low, high).T.astype(bf16)


def turn(core, embed):
    rows = embed.shape[0]
    return call(
        turn_kernel, (core.reshape(1),), (embed,), [((2, D // 2, rows), bf16)], 6, 10**9, 4 * embed.size
    )


def image_kernel(mass_ref, base_ref, *rest):
    *extra, out_ref = rest
    rows, protos = base_ref.shape
    total = jnp.zeros((rows, LANES), f32)
    for part in tiles(protos):
        scale = 1.0 / jnp.sum(mass_ref[:, :, part], axis=0)
        total = total + fold_lanes(base_ref[:, part].astype(f32) * view_rows(scale, rows))
    row = jnp.concatenate([as_row(total)] + [ref[...] for ref in extra], axis=0)
    out_ref[...] = jnp.broadcast_to(row[None], out_ref.shape)


def image_pass(masses, base, copies, *extra):
    rows, protos = base.shape
    return call(
        image_kernel,
        (),
        (masses, base, *extra),
        [((copies, 1 + len(extra), rows), f32)],
        8,
        3 * rows * protos,
        2 * rows * protos,
    )


def proto_kernel(image_ref, base_ref, mass_ref):
    column = as_column(1.0 / jnp.sum(image_ref[...], axis=0)[:1])
    for part in tiles(base_ref.shape[1]):
        mass = view_sums(base_ref[:, part].astype(f32) * spread_lanes(column, TILE))
        mass_ref[:, :, part] = jnp.broadcast_to(mass[None], (mass_ref.shape[0],) + mass.shape)


def proto_pass(images, base, copies):
    rows, protos = base.shape
    return call(
        proto_kernel,
        (),
        (images, base),
        [((copies, 2, protos), f32)],
        8,
        3 * rows * protos,
        2 * rows * protos,
    )


def grad_kernel(
    image_ref, soft_ref, mass_ref, unit_ref, embed_ref, embed_t_ref,
    radial_ref, away_ref, stay_ref, terms_ref, code_column, prob_column, total,
):
    step = pl.program_id(0)

    @pl.when(step == 0)
    def _():
        code_column[...] = as_column(factor / jnp.sum(image_ref[...], axis=0)[:1])
        prob_column[...] = as_column(factor / jnp.sum(soft_ref[...], axis=0)[1:2])
        total[...] = jnp.zeros_like(total)

    scores = lax.dot_general(embed_ref[...], unit_ref[...], NT, preferred_element_type=f32)
    rows = scores.shape[0]
    half = rows // 2
    soft = jnp.exp(scores * (1.0 / soft_temp))
    scale = 1.0 / jnp.sum(mass_ref[...], axis=0)
    codes = soft * soft * view_rows(scale, rows) * spread_lanes(code_column[...], TILE)
    swapped = jnp.concatenate([codes[half:], codes[:half]], axis=0)
    grad = (soft * spread_lanes(prob_column[...], TILE) - swapped).astype(bf16)
    radial_ref[...] = jnp.sum(grad.astype(f32) * scores, axis=0, keepdims=True)
    away = jnp.dot(embed_t_ref[0], grad, preferred_element_type=f32).astype(bf16)
    away_ref[...] = away.reshape(away_ref.shape)
    stay = jnp.dot(embed_t_ref[1], grad, preferred_element_type=f32)
    stay_ref[...] = stay.reshape(stay_ref.shape)
    total[...] += jnp.dot(grad, unit_ref[...], preferred_element_type=f32)

    @pl.when(step == pl.num_programs(0) - 1)
    def _():
        for start in range(0, D, TILE):
            part = slice(start, start + TILE)
            terms_ref[part, :] = total[:, part].T.astype(bf16)


def grad_pass(images, softs, masses, unit, embed, embed_t):
    rows, protos = embed.shape[0], unit.shape[0]
    depth = embed_t.shape[1]
    blocks = depth // LANES

    def full(values):
        return pl.BlockSpec(values.shape, lambda i: (0,) * values.ndim)

    halves = pl.BlockSpec((blocks, LANES, TILE), lambda i: (0, 0, i))
    return pl.pallas_call(
        grad_kernel,
        grid=(protos // TILE,),
        in_specs=[
            full(images),
            full(softs),
            pl.BlockSpec((masses.shape[0], 2, TILE), lambda i: (0, 0, i)),
            pl.BlockSpec((TILE, D), lambda i: (i, 0)),
            VMEM,
            VMEM,
        ],
        out_specs=[
            pl.BlockSpec((1, TILE), lambda i: (0, i)),
            halves,
            halves,
            pl.BlockSpec((D, rows), lambda i: (0, 0)),
        ],
        out_shape=[
            jax.ShapeDtypeStruct((1, protos), f32),
            pltpu.HBM((blocks, LANES, protos), bf16),
            pltpu.HBM((blocks, LANES, protos), f32),
            jax.ShapeDtypeStruct((D, rows), bf16),
        ],
        scratch_shapes=[
            pltpu.VMEM((rows, LANES), f32),
            pltpu.VMEM((rows, LANES), f32),
            pltpu.VMEM((rows, D), f32),
        ],
        compiler_params=pltpu.CompilerParams(
            dimension_semantics=("arbitrary",), vmem_limit_bytes=24 * 1024 * 1024
        ),
        cost_estimate=pl.CostEstimate(
            flops=8 * depth * rows * protos,
            bytes_accessed=10 * depth * protos,
            transcendentals=rows * protos,
        ),
    )(images, softs, masses, keep_hbm(unit), embed, embed_t)


def pair_kernel(place_ref, stay_ref, arrived_ref, turned_ref, one_ref, two_ref, length_ref, *rest):
    *others, out_ref = rest
    for part in tiles(out_ref.shape[1]):
        inverse = 1.0 / length_ref[:, part]
        radial = (one_ref[:, part] + two_ref[:, part]) * inverse
        total = stay_ref[0, :, part] + arrived_ref[0, :, part].astype(f32)
        total = (total - turned_ref[0, :, part].astype(f32) * radial) * inverse
        for ref in others:
            total = total + ref[:, part].astype(f32)
        out_ref[:, part] = total.astype(out_ref.dtype)


def pair_call(place, stay, arrived, turned, radials, length, others=()):
    blocks, height, protos = stay.shape

    def full(values):
        return pl.BlockSpec(values.shape, lambda i, p: (0,) * values.ndim)

    return pl.pallas_call(
        pair_kernel,
        grid_spec=pltpu.PrefetchScalarGridSpec(
            num_scalar_prefetch=1,
            grid=(1,),
            in_specs=[pl.BlockSpec((1, height, protos), lambda i, p: (p[0], 0, 0))] * 3
            + [full(values) for values in (*radials, length, *others)],
            out_specs=pl.BlockSpec((height, protos), lambda i, p: (0, 0)),
        ),
        out_shape=jax.ShapeDtypeStruct((height, protos), f32 if others else bf16),
        compiler_params=pltpu.CompilerParams(vmem_limit_bytes=10 * 1024 * 1024),
        cost_estimate=pl.CostEstimate(
            flops=10**9,
            bytes_accessed=10 * height * protos,
            transcendentals=0,
        ),
    )(
        place.reshape(1),
        keep_hbm(stay),
        arrived,
        keep_hbm(turned),
        *radials,
        length,
        *others,
    )


def body(hidden_states, ln_in_gain, w_in, w_out, ln_out_gain, prototypes):
    view_count, image_rows, local_width = hidden_states.shape
    row_count = view_count * image_rows
    col_count = lax.axis_size(COLS)
    row_block = row_count // col_count

    y_count = lax.axis_size("y")
    z_count = lax.axis_size("z")
    tall = row_count // y_count

    states_t = hidden_states.reshape(row_count, local_width).T
    gain_row = jnp.pad(jnp.concatenate([ln_in_gain, ln_out_gain]), (0, tall - 2 * local_width))
    pieces = jnp.concatenate(
        [
            states_t.reshape(local_width, y_count, tall).transpose(1, 0, 2),
            jnp.broadcast_to(gain_row[None, None], (y_count, 8, tall)),
        ],
        axis=1,
    )
    sent = jnp.broadcast_to(pieces[None], (z_count,) + pieces.shape)
    received = lax.all_to_all(
        sent.reshape(col_count, local_width + 8, tall), COLS, 0, 0
    )
    gains = received[:, local_width]
    gain_in = gains[:, :local_width].reshape(D).astype(f32)
    gain_out = gains[:, local_width : 2 * local_width].reshape(D).astype(f32)
    inputs_t = received[:, :local_width].reshape(D, tall)

    core = lax.axis_index("core")
    swap = [(0, 1), (1, 0)]
    w_in_t = w_in.T
    share = jnp.where(core == 0, w_in_t, w_out)
    shares = stack_shares(
        [
            lax.ppermute(share, "y", [(i, (i + step) % y_count) for i in range(y_count)])
            for step in range(1, y_count)
        ]
    )
    others = lax.ppermute(shares, "core", swap)

    inputs_f = inputs_t.astype(f32)
    center = jnp.mean(inputs_f, axis=0)
    spread = jnp.mean(inputs_f * inputs_f, axis=0) - center * center
    normed_t = (
        (inputs_f - center[None, :]) * lax.rsqrt(spread + norm_eps)[None, :] * gain_in[:, None]
    ).astype(bf16)
    block_part = feed_forward(core, normed_t.T, w_in_t, w_out, shares, others)
    block = scatter_sum(block_part.reshape(z_count, row_block, D), "z")
    picked = (
        jnp.arange(tall)[None, :]
        == lax.axis_index("z") * row_block + jnp.arange(row_block)[:, None]
    ).astype(bf16)
    own = lax.dot_general(picked, inputs_t, (((1,), (1,)), ((), ())), preferred_element_type=f32)
    resid = own + block
    center = jnp.mean(resid, axis=1, keepdims=True)
    spread = jnp.mean(resid * resid, axis=1, keepdims=True) - center * center
    final = (resid - center) * lax.rsqrt(spread + norm_eps) * gain_out[None, :]
    squared = jnp.sum(final * final, axis=1, keepdims=True)
    embed_part = (final * lax.rsqrt(squared + unit_eps)).astype(bf16)
    own_rows = gather_all(embed_part, "z").reshape(tall, D)

    x_index = lax.axis_index("x")
    x_count = lax.axis_size("x")
    unit, proto_len, turned = prepare(core, prototypes, x_count)
    proto_count = prototypes.shape[0]
    slice_width = turned.shape[1]

    row_parts = lax.axis_size(ROWS)
    y_index = lax.axis_index("y")
    steps = (1, 3, 2)
    rows_in = {
        step: lax.ppermute(own_rows, "y", [(i, (i + step) % y_count) for i in range(y_count)])
        for step in steps
    }
    places = jnp.stack([(y_index + y_count - step) % y_count for step in (0,) + steps])
    parts = [own_rows] + [rows_in[step] for step in steps]
    base, masses, soft_part, embed = score_pass(places, parts, unit, row_parts)
    embed_t = turn(core, embed)
    masses = lax.all_to_all(masses, ROWS, 0, 0)
    softs = images = lax.all_to_all(image_pass(masses, base, col_count, soft_part), COLS, 0, 0)
    for repeat in range(1, SINK_ITERS):
        masses = lax.all_to_all(proto_pass(images, base, row_parts), ROWS, 0, 0)
        images = lax.all_to_all(image_pass(masses, base, col_count), COLS, 0, 0)

    radial, away, stay, embed_terms = grad_pass(images, softs, masses, unit, embed, embed_t)
    arrived = lax.ppermute(away, "core", swap)
    radials = (radial, lax.ppermute(radial, "core", swap))

    def paired(step, others=()):
        place = (x_index + step) % x_count
        return pair_call(place, stay, arrived, turned, radials, proto_len, others)

    landed = tuple(
        lax.ppermute(paired(step), "x", [(i, (i + step) % x_count) for i in range(x_count)])
        for step in (2, 1, 3)
    )
    proto_grad = paired(0, landed)
    embed_grad_t = scatter_sum(embed_terms.reshape(col_count, local_width, row_count), COLS)
    embed_grad = embed_grad_t.T.reshape(view_count, image_rows, local_width)
    return (embed_grad, proto_grad)


def solution(mesh):
    sizes = {"x": mesh.shape["rows"] // 2, "core": 2, "z": mesh.shape["cols"] // 4, "y": 4}
    fine = Mesh(mesh.devices.reshape(tuple(sizes.values())), tuple(sizes))
    placed = (
        P(None, ROWS, COLS),
        P(COLS),
        P(None, COLS),
        P(COLS, None),
        P(COLS),
        P(COLS, None),
    )
    return jax.shard_map(
        body,
        mesh=fine,
        in_specs=placed,
        out_specs=(P(None, ROWS, COLS), P(ROWS, COLS)),
        check_vma=False,
    )
```

time: 260 us -> 206 us (0.79)
  Pallas kernels: 0 us -> 35.1 us
  other arithmetic: 36.1 us -> 4.04 us
  waiting for transfers between devices: 79 us -> 51.9 us
  matrix products: 23.6 us -> 0.33 us
  blocking collectives: 49.4 us -> 71.8 us
  starting transfers between devices: 50.2 us -> 34.7 us
  local copies, waits for them, and re-layouts: 18.7 us -> 5.82 us
    all_to_all x0 -> x5, blocking collectives: none -> 60 us  [the longest x2 19.9 us: body(): masses = lax.all_to_all(proto_pass(images, base, row_parts), ROWS, 0, 0)]
    all_to_all x4 -> x1, blocking collectives: 49.4 us -> 11.8 us  [gather_all(): return lax.all_to_all(copies, axes, 0, 0)]
    pallas_call x0 -> x15, Pallas kernels: none -> 35.1 us  [the longest x10 12.7 us: call(): pl.pallas_call(kernel, in_specs=[SMEM] * len(scalars) + [VMEM] * len(arra...]
    dot_general x9 -> x0, matrix products: 23.2 us -> none  [the longest x1 6.6 us: body(): lax.dot_general(embed, unit, (((1,), (1,)), ((), ())), preferred_element_...]
    all_to_all x3 -> x1, waiting for transfers between devices: 31.2 us -> 8.54 us  [body(): images = lax.all_to_all(image_pass(masses, base, col_count), COLS, 0, 0)]
    reduce_sum x13 -> x0, other arithmetic: 20 us -> none  [the longest x3 9.38 us: body(): image_part = jnp.sum(base * scale_proto[:, None, :], axis=2)]
    ppermute x7, waiting for transfers between devices: 22 us -> 5.63 us  [the longest x3 3.38 us: body(): lax.ppermute(paired(step), 'x', [(i, (i + step) % x_count) for i in range...]
    all_to_all x2, waiting for transfers between devices: 12.3 us -> 26 us  [scatter_sum(): return jnp.sum(lax.all_to_all(blocks, axes, 0, 0).astype(f32), axis=0)]
  transfers between devices with their start and end apart: 18 -> 16, of which waited for: 9 -> 8; matrix products, arithmetic and copies ran while one was open for 10% -> 3% of each run, Pallas kernels for 0% -> 5%
where the time goes in v7:
time: 206 us; the launch traced here: 205 us
  blocking collectives  71.8 us (35%)
  waiting for transfers between devices  51.9 us (25%)
  Pallas kernels  35.1 us (17%)
  starting transfers between devices  34.7 us (17%)
  local copies, waits for them, and re-layouts  5.82 us (3%)
  other arithmetic  4.04 us (2%)
    all_to_all x2, waiting for transfers between devices, scatter_sum(): return jnp.sum(lax.all_to_all(blocks, axes, 0, 0).astype(f32), axis=0)  26 us
    all_to_all x2, blocking collectives, body(): masses = lax.all_to_all(proto_pass(images, base, row_parts), ROWS, 0, 0)  19.9 us
    all_to_all x1, blocking collectives, body(): masses = lax.all_to_all(masses, ROWS, 0, 0)  14.9 us
    all_to_all x1, blocking collectives, body(): lax.all_to_all(image_pass(masses, base, col_count, soft_part), COLS, 0, 0)  13.3 us
    pallas_call x10, Pallas kernels, call(): pl.pallas_call(kernel, in_specs=[SMEM] * len(scalars) + [VMEM] * len(arra...  12.7 us
    pallas_call x1, Pallas kernels, grad_pass(): pl.pallas_call(grad_kernel, grid=(protos // TILE,), in_specs=[full(images...  12.4 us
    all_to_all x1, blocking collectives, gather_all(): return lax.all_to_all(copies, axes, 0, 0)  11.8 us
    all_to_all x1, blocking collectives, body(): images = lax.all_to_all(image_pass(masses, base, col_count), COLS, 0, 0)  11.8 us
  transfers between devices with their start and end apart: 16, of which 8 were waited for; matrix products, arithmetic and copies ran while one was open for 3% of the time, Pallas kernels for 5%

profile of v7, /device:TPU:1, one launch (start us, length us, event | category | flops | bytes accessed | tf_op | source)
XLA Modules:
  0.0 204.7 jit_solution(5350851966030818054)
XLA Ops:
  2.7 2.2 %collective-permute-start = (bf16[128,1024]{1,0:T(8,128)(2,1)S(1)}, bf16[128,1024]{1,0:T(8,128)(2,1)S(1)}, u32[]{:S(2)}, u32[]{:S(2)}) collective-permute-start(bf16[128,1024]{1,0:T(8,128)(2,1)S(1)} %broadcast_select_fusion), channel_id=1, source_target_pairs={{0,1},{1,2},{2,3},{3,0},{4,5},{5,6},{6,7},{7,4},{8,9},{9,10},{10,1... | collective-permute-start | bytes 786440 | tf_op jit(solution)/shard_map/ppermute | solution.py:435
  4.9 2.6 %collective-permute-start.1 = (bf16[128,1024]{1,0:T(8,128)(2,1)S(1)}, bf16[128,1024]{1,0:T(8,128)(2,1)S(1)}, u32[]{:S(2)}, u32[]{:S(2)}) collective-permute-start(bf16[128,1024]{1,0:T(8,128)(2,1)S(1)} %broadcast_select_fusion), channel_id=1, source_target_pairs={{0,2},{1,3},{2,0},{3,1},{4,6},{5,7},{6,4},{7,5},{8,10},{9,11},{10,... | collective-permute-start | bytes 786440 | tf_op jit(solution)/shard_map/ppermute | solution.py:435
  11.0 8.7 %all-to-all-start = ((bf16[32,40,128]{2,1,0:T(8,128)(2,1)}), bf16[32,40,128]{2,1,0:T(8,128)(2,1)S(1)}, u32[]{:S(2)}, u32[]{:S(2)}) async-start(bf16[32,40,128]{2,1,0:T(8,128)(2,1)} %bitcast.6), calls=%async_computation | async-start | bytes 655360 | tf_op jit(solution)/shard_map/all_to_all | solution.py:421
  20.7 11.6 %all-to-all-done = bf16[32,40,128]{2,1,0:T(8,128)(2,1)S(1)} async-done(((bf16[32,40,128]{2,1,0:T(8,128)(2,1)}), bf16[32,40,128]{2,1,0:T(8,128)(2,1)S(1)}, u32[]{:S(2)}, u32[]{:S(2)}) %all-to-all-start) | async-done | bytes 327712 | tf_op jit(solution)/shard_map/all_to_all | solution.py:421
  33.1 1.9 shard_map.78
  35.0 3.4 %all-to-all-start.1 = ((bf16[8,16,1024]{2,1,0:T(8,128)(2,1)}), bf16[8,16,1024]{2,1,0:T(8,128)(2,1)S(1)}, u32[]{:S(2)}, u32[]{:S(2)}) async-start(bf16[8,16,1024]{2,1,0:T(8,128)(2,1)} %bitcast.11), calls=%async_computation.1 | async-start | bytes 524288 | tf_op jit(solution)/shard_map/all_to_all | solution.py:37
  38.5 9.3 %all-to-all-done.1 = bf16[8,16,1024]{2,1,0:T(8,128)(2,1)S(1)} async-done(((bf16[8,16,1024]{2,1,0:T(8,128)(2,1)}), bf16[8,16,1024]{2,1,0:T(8,128)(2,1)S(1)}, u32[]{:S(2)}, u32[]{:S(2)}) %all-to-all-start.1) | async-done | bytes 262176 | tf_op jit(solution)/shard_map/all_to_all | solution.py:37
  48.5 11.8 %all_to_all.50 = bf16[8,16,1024]{2,1,0:T(8,128)(2,1)S(1)} all-to-all(bf16[8,16,1024]{2,1,0:T(8,128)(2,1)S(1)} %broadcast_in_dim.8), channel_id=1, replica_groups=mesh['x'=4,'core'=2,'z'=8,'y'=4] {'z'}, dimensions={0} | all-to-all | bytes 524288 | tf_op jit(solution)/shard_map/all_to_all | solution.py:29
  60.6 2.4 %collective-permute-start.5 = (bf16[128,1024]{1,0:T(8,128)(2,1)S(1)}, bf16[128,1024]{1,0:T(8,128)(2,1)S(1)}, u32[]{:S(2)}, u32[]{:S(2)}) collective-permute-start(bf16[128,1024]{1,0:T(8,128)(2,1)S(1)} %bitcast.34), channel_id=1, source_target_pairs={{0,3},{1,0},{2,1},{3,2},{4,7},{5,4},{6,5},{7,6},{8,11},{9,8},{10,9... | collective-permute-start | bytes 786440 | tf_op jit(solution)/shard_map/ppermute | solution.py:472
  63.6 2.2 %copy-done = bf16[2048,1024]{1,0:T(8,128)(2,1)S(1)} copy-done((bf16[2048,1024]{1,0:T(8,128)(2,1)S(1)}, bf16[2048,1024]{1,0:T(8,128)(2,1)}, u32[]{:S(2)}) %copy-start) | copy-done | bytes 4194328
  65.8 3.5 %shard_map.79 = (bf16[2048,1024]{1,0:T(8,128)(2,1)S(1)}, f32[1,2048]{1,0:T(1,128)S(1)}, bf16[4,128,2048]{2,1,0:T(8,128)(2,1)}) custom-call(s32[1]{0:T(128)} %bitcast.8.core_ref, bf16[2048,1024]{1,0:T(8,128)(2,1)S(1)} %copy-done), custom_call_target="tpu_custom_call" | custom-call | flops 12582912 | bytes 10485760 | tf_op jit(solution)/shard_map/pallas_call | solution.py:58
  69.3 1.1 collective-permute-done.6.rest_3_
  70.5 3.4 %shard_map.80 = (bf16[512,2048]{1,0:T(8,128)(2,1)S(1)}, f32[8,2,2048]{2,1,0:T(2,128)S(1)}, f32[1,512]{1,0:T(1,128)S(1)}, bf16[512,1024]{1,0:T(8,128)(2,1)S(1)}) custom-call(s32[4]{0:T(128)S(1)} %pad_add_fusion.place_ref, bf16[128,1024]{1,0:T(8,128)(2,1)S(1)} %bitcast.36, bf16[128,1024]{1,0:T(8,128)(2,1)S(1)} %collective-permute-done.4.rest_1_, ...), custom_call_target="tpu_custom_call" | custom-call | flops 2147483648 | bytes 8388608 | tf_op jit(solution)/shard_map/pallas_call | solution.py:58
  73.9 14.9 %all_to_all.51.mass_ref = f32[8,2,2048]{2,1,0:T(2,128)S(1)} all-to-all(f32[8,2,2048]{2,1,0:T(2,128)S(1)} %get-tuple-element.14), channel_id=1, replica_groups=mesh['x'=4,'core'=2,'z'=8,'y'=4] {'x','core'}, dimensions={0} | all-to-all | bytes 262144 | tf_op jit(solution)/shard_map/all_to_all | solution.py:479
  89.4 13.3 %all_to_all.52.image_ref.soft_ref = f32[32,2,512]{2,1,0:T(2,128)S(1)} all-to-all(f32[32,2,512]{2,1,0:T(2,128)S(1)} %shard_map.81), channel_id=1, replica_groups=mesh['x'=4,'core'=2,'z'=8,'y'=4] {'z','y'}, dimensions={0} | all-to-all | bytes 262144 | tf_op jit(solution)/shard_map/all_to_all | solution.py:480
  103.3 10.0 %all_to_all.53.mass_ref = f32[8,2,2048]{2,1,0:T(2,128)S(1)} all-to-all(f32[8,2,2048]{2,1,0:T(2,128)S(1)} %shard_map.82), channel_id=1, replica_groups=mesh['x'=4,'core'=2,'z'=8,'y'=4] {'x','core'}, dimensions={0} | all-to-all | bytes 262144 | tf_op jit(solution)/shard_map/all_to_all | solution.py:482
  113.8 11.8 %all_to_all.54.image_ref = f32[32,1,512]{2,1,0:T(1,128)S(1)} all-to-all(f32[32,1,512]{2,1,0:T(1,128)S(1)} %shard_map.83), channel_id=1, replica_groups=mesh['x'=4,'core'=2,'z'=8,'y'=4] {'z','y'}, dimensions={0} | all-to-all | bytes 131072 | tf_op jit(solution)/shard_map/all_to_all | solution.py:483
  126.2 9.9 %all_to_all.55.mass_ref = f32[8,2,2048]{2,1,0:T(2,128)S(1)} all-to-all(f32[8,2,2048]{2,1,0:T(2,128)S(1)} %shard_map.84), channel_id=1, replica_groups=mesh['x'=4,'core'=2,'z'=8,'y'=4] {'x','core'}, dimensions={0} | all-to-all | bytes 262144 | tf_op jit(solution)/shard_map/all_to_all | solution.py:482
  136.1 1.2 shard_map.85
  137.3 3.9 %all-to-all-start.8 = ((f32[32,1,512]{2,1,0:T(1,128)}), f32[32,1,512]{2,1,0:T(1,128)S(1)}, u32[]{:S(2)}, u32[]{:S(2)}) async-start(f32[32,1,512]{2,1,0:T(1,128)} %shard_map.85), calls=%async_computation.8 | async-start | bytes 131072 | tf_op jit(solution)/shard_map/all_to_all | solution.py:483
  141.6 8.5 %all-to-all-done.8.image_ref = f32[32,1,512]{2,1,0:T(1,128)S(1)} async-done(((f32[32,1,512]{2,1,0:T(1,128)}), f32[32,1,512]{2,1,0:T(1,128)S(1)}, u32[]{:S(2)}, u32[]{:S(2)}) %all-to-all-start.8) | async-done | bytes 65568 | tf_op jit(solution)/shard_map/all_to_all | solution.py:483
  150.1 12.4 %shard_map.87 = (f32[1,2048]{1,0:T(1,128)S(1)}, bf16[4,128,2048]{2,1,0:T(8,128)(2,1)}, f32[4,128,2048]{2,1,0:T(8,128)}, bf16[1024,512]{1,0:T(8,128)(2,1)}) custom-call(f32[32,1,512]{2,1,0:T(1,128)S(1)} %all-to-all-done.8.image_ref, f32[32,2,512]{2,1,0:T(2,128)S(1)} %all_to_all.52.image_ref.soft_ref, f32[8,2,2048]{2,1,0:T(2,128)S(1)} %all_to_all.55.mass_ref, ...), custom_call_target="tpu_custom_call" | custom-call | flops 4294967296 | bytes 10485760 | tf_op jit(solution)/shard_map/pallas_call | solution.py:317
  162.5 1.9 collective-permute-start.7
  164.4 4.7 %all-to-all-start.9 = ((bf16[32,32,512]{2,1,0:T(8,128)(2,1)}), bf16[32,32,512]{2,1,0:T(8,128)(2,1)}, u32[]{:S(2)}, u32[]{:S(2)}) async-start(bf16[32,32,512]{2,1,0:T(8,128)(2,1)} %bitcast.13), calls=%async_computation.9 | async-start | bytes 2097152 | tf_op jit(solution)/shard_map/all_to_all | solution.py:37
  169.2 1.1 collective-permute-done.8.two_ref
  170.4 2.4 %shard_map.90 = bf16[128,2048]{1,0:T(8,128)(2,1)} custom-call(s32[1]{0:T(128)} %bitcast.18.place_ref, f32[4,128,2048]{2,1,0:T(8,128)} %get-tuple-element.19.stay_ref, bf16[4,128,2048]{2,1,0:T(8,128)(2,1)S(1)} %collective-permute-done.7.arrived_ref, bf16[4,128,2048]{2,1,0:T(8,128)(2,1)} %get-tuple-element.21.turned_ref, ...), custom_call_target="tpu_custom_call" | custom-call | flops 1000000000 | bytes 2621440 | tf_op jit(solution)/shard_map/pallas_call | solution.py:374
  173.6 2.4 %shard_map.89 = bf16[128,2048]{1,0:T(8,128)(2,1)} custom-call(s32[1]{0:T(128)} %bitcast.17.place_ref, f32[4,128,2048]{2,1,0:T(8,128)} %get-tuple-element.19.stay_ref, bf16[4,128,2048]{2,1,0:T(8,128)(2,1)S(1)} %collective-permute-done.7.arrived_ref, bf16[4,128,2048]{2,1,0:T(8,128)(2,1)} %get-tuple-element.21.turned_ref, ...), custom_call_target="tpu_custom_call" | custom-call | flops 1000000000 | bytes 2621440 | tf_op jit(solution)/shard_map/pallas_call | solution.py:374
  176.6 2.4 %shard_map.88 = bf16[128,2048]{1,0:T(8,128)(2,1)} custom-call(s32[1]{0:T(128)} %bitcast.16.place_ref, f32[4,128,2048]{2,1,0:T(8,128)} %get-tuple-element.19.stay_ref, bf16[4,128,2048]{2,1,0:T(8,128)(2,1)S(1)} %collective-permute-done.7.arrived_ref, bf16[4,128,2048]{2,1,0:T(8,128)(2,1)} %get-tuple-element.21.turned_ref, ...), custom_call_target="tpu_custom_call" | custom-call | flops 1000000000 | bytes 2621440 | tf_op jit(solution)/shard_map/pallas_call | solution.py:374
  179.6 16.7 %all-to-all-done.9 = bf16[32,32,512]{2,1,0:T(8,128)(2,1)} async-done(((bf16[32,32,512]{2,1,0:T(8,128)(2,1)}), bf16[32,32,512]{2,1,0:T(8,128)(2,1)}, u32[]{:S(2)}, u32[]{:S(2)}) %all-to-all-start.9) | async-done | bytes 1048608 | tf_op jit(solution)/shard_map/all_to_all | solution.py:37
  196.3 1.4 convert_reduce_fusion
  198.4 3.4 %collective-permute-done.10.rest_1_ = bf16[128,2048]{1,0:T(8,128)(2,1)S(1)} collective-permute-done((bf16[128,2048]{1,0:T(8,128)(2,1)}, bf16[128,2048]{1,0:T(8,128)(2,1)S(1)}, u32[]{:S(2)}, u32[]{:S(2)}) %collective-permute-start.10) | collective-permute-done | bytes 524320 | tf_op jit(solution)/shard_map/ppermute | solution.py:494
  201.7 2.9 %shard_map.91 = f32[128,2048]{1,0:T(8,128)} custom-call(s32[1]{0:T(128)} %bitcast.15.place_ref, f32[4,128,2048]{2,1,0:T(8,128)} %get-tuple-element.19.stay_ref, bf16[4,128,2048]{2,1,0:T(8,128)(2,1)S(1)} %collective-permute-done.7.arrived_ref, bf16[4,128,2048]{2,1,0:T(8,128)(2,1)} %get-tuple-element.21.turned_ref, f32[1,2048]{1,0:T(1,128)S(1)} %get-tuple-element.22.one_ref, ...), custom_call_target="tpu_custom_call" | custom-call | flops 1000000000 | bytes 2621440 | tf_op jit(solution)/shard_map/pallas_call | solution.py:374
  (57 shorter events, 14.4 us)
Async XLA Ops:
  2.7 16.9 %collective-permute-start = (bf16[128,1024]{1,0:T(8,128)(2,1)S(1)}, bf16[128,1024]{1,0:T(8,128)(2,1)S(1)}, u32[]{:S(2)}, u32[]{:S(2)}) collective-permute-start(bf16[128,1024]{1,0:T(8,128)(2,1)S(1)} %broadcast_select_fusion), channel_id=1, source_target_pairs={{0,1},{1,2},{2,3},{3,0},{4,5},{5,6},{6,7},{7,4},{8,9},{9,10},{10,1... | collective-permute-start | bytes 786440 | tf_op jit(solution)/shard_map/ppermute | solution.py:435
  4.9 14.9 %collective-permute-start.1 = (bf16[128,1024]{1,0:T(8,128)(2,1)S(1)}, bf16[128,1024]{1,0:T(8,128)(2,1)S(1)}, u32[]{:S(2)}, u32[]{:S(2)}) collective-permute-start(bf16[128,1024]{1,0:T(8,128)(2,1)S(1)} %broadcast_select_fusion), channel_id=1, source_target_pairs={{0,2},{1,3},{2,0},{3,1},{4,6},{5,7},{6,4},{7,5},{8,10},{9,11},{10,... | collective-permute-start | bytes 786440 | tf_op jit(solution)/shard_map/ppermute | solution.py:435
  7.5 12.3 %collective-permute-start.2 = (bf16[128,1024]{1,0:T(8,128)(2,1)S(1)}, bf16[128,1024]{1,0:T(8,128)(2,1)S(1)}, u32[]{:S(2)}, u32[]{:S(2)}) collective-permute-start(bf16[128,1024]{1,0:T(8,128)(2,1)S(1)} %broadcast_select_fusion), channel_id=1, source_target_pairs={{0,3},{1,0},{2,1},{3,2},{4,7},{5,4},{6,5},{7,6},{8,11},{9,8},{10,9... | collective-permute-start | bytes 786440 | tf_op jit(solution)/shard_map/ppermute | solution.py:435
  11.0 21.3 %all-to-all-start = ((bf16[32,40,128]{2,1,0:T(8,128)(2,1)}), bf16[32,40,128]{2,1,0:T(8,128)(2,1)S(1)}, u32[]{:S(2)}, u32[]{:S(2)}) async-start(bf16[32,40,128]{2,1,0:T(8,128)(2,1)} %bitcast.6), calls=%async_computation | async-start | bytes 655360 | tf_op jit(solution)/shard_map/all_to_all | solution.py:421
  19.9 13.2 %copy-start.1 = (bf16[128,1024]{1,0:T(8,128)(2,1)S(1)}, bf16[128,1024]{1,0:T(8,128)(2,1)}, u32[]{:S(2)}) copy-start(bf16[128,1024]{1,0:T(8,128)(2,1)} %w_out_ref.1) | copy-start | bytes 786436
  19.9 13.2 %collective-permute-start.3 = (bf16[3,128,1024]{2,1,0:T(8,128)(2,1)S(1)}, bf16[3,128,1024]{2,1,0:T(8,128)(2,1)S(1)}, u32[]{:S(2)}, u32[]{:S(2)}) collective-permute-start(bf16[3,128,1024]{2,1,0:T(8,128)(2,1)S(1)} %shard_map.77.shares_ref), channel_id=1, source_target_pairs={{0,32},{32,0},{1,33},{33,1},{2,34},{34,2},{3,35},{35,3},{4,36},{36... | collective-permute-start | bytes 2359304 | tf_op jit(solution)/shard_map/ppermute | solution.py:439
  35.0 12.8 %all-to-all-start.1 = ((bf16[8,16,1024]{2,1,0:T(8,128)(2,1)}), bf16[8,16,1024]{2,1,0:T(8,128)(2,1)S(1)}, u32[]{:S(2)}, u32[]{:S(2)}) async-start(bf16[8,16,1024]{2,1,0:T(8,128)(2,1)} %bitcast.11), calls=%async_computation.1 | async-start | bytes 524288 | tf_op jit(solution)/shard_map/all_to_all | solution.py:37
  60.3 9.0 %collective-permute-start.4 = (bf16[128,1024]{1,0:T(8,128)(2,1)S(1)}, bf16[128,1024]{1,0:T(8,128)(2,1)S(1)}, u32[]{:S(2)}, u32[]{:S(2)}) collective-permute-start(bf16[128,1024]{1,0:T(8,128)(2,1)S(1)} %bitcast.33), channel_id=1, source_target_pairs={{0,1},{1,2},{2,3},{3,0},{4,5},{5,6},{6,7},{7,4},{8,9},{9,10},{10,1... | collective-permute-start | bytes 786440 | tf_op jit(solution)/shard_map/ppermute | solution.py:472
  60.6 8.7 %collective-permute-start.5 = (bf16[128,1024]{1,0:T(8,128)(2,1)S(1)}, bf16[128,1024]{1,0:T(8,128)(2,1)S(1)}, u32[]{:S(2)}, u32[]{:S(2)}) collective-permute-start(bf16[128,1024]{1,0:T(8,128)(2,1)S(1)} %bitcast.34), channel_id=1, source_target_pairs={{0,3},{1,0},{2,1},{3,2},{4,7},{5,4},{6,5},{7,6},{8,11},{9,8},{10,9... | collective-permute-start | bytes 786440 | tf_op jit(solution)/shard_map/ppermute | solution.py:472
  63.0 7.5 %collective-permute-start.6 = (bf16[128,1024]{1,0:T(8,128)(2,1)S(1)}, bf16[128,1024]{1,0:T(8,128)(2,1)S(1)}, u32[]{:S(2)}, u32[]{:S(2)}) collective-permute-start(bf16[128,1024]{1,0:T(8,128)(2,1)S(1)} %bitcast.35), channel_id=1, source_target_pairs={{0,2},{1,3},{2,0},{3,1},{4,6},{5,7},{6,4},{7,5},{8,10},{9,11},{10,... | collective-permute-start | bytes 786440 | tf_op jit(solution)/shard_map/ppermute | solution.py:472
  63.6 2.2 %copy-start = (bf16[2048,1024]{1,0:T(8,128)(2,1)S(1)}, bf16[2048,1024]{1,0:T(8,128)(2,1)}, u32[]{:S(2)}) copy-start(bf16[2048,1024]{1,0:T(8,128)(2,1)} %proto_ref.1) | copy-start | bytes 12582916
  69.3 4.6 %copy-start.2 = (bf16[2048,1024]{1,0:T(8,128)(2,1)}, bf16[2048,1024]{1,0:T(8,128)(2,1)S(1)}, u32[]{:S(2)}) copy-start(bf16[2048,1024]{1,0:T(8,128)(2,1)S(1)} %get-tuple-element.13.rest_4_.unit_ref) | copy-start | bytes 12582916
  137.3 12.8 %all-to-all-start.8 = ((f32[32,1,512]{2,1,0:T(1,128)}), f32[32,1,512]{2,1,0:T(1,128)S(1)}, u32[]{:S(2)}, u32[]{:S(2)}) async-start(f32[32,1,512]{2,1,0:T(1,128)} %shard_map.85), calls=%async_computation.8 | async-start | bytes 131072 | tf_op jit(solution)/shard_map/all_to_all | solution.py:483
  162.5 7.9 %collective-permute-start.7 = (bf16[4,128,2048]{2,1,0:T(8,128)(2,1)}, bf16[4,128,2048]{2,1,0:T(8,128)(2,1)S(1)}, u32[]{:S(2)}, u32[]{:S(2)}) collective-permute-start(bf16[4,128,2048]{2,1,0:T(8,128)(2,1)} %get-tuple-element.20), channel_id=1, source_target_pairs={{0,32},{32,0},{1,33},{33,1},{2,34},{34,2},{3,35},{35,3},{4,36},{36... | collective-permute-start | bytes 6291464 | tf_op jit(solution)/shard_map/ppermute | solution.py:486
  164.4 31.9 %all-to-all-start.9 = ((bf16[32,32,512]{2,1,0:T(8,128)(2,1)}), bf16[32,32,512]{2,1,0:T(8,128)(2,1)}, u32[]{:S(2)}, u32[]{:S(2)}) async-start(bf16[32,32,512]{2,1,0:T(8,128)(2,1)} %bitcast.13), calls=%async_computation.9 | async-start | bytes 2097152 | tf_op jit(solution)/shard_map/all_to_all | solution.py:37
  169.1 1.3 collective-permute-start.8
  172.8 25.6 %collective-permute-start.11 = (bf16[128,2048]{1,0:T(8,128)(2,1)}, bf16[128,2048]{1,0:T(8,128)(2,1)S(1)}, u32[]{:S(2)}, u32[]{:S(2)}) collective-permute-start(bf16[128,2048]{1,0:T(8,128)(2,1)} %shard_map.90), channel_id=1, source_target_pairs={{0,192},{64,0},{128,64},{192,128},{1,193},{65,1},{129,65},{193,129... | collective-permute-start | bytes 1572872 | tf_op jit(solution)/shard_map/ppermute | solution.py:494
  176.0 25.7 %collective-permute-start.10 = (bf16[128,2048]{1,0:T(8,128)(2,1)}, bf16[128,2048]{1,0:T(8,128)(2,1)S(1)}, u32[]{:S(2)}, u32[]{:S(2)}) collective-permute-start(bf16[128,2048]{1,0:T(8,128)(2,1)} %shard_map.89), channel_id=1, source_target_pairs={{0,64},{64,128},{128,192},{192,0},{1,65},{65,129},{129,193},{193,1... | collective-permute-start | bytes 1572872 | tf_op jit(solution)/shard_map/ppermute | solution.py:494
  179.0 22.7 %collective-permute-start.9 = (bf16[128,2048]{1,0:T(8,128)(2,1)}, bf16[128,2048]{1,0:T(8,128)(2,1)}, u32[]{:S(2)}, u32[]{:S(2)}) collective-permute-start(bf16[128,2048]{1,0:T(8,128)(2,1)} %shard_map.88), channel_id=1, source_target_pairs={{0,128},{64,192},{128,0},{192,64},{1,129},{65,193},{129,1},{193,65... | collective-permute-start | bytes 1572872 | tf_op jit(solution)/shard_map/ppermute | solution.py:494

commit v8 on v7

--- a/solution.py
+++ b/solution.py
@@ -353,49 +353,84 @@
     )(images, softs, masses, keep_hbm(unit), embed, embed_t)
 
 
-def pair_kernel(place_ref, stay_ref, arrived_ref, turned_ref, one_ref, two_ref, length_ref, *rest):
-    *others, out_ref = rest
+def pair_rows(refs, rows, part):
+    stay_ref, arrived_ref, turned_ref, one_ref, two_ref, length_ref = refs
+    inverse = 1.0 / length_ref[:, part]
+    radial = (one_ref[:, part] + two_ref[:, part]) * inverse
+    total = stay_ref[0, rows, part] + arrived_ref[0, rows, part].astype(f32)
+    return (total - turned_ref[0, rows, part].astype(f32) * radial) * inverse
+
+
+LOWER = slice(0, LANES // 2)
+UPPER = slice(LANES // 2, LANES)
+ALL = slice(0, LANES)
+
+
+def far_kernel(place_ref, *refs):
+    *given, lower_ref, upper_ref = refs
+    for part in tiles(lower_ref.shape[1]):
+        lower_ref[:, part] = pair_rows(given, LOWER, part).astype(bf16)
+        upper_ref[:, part] = pair_rows(given, UPPER, part).astype(bf16)
+
+
+def near_kernel(place_ref, *refs):
+    right, left, lines = refs[:3], refs[3:6], refs[6:9]
+    right_send, left_send, right_keep, left_keep = refs[9:]
+    for part in tiles(right_send.shape[1]):
+        right_send[:, part] = pair_rows((*right, *lines), UPPER, part).astype(bf16)
+        left_send[:, part] = pair_rows((*left, *lines), LOWER, part).astype(bf16)
+        right_keep[:, part] = pair_rows((*right, *lines), LOWER, part)
+        left_keep[:, part] = pair_rows((*left, *lines), UPPER, part)
+
+
+def own_kernel(place_ref, *refs):
+    *given, lower_ref, upper_ref, out_ref = refs
     for part in tiles(out_ref.shape[1]):
-        inverse = 1.0 / length_ref[:, part]
-        radial = (one_ref[:, part] + two_ref[:, part]) * inverse
-        total = stay_ref[0, :, part] + arrived_ref[0, :, part].astype(f32)
-        total = (total - turned_ref[0, :, part].astype(f32) * radial) * inverse
-        for ref in others:
-            total = total + ref[:, part].astype(f32)
-        out_ref[:, part] = total.astype(out_ref.dtype)
-
-
-def pair_call(place, stay, arrived, turned, radials, length, others=()):
-    blocks, height, protos = stay.shape
-
-    def full(values):
-        return pl.BlockSpec(values.shape, lambda i, p: (0,) * values.ndim)
-
+        out_ref[LOWER, part] = pair_rows(given, LOWER, part) + lower_ref[:, part].astype(f32)
+        out_ref[UPPER, part] = pair_rows(given, UPPER, part) + upper_ref[:, part].astype(f32)
+
+
+def relay_kernel(right_keep, left_keep, lower_ref, upper_ref, right_send, left_send):
+    for part in tiles(right_send.shape[1]):
+        right_send[:, part] = (right_keep[:, part] + lower_ref[:, part].astype(f32)).astype(bf16)
+        left_send[:, part] = (left_keep[:, part] + upper_ref[:, part].astype(f32)).astype(bf16)
+
+
+def final_kernel(sum_ref, lower_ref, upper_ref, out_ref):
+    for part in tiles(out_ref.shape[1]):
+        out_ref[LOWER, part] = sum_ref[LOWER, part] + lower_ref[:, part].astype(f32)
+        out_ref[UPPER, part] = sum_ref[UPPER, part] + upper_ref[:, part].astype(f32)
+
+
+def pair_call(kernel, places, parts, lines, outs, others=()):
+    blocks, height, protos = parts[0].shape
+
+    def picked(n):
+        return pl.BlockSpec((1, height, protos), lambda i, p: (p[n], 0, 0))
+
+    def full(shape):
+        return pl.BlockSpec(shape, lambda i, p: (0,) * len(shape))
+
+    stay, arrived, turned = parts
+    given = [keep_hbm(stay), arrived, keep_hbm(turned)] * len(places)
+    many = len(outs) > 1
+    shapes = [jax.ShapeDtypeStruct(shape, dtype) for shape, dtype in outs]
+    specs = [full(shape) for shape, dtype in outs]
     return pl.pallas_call(
-        pair_kernel,
+        kernel,
         grid_spec=pltpu.PrefetchScalarGridSpec(
             num_scalar_prefetch=1,
             grid=(1,),
-            in_specs=[pl.BlockSpec((1, height, protos), lambda i, p: (p[0], 0, 0))] * 3
-            + [full(values) for values in (*radials, length, *others)],
-            out_specs=pl.BlockSpec((height, protos), lambda i, p: (0, 0)),
+            in_specs=[picked(n) for n in range(len(places)) for _ in range(3)]
+            + [full(values.shape) for values in (*lines, *others)],
+            out_specs=specs if many else specs[0],
         ),
-        out_shape=jax.ShapeDtypeStruct((height, protos), f32 if others else bf16),
-        compiler_params=pltpu.CompilerParams(vmem_limit_bytes=10 * 1024 * 1024),
+        out_shape=shapes if many else shapes[0],
+        compiler_params=pltpu.CompilerParams(vmem_limit_bytes=16 * 1024 * 1024),
         cost_estimate=pl.CostEstimate(
-            flops=10**9,
-            bytes_accessed=10 * height * protos,
-            transcendentals=0,
+            flops=10**9, bytes_accessed=10 * height * protos, transcendentals=0
         ),
-    )(
-        place.reshape(1),
-        keep_hbm(stay),
-        arrived,
-        keep_hbm(turned),
-        *radials,
-        length,
-        *others,
-    )
+    )(jnp.stack(places), *given, *lines, *others)
 
 
 def body(hidden_states, ln_in_gain, w_in, w_out, ln_out_gain, prototypes):
@@ -484,17 +519,52 @@
 
     radial, away, stay, embed_terms = grad_pass(images, softs, masses, unit, embed, embed_t)
     arrived = lax.ppermute(away, "core", swap)
-    radials = (radial, lax.ppermute(radial, "core", swap))
-
-    def paired(step, others=()):
-        place = (x_index + step) % x_count
-        return pair_call(place, stay, arrived, turned, radials, proto_len, others)
-
-    landed = tuple(
-        lax.ppermute(paired(step), "x", [(i, (i + step) % x_count) for i in range(x_count)])
-        for step in (2, 1, 3)
-    )
-    proto_grad = paired(0, landed)
+    parts = (stay, arrived, turned)
+    lines = (radial, lax.ppermute(radial, "core", swap), proto_len)
+    flat = (slice_width // 2, proto_count)
+
+    def spot(step):
+        return (x_index + step) % x_count
+
+    def right(values):
+        return lax.ppermute(values, "x", [(i, (i + 1) % x_count) for i in range(x_count)])
+
+    def left(values):
+        return lax.ppermute(values, "x", [((i + 1) % x_count, i) for i in range(x_count)])
+
+    far_lower, far_upper = pair_call(far_kernel, (spot(2),), parts, lines, [(flat, bf16)] * 2)
+    came_lower, came_upper = right(far_lower), left(far_upper)
+    right_send, left_send, right_keep, left_keep = pair_call(
+        near_kernel, (spot(1), spot(3)), parts, lines, [(flat, bf16)] * 2 + [(flat, f32)] * 2
+    )
+    near_upper, near_lower = right(right_send), left(left_send)
+    own_sum = pair_call(
+        own_kernel,
+        (x_index,),
+        parts,
+        lines,
+        [((slice_width, proto_count), f32)],
+        (near_lower, near_upper),
+    )
+    right_relay, left_relay = call(
+        relay_kernel,
+        (),
+        (right_keep, left_keep, came_lower, came_upper),
+        [(flat, bf16)] * 2,
+        8,
+        10**8,
+        10**6,
+    )
+    last_lower, last_upper = right(right_relay), left(left_relay)
+    proto_grad = call(
+        final_kernel,
+        (),
+        (own_sum, last_lower, last_upper),
+        [((slice_width, proto_count), f32)],
+        8,
+        10**8,
+        10**6,
+    )
     embed_grad_t = scatter_sum(embed_terms.reshape(col_count, local_width, row_count), COLS)
     embed_grad = embed_grad_t.T.reshape(view_count, image_rows, local_width)
     return (embed_grad, proto_grad)

time: 206 us -> 203 us (0.985)
  waiting for transfers between devices: 51.9 us -> 43.9 us
  starting transfers between devices: 34.7 us -> 40.7 us
    ppermute x4 -> x7, starting transfers between devices: 2.19 us -> 8.21 us  [the longest x3 7.73 us: left(): lax.ppermute(values, 'x', [((i + 1) % x_count, i) for i in range(x_count)])]
    all_to_all x2, waiting for transfers between devices: 26 us -> 20.9 us  [scatter_sum(): return jnp.sum(lax.all_to_all(blocks, axes, 0, 0).astype(f32), axis=0)]
    pallas_call x4 -> x3, Pallas kernels: 10.1 us -> 6.45 us  [pair_call(): pl.pallas_call(kernel, grid_spec=pltpu.PrefetchScalarGridSpec(num_scalar_...]
    ppermute x4 -> x7, waiting for transfers between devices: 4.5 us -> 1.55 us  [the longest x1 1.13 us: body(): lines = (radial, lax.ppermute(radial, 'core', swap), proto_len)]
    pallas_call x10 -> x12, Pallas kernels: 12.7 us -> 14.7 us  [call(): pl.pallas_call(kernel, in_specs=[SMEM] * len(scalars) + [VMEM] * len(arra...]
  transfers between devices with their start and end apart: 16 -> 19, of which waited for: 8 -> 8; matrix products, arithmetic and copies ran while one was open for 3% -> 3% of each run, Pallas kernels for 5% -> 6%
where the time goes in v8:
time: 203 us; the launch traced here: 201 us
  blocking collectives  71.8 us (35%)
  waiting for transfers between devices  43.9 us (22%)
  starting transfers between devices  40.7 us (20%)
  Pallas kernels  33.5 us (17%)
  local copies, waits for them, and re-layouts  5.82 us (3%)
  other arithmetic  4.11 us (2%)
    all_to_all x2, waiting for transfers between devices, scatter_sum(): return jnp.sum(lax.all_to_all(blocks, axes, 0, 0).astype(f32), axis=0)  20.9 us
    all_to_all x2, blocking collectives, body(): masses = lax.all_to_all(proto_pass(images, base, row_parts), ROWS, 0, 0)  19.9 us
    all_to_all x1, blocking collectives, body(): masses = lax.all_to_all(masses, ROWS, 0, 0)  14.9 us
    pallas_call x12, Pallas kernels, call(): pl.pallas_call(kernel, in_specs=[SMEM] * len(scalars) + [VMEM] * len(arra...  14.7 us
    all_to_all x1, blocking collectives, body(): lax.all_to_all(image_pass(masses, base, col_count, soft_part), COLS, 0, 0)  13.3 us
    pallas_call x1, Pallas kernels, grad_pass(): pl.pallas_call(grad_kernel, grid=(protos // TILE,), in_specs=[full(images...  12.4 us
    all_to_all x1, blocking collectives, gather_all(): return lax.all_to_all(copies, axes, 0, 0)  11.8 us
    all_to_all x1, blocking collectives, body(): images = lax.all_to_all(image_pass(masses, base, col_count), COLS, 0, 0)  11.8 us
  transfers between devices with their start and end apart: 19, of which 8 were waited for; matrix products, arithmetic and copies ran while one was open for 3% of the time, Pallas kernels for 6%

profile of v8, /device:TPU:1, one launch (start us, length us, event | category | flops | bytes accessed | tf_op | source)
XLA Modules:
  0.0 201.1 jit_solution(15983106304361855945)
XLA Ops:
  2.7 2.2 %collective-permute-start = (bf16[128,1024]{1,0:T(8,128)(2,1)S(1)}, bf16[128,1024]{1,0:T(8,128)(2,1)S(1)}, u32[]{:S(2)}, u32[]{:S(2)}) collective-permute-start(bf16[128,1024]{1,0:T(8,128)(2,1)S(1)} %broadcast_select_fusion), channel_id=1, source_target_pairs={{0,1},{1,2},{2,3},{3,0},{4,5},{5,6},{6,7},{7,4},{8,9},{9,10},{10,1... | collective-permute-start | bytes 786440 | tf_op jit(solution)/shard_map/ppermute | solution.py:470
  4.9 2.6 %collective-permute-start.1 = (bf16[128,1024]{1,0:T(8,128)(2,1)S(1)}, bf16[128,1024]{1,0:T(8,128)(2,1)S(1)}, u32[]{:S(2)}, u32[]{:S(2)}) collective-permute-start(bf16[128,1024]{1,0:T(8,128)(2,1)S(1)} %broadcast_select_fusion), channel_id=1, source_target_pairs={{0,2},{1,3},{2,0},{3,1},{4,6},{5,7},{6,4},{7,5},{8,10},{9,11},{10,... | collective-permute-start | bytes 786440 | tf_op jit(solution)/shard_map/ppermute | solution.py:470
  11.0 8.7 %all-to-all-start = ((bf16[32,40,128]{2,1,0:T(8,128)(2,1)}), bf16[32,40,128]{2,1,0:T(8,128)(2,1)S(1)}, u32[]{:S(2)}, u32[]{:S(2)}) async-start(bf16[32,40,128]{2,1,0:T(8,128)(2,1)} %bitcast.6), calls=%async_computation | async-start | bytes 655360 | tf_op jit(solution)/shard_map/all_to_all | solution.py:456
  20.7 11.6 %all-to-all-done = bf16[32,40,128]{2,1,0:T(8,128)(2,1)S(1)} async-done(((bf16[32,40,128]{2,1,0:T(8,128)(2,1)}), bf16[32,40,128]{2,1,0:T(8,128)(2,1)S(1)}, u32[]{:S(2)}, u32[]{:S(2)}) %all-to-all-start) | async-done | bytes 327712 | tf_op jit(solution)/shard_map/all_to_all | solution.py:456
  33.1 1.9 shard_map.78
  35.0 3.4 %all-to-all-start.1 = ((bf16[8,16,1024]{2,1,0:T(8,128)(2,1)}), bf16[8,16,1024]{2,1,0:T(8,128)(2,1)S(1)}, u32[]{:S(2)}, u32[]{:S(2)}) async-start(bf16[8,16,1024]{2,1,0:T(8,128)(2,1)} %bitcast.11), calls=%async_computation.1 | async-start | bytes 524288 | tf_op jit(solution)/shard_map/all_to_all | solution.py:37
  38.5 9.3 %all-to-all-done.1 = bf16[8,16,1024]{2,1,0:T(8,128)(2,1)S(1)} async-done(((bf16[8,16,1024]{2,1,0:T(8,128)(2,1)}), bf16[8,16,1024]{2,1,0:T(8,128)(2,1)S(1)}, u32[]{:S(2)}, u32[]{:S(2)}) %all-to-all-start.1) | async-done | bytes 262176 | tf_op jit(solution)/shard_map/all_to_all | solution.py:37
  48.5 11.8 %all_to_all.50 = bf16[8,16,1024]{2,1,0:T(8,128)(2,1)S(1)} all-to-all(bf16[8,16,1024]{2,1,0:T(8,128)(2,1)S(1)} %broadcast_in_dim.8), channel_id=1, replica_groups=mesh['x'=4,'core'=2,'z'=8,'y'=4] {'z'}, dimensions={0} | all-to-all | bytes 524288 | tf_op jit(solution)/shard_map/all_to_all | solution.py:29
  60.6 2.4 %collective-permute-start.5 = (bf16[128,1024]{1,0:T(8,128)(2,1)S(1)}, bf16[128,1024]{1,0:T(8,128)(2,1)S(1)}, u32[]{:S(2)}, u32[]{:S(2)}) collective-permute-start(bf16[128,1024]{1,0:T(8,128)(2,1)S(1)} %bitcast.34), channel_id=1, source_target_pairs={{0,3},{1,0},{2,1},{3,2},{4,7},{5,4},{6,5},{7,6},{8,11},{9,8},{10,9... | collective-permute-start | bytes 786440 | tf_op jit(solution)/shard_map/ppermute | solution.py:507
  63.6 2.2 %copy-done = bf16[2048,1024]{1,0:T(8,128)(2,1)S(1)} copy-done((bf16[2048,1024]{1,0:T(8,128)(2,1)S(1)}, bf16[2048,1024]{1,0:T(8,128)(2,1)}, u32[]{:S(2)}) %copy-start) | copy-done | bytes 4194328
  65.8 3.5 %shard_map.79 = (bf16[2048,1024]{1,0:T(8,128)(2,1)S(1)}, f32[1,2048]{1,0:T(1,128)S(1)}, bf16[4,128,2048]{2,1,0:T(8,128)(2,1)}) custom-call(s32[1]{0:T(128)} %bitcast.8.core_ref, bf16[2048,1024]{1,0:T(8,128)(2,1)S(1)} %copy-done), custom_call_target="tpu_custom_call" | custom-call | flops 12582912 | bytes 10485760 | tf_op jit(solution)/shard_map/pallas_call | solution.py:58
  70.5 3.4 %shard_map.80 = (bf16[512,2048]{1,0:T(8,128)(2,1)S(1)}, f32[8,2,2048]{2,1,0:T(2,128)S(1)}, f32[1,512]{1,0:T(1,128)S(1)}, bf16[512,1024]{1,0:T(8,128)(2,1)S(1)}) custom-call(s32[4]{0:T(128)S(1)} %pad_add_fusion.place_ref, bf16[128,1024]{1,0:T(8,128)(2,1)S(1)} %bitcast.36, bf16[128,1024]{1,0:T(8,128)(2,1)S(1)} %collective-permute-done.4.rest_1_, ...), custom_call_target="tpu_custom_call" | custom-call | flops 2147483648 | bytes 8388608 | tf_op jit(solution)/shard_map/pallas_call | solution.py:58
  73.9 14.9 %all_to_all.51.mass_ref = f32[8,2,2048]{2,1,0:T(2,128)S(1)} all-to-all(f32[8,2,2048]{2,1,0:T(2,128)S(1)} %get-tuple-element.22), channel_id=1, replica_groups=mesh['x'=4,'core'=2,'z'=8,'y'=4] {'x','core'}, dimensions={0} | all-to-all | bytes 262144 | tf_op jit(solution)/shard_map/all_to_all | solution.py:514
  89.4 13.3 %all_to_all.52.image_ref.soft_ref = f32[32,2,512]{2,1,0:T(2,128)S(1)} all-to-all(f32[32,2,512]{2,1,0:T(2,128)S(1)} %shard_map.81), channel_id=1, replica_groups=mesh['x'=4,'core'=2,'z'=8,'y'=4] {'z','y'}, dimensions={0} | all-to-all | bytes 262144 | tf_op jit(solution)/shard_map/all_to_all | solution.py:515
  103.3 10.0 %all_to_all.53.mass_ref = f32[8,2,2048]{2,1,0:T(2,128)S(1)} all-to-all(f32[8,2,2048]{2,1,0:T(2,128)S(1)} %shard_map.82), channel_id=1, replica_groups=mesh['x'=4,'core'=2,'z'=8,'y'=4] {'x','core'}, dimensions={0} | all-to-all | bytes 262144 | tf_op jit(solution)/shard_map/all_to_all | solution.py:517
  113.8 11.8 %all_to_all.54.image_ref = f32[32,1,512]{2,1,0:T(1,128)S(1)} all-to-all(f32[32,1,512]{2,1,0:T(1,128)S(1)} %shard_map.83), channel_id=1, replica_groups=mesh['x'=4,'core'=2,'z'=8,'y'=4] {'z','y'}, dimensions={0} | all-to-all | bytes 131072 | tf_op jit(solution)/shard_map/all_to_all | solution.py:518
  126.2 9.9 %all_to_all.55.mass_ref = f32[8,2,2048]{2,1,0:T(2,128)S(1)} all-to-all(f32[8,2,2048]{2,1,0:T(2,128)S(1)} %shard_map.84), channel_id=1, replica_groups=mesh['x'=4,'core'=2,'z'=8,'y'=4] {'x','core'}, dimensions={0} | all-to-all | bytes 262144 | tf_op jit(solution)/shard_map/all_to_all | solution.py:517
  136.1 1.2 shard_map.85
  137.3 3.9 %all-to-all-start.8 = ((f32[32,1,512]{2,1,0:T(1,128)}), f32[32,1,512]{2,1,0:T(1,128)S(1)}, u32[]{:S(2)}, u32[]{:S(2)}) async-start(f32[32,1,512]{2,1,0:T(1,128)} %shard_map.85), calls=%async_computation.8 | async-start | bytes 131072 | tf_op jit(solution)/shard_map/all_to_all | solution.py:518
  141.6 8.5 %all-to-all-done.8.image_ref = f32[32,1,512]{2,1,0:T(1,128)S(1)} async-done(((f32[32,1,512]{2,1,0:T(1,128)}), f32[32,1,512]{2,1,0:T(1,128)S(1)}, u32[]{:S(2)}, u32[]{:S(2)}) %all-to-all-start.8) | async-done | bytes 65568 | tf_op jit(solution)/shard_map/all_to_all | solution.py:518
  150.1 12.4 %shard_map.87 = (f32[1,2048]{1,0:T(1,128)S(1)}, bf16[4,128,2048]{2,1,0:T(8,128)(2,1)}, f32[4,128,2048]{2,1,0:T(8,128)}, bf16[1024,512]{1,0:T(8,128)(2,1)}) custom-call(f32[32,1,512]{2,1,0:T(1,128)S(1)} %all-to-all-done.8.image_ref, f32[32,2,512]{2,1,0:T(2,128)S(1)} %all_to_all.52.image_ref.soft_ref, f32[8,2,2048]{2,1,0:T(2,128)S(1)} %all_to_all.55.mass_ref, ...), custom_call_target="tpu_custom_call" | custom-call | flops 4294967296 | bytes 10485760 | tf_op jit(solution)/shard_map/pallas_call | solution.py:317
  162.5 1.9 collective-permute-start.7
  164.4 4.7 %all-to-all-start.9 = ((bf16[32,32,512]{2,1,0:T(8,128)(2,1)}), bf16[32,32,512]{2,1,0:T(8,128)(2,1)}, u32[]{:S(2)}, u32[]{:S(2)}) async-start(bf16[32,32,512]{2,1,0:T(8,128)(2,1)} %bitcast.13), calls=%async_computation.9 | async-start | bytes 2097152 | tf_op jit(solution)/shard_map/all_to_all | solution.py:37
  169.2 1.1 collective-permute-done.8.refs_7_.refs_4_
  170.4 1.6 shard_map.90
  172.3 2.4 %collective-permute-start.12 = (bf16[64,2048]{1,0:T(8,128)(2,1)S(1)}, bf16[64,2048]{1,0:T(8,128)(2,1)S(1)}, u32[]{:S(2)}, u32[]{:S(2)}) collective-permute-start(bf16[64,2048]{1,0:T(8,128)(2,1)S(1)} %get-tuple-element.37), channel_id=1, source_target_pairs={{64,0},{128,64},{192,128},{0,192},{65,1},{129,65},{193,129},{1,193... | collective-permute-start | bytes 786440 | tf_op jit(solution)/shard_map/ppermute | solution.py:533
  174.8 3.2 %shard_map.88 = (bf16[64,2048]{1,0:T(8,128)(2,1)}, bf16[64,2048]{1,0:T(8,128)(2,1)S(1)}, f32[64,2048]{1,0:T(8,128)S(1)}, f32[64,2048]{1,0:T(8,128)S(1)}) custom-call(s32[2]{0:T(128)S(1)} %pad_add_fusion.1.place_ref, f32[4,128,2048]{2,1,0:T(8,128)} %get-tuple-element.27.refs_0_.refs_3_, bf16[4,128,2048]{2,1,0:T(8,128)(2,1)S(1)} %collective-permute-done.7.refs_1_.refs_4_, ...), custom_call_target="tpu_custom_call" | custom-call | flops 1000000000 | bytes 2621440 | tf_op jit(solution)/shard_map/pallas_call | solution.py:419
  178.0 2.7 %collective-permute-start.9 = (bf16[64,2048]{1,0:T(8,128)(2,1)S(1)}, bf16[64,2048]{1,0:T(8,128)(2,1)S(1)}, u32[]{:S(2)}, u32[]{:S(2)}) collective-permute-start(bf16[64,2048]{1,0:T(8,128)(2,1)S(1)} %get-tuple-element.32), channel_id=1, source_target_pairs={{64,0},{128,64},{192,128},{0,192},{65,1},{129,65},{193,129},{1,193... | collective-permute-start | bytes 786440 | tf_op jit(solution)/shard_map/ppermute | solution.py:533
  182.0 2.7 %collective-permute-start.14 = (bf16[64,2048]{1,0:T(8,128)(2,1)}, bf16[64,2048]{1,0:T(8,128)(2,1)S(1)}, u32[]{:S(2)}, u32[]{:S(2)}) collective-permute-start(bf16[64,2048]{1,0:T(8,128)(2,1)} %get-tuple-element.39), channel_id=1, source_target_pairs={{64,0},{128,64},{192,128},{0,192},{65,1},{129,65},{193,129},{1,193... | collective-permute-start | bytes 786440 | tf_op jit(solution)/shard_map/ppermute | solution.py:533
  184.7 11.6 %all-to-all-done.9 = bf16[32,32,512]{2,1,0:T(8,128)(2,1)} async-done(((bf16[32,32,512]{2,1,0:T(8,128)(2,1)}), bf16[32,32,512]{2,1,0:T(8,128)(2,1)}, u32[]{:S(2)}, u32[]{:S(2)}) %all-to-all-start.9) | async-done | bytes 1048608 | tf_op jit(solution)/shard_map/all_to_all | solution.py:37
  196.3 1.4 convert_reduce_fusion
  198.4 1.6 shard_map.89.sum_ref
  (65 shorter events, 16.2 us)
Async XLA Ops:
  2.7 16.9 %collective-permute-start = (bf16[128,1024]{1,0:T(8,128)(2,1)S(1)}, bf16[128,1024]{1,0:T(8,128)(2,1)S(1)}, u32[]{:S(2)}, u32[]{:S(2)}) collective-permute-start(bf16[128,1024]{1,0:T(8,128)(2,1)S(1)} %broadcast_select_fusion), channel_id=1, source_target_pairs={{0,1},{1,2},{2,3},{3,0},{4,5},{5,6},{6,7},{7,4},{8,9},{9,10},{10,1... | collective-permute-start | bytes 786440 | tf_op jit(solution)/shard_map/ppermute | solution.py:470
  4.9 14.9 %collective-permute-start.1 = (bf16[128,1024]{1,0:T(8,128)(2,1)S(1)}, bf16[128,1024]{1,0:T(8,128)(2,1)S(1)}, u32[]{:S(2)}, u32[]{:S(2)}) collective-permute-start(bf16[128,1024]{1,0:T(8,128)(2,1)S(1)} %broadcast_select_fusion), channel_id=1, source_target_pairs={{0,2},{1,3},{2,0},{3,1},{4,6},{5,7},{6,4},{7,5},{8,10},{9,11},{10,... | collective-permute-start | bytes 786440 | tf_op jit(solution)/shard_map/ppermute | solution.py:470
  7.5 12.3 %collective-permute-start.2 = (bf16[128,1024]{1,0:T(8,128)(2,1)S(1)}, bf16[128,1024]{1,0:T(8,128)(2,1)S(1)}, u32[]{:S(2)}, u32[]{:S(2)}) collective-permute-start(bf16[128,1024]{1,0:T(8,128)(2,1)S(1)} %broadcast_select_fusion), channel_id=1, source_target_pairs={{0,3},{1,0},{2,1},{3,2},{4,7},{5,4},{6,5},{7,6},{8,11},{9,8},{10,9... | collective-permute-start | bytes 786440 | tf_op jit(solution)/shard_map/ppermute | solution.py:470
  11.0 21.3 %all-to-all-start = ((bf16[32,40,128]{2,1,0:T(8,128)(2,1)}), bf16[32,40,128]{2,1,0:T(8,128)(2,1)S(1)}, u32[]{:S(2)}, u32[]{:S(2)}) async-start(bf16[32,40,128]{2,1,0:T(8,128)(2,1)} %bitcast.6), calls=%async_computation | async-start | bytes 655360 | tf_op jit(solution)/shard_map/all_to_all | solution.py:456
  19.9 13.2 %copy-start.1 = (bf16[128,1024]{1,0:T(8,128)(2,1)S(1)}, bf16[128,1024]{1,0:T(8,128)(2,1)}, u32[]{:S(2)}) copy-start(bf16[128,1024]{1,0:T(8,128)(2,1)} %w_out_ref.1) | copy-start | bytes 786436
  19.9 13.2 %collective-permute-start.3 = (bf16[3,128,1024]{2,1,0:T(8,128)(2,1)S(1)}, bf16[3,128,1024]{2,1,0:T(8,128)(2,1)S(1)}, u32[]{:S(2)}, u32[]{:S(2)}) collective-permute-start(bf16[3,128,1024]{2,1,0:T(8,128)(2,1)S(1)} %shard_map.77.shares_ref), channel_id=1, source_target_pairs={{0,32},{32,0},{1,33},{33,1},{2,34},{34,2},{3,35},{35,3},{4,36},{36... | collective-permute-start | bytes 2359304 | tf_op jit(solution)/shard_map/ppermute | solution.py:474
  35.0 12.8 %all-to-all-start.1 = ((bf16[8,16,1024]{2,1,0:T(8,128)(2,1)}), bf16[8,16,1024]{2,1,0:T(8,128)(2,1)S(1)}, u32[]{:S(2)}, u32[]{:S(2)}) async-start(bf16[8,16,1024]{2,1,0:T(8,128)(2,1)} %bitcast.11), calls=%async_computation.1 | async-start | bytes 524288 | tf_op jit(solution)/shard_map/all_to_all | solution.py:37
  60.3 9.0 %collective-permute-start.4 = (bf16[128,1024]{1,0:T(8,128)(2,1)S(1)}, bf16[128,1024]{1,0:T(8,128)(2,1)S(1)}, u32[]{:S(2)}, u32[]{:S(2)}) collective-permute-start(bf16[128,1024]{1,0:T(8,128)(2,1)S(1)} %bitcast.33), channel_id=1, source_target_pairs={{0,1},{1,2},{2,3},{3,0},{4,5},{5,6},{6,7},{7,4},{8,9},{9,10},{10,1... | collective-permute-start | bytes 786440 | tf_op jit(solution)/shard_map/ppermute | solution.py:507
  60.6 8.8 %collective-permute-start.5 = (bf16[128,1024]{1,0:T(8,128)(2,1)S(1)}, bf16[128,1024]{1,0:T(8,128)(2,1)S(1)}, u32[]{:S(2)}, u32[]{:S(2)}) collective-permute-start(bf16[128,1024]{1,0:T(8,128)(2,1)S(1)} %bitcast.34), channel_id=1, source_target_pairs={{0,3},{1,0},{2,1},{3,2},{4,7},{5,4},{6,5},{7,6},{8,11},{9,8},{10,9... | collective-permute-start | bytes 786440 | tf_op jit(solution)/shard_map/ppermute | solution.py:507
  63.0 7.5 %collective-permute-start.6 = (bf16[128,1024]{1,0:T(8,128)(2,1)S(1)}, bf16[128,1024]{1,0:T(8,128)(2,1)S(1)}, u32[]{:S(2)}, u32[]{:S(2)}) collective-permute-start(bf16[128,1024]{1,0:T(8,128)(2,1)S(1)} %bitcast.35), channel_id=1, source_target_pairs={{0,2},{1,3},{2,0},{3,1},{4,6},{5,7},{6,4},{7,5},{8,10},{9,11},{10,... | collective-permute-start | bytes 786440 | tf_op jit(solution)/shard_map/ppermute | solution.py:507
  63.6 2.2 %copy-start = (bf16[2048,1024]{1,0:T(8,128)(2,1)S(1)}, bf16[2048,1024]{1,0:T(8,128)(2,1)}, u32[]{:S(2)}) copy-start(bf16[2048,1024]{1,0:T(8,128)(2,1)} %proto_ref.1) | copy-start | bytes 12582916
  69.3 4.6 %copy-start.2 = (bf16[2048,1024]{1,0:T(8,128)(2,1)}, bf16[2048,1024]{1,0:T(8,128)(2,1)S(1)}, u32[]{:S(2)}) copy-start(bf16[2048,1024]{1,0:T(8,128)(2,1)S(1)} %get-tuple-element.21.rest_4_.unit_ref) | copy-start | bytes 12582916
  137.3 12.8 %all-to-all-start.8 = ((f32[32,1,512]{2,1,0:T(1,128)}), f32[32,1,512]{2,1,0:T(1,128)S(1)}, u32[]{:S(2)}, u32[]{:S(2)}) async-start(f32[32,1,512]{2,1,0:T(1,128)} %shard_map.85), calls=%async_computation.8 | async-start | bytes 131072 | tf_op jit(solution)/shard_map/all_to_all | solution.py:518
  162.5 7.9 %collective-permute-start.7 = (bf16[4,128,2048]{2,1,0:T(8,128)(2,1)}, bf16[4,128,2048]{2,1,0:T(8,128)(2,1)S(1)}, u32[]{:S(2)}, u32[]{:S(2)}) collective-permute-start(bf16[4,128,2048]{2,1,0:T(8,128)(2,1)} %get-tuple-element.28), channel_id=1, source_target_pairs={{0,32},{32,0},{1,33},{33,1},{2,34},{34,2},{3,35},{35,3},{4,36},{36... | collective-permute-start | bytes 6291464 | tf_op jit(solution)/shard_map/ppermute | solution.py:521
  164.4 31.9 %all-to-all-start.9 = ((bf16[32,32,512]{2,1,0:T(8,128)(2,1)}), bf16[32,32,512]{2,1,0:T(8,128)(2,1)}, u32[]{:S(2)}, u32[]{:S(2)}) async-start(bf16[32,32,512]{2,1,0:T(8,128)(2,1)} %bitcast.13), calls=%async_computation.9 | async-start | bytes 2097152 | tf_op jit(solution)/shard_map/all_to_all | solution.py:37
  169.1 1.3 collective-permute-start.8
  172.0 9.1 %collective-permute-start.11 = (bf16[64,2048]{1,0:T(8,128)(2,1)S(1)}, bf16[64,2048]{1,0:T(8,128)(2,1)S(1)}, u32[]{:S(2)}, u32[]{:S(2)}) collective-permute-start(bf16[64,2048]{1,0:T(8,128)(2,1)S(1)} %get-tuple-element.36), channel_id=1, source_target_pairs={{0,64},{64,128},{128,192},{192,0},{1,65},{65,129},{129,193},{193,1... | collective-permute-start | bytes 786440 | tf_op jit(solution)/shard_map/ppermute | solution.py:530
  172.3 8.8 %collective-permute-start.12 = (bf16[64,2048]{1,0:T(8,128)(2,1)S(1)}, bf16[64,2048]{1,0:T(8,128)(2,1)S(1)}, u32[]{:S(2)}, u32[]{:S(2)}) collective-permute-start(bf16[64,2048]{1,0:T(8,128)(2,1)S(1)} %get-tuple-element.37), channel_id=1, source_target_pairs={{64,0},{128,64},{192,128},{0,192},{65,1},{129,65},{193,129},{1,193... | collective-permute-start | bytes 786440 | tf_op jit(solution)/shard_map/ppermute | solution.py:533
  178.0 20.4 %collective-permute-start.10 = (bf16[64,2048]{1,0:T(8,128)(2,1)}, bf16[64,2048]{1,0:T(8,128)(2,1)S(1)}, u32[]{:S(2)}, u32[]{:S(2)}) collective-permute-start(bf16[64,2048]{1,0:T(8,128)(2,1)} %get-tuple-element.33), channel_id=1, source_target_pairs={{0,64},{64,128},{128,192},{192,0},{1,65},{65,129},{129,193},{193,1... | collective-permute-start | bytes 786440 | tf_op jit(solution)/shard_map/ppermute | solution.py:530
  178.0 20.4 %collective-permute-start.9 = (bf16[64,2048]{1,0:T(8,128)(2,1)S(1)}, bf16[64,2048]{1,0:T(8,128)(2,1)S(1)}, u32[]{:S(2)}, u32[]{:S(2)}) collective-permute-start(bf16[64,2048]{1,0:T(8,128)(2,1)S(1)} %get-tuple-element.32), channel_id=1, source_target_pairs={{64,0},{128,64},{192,128},{0,192},{65,1},{129,65},{193,129},{1,193... | collective-permute-start | bytes 786440 | tf_op jit(solution)/shard_map/ppermute | solution.py:533
  182.0 18.0 %collective-permute-start.13 = (bf16[64,2048]{1,0:T(8,128)(2,1)}, bf16[64,2048]{1,0:T(8,128)(2,1)S(1)}, u32[]{:S(2)}, u32[]{:S(2)}) collective-permute-start(bf16[64,2048]{1,0:T(8,128)(2,1)} %get-tuple-element.38), channel_id=1, source_target_pairs={{0,64},{64,128},{128,192},{192,0},{1,65},{65,129},{129,193},{193,1... | collective-permute-start | bytes 786440 | tf_op jit(solution)/shard_map/ppermute | solution.py:530
  182.0 18.0 %collective-permute-start.14 = (bf16[64,2048]{1,0:T(8,128)(2,1)}, bf16[64,2048]{1,0:T(8,128)(2,1)S(1)}, u32[]{:S(2)}, u32[]{:S(2)}) collective-permute-start(bf16[64,2048]{1,0:T(8,128)(2,1)} %get-tuple-element.39), channel_id=1, source_target_pairs={{64,0},{128,64},{192,128},{0,192},{65,1},{129,65},{193,129},{1,193... | collective-permute-start | bytes 786440 | tf_op jit(solution)/shard_map/ppermute | solution.py:533

commit v9 on v8

--- a/solution.py
+++ b/solution.py
@@ -1,3 +1,4 @@
+import functools
 import math
 
 import jax
@@ -100,6 +101,34 @@
 
 def tiles(count):
     return [slice(j, j + TILE) for j in range(0, count, TILE)]
+
+
+def pack_kernel(y_count, states_ref, in_ref, last_ref, out_ref):
+    width = in_ref.shape[1]
+    height = out_ref.shape[2]
+    pair = jnp.concatenate([in_ref[...].astype(f32), last_ref[...].astype(f32)], axis=0)
+    row = jnp.concatenate([pair, jnp.zeros((2, height - width), f32)], axis=1)
+    foot = jnp.concatenate([row, jnp.zeros((6, height), f32)], axis=0)
+    for way in range(y_count):
+        view, start = divmod(way * height, states_ref.shape[2])
+        block = states_ref[view, :, start : start + height].astype(f32)
+        piece = jnp.concatenate([block, foot], axis=0).astype(bf16)
+        for group in range(out_ref.shape[0] // y_count):
+            out_ref[group * y_count + way] = piece
+
+
+def pack_states(states, gain_in, gain_out, z_count, y_count):
+    views, width, rows = states.shape
+    height = views * rows // y_count
+    return call(
+        functools.partial(pack_kernel, y_count),
+        (),
+        (states, gain_in.reshape(1, width), gain_out.reshape(1, width)),
+        [((z_count * y_count, width + 8, height), bf16)],
+        4,
+        10**6,
+        10**6,
+    )
 
 
 def stack_kernel(first_ref, second_ref, third_ref, out_ref):
@@ -443,22 +472,12 @@
     z_count = lax.axis_size("z")
     tall = row_count // y_count
 
-    states_t = hidden_states.reshape(row_count, local_width).T
-    gain_row = jnp.pad(jnp.concatenate([ln_in_gain, ln_out_gain]), (0, tall - 2 * local_width))
-    pieces = jnp.concatenate(
-        [
-            states_t.reshape(local_width, y_count, tall).transpose(1, 0, 2),
-            jnp.broadcast_to(gain_row[None, None], (y_count, 8, tall)),
-        ],
-        axis=1,
-    )
-    sent = jnp.broadcast_to(pieces[None], (z_count,) + pieces.shape)
-    received = lax.all_to_all(
-        sent.reshape(col_count, local_width + 8, tall), COLS, 0, 0
-    )
-    gains = received[:, local_width]
-    gain_in = gains[:, :local_width].reshape(D).astype(f32)
-    gain_out = gains[:, local_width : 2 * local_width].reshape(D).astype(f32)
+    sent = pack_states(
+        hidden_states.transpose(0, 2, 1), ln_in_gain, ln_out_gain, z_count, y_count
+    )
+    received = lax.all_to_all(sent, COLS, 0, 0)
+    gain_in = received[:, local_width, :local_width].reshape(D).astype(f32)
+    gain_out = received[:, local_width + 1, :local_width].reshape(D).astype(f32)
     inputs_t = received[:, :local_width].reshape(D, tall)
 
     core = lax.axis_index("core")
@@ -565,7 +584,11 @@
         10**8,
         10**6,
     )
-    embed_grad_t = scatter_sum(embed_terms.reshape(col_count, local_width, row_count), COLS)
+    embed_parts = lax.all_to_all(
+        embed_terms.reshape(col_count, local_width, row_count), COLS, 0, 0
+    )
+    embed_parts, proto_grad = lax.optimization_barrier((embed_parts, proto_grad))
+    embed_grad_t = jnp.sum(embed_parts.astype(f32), axis=0)
     embed_grad = embed_grad_t.T.reshape(view_count, image_rows, local_width)
     return (embed_grad, proto_grad)
 

time: 203 us -> 198 us (0.975)
    all_to_all x2 -> x1, waiting for transfers between devices: 20.9 us -> 9.27 us  [scatter_sum(): return jnp.sum(lax.all_to_all(blocks, axes, 0, 0).astype(f32), axis=0)]
    ppermute x3, waiting for transfers between devices: 0.42 us -> 6.73 us  [right(): lax.ppermute(values, 'x', [(i, (i + 1) % x_count) for i in range(x_count)])]
    all_to_all x2 -> x1, starting transfers between devices: 8.08 us -> 3.41 us  [scatter_sum(): return jnp.sum(lax.all_to_all(blocks, axes, 0, 0).astype(f32), axis=0)]
    all_to_all x1 -> x2, starting transfers between devices: 8.69 us -> 12.6 us  [the longest x1 8.69 us: body(): received = lax.all_to_all(sent, COLS, 0, 0)]
    all_to_all x1 -> x2, waiting for transfers between devices: 11.6 us -> 15.3 us  [the longest x1 11.6 us: body(): received = lax.all_to_all(sent, COLS, 0, 0)]
    unnamed x8 -> x13, local copies, waits for them, and re-layouts: 3.29 us -> 5.35 us
    pallas_call x12 -> x13, Pallas kernels: 14.7 us -> 14.6 us  [call(): pl.pallas_call(kernel, in_specs=[SMEM] * len(scalars) + [VMEM] * len(arra...]
  transfers between devices with their start and end apart: 19 -> 19, of which waited for: 8 -> 9; matrix products, arithmetic and copies ran while one was open for 3% -> 0% of each run, Pallas kernels for 6% -> 6%
where the time goes in v9:
time: 198 us; the launch traced here: 197 us
  blocking collectives  71.8 us (36%)
  waiting for transfers between devices  42.1 us (21%)
  starting transfers between devices  40.2 us (20%)
  Pallas kernels  33.2 us (17%)
  local copies, waits for them, and re-layouts  6.31 us (3%)
  other arithmetic  2.12 us (1%)
    all_to_all x2, blocking collectives, body(): masses = lax.all_to_all(proto_pass(images, base, row_parts), ROWS, 0, 0)  19.9 us
    all_to_all x1, blocking collectives, body(): masses = lax.all_to_all(masses, ROWS, 0, 0)  14.9 us
    pallas_call x13, Pallas kernels, call(): pl.pallas_call(kernel, in_specs=[SMEM] * len(scalars) + [VMEM] * len(arra...  14.6 us
    all_to_all x1, blocking collectives, body(): lax.all_to_all(image_pass(masses, base, col_count, soft_part), COLS, 0, 0)  13.3 us
    pallas_call x1, Pallas kernels, grad_pass(): pl.pallas_call(grad_kernel, grid=(protos // TILE,), in_specs=[full(images...  12.5 us
    all_to_all x1, blocking collectives, gather_all(): return lax.all_to_all(copies, axes, 0, 0)  11.8 us
    all_to_all x1, blocking collectives, body(): images = lax.all_to_all(image_pass(masses, base, col_count), COLS, 0, 0)  11.8 us
    all_to_all x1, waiting for transfers between devices, body(): received = lax.all_to_all(sent, COLS, 0, 0)  11.6 us
  transfers between devices with their start and end apart: 19, of which 9 were waited for; matrix products, arithmetic and copies ran while one was open for 0% of the time, Pallas kernels for 6%

profile of v9, /device:TPU:1, one launch (start us, length us, event | category | flops | bytes accessed | tf_op | source)
XLA Modules:
  0.0 197.0 jit_solution(6924065873239546898)
XLA Ops:
  2.7 2.2 %collective-permute-start = (bf16[128,1024]{1,0:T(8,128)(2,1)S(1)}, bf16[128,1024]{1,0:T(8,128)(2,1)S(1)}, u32[]{:S(2)}, u32[]{:S(2)}) collective-permute-start(bf16[128,1024]{1,0:T(8,128)(2,1)S(1)} %broadcast_select_fusion), channel_id=1, source_target_pairs={{0,1},{1,2},{2,3},{3,0},{4,5},{5,6},{6,7},{7,4},{8,9},{9,10},{10,1... | collective-permute-start | bytes 786440 | tf_op jit(solution)/shard_map/ppermute | solution.py:489
  4.9 2.6 %collective-permute-start.1 = (bf16[128,1024]{1,0:T(8,128)(2,1)S(1)}, bf16[128,1024]{1,0:T(8,128)(2,1)S(1)}, u32[]{:S(2)}, u32[]{:S(2)}) collective-permute-start(bf16[128,1024]{1,0:T(8,128)(2,1)S(1)} %broadcast_select_fusion), channel_id=1, source_target_pairs={{0,2},{1,3},{2,0},{3,1},{4,6},{5,7},{6,4},{7,5},{8,10},{9,11},{10,... | collective-permute-start | bytes 786440 | tf_op jit(solution)/shard_map/ppermute | solution.py:489
  11.5 8.7 %all-to-all-start = ((bf16[32,40,128]{2,1,0:T(8,128)(2,1)}), bf16[32,40,128]{2,1,0:T(8,128)(2,1)S(1)}, u32[]{:S(2)}, u32[]{:S(2)}) async-start(bf16[32,40,128]{2,1,0:T(8,128)(2,1)} %shard_map.77), calls=%async_computation | async-start | bytes 655360 | tf_op jit(solution)/shard_map/all_to_all | solution.py:478
  21.2 11.6 %all-to-all-done = bf16[32,40,128]{2,1,0:T(8,128)(2,1)S(1)} async-done(((bf16[32,40,128]{2,1,0:T(8,128)(2,1)}), bf16[32,40,128]{2,1,0:T(8,128)(2,1)S(1)}, u32[]{:S(2)}, u32[]{:S(2)}) %all-to-all-start) | async-done | bytes 327712 | tf_op jit(solution)/shard_map/all_to_all | solution.py:478
  33.6 1.9 shard_map.79
  35.5 3.4 %all-to-all-start.1 = ((bf16[8,16,1024]{2,1,0:T(8,128)(2,1)}), bf16[8,16,1024]{2,1,0:T(8,128)(2,1)S(1)}, u32[]{:S(2)}, u32[]{:S(2)}) async-start(bf16[8,16,1024]{2,1,0:T(8,128)(2,1)} %bitcast.11), calls=%async_computation.1 | async-start | bytes 524288 | tf_op jit(solution)/shard_map/all_to_all | solution.py:38
  39.0 9.3 %all-to-all-done.1 = bf16[8,16,1024]{2,1,0:T(8,128)(2,1)S(1)} async-done(((bf16[8,16,1024]{2,1,0:T(8,128)(2,1)}), bf16[8,16,1024]{2,1,0:T(8,128)(2,1)S(1)}, u32[]{:S(2)}, u32[]{:S(2)}) %all-to-all-start.1) | async-done | bytes 262176 | tf_op jit(solution)/shard_map/all_to_all | solution.py:38
  49.0 11.8 %all_to_all.50 = bf16[8,16,1024]{2,1,0:T(8,128)(2,1)S(1)} all-to-all(bf16[8,16,1024]{2,1,0:T(8,128)(2,1)S(1)} %broadcast_in_dim.2), channel_id=1, replica_groups=mesh['x'=4,'core'=2,'z'=8,'y'=4] {'z'}, dimensions={0} | all-to-all | bytes 524288 | tf_op jit(solution)/shard_map/all_to_all | solution.py:30
  61.1 2.4 %collective-permute-start.5 = (bf16[128,1024]{1,0:T(8,128)(2,1)S(1)}, bf16[128,1024]{1,0:T(8,128)(2,1)S(1)}, u32[]{:S(2)}, u32[]{:S(2)}) collective-permute-start(bf16[128,1024]{1,0:T(8,128)(2,1)S(1)} %bitcast.28), channel_id=1, source_target_pairs={{0,3},{1,0},{2,1},{3,2},{4,7},{5,4},{6,5},{7,6},{8,11},{9,8},{10,9... | collective-permute-start | bytes 786440 | tf_op jit(solution)/shard_map/ppermute | solution.py:526
  64.0 2.2 %copy-done = bf16[2048,1024]{1,0:T(8,128)(2,1)S(1)} copy-done((bf16[2048,1024]{1,0:T(8,128)(2,1)S(1)}, bf16[2048,1024]{1,0:T(8,128)(2,1)}, u32[]{:S(2)}) %copy-start) | copy-done | bytes 4194328
  66.2 3.5 %shard_map.80 = (bf16[2048,1024]{1,0:T(8,128)(2,1)S(1)}, f32[1,2048]{1,0:T(1,128)S(1)}, bf16[4,128,2048]{2,1,0:T(8,128)(2,1)}) custom-call(s32[1]{0:T(128)} %bitcast.8.core_ref, bf16[2048,1024]{1,0:T(8,128)(2,1)S(1)} %copy-done), custom_call_target="tpu_custom_call" | custom-call | flops 12582912 | bytes 10485760 | tf_op jit(solution)/shard_map/pallas_call | solution.py:59
  71.0 3.4 %shard_map.81 = (bf16[512,2048]{1,0:T(8,128)(2,1)S(1)}, f32[8,2,2048]{2,1,0:T(2,128)S(1)}, f32[1,512]{1,0:T(1,128)S(1)}, bf16[512,1024]{1,0:T(8,128)(2,1)S(1)}) custom-call(s32[4]{0:T(128)S(1)} %pad_add_fusion.place_ref, bf16[128,1024]{1,0:T(8,128)(2,1)S(1)} %bitcast.30, bf16[128,1024]{1,0:T(8,128)(2,1)S(1)} %collective-permute-done.4.rest_1_, ...), custom_call_target="tpu_custom_call" | custom-call | flops 2147483648 | bytes 8388608 | tf_op jit(solution)/shard_map/pallas_call | solution.py:59
  74.4 14.9 %all_to_all.51.mass_ref = f32[8,2,2048]{2,1,0:T(2,128)S(1)} all-to-all(f32[8,2,2048]{2,1,0:T(2,128)S(1)} %get-tuple-element.24), channel_id=1, replica_groups=mesh['x'=4,'core'=2,'z'=8,'y'=4] {'x','core'}, dimensions={0} | all-to-all | bytes 262144 | tf_op jit(solution)/shard_map/all_to_all | solution.py:533
  89.9 13.3 %all_to_all.52.image_ref.soft_ref = f32[32,2,512]{2,1,0:T(2,128)S(1)} all-to-all(f32[32,2,512]{2,1,0:T(2,128)S(1)} %shard_map.82), channel_id=1, replica_groups=mesh['x'=4,'core'=2,'z'=8,'y'=4] {'z','y'}, dimensions={0} | all-to-all | bytes 262144 | tf_op jit(solution)/shard_map/all_to_all | solution.py:534
  103.8 10.0 %all_to_all.53.mass_ref = f32[8,2,2048]{2,1,0:T(2,128)S(1)} all-to-all(f32[8,2,2048]{2,1,0:T(2,128)S(1)} %shard_map.83), channel_id=1, replica_groups=mesh['x'=4,'core'=2,'z'=8,'y'=4] {'x','core'}, dimensions={0} | all-to-all | bytes 262144 | tf_op jit(solution)/shard_map/all_to_all | solution.py:536
  114.3 11.8 %all_to_all.54.image_ref = f32[32,1,512]{2,1,0:T(1,128)S(1)} all-to-all(f32[32,1,512]{2,1,0:T(1,128)S(1)} %shard_map.84), channel_id=1, replica_groups=mesh['x'=4,'core'=2,'z'=8,'y'=4] {'z','y'}, dimensions={0} | all-to-all | bytes 131072 | tf_op jit(solution)/shard_map/all_to_all | solution.py:537
  126.7 9.9 %all_to_all.55.mass_ref = f32[8,2,2048]{2,1,0:T(2,128)S(1)} all-to-all(f32[8,2,2048]{2,1,0:T(2,128)S(1)} %shard_map.85), channel_id=1, replica_groups=mesh['x'=4,'core'=2,'z'=8,'y'=4] {'x','core'}, dimensions={0} | all-to-all | bytes 262144 | tf_op jit(solution)/shard_map/all_to_all | solution.py:536
  136.6 1.2 shard_map.86
  137.8 3.9 %all-to-all-start.8 = ((f32[32,1,512]{2,1,0:T(1,128)}), f32[32,1,512]{2,1,0:T(1,128)S(1)}, u32[]{:S(2)}, u32[]{:S(2)}) async-start(f32[32,1,512]{2,1,0:T(1,128)} %shard_map.86), calls=%async_computation.8 | async-start | bytes 131072 | tf_op jit(solution)/shard_map/all_to_all | solution.py:537
  142.1 8.5 %all-to-all-done.8.image_ref = f32[32,1,512]{2,1,0:T(1,128)S(1)} async-done(((f32[32,1,512]{2,1,0:T(1,128)}), f32[32,1,512]{2,1,0:T(1,128)S(1)}, u32[]{:S(2)}, u32[]{:S(2)}) %all-to-all-start.8) | async-done | bytes 65568 | tf_op jit(solution)/shard_map/all_to_all | solution.py:537
  150.6 12.5 %shard_map.88 = (f32[1,2048]{1,0:T(1,128)S(1)}, bf16[4,128,2048]{2,1,0:T(8,128)(2,1)}, f32[4,128,2048]{2,1,0:T(8,128)}, bf16[1024,512]{1,0:T(8,128)(2,1)}) custom-call(f32[32,1,512]{2,1,0:T(1,128)S(1)} %all-to-all-done.8.image_ref, f32[32,2,512]{2,1,0:T(2,128)S(1)} %all_to_all.52.image_ref.soft_ref, f32[8,2,2048]{2,1,0:T(2,128)S(1)} %all_to_all.55.mass_ref, ...), custom_call_target="tpu_custom_call" | custom-call | flops 4294967296 | bytes 10485760 | tf_op jit(solution)/shard_map/pallas_call | solution.py:346
  163.1 1.9 collective-permute-start.7
  165.0 3.9 %all-to-all-start.9 = ((bf16[32,32,512]{2,1,0:T(8,128)(2,1)}), bf16[32,32,512]{2,1,0:T(8,128)(2,1)S(1)}, u32[]{:S(2)}, u32[]{:S(2)}) async-start(bf16[32,32,512]{2,1,0:T(8,128)(2,1)} %bitcast.13), calls=%async_computation.9 | async-start | bytes 2097152 | tf_op jit(solution)/shard_map/all_to_all | solution.py:587
  170.2 1.6 shard_map.91
  172.2 2.4 %collective-permute-start.12 = (bf16[64,2048]{1,0:T(8,128)(2,1)S(1)}, bf16[64,2048]{1,0:T(8,128)(2,1)S(1)}, u32[]{:S(2)}, u32[]{:S(2)}) collective-permute-start(bf16[64,2048]{1,0:T(8,128)(2,1)S(1)} %get-tuple-element.39), channel_id=1, source_target_pairs={{64,0},{128,64},{192,128},{0,192},{65,1},{129,65},{193,129},{1,193... | collective-permute-start | bytes 786440 | tf_op jit(solution)/shard_map/ppermute | solution.py:552
  174.6 2.8 %shard_map.89 = (bf16[64,2048]{1,0:T(8,128)(2,1)S(1)}, bf16[64,2048]{1,0:T(8,128)(2,1)S(1)}, f32[64,2048]{1,0:T(8,128)S(1)}, f32[64,2048]{1,0:T(8,128)S(1)}) custom-call(s32[2]{0:T(128)S(1)} %pad_add_fusion.1.place_ref, f32[4,128,2048]{2,1,0:T(8,128)} %get-tuple-element.29.refs_0_.refs_3_, bf16[4,128,2048]{2,1,0:T(8,128)(2,1)S(1)} %collective-permute-done.7.refs_1_.refs_4_, ...), custom_call_target="tpu_custom_call" | custom-call | flops 1000000000 | bytes 2621440 | tf_op jit(solution)/shard_map/pallas_call | solution.py:448
  177.6 2.7 %collective-permute-start.9 = (bf16[64,2048]{1,0:T(8,128)(2,1)S(1)}, bf16[64,2048]{1,0:T(8,128)(2,1)S(1)}, u32[]{:S(2)}, u32[]{:S(2)}) collective-permute-start(bf16[64,2048]{1,0:T(8,128)(2,1)S(1)} %get-tuple-element.34), channel_id=1, source_target_pairs={{64,0},{128,64},{192,128},{0,192},{65,1},{129,65},{193,129},{1,193... | collective-permute-start | bytes 786440 | tf_op jit(solution)/shard_map/ppermute | solution.py:552
  181.1 2.7 %collective-permute-start.14 = (bf16[64,2048]{1,0:T(8,128)(2,1)S(1)}, bf16[64,2048]{1,0:T(8,128)(2,1)S(1)}, u32[]{:S(2)}, u32[]{:S(2)}) collective-permute-start(bf16[64,2048]{1,0:T(8,128)(2,1)S(1)} %get-tuple-element.41), channel_id=1, source_target_pairs={{64,0},{128,64},{192,128},{0,192},{65,1},{129,65},{193,129},{1,193... | collective-permute-start | bytes 786440 | tf_op jit(solution)/shard_map/ppermute | solution.py:552
  183.7 2.1 %collective-permute-done.10.refs_7_ = bf16[64,2048]{1,0:T(8,128)(2,1)S(1)} collective-permute-done((bf16[64,2048]{1,0:T(8,128)(2,1)S(1)}, bf16[64,2048]{1,0:T(8,128)(2,1)S(1)}, u32[]{:S(2)}, u32[]{:S(2)}) %collective-permute-start.10) | collective-permute-done | bytes 262176 | tf_op jit(solution)/shard_map/ppermute | solution.py:549
  185.9 1.7 shard_map.90.sum_ref
  187.5 4.0 %collective-permute-done.13.lower_ref = bf16[64,2048]{1,0:T(8,128)(2,1)S(1)} collective-permute-done((bf16[64,2048]{1,0:T(8,128)(2,1)S(1)}, bf16[64,2048]{1,0:T(8,128)(2,1)S(1)}, u32[]{:S(2)}, u32[]{:S(2)}) %collective-permute-start.13) | collective-permute-done | bytes 262176 | tf_op jit(solution)/shard_map/ppermute | solution.py:549
  192.6 3.7 %all-to-all-done.9 = bf16[32,32,512]{2,1,0:T(8,128)(2,1)S(1)} async-done(((bf16[32,32,512]{2,1,0:T(8,128)(2,1)}), bf16[32,32,512]{2,1,0:T(8,128)(2,1)S(1)}, u32[]{:S(2)}, u32[]{:S(2)}) %all-to-all-start.9) | async-done | bytes 1048608 | tf_op jit(solution)/shard_map/all_to_all | solution.py:587
  (63 shorter events, 17.6 us)
Async XLA Ops:
  2.7 17.4 %collective-permute-start = (bf16[128,1024]{1,0:T(8,128)(2,1)S(1)}, bf16[128,1024]{1,0:T(8,128)(2,1)S(1)}, u32[]{:S(2)}, u32[]{:S(2)}) collective-permute-start(bf16[128,1024]{1,0:T(8,128)(2,1)S(1)} %broadcast_select_fusion), channel_id=1, source_target_pairs={{0,1},{1,2},{2,3},{3,0},{4,5},{5,6},{6,7},{7,4},{8,9},{9,10},{10,1... | collective-permute-start | bytes 786440 | tf_op jit(solution)/shard_map/ppermute | solution.py:489
  4.9 15.2 %collective-permute-start.1 = (bf16[128,1024]{1,0:T(8,128)(2,1)S(1)}, bf16[128,1024]{1,0:T(8,128)(2,1)S(1)}, u32[]{:S(2)}, u32[]{:S(2)}) collective-permute-start(bf16[128,1024]{1,0:T(8,128)(2,1)S(1)} %broadcast_select_fusion), channel_id=1, source_target_pairs={{0,2},{1,3},{2,0},{3,1},{4,6},{5,7},{6,4},{7,5},{8,10},{9,11},{10,... | collective-permute-start | bytes 786440 | tf_op jit(solution)/shard_map/ppermute | solution.py:489
  7.5 12.6 %collective-permute-start.2 = (bf16[128,1024]{1,0:T(8,128)(2,1)S(1)}, bf16[128,1024]{1,0:T(8,128)(2,1)S(1)}, u32[]{:S(2)}, u32[]{:S(2)}) collective-permute-start(bf16[128,1024]{1,0:T(8,128)(2,1)S(1)} %broadcast_select_fusion), channel_id=1, source_target_pairs={{0,3},{1,0},{2,1},{3,2},{4,7},{5,4},{6,5},{7,6},{8,11},{9,8},{10,9... | collective-permute-start | bytes 786440 | tf_op jit(solution)/shard_map/ppermute | solution.py:489
  8.6 0.8 copy-start.2
  9.4 0.7 copy-start.3
  10.0 0.7 copy-start.4
  11.5 21.3 %all-to-all-start = ((bf16[32,40,128]{2,1,0:T(8,128)(2,1)}), bf16[32,40,128]{2,1,0:T(8,128)(2,1)S(1)}, u32[]{:S(2)}, u32[]{:S(2)}) async-start(bf16[32,40,128]{2,1,0:T(8,128)(2,1)} %shard_map.77), calls=%async_computation | async-start | bytes 655360 | tf_op jit(solution)/shard_map/all_to_all | solution.py:478
  20.2 13.3 %copy-start.1 = (bf16[128,1024]{1,0:T(8,128)(2,1)S(1)}, bf16[128,1024]{1,0:T(8,128)(2,1)}, u32[]{:S(2)}) copy-start(bf16[128,1024]{1,0:T(8,128)(2,1)} %w_out_ref.1) | copy-start | bytes 786436
  20.3 13.3 %collective-permute-start.3 = (bf16[3,128,1024]{2,1,0:T(8,128)(2,1)S(1)}, bf16[3,128,1024]{2,1,0:T(8,128)(2,1)S(1)}, u32[]{:S(2)}, u32[]{:S(2)}) collective-permute-start(bf16[3,128,1024]{2,1,0:T(8,128)(2,1)S(1)} %shard_map.78.shares_ref), channel_id=1, source_target_pairs={{0,32},{32,0},{1,33},{33,1},{2,34},{34,2},{3,35},{35,3},{4,36},{36... | collective-permute-start | bytes 2359304 | tf_op jit(solution)/shard_map/ppermute | solution.py:493
  35.5 12.8 %all-to-all-start.1 = ((bf16[8,16,1024]{2,1,0:T(8,128)(2,1)}), bf16[8,16,1024]{2,1,0:T(8,128)(2,1)S(1)}, u32[]{:S(2)}, u32[]{:S(2)}) async-start(bf16[8,16,1024]{2,1,0:T(8,128)(2,1)} %bitcast.11), calls=%async_computation.1 | async-start | bytes 524288 | tf_op jit(solution)/shard_map/all_to_all | solution.py:38
  60.8 9.0 %collective-permute-start.4 = (bf16[128,1024]{1,0:T(8,128)(2,1)S(1)}, bf16[128,1024]{1,0:T(8,128)(2,1)S(1)}, u32[]{:S(2)}, u32[]{:S(2)}) collective-permute-start(bf16[128,1024]{1,0:T(8,128)(2,1)S(1)} %bitcast.27), channel_id=1, source_target_pairs={{0,1},{1,2},{2,3},{3,0},{4,5},{5,6},{6,7},{7,4},{8,9},{9,10},{10,1... | collective-permute-start | bytes 786440 | tf_op jit(solution)/shard_map/ppermute | solution.py:526
  61.1 8.8 %collective-permute-start.5 = (bf16[128,1024]{1,0:T(8,128)(2,1)S(1)}, bf16[128,1024]{1,0:T(8,128)(2,1)S(1)}, u32[]{:S(2)}, u32[]{:S(2)}) collective-permute-start(bf16[128,1024]{1,0:T(8,128)(2,1)S(1)} %bitcast.28), channel_id=1, source_target_pairs={{0,3},{1,0},{2,1},{3,2},{4,7},{5,4},{6,5},{7,6},{8,11},{9,8},{10,9... | collective-permute-start | bytes 786440 | tf_op jit(solution)/shard_map/ppermute | solution.py:526
  63.5 7.5 %collective-permute-start.6 = (bf16[128,1024]{1,0:T(8,128)(2,1)S(1)}, bf16[128,1024]{1,0:T(8,128)(2,1)S(1)}, u32[]{:S(2)}, u32[]{:S(2)}) collective-permute-start(bf16[128,1024]{1,0:T(8,128)(2,1)S(1)} %bitcast.29), channel_id=1, source_target_pairs={{0,2},{1,3},{2,0},{3,1},{4,6},{5,7},{6,4},{7,5},{8,10},{9,11},{10,... | collective-permute-start | bytes 786440 | tf_op jit(solution)/shard_map/ppermute | solution.py:526
  64.0 2.2 %copy-start = (bf16[2048,1024]{1,0:T(8,128)(2,1)S(1)}, bf16[2048,1024]{1,0:T(8,128)(2,1)}, u32[]{:S(2)}) copy-start(bf16[2048,1024]{1,0:T(8,128)(2,1)} %proto_ref.1) | copy-start | bytes 12582916
  69.7 4.7 %copy-start.5 = (bf16[2048,1024]{1,0:T(8,128)(2,1)}, bf16[2048,1024]{1,0:T(8,128)(2,1)S(1)}, u32[]{:S(2)}) copy-start(bf16[2048,1024]{1,0:T(8,128)(2,1)S(1)} %get-tuple-element.23.rest_4_.unit_ref) | copy-start | bytes 12582916
  137.8 12.8 %all-to-all-start.8 = ((f32[32,1,512]{2,1,0:T(1,128)}), f32[32,1,512]{2,1,0:T(1,128)S(1)}, u32[]{:S(2)}, u32[]{:S(2)}) async-start(f32[32,1,512]{2,1,0:T(1,128)} %shard_map.86), calls=%async_computation.8 | async-start | bytes 131072 | tf_op jit(solution)/shard_map/all_to_all | solution.py:537
  163.1 7.1 %collective-permute-start.7 = (bf16[4,128,2048]{2,1,0:T(8,128)(2,1)}, bf16[4,128,2048]{2,1,0:T(8,128)(2,1)S(1)}, u32[]{:S(2)}, u32[]{:S(2)}) collective-permute-start(bf16[4,128,2048]{2,1,0:T(8,128)(2,1)} %get-tuple-element.30), channel_id=1, source_target_pairs={{0,32},{32,0},{1,33},{33,1},{2,34},{34,2},{3,35},{35,3},{4,36},{36... | collective-permute-start | bytes 6291464 | tf_op jit(solution)/shard_map/ppermute | solution.py:540
  165.0 31.2 %all-to-all-start.9 = ((bf16[32,32,512]{2,1,0:T(8,128)(2,1)}), bf16[32,32,512]{2,1,0:T(8,128)(2,1)S(1)}, u32[]{:S(2)}, u32[]{:S(2)}) async-start(bf16[32,32,512]{2,1,0:T(8,128)(2,1)} %bitcast.13), calls=%async_computation.9 | async-start | bytes 2097152 | tf_op jit(solution)/shard_map/all_to_all | solution.py:587
  169.0 1.3 collective-permute-start.8
  171.8 9.0 %collective-permute-start.11 = (bf16[64,2048]{1,0:T(8,128)(2,1)S(1)}, bf16[64,2048]{1,0:T(8,128)(2,1)S(1)}, u32[]{:S(2)}, u32[]{:S(2)}) collective-permute-start(bf16[64,2048]{1,0:T(8,128)(2,1)S(1)} %get-tuple-element.38), channel_id=1, source_target_pairs={{0,64},{64,128},{128,192},{192,0},{1,65},{65,129},{129,193},{193,1... | collective-permute-start | bytes 786440 | tf_op jit(solution)/shard_map/ppermute | solution.py:549
  172.2 8.7 %collective-permute-start.12 = (bf16[64,2048]{1,0:T(8,128)(2,1)S(1)}, bf16[64,2048]{1,0:T(8,128)(2,1)S(1)}, u32[]{:S(2)}, u32[]{:S(2)}) collective-permute-start(bf16[64,2048]{1,0:T(8,128)(2,1)S(1)} %get-tuple-element.39), channel_id=1, source_target_pairs={{64,0},{128,64},{192,128},{0,192},{65,1},{129,65},{193,129},{1,193... | collective-permute-start | bytes 786440 | tf_op jit(solution)/shard_map/ppermute | solution.py:552
  177.5 8.4 %collective-permute-start.10 = (bf16[64,2048]{1,0:T(8,128)(2,1)S(1)}, bf16[64,2048]{1,0:T(8,128)(2,1)S(1)}, u32[]{:S(2)}, u32[]{:S(2)}) collective-permute-start(bf16[64,2048]{1,0:T(8,128)(2,1)S(1)} %get-tuple-element.35), channel_id=1, source_target_pairs={{0,64},{64,128},{128,192},{192,0},{1,65},{65,129},{129,193},{193,1... | collective-permute-start | bytes 786440 | tf_op jit(solution)/shard_map/ppermute | solution.py:549
  177.6 8.3 %collective-permute-start.9 = (bf16[64,2048]{1,0:T(8,128)(2,1)S(1)}, bf16[64,2048]{1,0:T(8,128)(2,1)S(1)}, u32[]{:S(2)}, u32[]{:S(2)}) collective-permute-start(bf16[64,2048]{1,0:T(8,128)(2,1)S(1)} %get-tuple-element.34), channel_id=1, source_target_pairs={{64,0},{128,64},{192,128},{0,192},{65,1},{129,65},{193,129},{1,193... | collective-permute-start | bytes 786440 | tf_op jit(solution)/shard_map/ppermute | solution.py:552
  181.0 10.5 %collective-permute-start.13 = (bf16[64,2048]{1,0:T(8,128)(2,1)S(1)}, bf16[64,2048]{1,0:T(8,128)(2,1)S(1)}, u32[]{:S(2)}, u32[]{:S(2)}) collective-permute-start(bf16[64,2048]{1,0:T(8,128)(2,1)S(1)} %get-tuple-element.40), channel_id=1, source_target_pairs={{0,64},{64,128},{128,192},{192,0},{1,65},{65,129},{129,193},{193,1... | collective-permute-start | bytes 786440 | tf_op jit(solution)/shard_map/ppermute | solution.py:549
  181.1 10.4 %collective-permute-start.14 = (bf16[64,2048]{1,0:T(8,128)(2,1)S(1)}, bf16[64,2048]{1,0:T(8,128)(2,1)S(1)}, u32[]{:S(2)}, u32[]{:S(2)}) collective-permute-start(bf16[64,2048]{1,0:T(8,128)(2,1)S(1)} %get-tuple-element.41), channel_id=1, source_target_pairs={{64,0},{128,64},{192,128},{0,192},{65,1},{129,65},{193,129},{1,193... | collective-permute-start | bytes 786440 | tf_op jit(solution)/shard_map/ppermute | solution.py:552

commit v10 on v9

--- a/solution.py
+++ b/solution.py
@@ -120,15 +120,20 @@
 def pack_states(states, gain_in, gain_out, z_count, y_count):
     views, width, rows = states.shape
     height = views * rows // y_count
-    return call(
+    shape = (z_count * y_count, width + 8, height)
+    arrays = (states, gain_in.reshape(1, width), gain_out.reshape(1, width))
+
+    def full(shape):
+        return pl.BlockSpec(shape, lambda i: (0,) * len(shape))
+
+    return pl.pallas_call(
         functools.partial(pack_kernel, y_count),
-        (),
-        (states, gain_in.reshape(1, width), gain_out.reshape(1, width)),
-        [((z_count * y_count, width + 8, height), bf16)],
-        4,
-        10**6,
-        10**6,
-    )
+        grid=(1,),
+        in_specs=[full(values.shape) for values in arrays],
+        out_specs=full(shape),
+        out_shape=jax.ShapeDtypeStruct(shape, bf16),
+        compiler_params=pltpu.CompilerParams(vmem_limit_bytes=4 * 1024 * 1024),
+    )(*[keep_hbm(values) for values in arrays])
 
 
 def stack_kernel(first_ref, second_ref, third_ref, out_ref):
@@ -263,7 +268,7 @@
     for part in tiles(protos):
         scale = 1.0 / jnp.sum(mass_ref[:, :, part], axis=0)
         total = total + fold_lanes(base_ref[:, part].astype(f32) * view_rows(scale, rows))
-    row = jnp.concatenate([as_row(total)] + [ref[...] for ref in extra], axis=0)
+    row = jnp.concatenate([as_row(total)] + [ref[...] for ref in extra], axis=1)
     out_ref[...] = jnp.broadcast_to(row[None], out_ref.shape)
 
 
@@ -273,7 +278,7 @@
         image_kernel,
         (),
         (masses, base, *extra),
-        [((copies, 1 + len(extra), rows), f32)],
+        [((copies, 1, (1 + len(extra)) * rows), f32)],
         8,
         3 * rows * protos,
         2 * rows * protos,
@@ -281,7 +286,7 @@
 
 
 def proto_kernel(image_ref, base_ref, mass_ref):
-    column = as_column(1.0 / jnp.sum(image_ref[...], axis=0)[:1])
+    column = as_column(1.0 / jnp.sum(image_ref[:, :, : base_ref.shape[0]], axis=0))
     for part in tiles(base_ref.shape[1]):
         mass = view_sums(base_ref[:, part].astype(f32) * spread_lanes(column, TILE))
         mass_ref[:, :, part] = jnp.broadcast_to(mass[None], (mass_ref.shape[0],) + mass.shape)
@@ -300,66 +305,72 @@
     )
 
 
+WIDE = 2 * TILE
+
+
 def grad_kernel(
-    image_ref, soft_ref, mass_ref, unit_ref, embed_ref, embed_t_ref,
-    radial_ref, away_ref, stay_ref, terms_ref, code_column, prob_column, total,
+    image_ref, soft_ref, mass_ref, unit_hbm, embed_ref, embed_t_ref,
+    radial_ref, away_hbm, stay_hbm, terms_ref,
+    unit_ref, away_ref, stay_ref, load_sems, away_sems, stay_sems,
 ):
-    step = pl.program_id(0)
-
-    @pl.when(step == 0)
-    def _():
-        code_column[...] = as_column(factor / jnp.sum(image_ref[...], axis=0)[:1])
-        prob_column[...] = as_column(factor / jnp.sum(soft_ref[...], axis=0)[1:2])
-        total[...] = jnp.zeros_like(total)
-
-    scores = lax.dot_general(embed_ref[...], unit_ref[...], NT, preferred_element_type=f32)
-    rows = scores.shape[0]
+    rows, protos = embed_ref.shape[0], unit_ref.shape[0]
+    loads = []
+    for n, part in enumerate(tiles(protos)):
+        load = pltpu.make_async_copy(unit_hbm.at[part], unit_ref.at[part], load_sems.at[n])
+        load.start()
+        loads.append(load)
+    code_column = spread_lanes(
+        as_column(factor / jnp.sum(image_ref[:, :, :rows], axis=0)), WIDE
+    )
+    prob_column = spread_lanes(
+        as_column(factor / jnp.sum(soft_ref[:, :, rows:], axis=0)), WIDE
+    )
     half = rows // 2
-    soft = jnp.exp(scores * (1.0 / soft_temp))
-    scale = 1.0 / jnp.sum(mass_ref[...], axis=0)
-    codes = soft * soft * view_rows(scale, rows) * spread_lanes(code_column[...], TILE)
-    swapped = jnp.concatenate([codes[half:], codes[:half]], axis=0)
-    grad = (soft * spread_lanes(prob_column[...], TILE) - swapped).astype(bf16)
-    radial_ref[...] = jnp.sum(grad.astype(f32) * scores, axis=0, keepdims=True)
-    away = jnp.dot(embed_t_ref[0], grad, preferred_element_type=f32).astype(bf16)
-    away_ref[...] = away.reshape(away_ref.shape)
-    stay = jnp.dot(embed_t_ref[1], grad, preferred_element_type=f32)
-    stay_ref[...] = stay.reshape(stay_ref.shape)
-    total[...] += jnp.dot(grad, unit_ref[...], preferred_element_type=f32)
-
-    @pl.when(step == pl.num_programs(0) - 1)
-    def _():
-        for start in range(0, D, TILE):
-            part = slice(start, start + TILE)
-            terms_ref[part, :] = total[:, part].T.astype(bf16)
+    stores = []
+    total = None
+    for n in range(protos // WIDE):
+        part = slice(n * WIDE, (n + 1) * WIDE)
+        for load in loads[n * (WIDE // TILE) : (n + 1) * (WIDE // TILE)]:
+            load.wait()
+        unit = unit_ref[part, :]
+        scores = lax.dot_general(embed_ref[...], unit, NT, preferred_element_type=f32)
+        soft = jnp.exp(scores * (1.0 / soft_temp))
+        scale = 1.0 / jnp.sum(mass_ref[:, :, part], axis=0)
+        codes = soft * soft * view_rows(scale, rows) * code_column
+        swapped = jnp.concatenate([codes[half:], codes[:half]], axis=0)
+        grad = (soft * prob_column - swapped).astype(bf16)
+        radial_ref[:, part] = jnp.sum(grad.astype(f32) * scores, axis=0, keepdims=True)
+        shape = away_ref.shape[:2] + (WIDE,)
+        away = jnp.dot(embed_t_ref[0], grad, preferred_element_type=f32).astype(bf16)
+        away_ref[:, :, part] = away.reshape(shape)
+        stay = jnp.dot(embed_t_ref[1], grad, preferred_element_type=f32)
+        stay_ref[:, :, part] = stay.reshape(shape)
+        for ref, hbm, sems in (
+            (away_ref, away_hbm, away_sems),
+            (stay_ref, stay_hbm, stay_sems),
+        ):
+            store = pltpu.make_async_copy(ref.at[:, :, part], hbm.at[:, :, part], sems.at[n])
+            store.start()
+            stores.append(store)
+        term = jnp.dot(grad, unit, preferred_element_type=f32)
+        total = term if total is None else total + term
+    for start in range(0, D, TILE):
+        part = slice(start, start + TILE)
+        terms_ref[part, :] = total[:, part].T.astype(bf16)
+    for store in stores:
+        store.wait()
 
 
 def grad_pass(images, softs, masses, unit, embed, embed_t):
     rows, protos = embed.shape[0], unit.shape[0]
     depth = embed_t.shape[1]
     blocks = depth // LANES
-
-    def full(values):
-        return pl.BlockSpec(values.shape, lambda i: (0,) * values.ndim)
-
-    halves = pl.BlockSpec((blocks, LANES, TILE), lambda i: (0, 0, i))
+    steps = protos // WIDE
+    anywhere = pl.BlockSpec(memory_space=pl.ANY)
     return pl.pallas_call(
         grad_kernel,
-        grid=(protos // TILE,),
-        in_specs=[
-            full(images),
-            full(softs),
-            pl.BlockSpec((masses.shape[0], 2, TILE), lambda i: (0, 0, i)),
-            pl.BlockSpec((TILE, D), lambda i: (i, 0)),
-            VMEM,
-            VMEM,
-        ],
-        out_specs=[
-            pl.BlockSpec((1, TILE), lambda i: (0, i)),
-            halves,
-            halves,
-            pl.BlockSpec((D, rows), lambda i: (0, 0)),
-        ],
+        in_specs=[VMEM, VMEM, VMEM, anywhere, VMEM, VMEM],
+        out_specs=[VMEM, anywhere, anywhere, VMEM],
         out_shape=[
             jax.ShapeDtypeStruct((1, protos), f32),
             pltpu.HBM((blocks, LANES, protos), bf16),
@@ -367,13 +378,14 @@
             jax.ShapeDtypeStruct((D, rows), bf16),
         ],
         scratch_shapes=[
-            pltpu.VMEM((rows, LANES), f32),
-            pltpu.VMEM((rows, LANES), f32),
-            pltpu.VMEM((rows, D), f32),
+            pltpu.VMEM((protos, D), bf16),
+            pltpu.VMEM((blocks, LANES, protos), bf16),
+            pltpu.VMEM((blocks, LANES, protos), f32),
+            pltpu.SemaphoreType.DMA((protos // TILE,)),
+            pltpu.SemaphoreType.DMA((steps,)),
+            pltpu.SemaphoreType.DMA((steps,)),
         ],
-        compiler_params=pltpu.CompilerParams(
-            dimension_semantics=("arbitrary",), vmem_limit_bytes=24 * 1024 * 1024
-        ),
+        compiler_params=pltpu.CompilerParams(vmem_limit_bytes=40 * 1024 * 1024),
         cost_estimate=pl.CostEstimate(
             flops=8 * depth * rows * protos,
             bytes_accessed=10 * depth * protos,

time: 198 us -> 195 us (0.985)
  local copies, waits for them, and re-layouts: 6.31 us -> 4.24 us
    unnamed x13 -> x7, local copies, waits for them, and re-layouts: 5.35 us -> 3.28 us
    pallas_call x13 -> x12, Pallas kernels: 14.6 us -> 13.9 us  [call(): pl.pallas_call(kernel, in_specs=[SMEM] * len(scalars) + [VMEM] * len(arra...]
    pallas_call x1 -> x2, Pallas kernels: 12.5 us -> 12 us  [the longest x1 10.4 us: grad_pass(): pl.pallas_call(grad_kernel, in_specs=[VMEM, VMEM, VMEM, anywhere, VMEM, V...]
  transfers between devices with their start and end apart: 19 -> 19, of which waited for: 9 -> 10; matrix products, arithmetic and copies ran while one was open for 0% -> 0% of each run, Pallas kernels for 6% -> 7%
where the time goes in v10:
time: 195 us; the launch traced here: 194 us
  blocking collectives  71.8 us (37%)
  waiting for transfers between devices  42.2 us (22%)
  starting transfers between devices  40.3 us (21%)
  Pallas kernels  31.9 us (16%)
  local copies, waits for them, and re-layouts  4.24 us (2%)
  other arithmetic  2.12 us (1%)
    all_to_all x2, blocking collectives, body(): masses = lax.all_to_all(proto_pass(images, base, row_parts), ROWS, 0, 0)  19.9 us
    all_to_all x1, blocking collectives, body(): masses = lax.all_to_all(masses, ROWS, 0, 0)  14.9 us
    pallas_call x12, Pallas kernels, call(): pl.pallas_call(kernel, in_specs=[SMEM] * len(scalars) + [VMEM] * len(arra...  13.9 us
    all_to_all x1, blocking collectives, body(): lax.all_to_all(image_pass(masses, base, col_count, soft_part), COLS, 0, 0)  13.3 us
    all_to_all x1, blocking collectives, gather_all(): return lax.all_to_all(copies, axes, 0, 0)  11.8 us
    all_to_all x1, blocking collectives, body(): images = lax.all_to_all(image_pass(masses, base, col_count), COLS, 0, 0)  11.8 us
    all_to_all x1, waiting for transfers between devices, body(): received = lax.all_to_all(sent, COLS, 0, 0)  10.9 us
    pallas_call x1, Pallas kernels, grad_pass(): pl.pallas_call(grad_kernel, in_specs=[VMEM, VMEM, VMEM, anywhere, VMEM, V...  10.4 us
  transfers between devices with their start and end apart: 19, of which 10 were waited for; matrix products, arithmetic and copies ran while one was open for 0% of the time, Pallas kernels for 7%

profile of v10, /device:TPU:1, one launch (start us, length us, event | category | flops | bytes accessed | tf_op | source)
XLA Modules:
  0.0 193.8 jit_solution(16730238494094798903)
XLA Ops:
  2.7 2.2 %collective-permute-start = (bf16[128,1024]{1,0:T(8,128)(2,1)S(1)}, bf16[128,1024]{1,0:T(8,128)(2,1)S(1)}, u32[]{:S(2)}, u32[]{:S(2)}) collective-permute-start(bf16[128,1024]{1,0:T(8,128)(2,1)S(1)} %broadcast_select_fusion), channel_id=1, source_target_pairs={{0,1},{1,2},{2,3},{3,0},{4,5},{5,6},{6,7},{7,4},{8,9},{9,10},{10,1... | collective-permute-start | bytes 786440 | tf_op jit(solution)/shard_map/ppermute | solution.py:501
  4.9 2.6 %collective-permute-start.1 = (bf16[128,1024]{1,0:T(8,128)(2,1)S(1)}, bf16[128,1024]{1,0:T(8,128)(2,1)S(1)}, u32[]{:S(2)}, u32[]{:S(2)}) collective-permute-start(bf16[128,1024]{1,0:T(8,128)(2,1)S(1)} %broadcast_select_fusion), channel_id=1, source_target_pairs={{0,2},{1,3},{2,0},{3,1},{4,6},{5,7},{6,4},{7,5},{8,10},{9,11},{10,... | collective-permute-start | bytes 786440 | tf_op jit(solution)/shard_map/ppermute | solution.py:501
  8.6 1.5 shard_map.77
  10.2 8.7 %all-to-all-start = ((bf16[32,40,128]{2,1,0:T(8,128)(2,1)}), bf16[32,40,128]{2,1,0:T(8,128)(2,1)S(1)}, u32[]{:S(2)}, u32[]{:S(2)}) async-start(bf16[32,40,128]{2,1,0:T(8,128)(2,1)} %shard_map.77), calls=%async_computation | async-start | bytes 655360 | tf_op jit(solution)/shard_map/all_to_all | solution.py:490
  20.6 10.9 %all-to-all-done = bf16[32,40,128]{2,1,0:T(8,128)(2,1)S(1)} async-done(((bf16[32,40,128]{2,1,0:T(8,128)(2,1)}), bf16[32,40,128]{2,1,0:T(8,128)(2,1)S(1)}, u32[]{:S(2)}, u32[]{:S(2)}) %all-to-all-start) | async-done | bytes 327712 | tf_op jit(solution)/shard_map/all_to_all | solution.py:490
  32.3 1.9 shard_map.79
  34.2 3.4 %all-to-all-start.1 = ((bf16[8,16,1024]{2,1,0:T(8,128)(2,1)}), bf16[8,16,1024]{2,1,0:T(8,128)(2,1)S(1)}, u32[]{:S(2)}, u32[]{:S(2)}) async-start(bf16[8,16,1024]{2,1,0:T(8,128)(2,1)} %bitcast.11), calls=%async_computation.1 | async-start | bytes 524288 | tf_op jit(solution)/shard_map/all_to_all | solution.py:38
  37.7 9.3 %all-to-all-done.1 = bf16[8,16,1024]{2,1,0:T(8,128)(2,1)S(1)} async-done(((bf16[8,16,1024]{2,1,0:T(8,128)(2,1)}), bf16[8,16,1024]{2,1,0:T(8,128)(2,1)S(1)}, u32[]{:S(2)}, u32[]{:S(2)}) %all-to-all-start.1) | async-done | bytes 262176 | tf_op jit(solution)/shard_map/all_to_all | solution.py:38
  47.7 11.8 %all_to_all.50 = bf16[8,16,1024]{2,1,0:T(8,128)(2,1)S(1)} all-to-all(bf16[8,16,1024]{2,1,0:T(8,128)(2,1)S(1)} %broadcast_in_dim.2), channel_id=1, replica_groups=mesh['x'=4,'core'=2,'z'=8,'y'=4] {'z'}, dimensions={0} | all-to-all | bytes 524288 | tf_op jit(solution)/shard_map/all_to_all | solution.py:30
  59.8 2.4 %collective-permute-start.5 = (bf16[128,1024]{1,0:T(8,128)(2,1)S(1)}, bf16[128,1024]{1,0:T(8,128)(2,1)S(1)}, u32[]{:S(2)}, u32[]{:S(2)}) collective-permute-start(bf16[128,1024]{1,0:T(8,128)(2,1)S(1)} %bitcast.28), channel_id=1, source_target_pairs={{0,3},{1,0},{2,1},{3,2},{4,7},{5,4},{6,5},{7,6},{8,11},{9,8},{10,9... | collective-permute-start | bytes 786440 | tf_op jit(solution)/shard_map/ppermute | solution.py:538
  62.7 2.2 %copy-done = bf16[2048,1024]{1,0:T(8,128)(2,1)S(1)} copy-done((bf16[2048,1024]{1,0:T(8,128)(2,1)S(1)}, bf16[2048,1024]{1,0:T(8,128)(2,1)}, u32[]{:S(2)}) %copy-start) | copy-done | bytes 4194328
  64.9 3.5 %shard_map.80 = (bf16[2048,1024]{1,0:T(8,128)(2,1)S(1)}, f32[1,2048]{1,0:T(1,128)S(1)}, bf16[4,128,2048]{2,1,0:T(8,128)(2,1)}) custom-call(s32[1]{0:T(128)} %bitcast.8.core_ref, bf16[2048,1024]{1,0:T(8,128)(2,1)S(1)} %copy-done), custom_call_target="tpu_custom_call" | custom-call | flops 12582912 | bytes 10485760 | tf_op jit(solution)/shard_map/pallas_call | solution.py:59
  69.7 3.4 %shard_map.81 = (bf16[512,2048]{1,0:T(8,128)(2,1)S(1)}, f32[8,2,2048]{2,1,0:T(2,128)S(1)}, f32[1,512]{1,0:T(1,128)S(1)}, bf16[512,1024]{1,0:T(8,128)(2,1)S(1)}) custom-call(s32[4]{0:T(128)S(1)} %pad_add_fusion.place_ref, bf16[128,1024]{1,0:T(8,128)(2,1)S(1)} %bitcast.30, bf16[128,1024]{1,0:T(8,128)(2,1)S(1)} %collective-permute-done.4.rest_1_, ...), custom_call_target="tpu_custom_call" | custom-call | flops 2147483648 | bytes 8388608 | tf_op jit(solution)/shard_map/pallas_call | solution.py:59
  73.1 14.9 %all_to_all.51.mass_ref = f32[8,2,2048]{2,1,0:T(2,128)S(1)} all-to-all(f32[8,2,2048]{2,1,0:T(2,128)S(1)} %get-tuple-element.24), channel_id=1, replica_groups=mesh['x'=4,'core'=2,'z'=8,'y'=4] {'x','core'}, dimensions={0} | all-to-all | bytes 262144 | tf_op jit(solution)/shard_map/all_to_all | solution.py:545
  88.6 13.3 %all_to_all.52.image_ref.soft_ref = f32[32,1,1024]{2,1,0:T(1,128)S(1)} all-to-all(f32[32,1,1024]{2,1,0:T(1,128)S(1)} %shard_map.82), channel_id=1, replica_groups=mesh['x'=4,'core'=2,'z'=8,'y'=4] {'z','y'}, dimensions={0} | all-to-all | bytes 262144 | tf_op jit(solution)/shard_map/all_to_all | solution.py:546
  102.5 10.0 %all_to_all.53.mass_ref = f32[8,2,2048]{2,1,0:T(2,128)S(1)} all-to-all(f32[8,2,2048]{2,1,0:T(2,128)S(1)} %shard_map.83), channel_id=1, replica_groups=mesh['x'=4,'core'=2,'z'=8,'y'=4] {'x','core'}, dimensions={0} | all-to-all | bytes 262144 | tf_op jit(solution)/shard_map/all_to_all | solution.py:548
  113.0 11.8 %all_to_all.54.image_ref = f32[32,1,512]{2,1,0:T(1,128)S(1)} all-to-all(f32[32,1,512]{2,1,0:T(1,128)S(1)} %shard_map.84), channel_id=1, replica_groups=mesh['x'=4,'core'=2,'z'=8,'y'=4] {'z','y'}, dimensions={0} | all-to-all | bytes 131072 | tf_op jit(solution)/shard_map/all_to_all | solution.py:549
  125.4 9.9 %all_to_all.55.mass_ref = f32[8,2,2048]{2,1,0:T(2,128)S(1)} all-to-all(f32[8,2,2048]{2,1,0:T(2,128)S(1)} %shard_map.85), channel_id=1, replica_groups=mesh['x'=4,'core'=2,'z'=8,'y'=4] {'x','core'}, dimensions={0} | all-to-all | bytes 262144 | tf_op jit(solution)/shard_map/all_to_all | solution.py:548
  136.5 3.9 %all-to-all-start.8 = ((f32[32,1,512]{2,1,0:T(1,128)}), f32[32,1,512]{2,1,0:T(1,128)S(1)}, u32[]{:S(2)}, u32[]{:S(2)}) async-start(f32[32,1,512]{2,1,0:T(1,128)} %shard_map.86), calls=%async_computation.8 | async-start | bytes 131072 | tf_op jit(solution)/shard_map/all_to_all | solution.py:549
  140.8 8.5 %all-to-all-done.8.image_ref = f32[32,1,512]{2,1,0:T(1,128)S(1)} async-done(((f32[32,1,512]{2,1,0:T(1,128)}), f32[32,1,512]{2,1,0:T(1,128)S(1)}, u32[]{:S(2)}, u32[]{:S(2)}) %all-to-all-start.8) | async-done | bytes 65568 | tf_op jit(solution)/shard_map/all_to_all | solution.py:549
  149.3 10.4 %shard_map.88 = (f32[1,2048]{1,0:T(1,128)S(1)}, bf16[4,128,2048]{2,1,0:T(8,128)(2,1)}, f32[4,128,2048]{2,1,0:T(8,128)}, bf16[1024,512]{1,0:T(8,128)(2,1)}) custom-call(f32[32,1,512]{2,1,0:T(1,128)S(1)} %all-to-all-done.8.image_ref, f32[32,1,1024]{2,1,0:T(1,128)S(1)} %all_to_all.52.image_ref.soft_ref, f32[8,2,2048]{2,1,0:T(2,128)S(1)} %all_to_all.55.mass_ref, ...), custom_call_target="tpu_custom_call" | custom-call | flops 4294967296 | bytes 10485760 | tf_op jit(solution)/shard_map/pallas_call | solution.py:370
  159.7 2.0 %collective-permute-start.7 = (bf16[4,128,2048]{2,1,0:T(8,128)(2,1)}, bf16[4,128,2048]{2,1,0:T(8,128)(2,1)S(1)}, u32[]{:S(2)}, u32[]{:S(2)}) collective-permute-start(bf16[4,128,2048]{2,1,0:T(8,128)(2,1)} %get-tuple-element.30), channel_id=1, source_target_pairs={{0,32},{32,0},{1,33},{33,1},{2,34},{34,2},{3,35},{35,3},{4,36},{36... | collective-permute-start | bytes 6291464 | tf_op jit(solution)/shard_map/ppermute | solution.py:552
  161.7 3.9 %all-to-all-start.9 = ((bf16[32,32,512]{2,1,0:T(8,128)(2,1)}), bf16[32,32,512]{2,1,0:T(8,128)(2,1)S(1)}, u32[]{:S(2)}, u32[]{:S(2)}) async-start(bf16[32,32,512]{2,1,0:T(8,128)(2,1)} %bitcast.13), calls=%async_computation.9 | async-start | bytes 2097152 | tf_op jit(solution)/shard_map/all_to_all | solution.py:599
  167.2 1.6 shard_map.91
  169.1 2.4 %collective-permute-start.12 = (bf16[64,2048]{1,0:T(8,128)(2,1)S(1)}, bf16[64,2048]{1,0:T(8,128)(2,1)S(1)}, u32[]{:S(2)}, u32[]{:S(2)}) collective-permute-start(bf16[64,2048]{1,0:T(8,128)(2,1)S(1)} %get-tuple-element.39), channel_id=1, source_target_pairs={{64,0},{128,64},{192,128},{0,192},{65,1},{129,65},{193,129},{1,193... | collective-permute-start | bytes 786440 | tf_op jit(solution)/shard_map/ppermute | solution.py:564
  171.6 2.8 %shard_map.89 = (bf16[64,2048]{1,0:T(8,128)(2,1)S(1)}, bf16[64,2048]{1,0:T(8,128)(2,1)S(1)}, f32[64,2048]{1,0:T(8,128)S(1)}, f32[64,2048]{1,0:T(8,128)S(1)}) custom-call(s32[2]{0:T(128)S(1)} %pad_add_fusion.1.place_ref, f32[4,128,2048]{2,1,0:T(8,128)} %get-tuple-element.29.refs_0_.refs_3_, bf16[4,128,2048]{2,1,0:T(8,128)(2,1)S(1)} %collective-permute-done.7.refs_1_.refs_4_, ...), custom_call_target="tpu_custom_call" | custom-call | flops 1000000000 | bytes 2621440 | tf_op jit(solution)/shard_map/pallas_call | solution.py:460
  174.5 2.7 %collective-permute-start.9 = (bf16[64,2048]{1,0:T(8,128)(2,1)S(1)}, bf16[64,2048]{1,0:T(8,128)(2,1)S(1)}, u32[]{:S(2)}, u32[]{:S(2)}) collective-permute-start(bf16[64,2048]{1,0:T(8,128)(2,1)S(1)} %get-tuple-element.34), channel_id=1, source_target_pairs={{64,0},{128,64},{192,128},{0,192},{65,1},{129,65},{193,129},{1,193... | collective-permute-start | bytes 786440 | tf_op jit(solution)/shard_map/ppermute | solution.py:564
  178.0 2.7 %collective-permute-start.14 = (bf16[64,2048]{1,0:T(8,128)(2,1)S(1)}, bf16[64,2048]{1,0:T(8,128)(2,1)S(1)}, u32[]{:S(2)}, u32[]{:S(2)}) collective-permute-start(bf16[64,2048]{1,0:T(8,128)(2,1)S(1)} %get-tuple-element.41), channel_id=1, source_target_pairs={{64,0},{128,64},{192,128},{0,192},{65,1},{129,65},{193,129},{1,193... | collective-permute-start | bytes 786440 | tf_op jit(solution)/shard_map/ppermute | solution.py:564
  180.7 2.1 %collective-permute-done.10.refs_7_ = bf16[64,2048]{1,0:T(8,128)(2,1)S(1)} collective-permute-done((bf16[64,2048]{1,0:T(8,128)(2,1)S(1)}, bf16[64,2048]{1,0:T(8,128)(2,1)S(1)}, u32[]{:S(2)}, u32[]{:S(2)}) %collective-permute-start.10) | collective-permute-done | bytes 262176 | tf_op jit(solution)/shard_map/ppermute | solution.py:561
  182.8 1.7 shard_map.90.sum_ref
  184.5 4.0 %collective-permute-done.13.lower_ref = bf16[64,2048]{1,0:T(8,128)(2,1)S(1)} collective-permute-done((bf16[64,2048]{1,0:T(8,128)(2,1)S(1)}, bf16[64,2048]{1,0:T(8,128)(2,1)S(1)}, u32[]{:S(2)}, u32[]{:S(2)}) %collective-permute-start.13) | collective-permute-done | bytes 262176 | tf_op jit(solution)/shard_map/ppermute | solution.py:561
  189.5 3.5 %all-to-all-done.9 = bf16[32,32,512]{2,1,0:T(8,128)(2,1)S(1)} async-done(((bf16[32,32,512]{2,1,0:T(8,128)(2,1)}), bf16[32,32,512]{2,1,0:T(8,128)(2,1)S(1)}, u32[]{:S(2)}, u32[]{:S(2)}) %all-to-all-start.9) | async-done | bytes 1048608 | tf_op jit(solution)/shard_map/all_to_all | solution.py:599
  (57 shorter events, 16.9 us)
Async XLA Ops:
  2.7 16.1 %collective-permute-start = (bf16[128,1024]{1,0:T(8,128)(2,1)S(1)}, bf16[128,1024]{1,0:T(8,128)(2,1)S(1)}, u32[]{:S(2)}, u32[]{:S(2)}) collective-permute-start(bf16[128,1024]{1,0:T(8,128)(2,1)S(1)} %broadcast_select_fusion), channel_id=1, source_target_pairs={{0,1},{1,2},{2,3},{3,0},{4,5},{5,6},{6,7},{7,4},{8,9},{9,10},{10,1... | collective-permute-start | bytes 786440 | tf_op jit(solution)/shard_map/ppermute | solution.py:501
  4.9 14.9 %collective-permute-start.1 = (bf16[128,1024]{1,0:T(8,128)(2,1)S(1)}, bf16[128,1024]{1,0:T(8,128)(2,1)S(1)}, u32[]{:S(2)}, u32[]{:S(2)}) collective-permute-start(bf16[128,1024]{1,0:T(8,128)(2,1)S(1)} %broadcast_select_fusion), channel_id=1, source_target_pairs={{0,2},{1,3},{2,0},{3,1},{4,6},{5,7},{6,4},{7,5},{8,10},{9,11},{10,... | collective-permute-start | bytes 786440 | tf_op jit(solution)/shard_map/ppermute | solution.py:501
  7.5 12.3 %collective-permute-start.2 = (bf16[128,1024]{1,0:T(8,128)(2,1)S(1)}, bf16[128,1024]{1,0:T(8,128)(2,1)S(1)}, u32[]{:S(2)}, u32[]{:S(2)}) collective-permute-start(bf16[128,1024]{1,0:T(8,128)(2,1)S(1)} %broadcast_select_fusion), channel_id=1, source_target_pairs={{0,3},{1,0},{2,1},{3,2},{4,7},{5,4},{6,5},{7,6},{8,11},{9,8},{10,9... | collective-permute-start | bytes 786440 | tf_op jit(solution)/shard_map/ppermute | solution.py:501
  10.2 21.3 %all-to-all-start = ((bf16[32,40,128]{2,1,0:T(8,128)(2,1)}), bf16[32,40,128]{2,1,0:T(8,128)(2,1)S(1)}, u32[]{:S(2)}, u32[]{:S(2)}) async-start(bf16[32,40,128]{2,1,0:T(8,128)(2,1)} %shard_map.77), calls=%async_computation | async-start | bytes 655360 | tf_op jit(solution)/shard_map/all_to_all | solution.py:490
  19.9 12.4 %copy-start.1 = (bf16[128,1024]{1,0:T(8,128)(2,1)S(1)}, bf16[128,1024]{1,0:T(8,128)(2,1)}, u32[]{:S(2)}) copy-start(bf16[128,1024]{1,0:T(8,128)(2,1)} %w_out_ref.1) | copy-start | bytes 786436
  19.9 12.3 %collective-permute-start.3 = (bf16[3,128,1024]{2,1,0:T(8,128)(2,1)S(1)}, bf16[3,128,1024]{2,1,0:T(8,128)(2,1)S(1)}, u32[]{:S(2)}, u32[]{:S(2)}) collective-permute-start(bf16[3,128,1024]{2,1,0:T(8,128)(2,1)S(1)} %shard_map.78.shares_ref), channel_id=1, source_target_pairs={{0,32},{32,0},{1,33},{33,1},{2,34},{34,2},{3,35},{35,3},{4,36},{36... | collective-permute-start | bytes 2359304 | tf_op jit(solution)/shard_map/ppermute | solution.py:505
  34.2 12.8 %all-to-all-start.1 = ((bf16[8,16,1024]{2,1,0:T(8,128)(2,1)}), bf16[8,16,1024]{2,1,0:T(8,128)(2,1)S(1)}, u32[]{:S(2)}, u32[]{:S(2)}) async-start(bf16[8,16,1024]{2,1,0:T(8,128)(2,1)} %bitcast.11), calls=%async_computation.1 | async-start | bytes 524288 | tf_op jit(solution)/shard_map/all_to_all | solution.py:38
  59.5 9.0 %collective-permute-start.4 = (bf16[128,1024]{1,0:T(8,128)(2,1)S(1)}, bf16[128,1024]{1,0:T(8,128)(2,1)S(1)}, u32[]{:S(2)}, u32[]{:S(2)}) collective-permute-start(bf16[128,1024]{1,0:T(8,128)(2,1)S(1)} %bitcast.27), channel_id=1, source_target_pairs={{0,1},{1,2},{2,3},{3,0},{4,5},{5,6},{6,7},{7,4},{8,9},{9,10},{10,1... | collective-permute-start | bytes 786440 | tf_op jit(solution)/shard_map/ppermute | solution.py:538
  59.8 8.8 %collective-permute-start.5 = (bf16[128,1024]{1,0:T(8,128)(2,1)S(1)}, bf16[128,1024]{1,0:T(8,128)(2,1)S(1)}, u32[]{:S(2)}, u32[]{:S(2)}) collective-permute-start(bf16[128,1024]{1,0:T(8,128)(2,1)S(1)} %bitcast.28), channel_id=1, source_target_pairs={{0,3},{1,0},{2,1},{3,2},{4,7},{5,4},{6,5},{7,6},{8,11},{9,8},{10,9... | collective-permute-start | bytes 786440 | tf_op jit(solution)/shard_map/ppermute | solution.py:538
  62.2 7.5 %collective-permute-start.6 = (bf16[128,1024]{1,0:T(8,128)(2,1)S(1)}, bf16[128,1024]{1,0:T(8,128)(2,1)S(1)}, u32[]{:S(2)}, u32[]{:S(2)}) collective-permute-start(bf16[128,1024]{1,0:T(8,128)(2,1)S(1)} %bitcast.29), channel_id=1, source_target_pairs={{0,2},{1,3},{2,0},{3,1},{4,6},{5,7},{6,4},{7,5},{8,10},{9,11},{10,... | collective-permute-start | bytes 786440 | tf_op jit(solution)/shard_map/ppermute | solution.py:538
  62.7 2.2 %copy-start = (bf16[2048,1024]{1,0:T(8,128)(2,1)S(1)}, bf16[2048,1024]{1,0:T(8,128)(2,1)}, u32[]{:S(2)}) copy-start(bf16[2048,1024]{1,0:T(8,128)(2,1)} %proto_ref.1) | copy-start | bytes 12582916
  68.4 4.7 %copy-start.2 = (bf16[2048,1024]{1,0:T(8,128)(2,1)}, bf16[2048,1024]{1,0:T(8,128)(2,1)S(1)}, u32[]{:S(2)}) copy-start(bf16[2048,1024]{1,0:T(8,128)(2,1)S(1)} %get-tuple-element.23.rest_4_.unit_hbm) | copy-start | bytes 12582916
  136.5 12.8 %all-to-all-start.8 = ((f32[32,1,512]{2,1,0:T(1,128)}), f32[32,1,512]{2,1,0:T(1,128)S(1)}, u32[]{:S(2)}, u32[]{:S(2)}) async-start(f32[32,1,512]{2,1,0:T(1,128)} %shard_map.86), calls=%async_computation.8 | async-start | bytes 131072 | tf_op jit(solution)/shard_map/all_to_all | solution.py:549
  159.7 7.4 %collective-permute-start.7 = (bf16[4,128,2048]{2,1,0:T(8,128)(2,1)}, bf16[4,128,2048]{2,1,0:T(8,128)(2,1)S(1)}, u32[]{:S(2)}, u32[]{:S(2)}) collective-permute-start(bf16[4,128,2048]{2,1,0:T(8,128)(2,1)} %get-tuple-element.30), channel_id=1, source_target_pairs={{0,32},{32,0},{1,33},{33,1},{2,34},{34,2},{3,35},{35,3},{4,36},{36... | collective-permute-start | bytes 6291464 | tf_op jit(solution)/shard_map/ppermute | solution.py:552
  161.7 31.2 %all-to-all-start.9 = ((bf16[32,32,512]{2,1,0:T(8,128)(2,1)}), bf16[32,32,512]{2,1,0:T(8,128)(2,1)S(1)}, u32[]{:S(2)}, u32[]{:S(2)}) async-start(bf16[32,32,512]{2,1,0:T(8,128)(2,1)} %bitcast.13), calls=%async_computation.9 | async-start | bytes 2097152 | tf_op jit(solution)/shard_map/all_to_all | solution.py:599
  165.7 1.5 collective-permute-start.8
  168.8 9.0 %collective-permute-start.11 = (bf16[64,2048]{1,0:T(8,128)(2,1)S(1)}, bf16[64,2048]{1,0:T(8,128)(2,1)S(1)}, u32[]{:S(2)}, u32[]{:S(2)}) collective-permute-start(bf16[64,2048]{1,0:T(8,128)(2,1)S(1)} %get-tuple-element.38), channel_id=1, source_target_pairs={{0,64},{64,128},{128,192},{192,0},{1,65},{65,129},{129,193},{193,1... | collective-permute-start | bytes 786440 | tf_op jit(solution)/shard_map/ppermute | solution.py:561
  169.1 8.7 %collective-permute-start.12 = (bf16[64,2048]{1,0:T(8,128)(2,1)S(1)}, bf16[64,2048]{1,0:T(8,128)(2,1)S(1)}, u32[]{:S(2)}, u32[]{:S(2)}) collective-permute-start(bf16[64,2048]{1,0:T(8,128)(2,1)S(1)} %get-tuple-element.39), channel_id=1, source_target_pairs={{64,0},{128,64},{192,128},{0,192},{65,1},{129,65},{193,129},{1,193... | collective-permute-start | bytes 786440 | tf_op jit(solution)/shard_map/ppermute | solution.py:564
  174.4 8.4 %collective-permute-start.10 = (bf16[64,2048]{1,0:T(8,128)(2,1)S(1)}, bf16[64,2048]{1,0:T(8,128)(2,1)S(1)}, u32[]{:S(2)}, u32[]{:S(2)}) collective-permute-start(bf16[64,2048]{1,0:T(8,128)(2,1)S(1)} %get-tuple-element.35), channel_id=1, source_target_pairs={{0,64},{64,128},{128,192},{192,0},{1,65},{65,129},{129,193},{193,1... | collective-permute-start | bytes 786440 | tf_op jit(solution)/shard_map/ppermute | solution.py:561
  174.5 8.3 %collective-permute-start.9 = (bf16[64,2048]{1,0:T(8,128)(2,1)S(1)}, bf16[64,2048]{1,0:T(8,128)(2,1)S(1)}, u32[]{:S(2)}, u32[]{:S(2)}) collective-permute-start(bf16[64,2048]{1,0:T(8,128)(2,1)S(1)} %get-tuple-element.34), channel_id=1, source_target_pairs={{64,0},{128,64},{192,128},{0,192},{65,1},{129,65},{193,129},{1,193... | collective-permute-start | bytes 786440 | tf_op jit(solution)/shard_map/ppermute | solution.py:564
  177.9 10.5 %collective-permute-start.13 = (bf16[64,2048]{1,0:T(8,128)(2,1)S(1)}, bf16[64,2048]{1,0:T(8,128)(2,1)S(1)}, u32[]{:S(2)}, u32[]{:S(2)}) collective-permute-start(bf16[64,2048]{1,0:T(8,128)(2,1)S(1)} %get-tuple-element.40), channel_id=1, source_target_pairs={{0,64},{64,128},{128,192},{192,0},{1,65},{65,129},{129,193},{193,1... | collective-permute-start | bytes 786440 | tf_op jit(solution)/shard_map/ppermute | solution.py:561
  178.0 10.4 %collective-permute-start.14 = (bf16[64,2048]{1,0:T(8,128)(2,1)S(1)}, bf16[64,2048]{1,0:T(8,128)(2,1)S(1)}, u32[]{:S(2)}, u32[]{:S(2)}) collective-permute-start(bf16[64,2048]{1,0:T(8,128)(2,1)S(1)} %get-tuple-element.41), channel_id=1, source_target_pairs={{64,0},{128,64},{192,128},{0,192},{65,1},{129,65},{193,129},{1,193... | collective-permute-start | bytes 786440 | tf_op jit(solution)/shard_map/ppermute | solution.py:564

commit v11 on v10

--- a/solution.py
+++ b/solution.py
@@ -156,19 +156,23 @@
             enter, leave = w_in_ref[...], w_out_ref[...]
         else:
             one, other = shares_ref[step - 1], others_ref[step - 1]
-            enter, leave = jnp.where(even, one, other), jnp.where(even, other, one)
-        wide = lax.dot_general(normed, enter, NT, preferred_element_type=f32)
+            enter, stacked = jnp.where(even, one, other), jnp.where(even, other, one)
+            width = stacked.shape[1]
+            leave = jnp.concatenate(
+                [stacked[j : j + width] for j in range(0, stacked.shape[0], width)], axis=1
+            )
+        wide = jnp.dot(normed, enter, preferred_element_type=f32)
         hidden = (0.5 * wide * (1.0 + lax.erf(wide * math.sqrt(0.5)))).astype(bf16)
         total = total + jnp.dot(hidden, leave, preferred_element_type=f32)
     out_ref[...] = total.astype(bf16)
 
 
-def feed_forward(core, normed, w_in_t, w_out, shares, others):
+def feed_forward(core, normed, w_in, w_out, shares, others):
     rows = normed.shape[0]
     return call(
         ffn_kernel,
         (core.reshape(1),),
-        (normed, w_in_t, w_out, shares, others),
+        (normed, w_in, w_out, shares, others),
         [((rows, D), bf16)],
         8,
         4 * rows * D * 4 * w_out.shape[0],
@@ -243,24 +247,6 @@
     )
 
 
-def turn_kernel(core_ref, embed_ref, turned_ref):
-    even = core_ref[0] == 0
-    for block in range(D // (2 * LANES)):
-        start = 2 * block * LANES
-        low = embed_ref[:, start : start + LANES].astype(f32)
-        high = embed_ref[:, start + LANES : start + 2 * LANES].astype(f32)
-        rows = slice(block * LANES, (block + 1) * LANES)
-        turned_ref[0, rows, :] = jnp.where(even, high, low).T.astype(bf16)
-        turned_ref[1, rows, :] = jnp.where(even, low, high).T.astype(bf16)
-
-
-def turn(core, embed):
-    rows = embed.shape[0]
-    return call(
-        turn_kernel, (core.reshape(1),), (embed,), [((2, D // 2, rows), bf16)], 6, 10**9, 4 * embed.size
-    )
-
-
 def image_kernel(mass_ref, base_ref, *rest):
     *extra, out_ref = rest
     rows, protos = base_ref.shape
@@ -309,9 +295,9 @@
 
 
 def grad_kernel(
-    image_ref, soft_ref, mass_ref, unit_hbm, embed_ref, embed_t_ref,
+    core_ref, image_ref, soft_ref, mass_ref, unit_hbm, embed_ref,
     radial_ref, away_hbm, stay_hbm, terms_ref,
-    unit_ref, away_ref, stay_ref, load_sems, away_sems, stay_sems,
+    unit_ref, away_ref, stay_ref, embed_t_ref, load_sems, away_sems, stay_sems,
 ):
     rows, protos = embed_ref.shape[0], unit_ref.shape[0]
     loads = []
@@ -319,6 +305,14 @@
         load = pltpu.make_async_copy(unit_hbm.at[part], unit_ref.at[part], load_sems.at[n])
         load.start()
         loads.append(load)
+    even = core_ref[0] == 0
+    for block in range(D // (2 * LANES)):
+        start = 2 * block * LANES
+        low = embed_ref[:, start : start + LANES].astype(f32)
+        high = embed_ref[:, start + LANES : start + 2 * LANES].astype(f32)
+        place = slice(block * LANES, (block + 1) * LANES)
+        embed_t_ref[0, place, :] = jnp.where(even, high, low).T.astype(bf16)
+        embed_t_ref[1, place, :] = jnp.where(even, low, high).T.astype(bf16)
     code_column = spread_lanes(
         as_column(factor / jnp.sum(image_ref[:, :, :rows], axis=0)), WIDE
     )
@@ -361,15 +355,15 @@
         store.wait()
 
 
-def grad_pass(images, softs, masses, unit, embed, embed_t):
+def grad_pass(core, images, softs, masses, unit, embed):
     rows, protos = embed.shape[0], unit.shape[0]
-    depth = embed_t.shape[1]
+    depth = D // 2
     blocks = depth // LANES
     steps = protos // WIDE
     anywhere = pl.BlockSpec(memory_space=pl.ANY)
     return pl.pallas_call(
         grad_kernel,
-        in_specs=[VMEM, VMEM, VMEM, anywhere, VMEM, VMEM],
+        in_specs=[SMEM, VMEM, VMEM, VMEM, anywhere, VMEM],
         out_specs=[VMEM, anywhere, anywhere, VMEM],
         out_shape=[
             jax.ShapeDtypeStruct((1, protos), f32),
@@ -381,6 +375,7 @@
             pltpu.VMEM((protos, D), bf16),
             pltpu.VMEM((blocks, LANES, protos), bf16),
             pltpu.VMEM((blocks, LANES, protos), f32),
+            pltpu.VMEM((2, depth, rows), bf16),
             pltpu.SemaphoreType.DMA((protos // TILE,)),
             pltpu.SemaphoreType.DMA((steps,)),
             pltpu.SemaphoreType.DMA((steps,)),
@@ -391,7 +386,7 @@
             bytes_accessed=10 * depth * protos,
             transcendentals=rows * protos,
         ),
-    )(images, softs, masses, keep_hbm(unit), embed, embed_t)
+    )(core.reshape(1), images, softs, masses, keep_hbm(unit), embed)
 
 
 def pair_rows(refs, rows, part):
@@ -494,8 +489,9 @@
 
     core = lax.axis_index("core")
     swap = [(0, 1), (1, 0)]
-    w_in_t = w_in.T
-    share = jnp.where(core == 0, w_in_t, w_out)
+    width = w_in.shape[1]
+    stacked = w_out.reshape(width, D // width, width).transpose(1, 0, 2).reshape(D, width)
+    share = jnp.where(core == 0, w_in, stacked)
     shares = stack_shares(
         [
             lax.ppermute(share, "y", [(i, (i + step) % y_count) for i in range(y_count)])
@@ -510,7 +506,7 @@
     normed_t = (
         (inputs_f - center[None, :]) * lax.rsqrt(spread + norm_eps)[None, :] * gain_in[:, None]
     ).astype(bf16)
-    block_part = feed_forward(core, normed_t.T, w_in_t, w_out, shares, others)
+    block_part = feed_forward(core, normed_t.T, w_in, w_out, shares, others)
     block = scatter_sum(block_part.reshape(z_count, row_block, D), "z")
     picked = (
         jnp.arange(tall)[None, :]
@@ -541,14 +537,13 @@
     places = jnp.stack([(y_index + y_count - step) % y_count for step in (0,) + steps])
     parts = [own_rows] + [rows_in[step] for step in steps]
     base, masses, soft_part, embed = score_pass(places, parts, unit, row_parts)
-    embed_t = turn(core, embed)
     masses = lax.all_to_all(masses, ROWS, 0, 0)
     softs = images = lax.all_to_all(image_pass(masses, base, col_count, soft_part), COLS, 0, 0)
     for repeat in range(1, SINK_ITERS):
         masses = lax.all_to_all(proto_pass(images, base, row_parts), ROWS, 0, 0)
         images = lax.all_to_all(image_pass(masses, base, col_count), COLS, 0, 0)
 
-    radial, away, stay, embed_terms = grad_pass(images, softs, masses, unit, embed, embed_t)
+    radial, away, stay, embed_terms = grad_pass(core, images, softs, masses, unit, embed)
     arrived = lax.ppermute(away, "core", swap)
     parts = (stay, arrived, turned)
     lines = (radial, lax.ppermute(radial, "core", swap), proto_len)

time: 195 us -> 193 us (0.990)
  blocking collectives: 71.8 us -> 85.9 us
  waiting for transfers between devices: 42.2 us -> 29.5 us
    all_to_all x1 -> x2, blocking collectives: 11.8 us -> 23.6 us  [body(): images = lax.all_to_all(image_pass(masses, base, col_count), COLS, 0, 0)]
    all_to_all x1 -> x0, waiting for transfers between devices: 8.54 us -> none  [body(): images = lax.all_to_all(image_pass(masses, base, col_count), COLS, 0, 0)]
    all_to_all x1 -> x0, starting transfers between devices: 3.86 us -> none  [body(): images = lax.all_to_all(image_pass(masses, base, col_count), COLS, 0, 0)]
    all_to_all x1, waiting for transfers between devices: 10.9 us -> 7.9 us  [body(): received = lax.all_to_all(sent, COLS, 0, 0)]
    all_to_all x1, blocking collectives: 14.9 us -> 17.6 us  [body(): masses = lax.all_to_all(masses, ROWS, 0, 0)]
    ppermute x1, starting transfers between devices: 0.68 us -> 2.81 us  [body(): others = lax.ppermute(shares, 'core', swap)]
    pallas_call x12 -> x11, Pallas kernels: 13.9 us -> 12.7 us  [call(): pl.pallas_call(kernel, in_specs=[SMEM] * len(scalars) + [VMEM] * len(arra...]
  transfers between devices with their start and end apart: 19 -> 18, of which waited for: 10 -> 8; matrix products, arithmetic and copies ran while one was open for 0% -> 0% of each run, Pallas kernels for 7% -> 6%
where the time goes in v11:
time: 193 us; the launch traced here: 192 us
  blocking collectives  85.9 us (45%)
  starting transfers between devices  38.7 us (20%)
  Pallas kernels  31.1 us (16%)
  waiting for transfers between devices  29.5 us (15%)
  local copies, waits for them, and re-layouts  4.16 us (2%)
    all_to_all x2, blocking collectives, body(): images = lax.all_to_all(image_pass(masses, base, col_count), COLS, 0, 0)  23.6 us
    all_to_all x2, blocking collectives, body(): masses = lax.all_to_all(proto_pass(images, base, row_parts), ROWS, 0, 0)  19.9 us
    all_to_all x1, blocking collectives, body(): masses = lax.all_to_all(masses, ROWS, 0, 0)  17.6 us
    all_to_all x1, blocking collectives, body(): lax.all_to_all(image_pass(masses, base, col_count, soft_part), COLS, 0, 0)  13.1 us
    pallas_call x11, Pallas kernels, call(): pl.pallas_call(kernel, in_specs=[SMEM] * len(scalars) + [VMEM] * len(arra...  12.7 us
    all_to_all x1, blocking collectives, gather_all(): return lax.all_to_all(copies, axes, 0, 0)  11.7 us
    pallas_call x1, Pallas kernels, grad_pass(): pl.pallas_call(grad_kernel, in_specs=[SMEM, VMEM, VMEM, VMEM, anywhere, V...  10.8 us
    all_to_all x1, waiting for transfers between devices, scatter_sum(): return jnp.sum(lax.all_to_all(blocks, axes, 0, 0).astype(f32), axis=0)  9.26 us
  transfers between devices with their start and end apart: 18, of which 8 were waited for; matrix products, arithmetic and copies ran while one was open for 0% of the time, Pallas kernels for 6%

profile of v11, /device:TPU:1, one launch (start us, length us, event | category | flops | bytes accessed | tf_op | source)
XLA Modules:
  0.0 191.8 jit_solution(4124856291242051707)
XLA Ops:
  1.7 2.2 %collective-permute-start = (bf16[1024,128]{1,0:T(8,128)(2,1)S(1)}, bf16[1024,128]{1,0:T(8,128)(2,1)S(1)}, u32[]{:S(2)}, u32[]{:S(2)}) collective-permute-start(bf16[1024,128]{1,0:T(8,128)(2,1)S(1)} %bitcast_select_fusion), channel_id=1, source_target_pairs={{0,1},{1,2},{2,3},{3,0},{4,5},{5,6},{6,7},{7,4},{8,9},{9,10},{10,1... | collective-permute-start | bytes 786440 | tf_op jit(solution)/shard_map/ppermute | solution.py:497
  3.9 2.6 %collective-permute-start.1 = (bf16[1024,128]{1,0:T(8,128)(2,1)S(1)}, bf16[1024,128]{1,0:T(8,128)(2,1)S(1)}, u32[]{:S(2)}, u32[]{:S(2)}) collective-permute-start(bf16[1024,128]{1,0:T(8,128)(2,1)S(1)} %bitcast_select_fusion), channel_id=1, source_target_pairs={{0,2},{1,3},{2,0},{3,1},{4,6},{5,7},{6,4},{7,5},{8,10},{9,11},{10,... | collective-permute-start | bytes 786440 | tf_op jit(solution)/shard_map/ppermute | solution.py:497
  7.6 1.5 shard_map.77
  9.1 8.7 %all-to-all-start = ((bf16[32,40,128]{2,1,0:T(8,128)(2,1)}), bf16[32,40,128]{2,1,0:T(8,128)(2,1)S(1)}, u32[]{:S(2)}, u32[]{:S(2)}) async-start(bf16[32,40,128]{2,1,0:T(8,128)(2,1)} %shard_map.77), calls=%async_computation | async-start | bytes 655360 | tf_op jit(solution)/shard_map/all_to_all | solution.py:485
  18.0 2.8 %collective-permute-start.3 = (bf16[3,1024,128]{2,1,0:T(8,128)(2,1)S(1)}, bf16[3,1024,128]{2,1,0:T(8,128)(2,1)S(1)}, u32[]{:S(2)}, u32[]{:S(2)}) collective-permute-start(bf16[3,1024,128]{2,1,0:T(8,128)(2,1)S(1)} %shard_map.78.shares_ref), channel_id=1, source_target_pairs={{0,32},{32,0},{1,33},{33,1},{2,34},{34,2},{3,35},{35,3},{4,36},{36... | collective-permute-start | bytes 2359304 | tf_op jit(solution)/shard_map/ppermute | solution.py:501
  20.8 7.9 %all-to-all-done = bf16[32,40,128]{2,1,0:T(8,128)(2,1)S(1)} async-done(((bf16[32,40,128]{2,1,0:T(8,128)(2,1)}), bf16[32,40,128]{2,1,0:T(8,128)(2,1)S(1)}, u32[]{:S(2)}, u32[]{:S(2)}) %all-to-all-start) | async-done | bytes 327712 | tf_op jit(solution)/shard_map/all_to_all | solution.py:485
  29.4 1.8 shard_map.79
  31.2 3.4 %all-to-all-start.1 = ((bf16[8,16,1024]{2,1,0:T(8,128)(2,1)}), bf16[8,16,1024]{2,1,0:T(8,128)(2,1)S(1)}, u32[]{:S(2)}, u32[]{:S(2)}) async-start(bf16[8,16,1024]{2,1,0:T(8,128)(2,1)} %bitcast.12), calls=%async_computation.1 | async-start | bytes 524288 | tf_op jit(solution)/shard_map/all_to_all | solution.py:38
  34.7 9.3 %all-to-all-done.1 = bf16[8,16,1024]{2,1,0:T(8,128)(2,1)S(1)} async-done(((bf16[8,16,1024]{2,1,0:T(8,128)(2,1)}), bf16[8,16,1024]{2,1,0:T(8,128)(2,1)S(1)}, u32[]{:S(2)}, u32[]{:S(2)}) %all-to-all-start.1) | async-done | bytes 262176 | tf_op jit(solution)/shard_map/all_to_all | solution.py:38
  44.7 11.7 %all_to_all.50 = bf16[8,16,1024]{2,1,0:T(8,128)(2,1)S(1)} all-to-all(bf16[8,16,1024]{2,1,0:T(8,128)(2,1)S(1)} %broadcast_in_dim.2), channel_id=1, replica_groups=mesh['x'=4,'core'=2,'z'=8,'y'=4] {'z'}, dimensions={0} | all-to-all | bytes 524288 | tf_op jit(solution)/shard_map/all_to_all | solution.py:30
  57.2 1.9 %collective-permute-start.5 = (bf16[128,1024]{1,0:T(8,128)(2,1)S(1)}, bf16[128,1024]{1,0:T(8,128)(2,1)S(1)}, u32[]{:S(2)}, u32[]{:S(2)}) collective-permute-start(bf16[128,1024]{1,0:T(8,128)(2,1)S(1)} %bitcast.34), channel_id=1, source_target_pairs={{0,3},{1,0},{2,1},{3,2},{4,7},{5,4},{6,5},{7,6},{8,11},{9,8},{10,9... | collective-permute-start | bytes 786440 | tf_op jit(solution)/shard_map/ppermute | solution.py:534
  59.6 2.2 %copy-done = bf16[2048,1024]{1,0:T(8,128)(2,1)S(1)} copy-done((bf16[2048,1024]{1,0:T(8,128)(2,1)S(1)}, bf16[2048,1024]{1,0:T(8,128)(2,1)}, u32[]{:S(2)}) %copy-start) | copy-done | bytes 4194328
  61.8 3.5 %shard_map.80 = (bf16[2048,1024]{1,0:T(8,128)(2,1)S(1)}, f32[1,2048]{1,0:T(1,128)S(1)}, bf16[4,128,2048]{2,1,0:T(8,128)(2,1)}) custom-call(s32[1]{0:T(128)} %bitcast.core_ref, bf16[2048,1024]{1,0:T(8,128)(2,1)S(1)} %copy-done), custom_call_target="tpu_custom_call" | custom-call | flops 12582912 | bytes 10485760 | tf_op jit(solution)/shard_map/pallas_call | solution.py:59
  66.2 3.5 %shard_map.81 = (bf16[512,2048]{1,0:T(8,128)(2,1)S(1)}, f32[8,2,2048]{2,1,0:T(2,128)S(1)}, f32[1,512]{1,0:T(1,128)S(1)}, bf16[512,1024]{1,0:T(8,128)(2,1)S(1)}) custom-call(s32[4]{0:T(128)S(1)} %pad_add_fusion.place_ref, bf16[128,1024]{1,0:T(8,128)(2,1)S(1)} %bitcast.36, bf16[128,1024]{1,0:T(8,128)(2,1)S(1)} %collective-permute-done.4.rest_1_, ...), custom_call_target="tpu_custom_call" | custom-call | flops 2147483648 | bytes 8388608 | tf_op jit(solution)/shard_map/pallas_call | solution.py:59
  69.6 17.6 %all_to_all.51.mass_ref = f32[8,2,2048]{2,1,0:T(2,128)S(1)} all-to-all(f32[8,2,2048]{2,1,0:T(2,128)S(1)} %get-tuple-element.24), channel_id=1, replica_groups=mesh['x'=4,'core'=2,'z'=8,'y'=4] {'x','core'}, dimensions={0} | all-to-all | bytes 262144 | tf_op jit(solution)/shard_map/all_to_all | solution.py:540
  87.7 13.1 %all_to_all.52.image_ref.soft_ref = f32[32,1,1024]{2,1,0:T(1,128)S(1)} all-to-all(f32[32,1,1024]{2,1,0:T(1,128)S(1)} %shard_map.82), channel_id=1, replica_groups=mesh['x'=4,'core'=2,'z'=8,'y'=4] {'z','y'}, dimensions={0} | all-to-all | bytes 262144 | tf_op jit(solution)/shard_map/all_to_all | solution.py:541
  101.4 10.0 %all_to_all.53.mass_ref = f32[8,2,2048]{2,1,0:T(2,128)S(1)} all-to-all(f32[8,2,2048]{2,1,0:T(2,128)S(1)} %shard_map.83), channel_id=1, replica_groups=mesh['x'=4,'core'=2,'z'=8,'y'=4] {'x','core'}, dimensions={0} | all-to-all | bytes 262144 | tf_op jit(solution)/shard_map/all_to_all | solution.py:543
  111.9 11.8 %all_to_all.54.image_ref = f32[32,1,512]{2,1,0:T(1,128)S(1)} all-to-all(f32[32,1,512]{2,1,0:T(1,128)S(1)} %shard_map.84), channel_id=1, replica_groups=mesh['x'=4,'core'=2,'z'=8,'y'=4] {'z','y'}, dimensions={0} | all-to-all | bytes 131072 | tf_op jit(solution)/shard_map/all_to_all | solution.py:544
  124.2 9.9 %all_to_all.55.mass_ref = f32[8,2,2048]{2,1,0:T(2,128)S(1)} all-to-all(f32[8,2,2048]{2,1,0:T(2,128)S(1)} %shard_map.85), channel_id=1, replica_groups=mesh['x'=4,'core'=2,'z'=8,'y'=4] {'x','core'}, dimensions={0} | all-to-all | bytes 262144 | tf_op jit(solution)/shard_map/all_to_all | solution.py:543
  134.7 11.8 %all_to_all.56.image_ref = f32[32,1,512]{2,1,0:T(1,128)S(1)} all-to-all(f32[32,1,512]{2,1,0:T(1,128)S(1)} %shard_map.86), channel_id=1, replica_groups=mesh['x'=4,'core'=2,'z'=8,'y'=4] {'z','y'}, dimensions={0} | all-to-all | bytes 131072 | tf_op jit(solution)/shard_map/all_to_all | solution.py:544
  146.6 10.8 %shard_map.87 = (f32[1,2048]{1,0:T(1,128)S(1)}, bf16[4,128,2048]{2,1,0:T(8,128)(2,1)}, f32[4,128,2048]{2,1,0:T(8,128)}, bf16[1024,512]{1,0:T(8,128)(2,1)}) custom-call(s32[1]{0:T(128)} %bitcast.core_ref, f32[32,1,512]{2,1,0:T(1,128)S(1)} %all_to_all.56.image_ref, f32[32,1,1024]{2,1,0:T(1,128)S(1)} %all_to_all.52.image_ref.soft_ref, ...), custom_call_target="tpu_custom_call" | custom-call | flops 4294967296 | bytes 10485760 | tf_op jit(solution)/shard_map/pallas_call | solution.py:364
  157.4 2.2 %collective-permute-start.7 = (bf16[4,128,2048]{2,1,0:T(8,128)(2,1)}, bf16[4,128,2048]{2,1,0:T(8,128)(2,1)S(1)}, u32[]{:S(2)}, u32[]{:S(2)}) collective-permute-start(bf16[4,128,2048]{2,1,0:T(8,128)(2,1)} %get-tuple-element.30), channel_id=1, source_target_pairs={{0,32},{32,0},{1,33},{33,1},{2,34},{34,2},{3,35},{35,3},{4,36},{36... | collective-permute-start | bytes 6291464 | tf_op jit(solution)/shard_map/ppermute | solution.py:547
  159.6 4.2 %all-to-all-start.9 = ((bf16[32,32,512]{2,1,0:T(8,128)(2,1)}), bf16[32,32,512]{2,1,0:T(8,128)(2,1)S(1)}, u32[]{:S(2)}, u32[]{:S(2)}) async-start(bf16[32,32,512]{2,1,0:T(8,128)(2,1)} %bitcast.14), calls=%async_computation.9 | async-start | bytes 2097152 | tf_op jit(solution)/shard_map/all_to_all | solution.py:594
  165.0 1.6 shard_map.90
  167.0 2.4 %collective-permute-start.12 = (bf16[64,2048]{1,0:T(8,128)(2,1)S(1)}, bf16[64,2048]{1,0:T(8,128)(2,1)S(1)}, u32[]{:S(2)}, u32[]{:S(2)}) collective-permute-start(bf16[64,2048]{1,0:T(8,128)(2,1)S(1)} %get-tuple-element.39), channel_id=1, source_target_pairs={{64,0},{128,64},{192,128},{0,192},{65,1},{129,65},{193,129},{1,193... | collective-permute-start | bytes 786440 | tf_op jit(solution)/shard_map/ppermute | solution.py:559
  169.4 2.8 %shard_map.88 = (bf16[64,2048]{1,0:T(8,128)(2,1)S(1)}, bf16[64,2048]{1,0:T(8,128)(2,1)S(1)}, f32[64,2048]{1,0:T(8,128)S(1)}, f32[64,2048]{1,0:T(8,128)S(1)}) custom-call(s32[2]{0:T(128)S(1)} %pad_add_fusion.1.place_ref, f32[4,128,2048]{2,1,0:T(8,128)} %get-tuple-element.29.refs_0_.refs_3_, bf16[4,128,2048]{2,1,0:T(8,128)(2,1)S(1)} %collective-permute-done.7.refs_1_.refs_4_, ...), custom_call_target="tpu_custom_call" | custom-call | flops 1000000000 | bytes 2621440 | tf_op jit(solution)/shard_map/pallas_call | solution.py:455
  172.3 2.7 %collective-permute-start.9 = (bf16[64,2048]{1,0:T(8,128)(2,1)S(1)}, bf16[64,2048]{1,0:T(8,128)(2,1)S(1)}, u32[]{:S(2)}, u32[]{:S(2)}) collective-permute-start(bf16[64,2048]{1,0:T(8,128)(2,1)S(1)} %get-tuple-element.34), channel_id=1, source_target_pairs={{64,0},{128,64},{192,128},{0,192},{65,1},{129,65},{193,129},{1,193... | collective-permute-start | bytes 786440 | tf_op jit(solution)/shard_map/ppermute | solution.py:559
  175.8 2.7 %collective-permute-start.14 = (bf16[64,2048]{1,0:T(8,128)(2,1)S(1)}, bf16[64,2048]{1,0:T(8,128)(2,1)S(1)}, u32[]{:S(2)}, u32[]{:S(2)}) collective-permute-start(bf16[64,2048]{1,0:T(8,128)(2,1)S(1)} %get-tuple-element.41), channel_id=1, source_target_pairs={{64,0},{128,64},{192,128},{0,192},{65,1},{129,65},{193,129},{1,193... | collective-permute-start | bytes 786440 | tf_op jit(solution)/shard_map/ppermute | solution.py:559
  178.5 2.1 %collective-permute-done.10.refs_7_ = bf16[64,2048]{1,0:T(8,128)(2,1)S(1)} collective-permute-done((bf16[64,2048]{1,0:T(8,128)(2,1)S(1)}, bf16[64,2048]{1,0:T(8,128)(2,1)S(1)}, u32[]{:S(2)}, u32[]{:S(2)}) %collective-permute-start.10) | collective-permute-done | bytes 262176 | tf_op jit(solution)/shard_map/ppermute | solution.py:556
  180.6 1.7 shard_map.89.sum_ref
  182.3 4.0 %collective-permute-done.13.lower_ref = bf16[64,2048]{1,0:T(8,128)(2,1)S(1)} collective-permute-done((bf16[64,2048]{1,0:T(8,128)(2,1)S(1)}, bf16[64,2048]{1,0:T(8,128)(2,1)S(1)}, u32[]{:S(2)}, u32[]{:S(2)}) %collective-permute-start.13) | collective-permute-done | bytes 262176 | tf_op jit(solution)/shard_map/ppermute | solution.py:556
  187.3 3.7 %all-to-all-done.9 = bf16[32,32,512]{2,1,0:T(8,128)(2,1)S(1)} async-done(((bf16[32,32,512]{2,1,0:T(8,128)(2,1)}), bf16[32,32,512]{2,1,0:T(8,128)(2,1)S(1)}, u32[]{:S(2)}, u32[]{:S(2)}) %all-to-all-start.9) | async-done | bytes 1048608 | tf_op jit(solution)/shard_map/all_to_all | solution.py:594
  (57 shorter events, 13.0 us)
Async XLA Ops:
  1.7 16.1 %collective-permute-start = (bf16[1024,128]{1,0:T(8,128)(2,1)S(1)}, bf16[1024,128]{1,0:T(8,128)(2,1)S(1)}, u32[]{:S(2)}, u32[]{:S(2)}) collective-permute-start(bf16[1024,128]{1,0:T(8,128)(2,1)S(1)} %bitcast_select_fusion), channel_id=1, source_target_pairs={{0,1},{1,2},{2,3},{3,0},{4,5},{5,6},{6,7},{7,4},{8,9},{9,10},{10,1... | collective-permute-start | bytes 786440 | tf_op jit(solution)/shard_map/ppermute | solution.py:497
  3.9 13.9 %collective-permute-start.1 = (bf16[1024,128]{1,0:T(8,128)(2,1)S(1)}, bf16[1024,128]{1,0:T(8,128)(2,1)S(1)}, u32[]{:S(2)}, u32[]{:S(2)}) collective-permute-start(bf16[1024,128]{1,0:T(8,128)(2,1)S(1)} %bitcast_select_fusion), channel_id=1, source_target_pairs={{0,2},{1,3},{2,0},{3,1},{4,6},{5,7},{6,4},{7,5},{8,10},{9,11},{10,... | collective-permute-start | bytes 786440 | tf_op jit(solution)/shard_map/ppermute | solution.py:497
  6.5 11.3 %collective-permute-start.2 = (bf16[1024,128]{1,0:T(8,128)(2,1)S(1)}, bf16[1024,128]{1,0:T(8,128)(2,1)S(1)}, u32[]{:S(2)}, u32[]{:S(2)}) collective-permute-start(bf16[1024,128]{1,0:T(8,128)(2,1)S(1)} %bitcast_select_fusion), channel_id=1, source_target_pairs={{0,3},{1,0},{2,1},{3,2},{4,7},{5,4},{6,5},{7,6},{8,11},{9,8},{10,9... | collective-permute-start | bytes 786440 | tf_op jit(solution)/shard_map/ppermute | solution.py:497
  9.1 19.5 %all-to-all-start = ((bf16[32,40,128]{2,1,0:T(8,128)(2,1)}), bf16[32,40,128]{2,1,0:T(8,128)(2,1)S(1)}, u32[]{:S(2)}, u32[]{:S(2)}) async-start(bf16[32,40,128]{2,1,0:T(8,128)(2,1)} %shard_map.77), calls=%async_computation | async-start | bytes 655360 | tf_op jit(solution)/shard_map/all_to_all | solution.py:485
  17.9 11.5 %copy-start.1 = (bf16[128,1024]{1,0:T(8,128)(2,1)S(1)}, bf16[128,1024]{1,0:T(8,128)(2,1)}, u32[]{:S(2)}) copy-start(bf16[128,1024]{1,0:T(8,128)(2,1)} %w_out_ref.1) | copy-start | bytes 786436
  17.9 11.5 %copy-start.2 = (bf16[1024,128]{1,0:T(8,128)(2,1)S(1)}, bf16[1024,128]{1,0:T(8,128)(2,1)}, u32[]{:S(2)}) copy-start(bf16[1024,128]{1,0:T(8,128)(2,1)} %w_in_ref.1) | copy-start | bytes 786436
  18.0 11.5 %collective-permute-start.3 = (bf16[3,1024,128]{2,1,0:T(8,128)(2,1)S(1)}, bf16[3,1024,128]{2,1,0:T(8,128)(2,1)S(1)}, u32[]{:S(2)}, u32[]{:S(2)}) collective-permute-start(bf16[3,1024,128]{2,1,0:T(8,128)(2,1)S(1)} %shard_map.78.shares_ref), channel_id=1, source_target_pairs={{0,32},{32,0},{1,33},{33,1},{2,34},{34,2},{3,35},{35,3},{4,36},{36... | collective-permute-start | bytes 2359304 | tf_op jit(solution)/shard_map/ppermute | solution.py:501
  31.2 12.8 %all-to-all-start.1 = ((bf16[8,16,1024]{2,1,0:T(8,128)(2,1)}), bf16[8,16,1024]{2,1,0:T(8,128)(2,1)S(1)}, u32[]{:S(2)}, u32[]{:S(2)}) async-start(bf16[8,16,1024]{2,1,0:T(8,128)(2,1)} %bitcast.12), calls=%async_computation.1 | async-start | bytes 524288 | tf_op jit(solution)/shard_map/all_to_all | solution.py:38
  56.4 9.0 %collective-permute-start.4 = (bf16[128,1024]{1,0:T(8,128)(2,1)S(1)}, bf16[128,1024]{1,0:T(8,128)(2,1)S(1)}, u32[]{:S(2)}, u32[]{:S(2)}) collective-permute-start(bf16[128,1024]{1,0:T(8,128)(2,1)S(1)} %bitcast.33), channel_id=1, source_target_pairs={{0,1},{1,2},{2,3},{3,0},{4,5},{5,6},{6,7},{7,4},{8,9},{9,10},{10,1... | collective-permute-start | bytes 786440 | tf_op jit(solution)/shard_map/ppermute | solution.py:534
  57.2 8.2 %collective-permute-start.5 = (bf16[128,1024]{1,0:T(8,128)(2,1)S(1)}, bf16[128,1024]{1,0:T(8,128)(2,1)S(1)}, u32[]{:S(2)}, u32[]{:S(2)}) collective-permute-start(bf16[128,1024]{1,0:T(8,128)(2,1)S(1)} %bitcast.34), channel_id=1, source_target_pairs={{0,3},{1,0},{2,1},{3,2},{4,7},{5,4},{6,5},{7,6},{8,11},{9,8},{10,9... | collective-permute-start | bytes 786440 | tf_op jit(solution)/shard_map/ppermute | solution.py:534
  59.1 7.1 %collective-permute-start.6 = (bf16[128,1024]{1,0:T(8,128)(2,1)S(1)}, bf16[128,1024]{1,0:T(8,128)(2,1)S(1)}, u32[]{:S(2)}, u32[]{:S(2)}) collective-permute-start(bf16[128,1024]{1,0:T(8,128)(2,1)S(1)} %bitcast.35), channel_id=1, source_target_pairs={{0,2},{1,3},{2,0},{3,1},{4,6},{5,7},{6,4},{7,5},{8,10},{9,11},{10,... | collective-permute-start | bytes 786440 | tf_op jit(solution)/shard_map/ppermute | solution.py:534
  59.6 2.2 %copy-start = (bf16[2048,1024]{1,0:T(8,128)(2,1)S(1)}, bf16[2048,1024]{1,0:T(8,128)(2,1)}, u32[]{:S(2)}) copy-start(bf16[2048,1024]{1,0:T(8,128)(2,1)} %proto_ref.1) | copy-start | bytes 12582916
  65.3 4.3 %copy-start.3 = (bf16[2048,1024]{1,0:T(8,128)(2,1)}, bf16[2048,1024]{1,0:T(8,128)(2,1)S(1)}, u32[]{:S(2)}) copy-start(bf16[2048,1024]{1,0:T(8,128)(2,1)S(1)} %get-tuple-element.23.rest_4_.unit_hbm) | copy-start | bytes 12582916
  157.4 7.6 %collective-permute-start.7 = (bf16[4,128,2048]{2,1,0:T(8,128)(2,1)}, bf16[4,128,2048]{2,1,0:T(8,128)(2,1)S(1)}, u32[]{:S(2)}, u32[]{:S(2)}) collective-permute-start(bf16[4,128,2048]{2,1,0:T(8,128)(2,1)} %get-tuple-element.30), channel_id=1, source_target_pairs={{0,32},{32,0},{1,33},{33,1},{2,34},{34,2},{3,35},{35,3},{4,36},{36... | collective-permute-start | bytes 6291464 | tf_op jit(solution)/shard_map/ppermute | solution.py:547
  159.6 31.4 %all-to-all-start.9 = ((bf16[32,32,512]{2,1,0:T(8,128)(2,1)}), bf16[32,32,512]{2,1,0:T(8,128)(2,1)S(1)}, u32[]{:S(2)}, u32[]{:S(2)}) async-start(bf16[32,32,512]{2,1,0:T(8,128)(2,1)} %bitcast.14), calls=%async_computation.9 | async-start | bytes 2097152 | tf_op jit(solution)/shard_map/all_to_all | solution.py:594
  163.7 1.3 collective-permute-start.8
  166.6 9.0 %collective-permute-start.11 = (bf16[64,2048]{1,0:T(8,128)(2,1)S(1)}, bf16[64,2048]{1,0:T(8,128)(2,1)S(1)}, u32[]{:S(2)}, u32[]{:S(2)}) collective-permute-start(bf16[64,2048]{1,0:T(8,128)(2,1)S(1)} %get-tuple-element.38), channel_id=1, source_target_pairs={{0,64},{64,128},{128,192},{192,0},{1,65},{65,129},{129,193},{193,1... | collective-permute-start | bytes 786440 | tf_op jit(solution)/shard_map/ppermute | solution.py:556
  167.0 8.7 %collective-permute-start.12 = (bf16[64,2048]{1,0:T(8,128)(2,1)S(1)}, bf16[64,2048]{1,0:T(8,128)(2,1)S(1)}, u32[]{:S(2)}, u32[]{:S(2)}) collective-permute-start(bf16[64,2048]{1,0:T(8,128)(2,1)S(1)} %get-tuple-element.39), channel_id=1, source_target_pairs={{64,0},{128,64},{192,128},{0,192},{65,1},{129,65},{193,129},{1,193... | collective-permute-start | bytes 786440 | tf_op jit(solution)/shard_map/ppermute | solution.py:559
  172.2 8.4 %collective-permute-start.10 = (bf16[64,2048]{1,0:T(8,128)(2,1)S(1)}, bf16[64,2048]{1,0:T(8,128)(2,1)S(1)}, u32[]{:S(2)}, u32[]{:S(2)}) collective-permute-start(bf16[64,2048]{1,0:T(8,128)(2,1)S(1)} %get-tuple-element.35), channel_id=1, source_target_pairs={{0,64},{64,128},{128,192},{192,0},{1,65},{65,129},{129,193},{193,1... | collective-permute-start | bytes 786440 | tf_op jit(solution)/shard_map/ppermute | solution.py:556
  172.3 8.3 %collective-permute-start.9 = (bf16[64,2048]{1,0:T(8,128)(2,1)S(1)}, bf16[64,2048]{1,0:T(8,128)(2,1)S(1)}, u32[]{:S(2)}, u32[]{:S(2)}) collective-permute-start(bf16[64,2048]{1,0:T(8,128)(2,1)S(1)} %get-tuple-element.34), channel_id=1, source_target_pairs={{64,0},{128,64},{192,128},{0,192},{65,1},{129,65},{193,129},{1,193... | collective-permute-start | bytes 786440 | tf_op jit(solution)/shard_map/ppermute | solution.py:559
  175.8 10.5 %collective-permute-start.13 = (bf16[64,2048]{1,0:T(8,128)(2,1)S(1)}, bf16[64,2048]{1,0:T(8,128)(2,1)S(1)}, u32[]{:S(2)}, u32[]{:S(2)}) collective-permute-start(bf16[64,2048]{1,0:T(8,128)(2,1)S(1)} %get-tuple-element.40), channel_id=1, source_target_pairs={{0,64},{64,128},{128,192},{192,0},{1,65},{65,129},{129,193},{193,1... | collective-permute-start | bytes 786440 | tf_op jit(solution)/shard_map/ppermute | solution.py:556
  175.8 10.4 %collective-permute-start.14 = (bf16[64,2048]{1,0:T(8,128)(2,1)S(1)}, bf16[64,2048]{1,0:T(8,128)(2,1)S(1)}, u32[]{:S(2)}, u32[]{:S(2)}) collective-permute-start(bf16[64,2048]{1,0:T(8,128)(2,1)S(1)} %get-tuple-element.41), channel_id=1, source_target_pairs={{64,0},{128,64},{192,128},{0,192},{65,1},{129,65},{193,129},{1,193... | collective-permute-start | bytes 786440 | tf_op jit(solution)/shard_map/ppermute | solution.py:559

commit v12 on v11

--- a/solution.py
+++ b/solution.py
@@ -103,7 +103,9 @@
     return [slice(j, j + TILE) for j in range(0, count, TILE)]
 
 
-def pack_kernel(y_count, states_ref, in_ref, last_ref, out_ref):
+def pack_kernel(
+    y_count, core_ref, states_ref, in_ref, last_ref, w_in_ref, w_out_ref, out_ref, share_ref
+):
     width = in_ref.shape[1]
     height = out_ref.shape[2]
     pair = jnp.concatenate([in_ref[...].astype(f32), last_ref[...].astype(f32)], axis=0)
@@ -115,13 +117,18 @@
         piece = jnp.concatenate([block, foot], axis=0).astype(bf16)
         for group in range(out_ref.shape[0] // y_count):
             out_ref[group * y_count + way] = piece
-
-
-def pack_states(states, gain_in, gain_out, z_count, y_count):
+    even = core_ref[0] == 0
+    units = w_in_ref.shape[1]
+    for start in range(0, D, units):
+        part = slice(start, start + units)
+        share_ref[part, :] = jnp.where(even, w_in_ref[part, :], w_out_ref[:, part])
+
+
+def pack(core, states, gain_in, gain_out, w_in, w_out, z_count, y_count):
     views, width, rows = states.shape
     height = views * rows // y_count
     shape = (z_count * y_count, width + 8, height)
-    arrays = (states, gain_in.reshape(1, width), gain_out.reshape(1, width))
+    arrays = (states, gain_in.reshape(1, width), gain_out.reshape(1, width), w_in, w_out)
 
     def full(shape):
         return pl.BlockSpec(shape, lambda i: (0,) * len(shape))
@@ -129,11 +136,14 @@
     return pl.pallas_call(
         functools.partial(pack_kernel, y_count),
         grid=(1,),
-        in_specs=[full(values.shape) for values in arrays],
-        out_specs=full(shape),
-        out_shape=jax.ShapeDtypeStruct(shape, bf16),
-        compiler_params=pltpu.CompilerParams(vmem_limit_bytes=4 * 1024 * 1024),
-    )(*[keep_hbm(values) for values in arrays])
+        in_specs=[SMEM] + [full(values.shape) for values in arrays],
+        out_specs=[full(shape), full(w_in.shape)],
+        out_shape=[
+            jax.ShapeDtypeStruct(shape, bf16),
+            jax.ShapeDtypeStruct(w_in.shape, bf16),
+        ],
+        compiler_params=pltpu.CompilerParams(vmem_limit_bytes=6 * 1024 * 1024),
+    )(core.reshape(1), *[keep_hbm(values) for values in arrays])
 
 
 def stack_kernel(first_ref, second_ref, third_ref, out_ref):
@@ -479,19 +489,16 @@
     z_count = lax.axis_size("z")
     tall = row_count // y_count
 
-    sent = pack_states(
-        hidden_states.transpose(0, 2, 1), ln_in_gain, ln_out_gain, z_count, y_count
+    core = lax.axis_index("core")
+    swap = [(0, 1), (1, 0)]
+    sent, share = pack(
+        core, hidden_states.transpose(0, 2, 1), ln_in_gain, ln_out_gain, w_in, w_out, z_count, y_count
     )
     received = lax.all_to_all(sent, COLS, 0, 0)
     gain_in = received[:, local_width, :local_width].reshape(D).astype(f32)
     gain_out = received[:, local_width + 1, :local_width].reshape(D).astype(f32)
     inputs_t = received[:, :local_width].reshape(D, tall)
 
-    core = lax.axis_index("core")
-    swap = [(0, 1), (1, 0)]
-    width = w_in.shape[1]
-    stacked = w_out.reshape(width, D // width, width).transpose(1, 0, 2).reshape(D, width)
-    share = jnp.where(core == 0, w_in, stacked)
     shares = stack_shares(
         [
             lax.ppermute(share, "y", [(i, (i + step) % y_count) for i in range(y_count)])

time: 193 us -> 192 us (level)
  transfers between devices with their start and end apart: 18 -> 18, of which waited for: 8 -> 9; matrix products, arithmetic and copies ran while one was open for 0% -> 0% of each run, Pallas kernels for 6% -> 6%
where the time goes in v12:
time: 192 us; the launch traced here: 191 us
  blocking collectives  85.1 us (44%)
  starting transfers between devices  38.5 us (20%)
  Pallas kernels  31.5 us (16%)
  waiting for transfers between devices  30.3 us (16%)
  local copies, waits for them, and re-layouts  3.16 us (2%)
    all_to_all x2, blocking collectives, body(): images = lax.all_to_all(image_pass(masses, base, col_count), COLS, 0, 0)  23.6 us
    all_to_all x2, blocking collectives, body(): masses = lax.all_to_all(proto_pass(images, base, row_parts), ROWS, 0, 0)  19.9 us
    all_to_all x1, blocking collectives, body(): masses = lax.all_to_all(masses, ROWS, 0, 0)  16.7 us
    all_to_all x1, blocking collectives, body(): lax.all_to_all(image_pass(masses, base, col_count, soft_part), COLS, 0, 0)  13.1 us
    pallas_call x11, Pallas kernels, call(): pl.pallas_call(kernel, in_specs=[SMEM] * len(scalars) + [VMEM] * len(arra...  12.7 us
    all_to_all x1, blocking collectives, gather_all(): return lax.all_to_all(copies, axes, 0, 0)  11.7 us
    pallas_call x1, Pallas kernels, grad_pass(): pl.pallas_call(grad_kernel, in_specs=[SMEM, VMEM, VMEM, VMEM, anywhere, V...  10.8 us
    all_to_all x1, waiting for transfers between devices, scatter_sum(): return jnp.sum(lax.all_to_all(blocks, axes, 0, 0).astype(f32), axis=0)  9.16 us
  transfers between devices with their start and end apart: 18, of which 9 were waited for; matrix products, arithmetic and copies ran while one was open for 0% of the time, Pallas kernels for 6%

profile of v12, /device:TPU:1, one launch (start us, length us, event | category | flops | bytes accessed | tf_op | source)
XLA Modules:
  0.0 190.9 jit_solution(5583034780723119596)
XLA Ops:
  0.6 1.9 shard_map.77
  2.5 2.1 %collective-permute-start = (bf16[1024,128]{1,0:T(8,128)(2,1)S(1)}, bf16[1024,128]{1,0:T(8,128)(2,1)S(1)}, u32[]{:S(2)}, u32[]{:S(2)}) collective-permute-start(bf16[1024,128]{1,0:T(8,128)(2,1)S(1)} %get-tuple-element.26), channel_id=1, source_target_pairs={{0,1},{1,2},{2,3},{3,0},{4,5},{5,6},{6,7},{7,4},{8,9},{9,10},{10,1... | collective-permute-start | bytes 786440 | tf_op jit(solution)/shard_map/ppermute | solution.py:504
  4.7 2.6 %collective-permute-start.1 = (bf16[1024,128]{1,0:T(8,128)(2,1)S(1)}, bf16[1024,128]{1,0:T(8,128)(2,1)S(1)}, u32[]{:S(2)}, u32[]{:S(2)}) collective-permute-start(bf16[1024,128]{1,0:T(8,128)(2,1)S(1)} %get-tuple-element.26), channel_id=1, source_target_pairs={{0,2},{1,3},{2,0},{3,1},{4,6},{5,7},{6,4},{7,5},{8,10},{9,11},{10,... | collective-permute-start | bytes 786440 | tf_op jit(solution)/shard_map/ppermute | solution.py:504
  8.4 8.7 %all-to-all-start = ((bf16[32,40,128]{2,1,0:T(8,128)(2,1)}), bf16[32,40,128]{2,1,0:T(8,128)(2,1)S(1)}, u32[]{:S(2)}, u32[]{:S(2)}) async-start(bf16[32,40,128]{2,1,0:T(8,128)(2,1)} %get-tuple-element.25), calls=%async_computation | async-start | bytes 655360 | tf_op jit(solution)/shard_map/all_to_all | solution.py:497
  18.7 1.6 collective-permute-start.3
  20.3 7.9 %all-to-all-done = bf16[32,40,128]{2,1,0:T(8,128)(2,1)S(1)} async-done(((bf16[32,40,128]{2,1,0:T(8,128)(2,1)}), bf16[32,40,128]{2,1,0:T(8,128)(2,1)S(1)}, u32[]{:S(2)}, u32[]{:S(2)}) %all-to-all-start) | async-done | bytes 327712 | tf_op jit(solution)/shard_map/all_to_all | solution.py:497
  29.0 1.8 shard_map.79
  30.8 3.4 %all-to-all-start.1 = ((bf16[8,16,1024]{2,1,0:T(8,128)(2,1)}), bf16[8,16,1024]{2,1,0:T(8,128)(2,1)S(1)}, u32[]{:S(2)}, u32[]{:S(2)}) async-start(bf16[8,16,1024]{2,1,0:T(8,128)(2,1)} %bitcast.10), calls=%async_computation.1 | async-start | bytes 524288 | tf_op jit(solution)/shard_map/all_to_all | solution.py:38
  34.3 9.2 %all-to-all-done.1 = bf16[8,16,1024]{2,1,0:T(8,128)(2,1)S(1)} async-done(((bf16[8,16,1024]{2,1,0:T(8,128)(2,1)}), bf16[8,16,1024]{2,1,0:T(8,128)(2,1)S(1)}, u32[]{:S(2)}, u32[]{:S(2)}) %all-to-all-start.1) | async-done | bytes 262176 | tf_op jit(solution)/shard_map/all_to_all | solution.py:38
  44.2 11.7 %all_to_all.50 = bf16[8,16,1024]{2,1,0:T(8,128)(2,1)S(1)} all-to-all(bf16[8,16,1024]{2,1,0:T(8,128)(2,1)S(1)} %broadcast_in_dim.2), channel_id=1, replica_groups=mesh['x'=4,'core'=2,'z'=8,'y'=4] {'z'}, dimensions={0} | all-to-all | bytes 524288 | tf_op jit(solution)/shard_map/all_to_all | solution.py:30
  56.8 1.8 collective-permute-start.5
  60.2 2.2 %copy-done = bf16[2048,1024]{1,0:T(8,128)(2,1)S(1)} copy-done((bf16[2048,1024]{1,0:T(8,128)(2,1)S(1)}, bf16[2048,1024]{1,0:T(8,128)(2,1)}, u32[]{:S(2)}) %copy-start) | copy-done | bytes 4194328
  62.3 3.5 %shard_map.80 = (bf16[2048,1024]{1,0:T(8,128)(2,1)S(1)}, f32[1,2048]{1,0:T(1,128)S(1)}, bf16[4,128,2048]{2,1,0:T(8,128)(2,1)}) custom-call(s32[1]{0:T(128)} %bitcast.core_ref, bf16[2048,1024]{1,0:T(8,128)(2,1)S(1)} %copy-done), custom_call_target="tpu_custom_call" | custom-call | flops 12582912 | bytes 10485760 | tf_op jit(solution)/shard_map/pallas_call | solution.py:59
  66.0 3.5 %shard_map.81 = (bf16[512,2048]{1,0:T(8,128)(2,1)S(1)}, f32[8,2,2048]{2,1,0:T(2,128)S(1)}, f32[1,512]{1,0:T(1,128)S(1)}, bf16[512,1024]{1,0:T(8,128)(2,1)S(1)}) custom-call(s32[4]{0:T(128)S(1)} %pad_add_fusion.place_ref, bf16[128,1024]{1,0:T(8,128)(2,1)S(1)} %bitcast.27, bf16[128,1024]{1,0:T(8,128)(2,1)S(1)} %collective-permute-done.4.rest_1_, ...), custom_call_target="tpu_custom_call" | custom-call | flops 2147483648 | bytes 8388608 | tf_op jit(solution)/shard_map/pallas_call | solution.py:59
  69.5 16.7 %all_to_all.51.mass_ref = f32[8,2,2048]{2,1,0:T(2,128)S(1)} all-to-all(f32[8,2,2048]{2,1,0:T(2,128)S(1)} %get-tuple-element.28), channel_id=1, replica_groups=mesh['x'=4,'core'=2,'z'=8,'y'=4] {'x','core'}, dimensions={0} | all-to-all | bytes 262144 | tf_op jit(solution)/shard_map/all_to_all | solution.py:547
  86.8 13.1 %all_to_all.52.image_ref.soft_ref = f32[32,1,1024]{2,1,0:T(1,128)S(1)} all-to-all(f32[32,1,1024]{2,1,0:T(1,128)S(1)} %shard_map.82), channel_id=1, replica_groups=mesh['x'=4,'core'=2,'z'=8,'y'=4] {'z','y'}, dimensions={0} | all-to-all | bytes 262144 | tf_op jit(solution)/shard_map/all_to_all | solution.py:548
  100.4 10.0 %all_to_all.53.mass_ref = f32[8,2,2048]{2,1,0:T(2,128)S(1)} all-to-all(f32[8,2,2048]{2,1,0:T(2,128)S(1)} %shard_map.83), channel_id=1, replica_groups=mesh['x'=4,'core'=2,'z'=8,'y'=4] {'x','core'}, dimensions={0} | all-to-all | bytes 262144 | tf_op jit(solution)/shard_map/all_to_all | solution.py:550
  110.9 11.8 %all_to_all.54.image_ref = f32[32,1,512]{2,1,0:T(1,128)S(1)} all-to-all(f32[32,1,512]{2,1,0:T(1,128)S(1)} %shard_map.84), channel_id=1, replica_groups=mesh['x'=4,'core'=2,'z'=8,'y'=4] {'z','y'}, dimensions={0} | all-to-all | bytes 131072 | tf_op jit(solution)/shard_map/all_to_all | solution.py:551
  123.3 9.9 %all_to_all.55.mass_ref = f32[8,2,2048]{2,1,0:T(2,128)S(1)} all-to-all(f32[8,2,2048]{2,1,0:T(2,128)S(1)} %shard_map.85), channel_id=1, replica_groups=mesh['x'=4,'core'=2,'z'=8,'y'=4] {'x','core'}, dimensions={0} | all-to-all | bytes 262144 | tf_op jit(solution)/shard_map/all_to_all | solution.py:550
  133.8 11.8 %all_to_all.56.image_ref = f32[32,1,512]{2,1,0:T(1,128)S(1)} all-to-all(f32[32,1,512]{2,1,0:T(1,128)S(1)} %shard_map.86), channel_id=1, replica_groups=mesh['x'=4,'core'=2,'z'=8,'y'=4] {'z','y'}, dimensions={0} | all-to-all | bytes 131072 | tf_op jit(solution)/shard_map/all_to_all | solution.py:551
  145.6 10.8 %shard_map.87 = (f32[1,2048]{1,0:T(1,128)S(1)}, bf16[4,128,2048]{2,1,0:T(8,128)(2,1)}, f32[4,128,2048]{2,1,0:T(8,128)}, bf16[1024,512]{1,0:T(8,128)(2,1)}) custom-call(s32[1]{0:T(128)} %bitcast.core_ref, f32[32,1,512]{2,1,0:T(1,128)S(1)} %all_to_all.56.image_ref, f32[32,1,1024]{2,1,0:T(1,128)S(1)} %all_to_all.52.image_ref.soft_ref, ...), custom_call_target="tpu_custom_call" | custom-call | flops 4294967296 | bytes 10485760 | tf_op jit(solution)/shard_map/pallas_call | solution.py:374
  156.4 2.2 %collective-permute-start.7 = (bf16[4,128,2048]{2,1,0:T(8,128)(2,1)}, bf16[4,128,2048]{2,1,0:T(8,128)(2,1)S(1)}, u32[]{:S(2)}, u32[]{:S(2)}) collective-permute-start(bf16[4,128,2048]{2,1,0:T(8,128)(2,1)} %get-tuple-element.34), channel_id=1, source_target_pairs={{0,32},{32,0},{1,33},{33,1},{2,34},{34,2},{3,35},{35,3},{4,36},{36... | collective-permute-start | bytes 6291464 | tf_op jit(solution)/shard_map/ppermute | solution.py:554
  158.6 4.2 %all-to-all-start.9 = ((bf16[32,32,512]{2,1,0:T(8,128)(2,1)}), bf16[32,32,512]{2,1,0:T(8,128)(2,1)S(1)}, u32[]{:S(2)}, u32[]{:S(2)}) async-start(bf16[32,32,512]{2,1,0:T(8,128)(2,1)} %bitcast.12), calls=%async_computation.9 | async-start | bytes 2097152 | tf_op jit(solution)/shard_map/all_to_all | solution.py:601
  164.0 1.6 shard_map.90
  166.0 2.4 %collective-permute-start.12 = (bf16[64,2048]{1,0:T(8,128)(2,1)S(1)}, bf16[64,2048]{1,0:T(8,128)(2,1)S(1)}, u32[]{:S(2)}, u32[]{:S(2)}) collective-permute-start(bf16[64,2048]{1,0:T(8,128)(2,1)S(1)} %get-tuple-element.43), channel_id=1, source_target_pairs={{64,0},{128,64},{192,128},{0,192},{65,1},{129,65},{193,129},{1,193... | collective-permute-start | bytes 786440 | tf_op jit(solution)/shard_map/ppermute | solution.py:566
  168.5 2.8 %shard_map.88 = (bf16[64,2048]{1,0:T(8,128)(2,1)S(1)}, bf16[64,2048]{1,0:T(8,128)(2,1)S(1)}, f32[64,2048]{1,0:T(8,128)S(1)}, f32[64,2048]{1,0:T(8,128)S(1)}) custom-call(s32[2]{0:T(128)S(1)} %pad_add_fusion.1.place_ref, f32[4,128,2048]{2,1,0:T(8,128)} %get-tuple-element.33.refs_0_.refs_3_, bf16[4,128,2048]{2,1,0:T(8,128)(2,1)S(1)} %collective-permute-done.7.refs_1_.refs_4_, ...), custom_call_target="tpu_custom_call" | custom-call | flops 1000000000 | bytes 2621440 | tf_op jit(solution)/shard_map/pallas_call | solution.py:465
  171.4 2.7 %collective-permute-start.9 = (bf16[64,2048]{1,0:T(8,128)(2,1)S(1)}, bf16[64,2048]{1,0:T(8,128)(2,1)S(1)}, u32[]{:S(2)}, u32[]{:S(2)}) collective-permute-start(bf16[64,2048]{1,0:T(8,128)(2,1)S(1)} %get-tuple-element.38), channel_id=1, source_target_pairs={{64,0},{128,64},{192,128},{0,192},{65,1},{129,65},{193,129},{1,193... | collective-permute-start | bytes 786440 | tf_op jit(solution)/shard_map/ppermute | solution.py:566
  174.9 2.7 %collective-permute-start.14 = (bf16[64,2048]{1,0:T(8,128)(2,1)S(1)}, bf16[64,2048]{1,0:T(8,128)(2,1)S(1)}, u32[]{:S(2)}, u32[]{:S(2)}) collective-permute-start(bf16[64,2048]{1,0:T(8,128)(2,1)S(1)} %get-tuple-element.45), channel_id=1, source_target_pairs={{64,0},{128,64},{192,128},{0,192},{65,1},{129,65},{193,129},{1,193... | collective-permute-start | bytes 786440 | tf_op jit(solution)/shard_map/ppermute | solution.py:566
  177.5 2.1 %collective-permute-done.10.refs_7_ = bf16[64,2048]{1,0:T(8,128)(2,1)S(1)} collective-permute-done((bf16[64,2048]{1,0:T(8,128)(2,1)S(1)}, bf16[64,2048]{1,0:T(8,128)(2,1)S(1)}, u32[]{:S(2)}, u32[]{:S(2)}) %collective-permute-start.10) | collective-permute-done | bytes 262176 | tf_op jit(solution)/shard_map/ppermute | solution.py:563
  179.7 1.7 shard_map.89.sum_ref
  181.3 4.0 %collective-permute-done.13.lower_ref = bf16[64,2048]{1,0:T(8,128)(2,1)S(1)} collective-permute-done((bf16[64,2048]{1,0:T(8,128)(2,1)S(1)}, bf16[64,2048]{1,0:T(8,128)(2,1)S(1)}, u32[]{:S(2)}, u32[]{:S(2)}) %collective-permute-start.13) | collective-permute-done | bytes 262176 | tf_op jit(solution)/shard_map/ppermute | solution.py:563
  186.4 3.7 %all-to-all-done.9 = bf16[32,32,512]{2,1,0:T(8,128)(2,1)S(1)} async-done(((bf16[32,32,512]{2,1,0:T(8,128)(2,1)}), bf16[32,32,512]{2,1,0:T(8,128)(2,1)S(1)}, u32[]{:S(2)}, u32[]{:S(2)}) %all-to-all-start.9) | async-done | bytes 1048608 | tf_op jit(solution)/shard_map/all_to_all | solution.py:601
  (55 shorter events, 14.0 us)
Async XLA Ops:
  2.5 14.5 %collective-permute-start = (bf16[1024,128]{1,0:T(8,128)(2,1)S(1)}, bf16[1024,128]{1,0:T(8,128)(2,1)S(1)}, u32[]{:S(2)}, u32[]{:S(2)}) collective-permute-start(bf16[1024,128]{1,0:T(8,128)(2,1)S(1)} %get-tuple-element.26), channel_id=1, source_target_pairs={{0,1},{1,2},{2,3},{3,0},{4,5},{5,6},{6,7},{7,4},{8,9},{9,10},{10,1... | collective-permute-start | bytes 786440 | tf_op jit(solution)/shard_map/ppermute | solution.py:504
  4.7 13.9 %collective-permute-start.1 = (bf16[1024,128]{1,0:T(8,128)(2,1)S(1)}, bf16[1024,128]{1,0:T(8,128)(2,1)S(1)}, u32[]{:S(2)}, u32[]{:S(2)}) collective-permute-start(bf16[1024,128]{1,0:T(8,128)(2,1)S(1)} %get-tuple-element.26), channel_id=1, source_target_pairs={{0,2},{1,3},{2,0},{3,1},{4,6},{5,7},{6,4},{7,5},{8,10},{9,11},{10,... | collective-permute-start | bytes 786440 | tf_op jit(solution)/shard_map/ppermute | solution.py:504
  7.3 11.3 %collective-permute-start.2 = (bf16[1024,128]{1,0:T(8,128)(2,1)S(1)}, bf16[1024,128]{1,0:T(8,128)(2,1)S(1)}, u32[]{:S(2)}, u32[]{:S(2)}) collective-permute-start(bf16[1024,128]{1,0:T(8,128)(2,1)S(1)} %get-tuple-element.26), channel_id=1, source_target_pairs={{0,3},{1,0},{2,1},{3,2},{4,7},{5,4},{6,5},{7,6},{8,11},{9,8},{10,9... | collective-permute-start | bytes 786440 | tf_op jit(solution)/shard_map/ppermute | solution.py:504
  8.4 19.9 %all-to-all-start = ((bf16[32,40,128]{2,1,0:T(8,128)(2,1)}), bf16[32,40,128]{2,1,0:T(8,128)(2,1)S(1)}, u32[]{:S(2)}, u32[]{:S(2)}) async-start(bf16[32,40,128]{2,1,0:T(8,128)(2,1)} %get-tuple-element.25), calls=%async_computation | async-start | bytes 655360 | tf_op jit(solution)/shard_map/all_to_all | solution.py:497
  18.7 10.3 %copy-start.1 = (bf16[1024,128]{1,0:T(8,128)(2,1)S(1)}, bf16[1024,128]{1,0:T(8,128)(2,1)}, u32[]{:S(2)}) copy-start(bf16[1024,128]{1,0:T(8,128)(2,1)} %w_in_ref.3) | copy-start | bytes 786436
  18.7 10.3 %copy-start.2 = (bf16[128,1024]{1,0:T(8,128)(2,1)S(1)}, bf16[128,1024]{1,0:T(8,128)(2,1)}, u32[]{:S(2)}) copy-start(bf16[128,1024]{1,0:T(8,128)(2,1)} %w_out_ref.3) | copy-start | bytes 786436
  18.7 10.3 %collective-permute-start.3 = (bf16[3,1024,128]{2,1,0:T(8,128)(2,1)S(1)}, bf16[3,1024,128]{2,1,0:T(8,128)(2,1)S(1)}, u32[]{:S(2)}, u32[]{:S(2)}) collective-permute-start(bf16[3,1024,128]{2,1,0:T(8,128)(2,1)S(1)} %shard_map.78.shares_ref), channel_id=1, source_target_pairs={{0,32},{32,0},{1,33},{33,1},{2,34},{34,2},{3,35},{35,3},{4,36},{36... | collective-permute-start | bytes 2359304 | tf_op jit(solution)/shard_map/ppermute | solution.py:508
  30.8 12.7 %all-to-all-start.1 = ((bf16[8,16,1024]{2,1,0:T(8,128)(2,1)}), bf16[8,16,1024]{2,1,0:T(8,128)(2,1)S(1)}, u32[]{:S(2)}, u32[]{:S(2)}) async-start(bf16[8,16,1024]{2,1,0:T(8,128)(2,1)} %bitcast.10), calls=%async_computation.1 | async-start | bytes 524288 | tf_op jit(solution)/shard_map/all_to_all | solution.py:38
  55.9 10.0 %collective-permute-start.4 = (bf16[128,1024]{1,0:T(8,128)(2,1)S(1)}, bf16[128,1024]{1,0:T(8,128)(2,1)S(1)}, u32[]{:S(2)}, u32[]{:S(2)}) collective-permute-start(bf16[128,1024]{1,0:T(8,128)(2,1)S(1)} %bitcast.24), channel_id=1, source_target_pairs={{0,1},{1,2},{2,3},{3,0},{4,5},{5,6},{6,7},{7,4},{8,9},{9,10},{10,1... | collective-permute-start | bytes 786440 | tf_op jit(solution)/shard_map/ppermute | solution.py:541
  56.8 9.1 %collective-permute-start.5 = (bf16[128,1024]{1,0:T(8,128)(2,1)S(1)}, bf16[128,1024]{1,0:T(8,128)(2,1)S(1)}, u32[]{:S(2)}, u32[]{:S(2)}) collective-permute-start(bf16[128,1024]{1,0:T(8,128)(2,1)S(1)} %bitcast.25), channel_id=1, source_target_pairs={{0,3},{1,0},{2,1},{3,2},{4,7},{5,4},{6,5},{7,6},{8,11},{9,8},{10,9... | collective-permute-start | bytes 786440 | tf_op jit(solution)/shard_map/ppermute | solution.py:541
  58.6 7.5 %collective-permute-start.6 = (bf16[128,1024]{1,0:T(8,128)(2,1)S(1)}, bf16[128,1024]{1,0:T(8,128)(2,1)S(1)}, u32[]{:S(2)}, u32[]{:S(2)}) collective-permute-start(bf16[128,1024]{1,0:T(8,128)(2,1)S(1)} %bitcast.26), channel_id=1, source_target_pairs={{0,2},{1,3},{2,0},{3,1},{4,6},{5,7},{6,4},{7,5},{8,10},{9,11},{10,... | collective-permute-start | bytes 786440 | tf_op jit(solution)/shard_map/ppermute | solution.py:541
  60.2 2.2 %copy-start = (bf16[2048,1024]{1,0:T(8,128)(2,1)S(1)}, bf16[2048,1024]{1,0:T(8,128)(2,1)}, u32[]{:S(2)}) copy-start(bf16[2048,1024]{1,0:T(8,128)(2,1)} %proto_ref.1) | copy-start | bytes 12582916
  65.9 3.6 %copy-start.3 = (bf16[2048,1024]{1,0:T(8,128)(2,1)}, bf16[2048,1024]{1,0:T(8,128)(2,1)S(1)}, u32[]{:S(2)}) copy-start(bf16[2048,1024]{1,0:T(8,128)(2,1)S(1)} %get-tuple-element.27.rest_4_.unit_hbm) | copy-start | bytes 12582916
  156.4 7.6 %collective-permute-start.7 = (bf16[4,128,2048]{2,1,0:T(8,128)(2,1)}, bf16[4,128,2048]{2,1,0:T(8,128)(2,1)S(1)}, u32[]{:S(2)}, u32[]{:S(2)}) collective-permute-start(bf16[4,128,2048]{2,1,0:T(8,128)(2,1)} %get-tuple-element.34), channel_id=1, source_target_pairs={{0,32},{32,0},{1,33},{33,1},{2,34},{34,2},{3,35},{35,3},{4,36},{36... | collective-permute-start | bytes 6291464 | tf_op jit(solution)/shard_map/ppermute | solution.py:554
  158.6 31.4 %all-to-all-start.9 = ((bf16[32,32,512]{2,1,0:T(8,128)(2,1)}), bf16[32,32,512]{2,1,0:T(8,128)(2,1)S(1)}, u32[]{:S(2)}, u32[]{:S(2)}) async-start(bf16[32,32,512]{2,1,0:T(8,128)(2,1)} %bitcast.12), calls=%async_computation.9 | async-start | bytes 2097152 | tf_op jit(solution)/shard_map/all_to_all | solution.py:601
  162.8 1.3 collective-permute-start.8
  165.6 9.0 %collective-permute-start.11 = (bf16[64,2048]{1,0:T(8,128)(2,1)S(1)}, bf16[64,2048]{1,0:T(8,128)(2,1)S(1)}, u32[]{:S(2)}, u32[]{:S(2)}) collective-permute-start(bf16[64,2048]{1,0:T(8,128)(2,1)S(1)} %get-tuple-element.42), channel_id=1, source_target_pairs={{0,64},{64,128},{128,192},{192,0},{1,65},{65,129},{129,193},{193,1... | collective-permute-start | bytes 786440 | tf_op jit(solution)/shard_map/ppermute | solution.py:563
  166.0 8.6 %collective-permute-start.12 = (bf16[64,2048]{1,0:T(8,128)(2,1)S(1)}, bf16[64,2048]{1,0:T(8,128)(2,1)S(1)}, u32[]{:S(2)}, u32[]{:S(2)}) collective-permute-start(bf16[64,2048]{1,0:T(8,128)(2,1)S(1)} %get-tuple-element.43), channel_id=1, source_target_pairs={{64,0},{128,64},{192,128},{0,192},{65,1},{129,65},{193,129},{1,193... | collective-permute-start | bytes 786440 | tf_op jit(solution)/shard_map/ppermute | solution.py:566
  171.3 8.4 %collective-permute-start.10 = (bf16[64,2048]{1,0:T(8,128)(2,1)S(1)}, bf16[64,2048]{1,0:T(8,128)(2,1)S(1)}, u32[]{:S(2)}, u32[]{:S(2)}) collective-permute-start(bf16[64,2048]{1,0:T(8,128)(2,1)S(1)} %get-tuple-element.39), channel_id=1, source_target_pairs={{0,64},{64,128},{128,192},{192,0},{1,65},{65,129},{129,193},{193,1... | collective-permute-start | bytes 786440 | tf_op jit(solution)/shard_map/ppermute | solution.py:563
  171.4 8.3 %collective-permute-start.9 = (bf16[64,2048]{1,0:T(8,128)(2,1)S(1)}, bf16[64,2048]{1,0:T(8,128)(2,1)S(1)}, u32[]{:S(2)}, u32[]{:S(2)}) collective-permute-start(bf16[64,2048]{1,0:T(8,128)(2,1)S(1)} %get-tuple-element.38), channel_id=1, source_target_pairs={{64,0},{128,64},{192,128},{0,192},{65,1},{129,65},{193,129},{1,193... | collective-permute-start | bytes 786440 | tf_op jit(solution)/shard_map/ppermute | solution.py:566
  174.8 10.5 %collective-permute-start.13 = (bf16[64,2048]{1,0:T(8,128)(2,1)S(1)}, bf16[64,2048]{1,0:T(8,128)(2,1)S(1)}, u32[]{:S(2)}, u32[]{:S(2)}) collective-permute-start(bf16[64,2048]{1,0:T(8,128)(2,1)S(1)} %get-tuple-element.44), channel_id=1, source_target_pairs={{0,64},{64,128},{128,192},{192,0},{1,65},{65,129},{129,193},{193,1... | collective-permute-start | bytes 786440 | tf_op jit(solution)/shard_map/ppermute | solution.py:563
  174.9 10.4 %collective-permute-start.14 = (bf16[64,2048]{1,0:T(8,128)(2,1)S(1)}, bf16[64,2048]{1,0:T(8,128)(2,1)S(1)}, u32[]{:S(2)}, u32[]{:S(2)}) collective-permute-start(bf16[64,2048]{1,0:T(8,128)(2,1)S(1)} %get-tuple-element.45), channel_id=1, source_target_pairs={{64,0},{128,64},{192,128},{0,192},{65,1},{129,65},{193,129},{1,193... | collective-permute-start | bytes 786440 | tf_op jit(solution)/shard_map/ppermute | solution.py:566

commit v13 on v12

--- a/solution.py
+++ b/solution.py
@@ -306,8 +306,8 @@
 
 def grad_kernel(
     core_ref, image_ref, soft_ref, mass_ref, unit_hbm, embed_ref,
-    radial_ref, away_hbm, stay_hbm, terms_ref,
-    unit_ref, away_ref, stay_ref, embed_t_ref, load_sems, away_sems, stay_sems,
+    radial_ref, away_hbm, grad_hbm, embed_t_ref, terms_ref,
+    unit_ref, away_ref, grad_ref, load_sems, away_sems, grad_sems,
 ):
     rows, protos = embed_ref.shape[0], unit_ref.shape[0]
     loads = []
@@ -347,13 +347,13 @@
         shape = away_ref.shape[:2] + (WIDE,)
         away = jnp.dot(embed_t_ref[0], grad, preferred_element_type=f32).astype(bf16)
         away_ref[:, :, part] = away.reshape(shape)
-        stay = jnp.dot(embed_t_ref[1], grad, preferred_element_type=f32)
-        stay_ref[:, :, part] = stay.reshape(shape)
-        for ref, hbm, sems in (
-            (away_ref, away_hbm, away_sems),
-            (stay_ref, stay_hbm, stay_sems),
+        grad_ref[:, part] = grad
+        for store in (
+            pltpu.make_async_copy(
+                away_ref.at[:, :, part], away_hbm.at[:, :, part], away_sems.at[n]
+            ),
+            pltpu.make_async_copy(grad_ref.at[:, part], grad_hbm.at[:, part], grad_sems.at[n]),
         ):
-            store = pltpu.make_async_copy(ref.at[:, :, part], hbm.at[:, :, part], sems.at[n])
             store.start()
             stores.append(store)
         term = jnp.dot(grad, unit, preferred_element_type=f32)
@@ -374,18 +374,18 @@
     return pl.pallas_call(
         grad_kernel,
         in_specs=[SMEM, VMEM, VMEM, VMEM, anywhere, VMEM],
-        out_specs=[VMEM, anywhere, anywhere, VMEM],
+        out_specs=[VMEM, anywhere, anywhere, VMEM, VMEM],
         out_shape=[
             jax.ShapeDtypeStruct((1, protos), f32),
             pltpu.HBM((blocks, LANES, protos), bf16),
-            pltpu.HBM((blocks, LANES, protos), f32),
-            jax.ShapeDtypeStruct((D, rows), bf16),
+            pltpu.HBM((rows, protos), bf16),
+            jax.ShapeDtypeStruct((2, depth, rows), bf16),
+            pltpu.HBM((D, rows), bf16),
         ],
         scratch_shapes=[
             pltpu.VMEM((protos, D), bf16),
             pltpu.VMEM((blocks, LANES, protos), bf16),
-            pltpu.VMEM((blocks, LANES, protos), f32),
-            pltpu.VMEM((2, depth, rows), bf16),
+            pltpu.VMEM((rows, protos), bf16),
             pltpu.SemaphoreType.DMA((protos // TILE,)),
             pltpu.SemaphoreType.DMA((steps,)),
             pltpu.SemaphoreType.DMA((steps,)),
@@ -397,6 +397,33 @@
             transcendentals=rows * protos,
         ),
     )(core.reshape(1), images, softs, masses, keep_hbm(unit), embed)
+
+
+def stay_kernel(embed_t_ref, grad_ref, out_ref):
+    stay = jnp.dot(embed_t_ref[0], grad_ref[...], preferred_element_type=f32)
+    out_ref[...] = stay.reshape(out_ref.shape)
+
+
+def stay_pass(embed_t, grad):
+    _, depth, rows = embed_t.shape
+    protos = grad.shape[1]
+    blocks = depth // LANES
+    return pl.pallas_call(
+        stay_kernel,
+        grid=(protos // TILE,),
+        in_specs=[
+            pl.BlockSpec((1, depth, rows), lambda i: (1, 0, 0)),
+            pl.BlockSpec((rows, TILE), lambda i: (0, i)),
+        ],
+        out_specs=pl.BlockSpec((blocks, LANES, TILE), lambda i: (0, 0, i)),
+        out_shape=pltpu.HBM((blocks, LANES, protos), f32),
+        compiler_params=pltpu.CompilerParams(
+            dimension_semantics=("arbitrary",), vmem_limit_bytes=10 * 1024 * 1024
+        ),
+        cost_estimate=pl.CostEstimate(
+            flops=2 * depth * rows * protos, bytes_accessed=6 * rows * protos, transcendentals=0
+        ),
+    )(embed_t, keep_hbm(grad))
 
 
 def pair_rows(refs, rows, part):
@@ -550,7 +577,8 @@
         masses = lax.all_to_all(proto_pass(images, base, row_parts), ROWS, 0, 0)
         images = lax.all_to_all(image_pass(masses, base, col_count), COLS, 0, 0)
 
-    radial, away, stay, embed_terms = grad_pass(core, images, softs, masses, unit, embed)
+    radial, away, grad, embed_t, embed_terms = grad_pass(core, images, softs, masses, unit, embed)
+    stay = stay_pass(embed_t, grad)
     arrived = lax.ppermute(away, "core", swap)
     parts = (stay, arrived, turned)
     lines = (radial, lax.ppermute(radial, "core", swap), proto_len)

time: 192 us -> 193 us (level)
  waiting for transfers between devices: 30.3 us -> 25.3 us
  Pallas kernels: 31.5 us -> 35.2 us
    pallas_call x0 -> x1, Pallas kernels: none -> 5.02 us  [stay_pass(): pl.pallas_call(stay_kernel, grid=(protos // TILE,), in_specs=[pl.BlockSpe...]
    all_to_all x1, waiting for transfers between devices: 3.69 us -> 0.01 us  [body(): lax.all_to_all(embed_terms.reshape(col_count, local_width, row_count), CO...]
  transfers between devices with their start and end apart: 18 -> 18, of which waited for: 9 -> 7; matrix products, arithmetic and copies ran while one was open for 0% -> 0% of each run, Pallas kernels for 6% -> 8%
where the time goes in v13:
time: 193 us; the launch traced here: 192 us
  blocking collectives  85.1 us (44%)
  starting transfers between devices  39.2 us (20%)
  Pallas kernels  35.2 us (18%)
  waiting for transfers between devices  25.3 us (13%)
  local copies, waits for them, and re-layouts  3.16 us (2%)
  other arithmetic  2.36 us (1%)
    all_to_all x2, blocking collectives, body(): images = lax.all_to_all(image_pass(masses, base, col_count), COLS, 0, 0)  23.6 us
    all_to_all x2, blocking collectives, body(): masses = lax.all_to_all(proto_pass(images, base, row_parts), ROWS, 0, 0)  19.9 us
    all_to_all x1, blocking collectives, body(): masses = lax.all_to_all(masses, ROWS, 0, 0)  16.7 us
    all_to_all x1, blocking collectives, body(): lax.all_to_all(image_pass(masses, base, col_count, soft_part), COLS, 0, 0)  13.1 us
    pallas_call x11, Pallas kernels, call(): pl.pallas_call(kernel, in_specs=[SMEM] * len(scalars) + [VMEM] * len(arra...  12.6 us
    all_to_all x1, blocking collectives, gather_all(): return lax.all_to_all(copies, axes, 0, 0)  11.7 us
    pallas_call x1, Pallas kernels, grad_pass(): pl.pallas_call(grad_kernel, in_specs=[SMEM, VMEM, VMEM, VMEM, anywhere, V...  9.67 us
    all_to_all x1, waiting for transfers between devices, scatter_sum(): return jnp.sum(lax.all_to_all(blocks, axes, 0, 0).astype(f32), axis=0)  9.16 us
  transfers between devices with their start and end apart: 18, of which 7 were waited for; matrix products, arithmetic and copies ran while one was open for 0% of the time, Pallas kernels for 8%

profile of v13, /device:TPU:1, one launch (start us, length us, event | category | flops | bytes accessed | tf_op | source)
XLA Modules:
  0.0 191.6 jit_solution(16204783116728947412)
XLA Ops:
  0.6 1.9 shard_map.77
  2.5 2.1 %collective-permute-start = (bf16[1024,128]{1,0:T(8,128)(2,1)S(1)}, bf16[1024,128]{1,0:T(8,128)(2,1)S(1)}, u32[]{:S(2)}, u32[]{:S(2)}) collective-permute-start(bf16[1024,128]{1,0:T(8,128)(2,1)S(1)} %get-tuple-element.27), channel_id=1, source_target_pairs={{0,1},{1,2},{2,3},{3,0},{4,5},{5,6},{6,7},{7,4},{8,9},{9,10},{10,1... | collective-permute-start | bytes 786440 | tf_op jit(solution)/shard_map/ppermute | solution.py:531
  4.7 2.6 %collective-permute-start.1 = (bf16[1024,128]{1,0:T(8,128)(2,1)S(1)}, bf16[1024,128]{1,0:T(8,128)(2,1)S(1)}, u32[]{:S(2)}, u32[]{:S(2)}) collective-permute-start(bf16[1024,128]{1,0:T(8,128)(2,1)S(1)} %get-tuple-element.27), channel_id=1, source_target_pairs={{0,2},{1,3},{2,0},{3,1},{4,6},{5,7},{6,4},{7,5},{8,10},{9,11},{10,... | collective-permute-start | bytes 786440 | tf_op jit(solution)/shard_map/ppermute | solution.py:531
  8.4 8.7 %all-to-all-start = ((bf16[32,40,128]{2,1,0:T(8,128)(2,1)}), bf16[32,40,128]{2,1,0:T(8,128)(2,1)S(1)}, u32[]{:S(2)}, u32[]{:S(2)}) async-start(bf16[32,40,128]{2,1,0:T(8,128)(2,1)} %get-tuple-element.26), calls=%async_computation | async-start | bytes 655360 | tf_op jit(solution)/shard_map/all_to_all | solution.py:524
  18.7 1.6 collective-permute-start.3
  20.3 7.9 %all-to-all-done = bf16[32,40,128]{2,1,0:T(8,128)(2,1)S(1)} async-done(((bf16[32,40,128]{2,1,0:T(8,128)(2,1)}), bf16[32,40,128]{2,1,0:T(8,128)(2,1)S(1)}, u32[]{:S(2)}, u32[]{:S(2)}) %all-to-all-start) | async-done | bytes 327712 | tf_op jit(solution)/shard_map/all_to_all | solution.py:524
  29.0 1.8 shard_map.79
  30.8 3.4 %all-to-all-start.1 = ((bf16[8,16,1024]{2,1,0:T(8,128)(2,1)}), bf16[8,16,1024]{2,1,0:T(8,128)(2,1)S(1)}, u32[]{:S(2)}, u32[]{:S(2)}) async-start(bf16[8,16,1024]{2,1,0:T(8,128)(2,1)} %bitcast.10), calls=%async_computation.1 | async-start | bytes 524288 | tf_op jit(solution)/shard_map/all_to_all | solution.py:38
  34.3 9.2 %all-to-all-done.1 = bf16[8,16,1024]{2,1,0:T(8,128)(2,1)S(1)} async-done(((bf16[8,16,1024]{2,1,0:T(8,128)(2,1)}), bf16[8,16,1024]{2,1,0:T(8,128)(2,1)S(1)}, u32[]{:S(2)}, u32[]{:S(2)}) %all-to-all-start.1) | async-done | bytes 262176 | tf_op jit(solution)/shard_map/all_to_all | solution.py:38
  44.2 11.7 %all_to_all.50 = bf16[8,16,1024]{2,1,0:T(8,128)(2,1)S(1)} all-to-all(bf16[8,16,1024]{2,1,0:T(8,128)(2,1)S(1)} %broadcast_in_dim.2), channel_id=1, replica_groups=mesh['x'=4,'core'=2,'z'=8,'y'=4] {'z'}, dimensions={0} | all-to-all | bytes 524288 | tf_op jit(solution)/shard_map/all_to_all | solution.py:30
  56.8 1.8 collective-permute-start.5
  60.2 2.2 %copy-done = bf16[2048,1024]{1,0:T(8,128)(2,1)S(1)} copy-done((bf16[2048,1024]{1,0:T(8,128)(2,1)S(1)}, bf16[2048,1024]{1,0:T(8,128)(2,1)}, u32[]{:S(2)}) %copy-start) | copy-done | bytes 4194328
  62.3 3.4 %shard_map.80 = (bf16[2048,1024]{1,0:T(8,128)(2,1)S(1)}, f32[1,2048]{1,0:T(1,128)S(1)}, bf16[4,128,2048]{2,1,0:T(8,128)(2,1)}) custom-call(s32[1]{0:T(128)} %bitcast.core_ref, bf16[2048,1024]{1,0:T(8,128)(2,1)S(1)} %copy-done), custom_call_target="tpu_custom_call" | custom-call | flops 12582912 | bytes 10485760 | tf_op jit(solution)/shard_map/pallas_call | solution.py:59
  66.0 3.4 %shard_map.81 = (bf16[512,2048]{1,0:T(8,128)(2,1)S(1)}, f32[8,2,2048]{2,1,0:T(2,128)S(1)}, f32[1,512]{1,0:T(1,128)S(1)}, bf16[512,1024]{1,0:T(8,128)(2,1)S(1)}) custom-call(s32[4]{0:T(128)S(1)} %pad_add_fusion.place_ref, bf16[128,1024]{1,0:T(8,128)(2,1)S(1)} %bitcast.27, bf16[128,1024]{1,0:T(8,128)(2,1)S(1)} %collective-permute-done.4.rest_1_, ...), custom_call_target="tpu_custom_call" | custom-call | flops 2147483648 | bytes 8388608 | tf_op jit(solution)/shard_map/pallas_call | solution.py:59
  69.5 16.7 %all_to_all.51.mass_ref = f32[8,2,2048]{2,1,0:T(2,128)S(1)} all-to-all(f32[8,2,2048]{2,1,0:T(2,128)S(1)} %get-tuple-element.29), channel_id=1, replica_groups=mesh['x'=4,'core'=2,'z'=8,'y'=4] {'x','core'}, dimensions={0} | all-to-all | bytes 262144 | tf_op jit(solution)/shard_map/all_to_all | solution.py:574
  86.8 13.1 %all_to_all.52.image_ref.soft_ref = f32[32,1,1024]{2,1,0:T(1,128)S(1)} all-to-all(f32[32,1,1024]{2,1,0:T(1,128)S(1)} %shard_map.82), channel_id=1, replica_groups=mesh['x'=4,'core'=2,'z'=8,'y'=4] {'z','y'}, dimensions={0} | all-to-all | bytes 262144 | tf_op jit(solution)/shard_map/all_to_all | solution.py:575
  100.4 10.0 %all_to_all.53.mass_ref = f32[8,2,2048]{2,1,0:T(2,128)S(1)} all-to-all(f32[8,2,2048]{2,1,0:T(2,128)S(1)} %shard_map.83), channel_id=1, replica_groups=mesh['x'=4,'core'=2,'z'=8,'y'=4] {'x','core'}, dimensions={0} | all-to-all | bytes 262144 | tf_op jit(solution)/shard_map/all_to_all | solution.py:577
  110.9 11.8 %all_to_all.54.image_ref = f32[32,1,512]{2,1,0:T(1,128)S(1)} all-to-all(f32[32,1,512]{2,1,0:T(1,128)S(1)} %shard_map.84), channel_id=1, replica_groups=mesh['x'=4,'core'=2,'z'=8,'y'=4] {'z','y'}, dimensions={0} | all-to-all | bytes 131072 | tf_op jit(solution)/shard_map/all_to_all | solution.py:578
  123.3 9.9 %all_to_all.55.mass_ref = f32[8,2,2048]{2,1,0:T(2,128)S(1)} all-to-all(f32[8,2,2048]{2,1,0:T(2,128)S(1)} %shard_map.85), channel_id=1, replica_groups=mesh['x'=4,'core'=2,'z'=8,'y'=4] {'x','core'}, dimensions={0} | all-to-all | bytes 262144 | tf_op jit(solution)/shard_map/all_to_all | solution.py:577
  133.7 11.8 %all_to_all.56.image_ref = f32[32,1,512]{2,1,0:T(1,128)S(1)} all-to-all(f32[32,1,512]{2,1,0:T(1,128)S(1)} %shard_map.86), channel_id=1, replica_groups=mesh['x'=4,'core'=2,'z'=8,'y'=4] {'z','y'}, dimensions={0} | all-to-all | bytes 131072 | tf_op jit(solution)/shard_map/all_to_all | solution.py:578
  145.6 9.7 %shard_map.87 = (f32[1,2048]{1,0:T(1,128)S(1)}, bf16[4,128,2048]{2,1,0:T(8,128)(2,1)}, bf16[512,2048]{1,0:T(8,128)(2,1)}, bf16[2,512,512]{2,1,0:T(8,128)(2,1)S(1)}, bf16[1024,512]{1,0:T(8,128)(2,1)}) custom-call(s32[1]{0:T(128)} %bitcast.core_ref, f32[32,1,512]{2,1,0:T(1,128)S(1)} %all_to_all.56.image_ref, f32[32,1,1024]{2,1,0:T(1,128)S(1)} %all_to_all.52.image_ref.soft_ref, ...), custom_call_target="tpu_custom_call" | custom-call | flops 4294967296 | bytes 10485760 | tf_op jit(solution)/shard_map/pallas_call | solution.py:374
  155.3 2.2 %collective-permute-start.7 = (bf16[4,128,2048]{2,1,0:T(8,128)(2,1)}, bf16[4,128,2048]{2,1,0:T(8,128)(2,1)S(1)}, u32[]{:S(2)}, u32[]{:S(2)}) collective-permute-start(bf16[4,128,2048]{2,1,0:T(8,128)(2,1)} %get-tuple-element.36), channel_id=1, source_target_pairs={{0,32},{32,0},{1,33},{33,1},{2,34},{34,2},{3,35},{35,3},{4,36},{36... | collective-permute-start | bytes 6291464 | tf_op jit(solution)/shard_map/ppermute | solution.py:582
  157.4 4.7 %all-to-all-start.9 = ((bf16[32,32,512]{2,1,0:T(8,128)(2,1)}), bf16[32,32,512]{2,1,0:T(8,128)(2,1)}, u32[]{:S(2)}, u32[]{:S(2)}) async-start(bf16[32,32,512]{2,1,0:T(8,128)(2,1)} %bitcast.30), calls=%async_computation.9 | async-start | bytes 2097152 | tf_op jit(solution)/shard_map/all_to_all | solution.py:629
  162.5 5.0 %shard_map.88.refs_0_.refs_3_ = f32[4,128,2048]{2,1,0:T(8,128)} custom-call(bf16[2,512,512]{2,1,0:T(8,128)(2,1)S(1)} %get-tuple-element.34.embed_t_ref, bf16[512,2048]{1,0:T(8,128)(2,1)} %get-tuple-element.35.grad_ref), custom_call_target="tpu_custom_call" | custom-call | flops 1073741824 | bytes 6291456 | tf_op jit(solution)/shard_map/pallas_call | solution.py:411
  167.5 1.6 shard_map.91
  169.5 2.4 %collective-permute-start.12 = (bf16[64,2048]{1,0:T(8,128)(2,1)S(1)}, bf16[64,2048]{1,0:T(8,128)(2,1)S(1)}, u32[]{:S(2)}, u32[]{:S(2)}) collective-permute-start(bf16[64,2048]{1,0:T(8,128)(2,1)S(1)} %get-tuple-element.45), channel_id=1, source_target_pairs={{64,0},{128,64},{192,128},{0,192},{65,1},{129,65},{193,129},{1,193... | collective-permute-start | bytes 786440 | tf_op jit(solution)/shard_map/ppermute | solution.py:594
  171.9 2.8 %shard_map.89 = (bf16[64,2048]{1,0:T(8,128)(2,1)S(1)}, bf16[64,2048]{1,0:T(8,128)(2,1)S(1)}, f32[64,2048]{1,0:T(8,128)S(1)}, f32[64,2048]{1,0:T(8,128)S(1)}) custom-call(s32[2]{0:T(128)S(1)} %pad_add_fusion.1.place_ref, f32[4,128,2048]{2,1,0:T(8,128)} %shard_map.88.refs_0_.refs_3_, bf16[4,128,2048]{2,1,0:T(8,128)(2,1)S(1)} %collective-permute-done.7.refs_1_.refs_4_, ...), custom_call_target="tpu_custom_call" | custom-call | flops 1000000000 | bytes 2621440 | tf_op jit(solution)/shard_map/pallas_call | solution.py:492
  174.8 2.7 %collective-permute-start.9 = (bf16[64,2048]{1,0:T(8,128)(2,1)S(1)}, bf16[64,2048]{1,0:T(8,128)(2,1)S(1)}, u32[]{:S(2)}, u32[]{:S(2)}) collective-permute-start(bf16[64,2048]{1,0:T(8,128)(2,1)S(1)} %get-tuple-element.40), channel_id=1, source_target_pairs={{64,0},{128,64},{192,128},{0,192},{65,1},{129,65},{193,129},{1,193... | collective-permute-start | bytes 786440 | tf_op jit(solution)/shard_map/ppermute | solution.py:594
  178.1 2.7 %collective-permute-start.14 = (bf16[64,2048]{1,0:T(8,128)(2,1)S(1)}, bf16[64,2048]{1,0:T(8,128)(2,1)S(1)}, u32[]{:S(2)}, u32[]{:S(2)}) collective-permute-start(bf16[64,2048]{1,0:T(8,128)(2,1)S(1)} %get-tuple-element.47), channel_id=1, source_target_pairs={{64,0},{128,64},{192,128},{0,192},{65,1},{129,65},{193,129},{1,193... | collective-permute-start | bytes 786440 | tf_op jit(solution)/shard_map/ppermute | solution.py:594
  180.7 2.2 %collective-permute-done.10.refs_7_ = bf16[64,2048]{1,0:T(8,128)(2,1)S(1)} collective-permute-done((bf16[64,2048]{1,0:T(8,128)(2,1)S(1)}, bf16[64,2048]{1,0:T(8,128)(2,1)S(1)}, u32[]{:S(2)}, u32[]{:S(2)}) %collective-permute-start.10) | collective-permute-done | bytes 262176 | tf_op jit(solution)/shard_map/ppermute | solution.py:591
  182.9 1.7 shard_map.90.sum_ref
  184.6 4.0 %collective-permute-done.13.lower_ref = bf16[64,2048]{1,0:T(8,128)(2,1)S(1)} collective-permute-done((bf16[64,2048]{1,0:T(8,128)(2,1)S(1)}, bf16[64,2048]{1,0:T(8,128)(2,1)S(1)}, u32[]{:S(2)}, u32[]{:S(2)}) %collective-permute-start.13) | collective-permute-done | bytes 262176 | tf_op jit(solution)/shard_map/ppermute | solution.py:591
  (56 shorter events, 14.1 us)
Async XLA Ops:
  2.5 14.5 %collective-permute-start = (bf16[1024,128]{1,0:T(8,128)(2,1)S(1)}, bf16[1024,128]{1,0:T(8,128)(2,1)S(1)}, u32[]{:S(2)}, u32[]{:S(2)}) collective-permute-start(bf16[1024,128]{1,0:T(8,128)(2,1)S(1)} %get-tuple-element.27), channel_id=1, source_target_pairs={{0,1},{1,2},{2,3},{3,0},{4,5},{5,6},{6,7},{7,4},{8,9},{9,10},{10,1... | collective-permute-start | bytes 786440 | tf_op jit(solution)/shard_map/ppermute | solution.py:531
  4.7 13.9 %collective-permute-start.1 = (bf16[1024,128]{1,0:T(8,128)(2,1)S(1)}, bf16[1024,128]{1,0:T(8,128)(2,1)S(1)}, u32[]{:S(2)}, u32[]{:S(2)}) collective-permute-start(bf16[1024,128]{1,0:T(8,128)(2,1)S(1)} %get-tuple-element.27), channel_id=1, source_target_pairs={{0,2},{1,3},{2,0},{3,1},{4,6},{5,7},{6,4},{7,5},{8,10},{9,11},{10,... | collective-permute-start | bytes 786440 | tf_op jit(solution)/shard_map/ppermute | solution.py:531
  7.3 11.3 %collective-permute-start.2 = (bf16[1024,128]{1,0:T(8,128)(2,1)S(1)}, bf16[1024,128]{1,0:T(8,128)(2,1)S(1)}, u32[]{:S(2)}, u32[]{:S(2)}) collective-permute-start(bf16[1024,128]{1,0:T(8,128)(2,1)S(1)} %get-tuple-element.27), channel_id=1, source_target_pairs={{0,3},{1,0},{2,1},{3,2},{4,7},{5,4},{6,5},{7,6},{8,11},{9,8},{10,9... | collective-permute-start | bytes 786440 | tf_op jit(solution)/shard_map/ppermute | solution.py:531
  8.4 19.9 %all-to-all-start = ((bf16[32,40,128]{2,1,0:T(8,128)(2,1)}), bf16[32,40,128]{2,1,0:T(8,128)(2,1)S(1)}, u32[]{:S(2)}, u32[]{:S(2)}) async-start(bf16[32,40,128]{2,1,0:T(8,128)(2,1)} %get-tuple-element.26), calls=%async_computation | async-start | bytes 655360 | tf_op jit(solution)/shard_map/all_to_all | solution.py:524
  18.7 10.3 %copy-start.1 = (bf16[1024,128]{1,0:T(8,128)(2,1)S(1)}, bf16[1024,128]{1,0:T(8,128)(2,1)}, u32[]{:S(2)}) copy-start(bf16[1024,128]{1,0:T(8,128)(2,1)} %w_in_ref.3) | copy-start | bytes 786436
  18.7 10.3 %copy-start.2 = (bf16[128,1024]{1,0:T(8,128)(2,1)S(1)}, bf16[128,1024]{1,0:T(8,128)(2,1)}, u32[]{:S(2)}) copy-start(bf16[128,1024]{1,0:T(8,128)(2,1)} %w_out_ref.3) | copy-start | bytes 786436
  18.7 10.3 %collective-permute-start.3 = (bf16[3,1024,128]{2,1,0:T(8,128)(2,1)S(1)}, bf16[3,1024,128]{2,1,0:T(8,128)(2,1)S(1)}, u32[]{:S(2)}, u32[]{:S(2)}) collective-permute-start(bf16[3,1024,128]{2,1,0:T(8,128)(2,1)S(1)} %shard_map.78.shares_ref), channel_id=1, source_target_pairs={{0,32},{32,0},{1,33},{33,1},{2,34},{34,2},{3,35},{35,3},{4,36},{36... | collective-permute-start | bytes 2359304 | tf_op jit(solution)/shard_map/ppermute | solution.py:535
  30.8 12.7 %all-to-all-start.1 = ((bf16[8,16,1024]{2,1,0:T(8,128)(2,1)}), bf16[8,16,1024]{2,1,0:T(8,128)(2,1)S(1)}, u32[]{:S(2)}, u32[]{:S(2)}) async-start(bf16[8,16,1024]{2,1,0:T(8,128)(2,1)} %bitcast.10), calls=%async_computation.1 | async-start | bytes 524288 | tf_op jit(solution)/shard_map/all_to_all | solution.py:38
  55.9 10.0 %collective-permute-start.4 = (bf16[128,1024]{1,0:T(8,128)(2,1)S(1)}, bf16[128,1024]{1,0:T(8,128)(2,1)S(1)}, u32[]{:S(2)}, u32[]{:S(2)}) collective-permute-start(bf16[128,1024]{1,0:T(8,128)(2,1)S(1)} %bitcast.24), channel_id=1, source_target_pairs={{0,1},{1,2},{2,3},{3,0},{4,5},{5,6},{6,7},{7,4},{8,9},{9,10},{10,1... | collective-permute-start | bytes 786440 | tf_op jit(solution)/shard_map/ppermute | solution.py:568
  56.8 9.1 %collective-permute-start.5 = (bf16[128,1024]{1,0:T(8,128)(2,1)S(1)}, bf16[128,1024]{1,0:T(8,128)(2,1)S(1)}, u32[]{:S(2)}, u32[]{:S(2)}) collective-permute-start(bf16[128,1024]{1,0:T(8,128)(2,1)S(1)} %bitcast.25), channel_id=1, source_target_pairs={{0,3},{1,0},{2,1},{3,2},{4,7},{5,4},{6,5},{7,6},{8,11},{9,8},{10,9... | collective-permute-start | bytes 786440 | tf_op jit(solution)/shard_map/ppermute | solution.py:568
  58.6 7.5 %collective-permute-start.6 = (bf16[128,1024]{1,0:T(8,128)(2,1)S(1)}, bf16[128,1024]{1,0:T(8,128)(2,1)S(1)}, u32[]{:S(2)}, u32[]{:S(2)}) collective-permute-start(bf16[128,1024]{1,0:T(8,128)(2,1)S(1)} %bitcast.26), channel_id=1, source_target_pairs={{0,2},{1,3},{2,0},{3,1},{4,6},{5,7},{6,4},{7,5},{8,10},{9,11},{10,... | collective-permute-start | bytes 786440 | tf_op jit(solution)/shard_map/ppermute | solution.py:568
  60.2 2.2 %copy-start = (bf16[2048,1024]{1,0:T(8,128)(2,1)S(1)}, bf16[2048,1024]{1,0:T(8,128)(2,1)}, u32[]{:S(2)}) copy-start(bf16[2048,1024]{1,0:T(8,128)(2,1)} %proto_ref.1) | copy-start | bytes 12582916
  65.8 3.7 %copy-start.3 = (bf16[2048,1024]{1,0:T(8,128)(2,1)}, bf16[2048,1024]{1,0:T(8,128)(2,1)S(1)}, u32[]{:S(2)}) copy-start(bf16[2048,1024]{1,0:T(8,128)(2,1)S(1)} %get-tuple-element.28.rest_4_.unit_hbm) | copy-start | bytes 12582916
  155.3 12.3 %collective-permute-start.7 = (bf16[4,128,2048]{2,1,0:T(8,128)(2,1)}, bf16[4,128,2048]{2,1,0:T(8,128)(2,1)S(1)}, u32[]{:S(2)}, u32[]{:S(2)}) collective-permute-start(bf16[4,128,2048]{2,1,0:T(8,128)(2,1)} %get-tuple-element.36), channel_id=1, source_target_pairs={{0,32},{32,0},{1,33},{33,1},{2,34},{34,2},{3,35},{35,3},{4,36},{36... | collective-permute-start | bytes 6291464 | tf_op jit(solution)/shard_map/ppermute | solution.py:582
  157.4 32.1 %all-to-all-start.9 = ((bf16[32,32,512]{2,1,0:T(8,128)(2,1)}), bf16[32,32,512]{2,1,0:T(8,128)(2,1)}, u32[]{:S(2)}, u32[]{:S(2)}) async-start(bf16[32,32,512]{2,1,0:T(8,128)(2,1)} %bitcast.30), calls=%async_computation.9 | async-start | bytes 2097152 | tf_op jit(solution)/shard_map/all_to_all | solution.py:629
  162.2 5.4 %collective-permute-start.8 = (f32[1,2048]{1,0:T(1,128)S(1)}, f32[1,2048]{1,0:T(1,128)S(1)}, u32[]{:S(2)}, u32[]{:S(2)}) collective-permute-start(f32[1,2048]{1,0:T(1,128)S(1)} %get-tuple-element.38.refs_6_.refs_3_), channel_id=1, source_target_pairs={{0,32},{32,0},{1,33},{33,1},{2,34},{34,2},{3,35},{35,3},{4,36},{36... | collective-permute-start | bytes 24584 | tf_op jit(solution)/shard_map/ppermute | solution.py:584
  169.1 8.8 %collective-permute-start.11 = (bf16[64,2048]{1,0:T(8,128)(2,1)S(1)}, bf16[64,2048]{1,0:T(8,128)(2,1)S(1)}, u32[]{:S(2)}, u32[]{:S(2)}) collective-permute-start(bf16[64,2048]{1,0:T(8,128)(2,1)S(1)} %get-tuple-element.44), channel_id=1, source_target_pairs={{0,64},{64,128},{128,192},{192,0},{1,65},{65,129},{129,193},{193,1... | collective-permute-start | bytes 786440 | tf_op jit(solution)/shard_map/ppermute | solution.py:591
  169.5 8.4 %collective-permute-start.12 = (bf16[64,2048]{1,0:T(8,128)(2,1)S(1)}, bf16[64,2048]{1,0:T(8,128)(2,1)S(1)}, u32[]{:S(2)}, u32[]{:S(2)}) collective-permute-start(bf16[64,2048]{1,0:T(8,128)(2,1)S(1)} %get-tuple-element.45), channel_id=1, source_target_pairs={{64,0},{128,64},{192,128},{0,192},{65,1},{129,65},{193,129},{1,193... | collective-permute-start | bytes 786440 | tf_op jit(solution)/shard_map/ppermute | solution.py:594
  174.8 8.1 %collective-permute-start.10 = (bf16[64,2048]{1,0:T(8,128)(2,1)S(1)}, bf16[64,2048]{1,0:T(8,128)(2,1)S(1)}, u32[]{:S(2)}, u32[]{:S(2)}) collective-permute-start(bf16[64,2048]{1,0:T(8,128)(2,1)S(1)} %get-tuple-element.41), channel_id=1, source_target_pairs={{0,64},{64,128},{128,192},{192,0},{1,65},{65,129},{129,193},{193,1... | collective-permute-start | bytes 786440 | tf_op jit(solution)/shard_map/ppermute | solution.py:591
  174.8 8.1 %collective-permute-start.9 = (bf16[64,2048]{1,0:T(8,128)(2,1)S(1)}, bf16[64,2048]{1,0:T(8,128)(2,1)S(1)}, u32[]{:S(2)}, u32[]{:S(2)}) collective-permute-start(bf16[64,2048]{1,0:T(8,128)(2,1)S(1)} %get-tuple-element.40), channel_id=1, source_target_pairs={{64,0},{128,64},{192,128},{0,192},{65,1},{129,65},{193,129},{1,193... | collective-permute-start | bytes 786440 | tf_op jit(solution)/shard_map/ppermute | solution.py:594
  178.0 10.5 %collective-permute-start.13 = (bf16[64,2048]{1,0:T(8,128)(2,1)S(1)}, bf16[64,2048]{1,0:T(8,128)(2,1)S(1)}, u32[]{:S(2)}, u32[]{:S(2)}) collective-permute-start(bf16[64,2048]{1,0:T(8,128)(2,1)S(1)} %get-tuple-element.46), channel_id=1, source_target_pairs={{0,64},{64,128},{128,192},{192,0},{1,65},{65,129},{129,193},{193,1... | collective-permute-start | bytes 786440 | tf_op jit(solution)/shard_map/ppermute | solution.py:591
  178.1 10.4 %collective-permute-start.14 = (bf16[64,2048]{1,0:T(8,128)(2,1)S(1)}, bf16[64,2048]{1,0:T(8,128)(2,1)S(1)}, u32[]{:S(2)}, u32[]{:S(2)}) collective-permute-start(bf16[64,2048]{1,0:T(8,128)(2,1)S(1)} %get-tuple-element.47), channel_id=1, source_target_pairs={{64,0},{128,64},{192,128},{0,192},{65,1},{129,65},{193,129},{1,193... | collective-permute-start | bytes 786440 | tf_op jit(solution)/shard_map/ppermute | solution.py:594
